TPU v7x, 32 devices: a whole 2x2x4 slice. The times are simulated.
32 devices in a mesh: groups: 2 (over y), dom: 8 (over z, x), edge: 2 (over core).
Axes of the slice: x: 2, y: 2, z: 4, core: 2. Of those that a mesh axis runs over, the one named last changes fastest.
Arguments:
- entities: float32 [400, 4096], P(None, ('groups', 'dom')), parts along dimension 1, may hold values from -2.5 to 2.5
- entity_state: float32 [4096], P(('groups', 'dom')), parts along dimension 0, may hold values from 0.1 to 1
- relations: float32 [400, 4096], P(None, 'groups'), parts along dimension 1, may hold values from -4 to 4
- relation_state: float32 [4096], P('groups'), parts along dimension 0, may hold values from 0.1 to 1
- src_rows: int32 [6, 128, 128], P(None, ('groups', 'dom', 'edge')), parts along dimension 1, may hold values from 0 to 255
- rel_ids: int32 [6, 128, 128], P(None, ('groups', 'dom', 'edge')), parts along dimension 1, may hold values from 0 to 2047
- dst_rows: int32 [6, 128, 128], P(None, ('groups', 'dom', 'edge')), parts along dimension 1, may hold values from 0 to 255
- counts: int32 [6, 128], P(None, ('groups', 'dom', 'edge')), parts along dimension 1, may hold values from 1 to 128
- neg_blocks: int32 [6, 128], P(None, ('groups', 'dom', 'edge')), parts along dimension 1, may hold values from 0 to 3
Outputs:
- new_entities: float32 [400, 4096], P(None, ('groups', 'dom')), parts along dimension 1
- new_entity_state: float32 [4096], P(('groups', 'dom')), parts along dimension 0
- new_relations: float32 [400, 4096], P(None, 'groups'), parts along dimension 1
- new_relation_state: float32 [4096], P('groups'), parts along dimension 0
There are 2 independent parts, one for each index of `groups`. A program takes and returns all parts, laid end to end along the dimension named above; each array names one. Nothing has to cross between parts.
All inputs are finite; a program needn't handle non-finite values.
Results may differ from a plain program's by a relative error of at most 0.0024.
Values may be sent and summed in bfloat16 or wider, within the bound.
No kernel may reach another device: no remote copies, remote signals or barrier semaphores. Data moves between devices by JAX's collectives and lax.ppermute only.
A program may use at most 128 MiB of HBM per device.

v0:
```python
import functools

import jax
import jax.numpy as jnp
from jax import lax
from jax.experimental import pallas as pl
from jax.experimental.pallas import tpu as pltpu
from jax.sharding import PartitionSpec as P

learn_rate = 0.1
BF = jnp.bfloat16
F32 = jnp.float32
VMEM_LIMIT = 24 * 1024 * 1024
NN = (((1,), (0,)), ((), ()))
NT = (((1,), (1,)), ((), ()))
TN = (((0,), (0,)), ((), ()))


def mm(a, b, dims=NN):
    return lax.dot_general(a, b, dims, preferred_element_type=F32)


def vmem():
    return pl.BlockSpec(memory_space=pltpu.VMEM)


def smem():
    return pl.BlockSpec(memory_space=pltpu.SMEM)


def anywhere():
    return pl.BlockSpec(memory_space=pl.ANY)


def in_hbm(x):
    return pltpu.with_memory_space_constraint(x, pltpu.HBM)


def cost(flops, size):
    return pl.CostEstimate(flops=flops, bytes_accessed=size, transcendentals=0)


def params():
    return pltpu.CompilerParams(vmem_limit_bytes=VMEM_LIMIT)


def shifted(x, by):
    n = lax.axis_size("dom")
    return lax.ppermute(x, "dom", [(i, (i + by) % n) for i in range(n)])


def swapped(x, bits):
    n = lax.axis_size("dom")
    return lax.ppermute(x, "dom", [(i, i ^ bits) for i in range(n)])


def across(x):
    return lax.ppermute(x, "edge", [(0, 1), (1, 0)])


def one_hot(rows_ref, t, count, base):
    blocks, width = rows_ref.shape[1:]
    at = lax.broadcasted_iota(jnp.int32, (count, width), 0)
    idx = rows_ref[t]
    return jnp.concatenate(
        [
            jnp.where(at == base(idx[b : b + 1, :]), 1.0, 0.0).astype(BF)
            for b in range(blocks)
        ],
        axis=1,
    )


def relvec_kernel(t, ids_ref, rel_ref, out_ref):
    rels = rel_ref.shape[1]
    tile = min(rels, 512)
    out = None
    for lo in range(0, rels, tile):
        hot = one_hot(ids_ref, t, tile, lambda i, lo=lo: i - lo)
        part = mm(rel_ref[:, lo : lo + tile], hot)
        out = part if out is None else out + part
    out_ref[...] = out.astype(BF)


def relvec(t, rel_ids, rel16):
    width, rels = rel16.shape
    slots = rel_ids.shape[1] * rel_ids.shape[2]
    return pl.pallas_call(
        functools.partial(relvec_kernel, t),
        in_specs=[vmem()] * 2,
        out_specs=vmem(),
        out_shape=jax.ShapeDtypeStruct((width, slots), BF),
        compiler_params=params(),
        cost_estimate=cost(width * slots, width * slots),
        name="relvec",
    )(rel_ids, rel16)


def relsum_kernel(t, first, ids_ref, drel_ref, *refs):
    step = pl.program_id(0)
    out_ref = refs[-1]
    tile = out_ref.shape[1]
    hot = one_hot(ids_ref, t, tile, lambda i: i - step * tile)
    part = mm(drel_ref[...], hot, NT)
    out_ref[...] = part if first else refs[0][...] + part


def relsum(t, rel_ids, drel, acc, rels):
    width, slots = drel.shape
    tile = min(rels, 512)
    wide = pl.BlockSpec((width, tile), lambda i: (0, i))
    ins = [rel_ids, drel] + ([] if acc is None else [acc])
    return pl.pallas_call(
        functools.partial(relsum_kernel, t, acc is None),
        grid=(rels // tile,),
        in_specs=[
            pl.BlockSpec(rel_ids.shape, lambda i: (0, 0, 0)),
            pl.BlockSpec((width, slots), lambda i: (0, 0)),
        ]
        + ([] if acc is None else [wide]),
        out_specs=wide,
        out_shape=jax.ShapeDtypeStruct((width, rels), F32),
        input_output_aliases={} if acc is None else {2: 0},
        compiler_params=params(),
        cost_estimate=cost(width * slots, width * slots),
        name="relsum",
    )(*ins)


class Limits:
    scratch = lambda shape: [
        pltpu.SMEM((shape[1], shape[0]), jnp.int32),
        pltpu.SMEM((shape[1], shape[0]), jnp.int32),
        pltpu.SemaphoreType.DMA((2,)),
    ]

    def __init__(self, t, from_cnt, from_neg, cnt, neg, sems):
        self.t, self.cnt, self.neg = t, cnt, neg
        self.copies = [
            pltpu.make_async_copy(from_cnt, cnt, sems.at[0]),
            pltpu.make_async_copy(from_neg, neg, sems.at[1]),
        ]
        for copy in self.copies:
            copy.start()

    def wait(self):
        for copy in self.copies:
            copy.wait()

    def count(self, b):
        return self.cnt[b, self.t]

    def negative(self, b):
        return self.neg[b, self.t]


def place():
    dom = lax.axis_index("dom")
    return dom // 2, lax.rem(dom, 2), lax.axis_index("edge")


def localize(edge, half):
    def local(idx):
        moved = idx + edge * half
        return jnp.where(moved >= 2 * half, moved - 2 * half, moved)

    return local


def halves(x):
    hd = x.shape[0] // 2
    return x[:hd], x[hd:]


def make_query(source, rel):
    (s_re, s_im), (w_re, w_im) = halves(source), halves(rel)
    return jnp.concatenate(
        [s_re * w_re - s_im * w_im, s_re * w_im + s_im * w_re], axis=0
    ).astype(BF)


def conj_times(dq, v):
    (dq_re, dq_im), (v_re, v_im) = halves(dq), halves(v)
    return jnp.concatenate(
        [dq_re * v_re + dq_im * v_im, dq_im * v_re - dq_re * v_im], axis=0
    ).astype(BF)


def positive_factors(shape, limits, query, target):
    _, blocks, width = shape
    pos = jnp.sum(query.astype(F32) * target, axis=0, keepdims=True)
    lane = lax.broadcasted_iota(jnp.int32, (1, width), 1)
    valid = jnp.concatenate(
        [jnp.where(lane < limits.count(b), 1.0, 0.0) for b in range(blocks)], axis=1
    )
    return -jax.nn.sigmoid(-pos) * valid


def target_side(shape, limits, query, query_t, target, o_ref, w_ref):
    _, blocks, width = shape
    lanes = lambda b: pl.ds(pl.multiple_of(b * width, width), width)
    count = limits.count
    o_ref[...] = target.astype(BF)
    limits.wait()
    gpos = positive_factors(shape, limits, query, target)
    row_i = lax.broadcasted_iota(jnp.int32, (width, width), 0)
    col_j = lax.broadcasted_iota(jnp.int32, (width, width), 1)
    for b in range(blocks):
        nb = limits.negative(b)
        neg = o_ref[:, lanes(nb)]
        at = slice(b * width, (b + 1) * width)
        scores = mm(query[:, at], neg, TN) if query_t is None else mm(query_t[at], neg)
        keep = jnp.logical_and(row_i < count(b), col_j < count(nb))
        w_ref[:, at] = jnp.where(keep, jax.nn.sigmoid(scores) / width, 0.0).astype(BF)
    return gpos


def target_terms(shape, limits, query, gpos, w_ref, d_ref):
    _, blocks, width = shape
    d_ref[...] = gpos * query.astype(F32)
    for b in range(blocks):
        at = slice(b * width, (b + 1) * width)
        to = pl.ds(pl.multiple_of(limits.negative(b) * width, width), width)
        d_ref[:, to] += mm(query[:, at], w_ref[:, at])
    return d_ref[...].astype(BF)


def make_dquery(shape, limits, gpos, o_ref, w_ref):
    _, blocks, width = shape
    lanes = lambda b: pl.ds(pl.multiple_of(b * width, width), width)
    out = []
    for b in range(blocks):
        nb = limits.negative(b)
        at = slice(b * width, (b + 1) * width)
        own = gpos[:, at] * o_ref[:, at].astype(F32)
        out.append(own + mm(o_ref[:, lanes(nb)], w_ref[:, at], NT))
    return jnp.concatenate(out, axis=1)


def first_kernel(
    shape, cnt_ref, neg_ref, src_ref, dst_ref, ids_ref, ent_ref, state_ref, rel_ref,
    g_mine, g_other, drel_ref, rel16_ref, ent_mine, state_mine,
    cnt, neg, lim_sems, src, dst, ids, ent, state, rel_buf, o_scr, d_scr, w_scr, in_sems, sems,
):
    rels = rel_buf.shape[1]
    tile = min(rels, 512)
    spans = range(0, rels, tile)
    inputs = [
        pltpu.make_async_copy(there, here, in_sems.at[i])
        for i, (there, here) in enumerate(
            [(src_ref.at[:1], src), (dst_ref.at[:1], dst), (ids_ref.at[:1], ids), (ent_ref, ent), (state_ref, state)]
        )
    ]
    loads = [
        pltpu.make_async_copy(
            rel_ref.at[:, lo : lo + tile], rel_buf.at[:, lo : lo + tile], sems.at[i]
        )
        for i, lo in enumerate(spans)
    ]
    for load in inputs:
        load.start()
    limits = Limits(0, cnt_ref, neg_ref, cnt, neg, lim_sems)
    for load in loads:
        load.start()
    half = ent.shape[1] // 2
    _, _, edge = place()
    local = localize(edge, half)
    inputs[0].wait()
    s_hot = one_hot(src, 0, 2 * half, local)
    inputs[1].wait()
    d_hot = one_hot(dst, 0, 2 * half, local)
    inputs[2].wait()
    ids_hot = [one_hot(ids, 0, tile, lambda i, lo=lo: i - lo) for lo in spans]
    inputs[3].wait()
    inputs[4].wait()
    mine = pl.ds(pl.multiple_of(edge * half, half), half)
    ent_mine[...] = ent[:, mine]
    state_mine[...] = state[:, mine]
    table = jnp.concatenate(
        [ent[:, pl.ds(pl.multiple_of(h * half, half), half)].astype(BF) for h in (edge, 1 - edge)],
        axis=1,
    )
    source = mm(table, s_hot)
    target = mm(table, d_hot)
    rel = None
    for load, lo, hot in zip(loads, spans, ids_hot):
        load.wait()
        low = rel_buf[:, lo : lo + tile].astype(BF)
        rel16_ref[:, lo : lo + tile] = low
        part = mm(low, hot)
        rel = part if rel is None else rel + part
    query = make_query(source, rel)
    gpos = target_side(shape, limits, query, None, target, o_scr, w_scr)
    dq = make_dquery(shape, limits, gpos, o_scr, w_scr)
    drel_ref[...] = conj_times(dq, source)
    total = mm(conj_times(dq, rel), s_hot, NT) + mm(
        target_terms(shape, limits, query, gpos, w_scr, d_scr), d_hot, NT
    )
    g_mine[...] = total[:, :half]
    g_other[...] = total[:, half:].astype(BF)


def first_round(cnt, neg, src, dst, rel_ids, entities, state, relations):
    dim, rows = entities.shape
    rels = relations.shape[1]
    _, blocks, width = src.shape
    slots = blocks * width
    sds = jax.ShapeDtypeStruct
    return pl.pallas_call(
        functools.partial(first_kernel, src.shape),
        in_specs=[anywhere()] * 8,
        out_specs=[vmem()] * 6,
        out_shape=[
            sds((dim, rows // 2), F32),
            sds((dim, rows // 2), BF),
            sds((dim, slots), BF),
            sds((dim, rels), BF),
            sds((dim, rows // 2), F32),
            sds((1, rows // 2), F32),
        ],
        scratch_shapes=Limits.scratch(src.shape)
        + [
            pltpu.VMEM((1, blocks, width), jnp.int32),
            pltpu.VMEM((1, blocks, width), jnp.int32),
            pltpu.VMEM((1, blocks, width), jnp.int32),
            pltpu.VMEM((dim, rows), F32),
            pltpu.VMEM((1, rows), F32),
            pltpu.VMEM((dim, rels), F32),
            pltpu.VMEM((dim, slots), BF),
            pltpu.VMEM((dim, slots), F32),
            pltpu.VMEM((width, slots), BF),
            pltpu.SemaphoreType.DMA((5,)),
            pltpu.SemaphoreType.DMA((-(-rels // min(rels, 512)),)),
        ],
        compiler_params=params(),
        cost_estimate=cost(2 * dim * slots * (rels + 4 * rows), 8 * dim * rels),
        name="first_round",
    )(*(in_hbm(x) for x in (cnt, neg, src, dst, rel_ids, entities, state, relations)))


def source_kernel(
    t, shape, cnt_ref, neg_ref, src_ref, dst_ref, own0, own1, rel_ref,
    query_ref, query_t_ref, source_ref, s_hot_ref, d_hot_ref, d_hot_t_ref,
    v_hot_t_ref, n_hot_ref, n_hot_t_ref, mask_ref, cnt, neg, sems,
):
    limits = Limits(t, cnt_ref, neg_ref, cnt, neg, sems)
    _, blocks, width = shape
    half = own0.shape[1]
    local = localize(place()[2], half)
    s_hot = one_hot(src_ref, t, 2 * half, local)
    d_hot = one_hot(dst_ref, t, 2 * half, local)
    s_hot_ref[...] = s_hot
    d_hot_ref[...] = d_hot
    d_hot_t_ref[...] = d_hot.T
    source = mm(jnp.concatenate([own0[...], own1[...]], axis=1), s_hot)
    source_ref[...] = source.astype(BF)
    query = make_query(source, rel_ref[...].astype(F32))
    query_ref[...] = query
    query_t_ref[...] = query.T
    limits.wait()
    row_i = lax.broadcasted_iota(jnp.int32, (width, width), 0)
    col_j = lax.broadcasted_iota(jnp.int32, (width, width), 1)
    slot = lax.broadcasted_iota(jnp.int32, (width, 2 * half), 0)
    for b in range(blocks):
        nb = limits.negative(b)
        at = slice(b * width, (b + 1) * width)
        there = pl.ds(pl.multiple_of(nb * width, width), width)
        n_hot_ref[:, at] = d_hot_ref[:, there]
        n_hot_t_ref[at] = d_hot_t_ref[there, :]
        keep = jnp.logical_and(row_i < limits.count(b), col_j < limits.count(nb))
        mask_ref[:, at] = jnp.where(keep, 1.0 / width, 0.0)
        hot = d_hot_t_ref[at].astype(F32)
        v_hot_t_ref[at] = jnp.where(slot < limits.count(b), hot, 0.0).astype(BF)


def source_side(t, shape, cnt, neg, src, dst, own, rel):
    dim, slots = rel.shape
    width = shape[2]
    rows = 2 * own[0].shape[1]
    sds = lambda *shape: jax.ShapeDtypeStruct(shape, BF)
    return pl.pallas_call(
        functools.partial(source_kernel, t, shape),
        in_specs=[anywhere()] * 2 + [vmem()] * 5,
        out_specs=[vmem()] * 10,
        out_shape=[
            sds(dim, slots), sds(slots, dim), sds(dim, slots),
            sds(rows, slots), sds(rows, slots), sds(slots, rows),
            sds(slots, rows), sds(rows, slots), sds(slots, rows),
            jax.ShapeDtypeStruct((width, slots), F32),
        ],
        scratch_shapes=Limits.scratch(shape),
        compiler_params=params(),
        cost_estimate=cost(dim * slots, dim * slots),
        name="source_side",
    )(cnt, neg, src, dst, *own, rel)


def near_kernel(query_t_ref, far0, out_ref):
    out_ref[...] = mm(query_t_ref[...], far0[...])


def near_products(query_t, far0):
    slots, half = query_t.shape[0], far0.shape[1]
    return pl.pallas_call(
        near_kernel,
        in_specs=[vmem()] * 2,
        out_specs=vmem(),
        out_shape=jax.ShapeDtypeStruct((slots, half), F32),
        compiler_params=params(),
        cost_estimate=cost(slots * half, slots * half),
        name="near_products",
    )(query_t, far0)


def target_kernel(
    near, far1, query_ref, query_t_ref, v_hot_t_ref, n_hot_ref, n_hot_t_ref, mask_ref,
    gd_mine, gd_other, w_ref,
):
    width, slots = mask_ref.shape
    half = far1.shape[1]
    products = jnp.concatenate([near[...], mm(query_t_ref[...], far1[...])], axis=1)
    high = products.astype(BF)
    low = (products - high.astype(F32)).astype(BF)
    factors = []
    for lo in range(0, slots, width):
        at = slice(lo, lo + width)
        n_hot = n_hot_ref[:, at]
        scores = mm(high[at], n_hot) + mm(low[at], n_hot)
        weight = (jax.nn.sigmoid(scores) * mask_ref[:, at]).astype(BF)
        w_ref[:, at] = weight
        positive = jax.nn.sigmoid(-products[at]) * v_hot_t_ref[at].astype(F32)
        factors.append((mm(weight, n_hot_t_ref[at]) - positive).astype(BF))
    gd = mm(query_ref[...], jnp.concatenate(factors, axis=0))
    gd_mine[...] = gd[:, :half]
    gd_other[...] = gd[:, half:].astype(BF)


def target_grad(near, far1, query, query_t, v_hot_t, n_hot, n_hot_t, mask):
    dim, slots = query.shape
    half = far1.shape[1]
    sds = jax.ShapeDtypeStruct
    return pl.pallas_call(
        target_kernel,
        in_specs=[vmem()] * 8,
        out_specs=[vmem()] * 3,
        out_shape=[sds((dim, half), F32), sds((dim, half), BF), sds(mask.shape, BF)],
        compiler_params=params(),
        cost_estimate=cost(4 * dim * slots * half, 12 * dim * slots),
        name="target_grad",
    )(near, far1, query, query_t, v_hot_t, n_hot, n_hot_t, mask)


def source_grad_kernel(
    t, shape, cnt_ref, neg_ref, _, far0, far1, d_hot_ref, query_ref, w_ref, source_ref, rel_ref, s_hot_ref,
    gs_mine, gs_other, drel_ref, cnt, neg, sems, o_scr,
):
    limits = Limits(t, cnt_ref, neg_ref, cnt, neg, sems)
    half = gs_mine.shape[1]
    target = mm(jnp.concatenate([far0[...], far1[...]], axis=1), d_hot_ref[...])
    o_scr[...] = target.astype(BF)
    limits.wait()
    gpos = positive_factors(shape, limits, query_ref[...], target)
    dq = make_dquery(shape, limits, gpos, o_scr, w_ref)
    drel_ref[...] = conj_times(dq, source_ref[...].astype(F32))
    gs = mm(conj_times(dq, rel_ref[...].astype(F32)), s_hot_ref[...], NT)
    gs_mine[...] = gs[:, :half]
    gs_other[...] = gs[:, half:].astype(BF)


def source_grad(t, shape, cnt, neg, after, far, d_hot, query, weight, source, rel, s_hot):
    dim, slots = rel.shape
    half = s_hot.shape[0] // 2
    sds = jax.ShapeDtypeStruct
    return pl.pallas_call(
        functools.partial(source_grad_kernel, t, shape),
        in_specs=[anywhere()] * 3 + [vmem()] * 8,
        out_specs=[vmem()] * 3,
        out_shape=[sds((dim, half), F32), sds((dim, half), BF), sds((dim, slots), BF)],
        scratch_shapes=Limits.scratch(shape) + [pltpu.VMEM((dim, slots), BF)],
        compiler_params=params(),
        cost_estimate=cost(dim * slots, dim * slots),
        name="source_grad",
    )(cnt, neg, after, *far, d_hot, query, weight, source, rel, s_hot)


def last_kernel(
    t, shape, cnt_ref, neg_ref, far0, far1, query_ref, query_t_ref, d_hot_ref, source_ref, rel_ref,
    drel_ref, dsource_ref, dterm_ref, cnt, neg, sems, o_scr, d_scr, w_scr,
):
    limits = Limits(t, cnt_ref, neg_ref, cnt, neg, sems)
    far = jnp.concatenate([far0[...], far1[...]], axis=1)
    target = mm(far, d_hot_ref[...])
    query = query_ref[...]
    gpos = target_side(shape, limits, query, query_t_ref, target, o_scr, w_scr)
    dterm_ref[...] = target_terms(shape, limits, query, gpos, w_scr, d_scr)
    dq = make_dquery(shape, limits, gpos, o_scr, w_scr)
    drel_ref[...] = conj_times(dq, source_ref[...].astype(F32))
    dsource_ref[...] = conj_times(dq, rel_ref[...].astype(F32))


def last_terms(t, shape, cnt, neg, far, query, query_t, d_hot, source, rel):
    dim, slots = query.shape
    sds = jax.ShapeDtypeStruct
    return pl.pallas_call(
        functools.partial(last_kernel, t, shape),
        in_specs=[anywhere()] * 2 + [vmem()] * 7,
        out_specs=[vmem()] * 3,
        out_shape=[sds((dim, slots), BF)] * 3,
        scratch_shapes=Limits.scratch(shape)
        + [
            pltpu.VMEM((dim, slots), BF),
            pltpu.VMEM((dim, slots), F32),
            pltpu.VMEM((shape[2], slots), BF),
        ],
        compiler_params=params(),
        cost_estimate=cost(6 * dim * slots * shape[2], 12 * dim * slots),
        name="last_terms",
    )(cnt, neg, *far, query, query_t, d_hot, source, rel)


def both_kernel(_, dsource_ref, s_hot_ref, dterm_ref, d_hot_t_ref, gs_mine, gs_other, gd_mine, gd_other):
    half = gs_mine.shape[1]
    for terms, hot, dims, mine, other in (
        (dterm_ref, d_hot_t_ref, NN, gd_mine, gd_other),
        (dsource_ref, s_hot_ref, NT, gs_mine, gs_other),
    ):
        grad = mm(terms[...], hot[...], dims)
        mine[...] = grad[:, :half]
        other[...] = grad[:, half:].astype(BF)


def both_grads(after, dsource, s_hot, dterm, d_hot_t):
    dim, slots = dterm.shape
    half = s_hot.shape[0] // 2
    sds = jax.ShapeDtypeStruct
    return pl.pallas_call(
        both_kernel,
        in_specs=[anywhere()] + [vmem()] * 4,
        out_specs=[vmem()] * 4,
        out_shape=[sds((dim, half), F32), sds((dim, half), BF)] * 2,
        compiler_params=params(),
        cost_estimate=cost(8 * dim * slots * half, 12 * dim * slots),
        name="both_grads",
    )(after, dsource, s_hot, dterm, d_hot_t)


def update_kernel(n_grads, last, *refs):
    ent_ref, state_ref, grads = refs[0], refs[1], refs[2 : 2 + n_grads]
    grad = grads[0][...].astype(F32)
    for g in grads[1:]:
        grad = grad + g[...].astype(F32)
    dim = grad.shape[0]
    state = state_ref[...] + jnp.sum(grad * grad, axis=0, keepdims=True) / dim
    new = ent_ref[...] - grad * (learn_rate / jnp.sqrt(state))
    if last:
        refs[-1][:dim] = new
        refs[-1][dim:] = jnp.broadcast_to(state, (refs[-1].shape[0] - dim, state.shape[1]))
    else:
        refs[-3][...] = new
        refs[-2][...] = state
        refs[-1][...] = new.astype(BF)


def update(ent, state, grads, after, last=False):
    dim, half = ent.shape
    sds = jax.ShapeDtypeStruct
    outs = [sds((dim, half), F32), sds((1, half), F32), sds((dim, half), BF)]
    if last:
        outs = [sds((dim + 8, half), F32)]
    return pl.pallas_call(
        functools.partial(update_kernel, len(grads), last),
        in_specs=[vmem()] * (2 + len(grads)) + [anywhere()] * len(after),
        out_specs=[vmem()] * len(outs),
        out_shape=outs,
        compiler_params=params(),
        cost_estimate=cost(10 * dim * half, 16 * dim * half),
        name="update",
    )(ent, state, *grads, *after)


def pair_kernel(a_ref, b_ref, out_ref):
    out_ref[...] = (a_ref[...] + b_ref[...].astype(F32)).astype(out_ref.dtype)


def sum_pair(a, b, dtype=BF):
    return pl.pallas_call(
        pair_kernel,
        in_specs=[vmem()] * 2,
        out_specs=vmem(),
        out_shape=jax.ShapeDtypeStruct(a.shape, dtype),
        compiler_params=params(),
        name="sum_pair",
    )(a, b)


def held_kernel(x_ref, *refs):
    pass


def held(x, after):
    return pl.pallas_call(
        held_kernel,
        in_specs=[anywhere()] * (1 + len(after)),
        out_specs=anywhere(),
        out_shape=jax.ShapeDtypeStruct(x.shape, x.dtype),
        input_output_aliases={0: 0},
        compiler_params=params(),
        name="held",
    )(x, *after)


def whole_kernel(mine, theirs, ent_out, state_out, token):
    token[...] = jnp.zeros_like(token)
    dim, rows = ent_out.shape
    half = rows // 2
    edge = place()[2]
    for core, part in ((edge, mine), (1 - edge, theirs)):
        at = pl.ds(pl.multiple_of(core * half, half), half)
        ent_out[:, at] = part[:dim]
        state_out[:, at] = part[dim : dim + 1]


def whole_partition(mine, theirs):
    dim, half = mine.shape[0] - 8, mine.shape[1]
    return pl.pallas_call(
        whole_kernel,
        in_specs=[vmem()] * 2,
        out_specs=[vmem()] * 3,
        out_shape=[
            jax.ShapeDtypeStruct((dim, 2 * half), F32),
            jax.ShapeDtypeStruct((1, 2 * half), F32),
            jax.ShapeDtypeStruct((8, 128), F32),
        ],
        compiler_params=params(),
        name="whole_partition",
    )(mine, theirs)


def first_column(owner, core, w):
    return pl.multiple_of((2 * owner + core) * w, w)


def pieces_kernel(t, nz, same, ids_ref, drel_ref, acc_ref, *refs):
    mine, other = refs[-nz - 1 : -1], refs[-1]
    w = other.shape[2]
    z, x, edge = place()
    drel = drel_ref[...]
    for k in range(nz):
        owner = 2 * lax.bitwise_xor(z, k) + (x if same else 1 - x)
        at = [first_column(owner, core, w) for core in (edge, 1 - edge)]
        hot = jnp.concatenate([one_hot(ids_ref, t, w, lambda i, lo=lo: i - lo) for lo in at], axis=0)
        part = mm(drel, hot, NT)
        mine[k][...] = acc_ref[:, pl.ds(at[0], w)] + part[:, :w]
        other[k] = (acc_ref[:, pl.ds(at[1], w)] + part[:, w:]).astype(BF)


def pieces(t, n, same, rel_ids, drel, acc, after):
    dim, rels = acc.shape
    w = rels // (2 * n)
    sds = jax.ShapeDtypeStruct
    out = pl.pallas_call(
        functools.partial(pieces_kernel, t, n // 2, same),
        in_specs=[vmem()] * 3 + [anywhere()] * len(after),
        out_specs=[vmem()] * (n // 2 + 1),
        out_shape=[sds((dim, w), F32)] * (n // 2) + [sds((n // 2, dim, w), BF)],
        compiler_params=params(),
        cost_estimate=cost(dim * rels * drel.shape[1], 4 * dim * rels),
        name="pieces",
    )(rel_ids, drel, acc, *after)
    return out[:-1], out[-1]


def add_kernel(n, *refs):
    for k in range(n):
        refs[n + 1 + k][...] = (refs[k][...] + refs[n][k].astype(F32)).astype(BF)


def add_each(mine, theirs):
    n = len(mine)
    return pl.pallas_call(
        functools.partial(add_kernel, n),
        in_specs=[vmem()] * (n + 1),
        out_specs=[vmem()] * n,
        out_shape=[jax.ShapeDtypeStruct(x.shape, BF) for x in mine],
        compiler_params=params(),
        name="add_each",
    )(*mine, theirs)


def sum_kernel(k, count, mine, theirs, *refs):
    total = mine[...] + theirs[k].astype(F32)
    for r in refs[:count]:
        total = total + r[...].astype(F32)
    refs[-1][...] = total.astype(BF)


def sum_piece(k, mine, theirs, parts, after):
    return pl.pallas_call(
        functools.partial(sum_kernel, k, len(parts)),
        in_specs=[vmem()] * (2 + len(parts)) + [anywhere()] * len(after),
        out_specs=vmem(),
        out_shape=jax.ShapeDtypeStruct(mine.shape, BF),
        compiler_params=params(),
        name="sum_piece",
    )(mine, theirs, *parts, *after)


def stacked_kernel(*refs):
    for i in range(refs[-1].shape[0]):
        refs[-1][i] = refs[i][...]


def stacked(parts, after):
    return pl.pallas_call(
        stacked_kernel,
        in_specs=[vmem()] * len(parts) + [anywhere()] * len(after),
        out_specs=vmem(),
        out_shape=jax.ShapeDtypeStruct((len(parts), *parts[0].shape), parts[0].dtype),
        compiler_params=params(),
        name="stacked",
    )(*parts, *after)


def relnew_kernel(nz, same, ks, rel_ref, state_ref, *refs):
    mine, theirs = refs[: len(ks)], refs[len(ks)]
    rel_out, state_out, buf, sems = refs[-4:]
    w = mine[0].shape[1]
    state_out[...] = refs[len(ks) + (1 if same else 2)][...]
    z, x, edge = place()
    copies = []
    for i in range(2 * len(ks)):
        owner = 2 * lax.bitwise_xor(z, ks[i // 2]) + (x if same else 1 - x)
        at = pl.ds(first_column(owner, edge if i % 2 == 0 else 1 - edge, w), w)
        grad = (mine[i // 2][...] if i % 2 == 0 else theirs[i // 2]).astype(F32)
        state = state_ref[:, at] + jnp.sum(grad * grad, axis=0, keepdims=True) / grad.shape[0]
        state_out[:, at] = state
        buf[i] = rel_ref[:, at] - grad * (learn_rate / jnp.sqrt(state))
        copy = pltpu.make_async_copy(buf.at[i], rel_out.at[:, at], sems.at[i])
        copy.start()
        copies.append(copy)
    for copy in copies:
        copy.wait()


def relnew(nz, same, ks, relations, state, mine, theirs, before, after):
    dim, rels = relations.shape
    w = mine[0].shape[1]
    count = 2 * len(ks)
    start = [state] if before is None else list(before)
    return pl.pallas_call(
        functools.partial(relnew_kernel, nz, same, ks),
        in_specs=[vmem()] * (3 + len(ks))
        + ([anywhere()] if before else [])
        + [vmem()]
        + [anywhere()] * len(after),
        out_specs=[anywhere(), vmem()],
        out_shape=[jax.ShapeDtypeStruct((dim, rels), F32), jax.ShapeDtypeStruct((1, rels), F32)],
        input_output_aliases={3 + len(ks): 0} if before else {},
        scratch_shapes=[pltpu.VMEM((count, dim, w), F32), pltpu.SemaphoreType.DMA((count,))],
        compiler_params=params(),
        cost_estimate=cost(4 * dim * w * count, 4 * dim * w * count),
        name="relnew",
    )(relations, state, *mine, theirs, *start, *after)


def relation_update(t, rel_ids, drel, acc, relations, state, send, finish):
    n = lax.axis_size("dom")
    dim, rels = relations.shape
    if n < 4 or n & (n - 1) or rels % (256 * n):
        total = lax.psum(relsum(t, rel_ids, drel, acc, rels), ("dom", "edge"))
        state = state + jnp.mean(total * total, axis=0)
        return relations - learn_rate * total / jnp.sqrt(state)[None, :], state, finish(send(drel), [])
    nz = n // 2
    mine_x, other_x = pieces(t, n, False, rel_ids, drel, acc, [])
    grads = send(other_x)
    mine_s, other_s = pieces(t, n, True, rel_ids, drel, acc, [other_x])
    to_x = add_each(mine_x, across(other_x))
    theirs = across(other_s)
    down = range(nz - 1, -1, -1)
    from_x = {k: swapped(to_x[k], 1) for k in down}
    turned = {
        k: sum_piece(k, mine_s[k], theirs, [from_x[k]], grads[1:2] if k == nz - 1 else [])
        for k in down[:-1]
    }
    from_z = [swapped(turned[k], 2 * k) for k in down[:-1]]
    done = finish(grads, [turned[nz - 1]])
    summed = sum_piece(0, mine_s[0], theirs, [from_x[0]] + from_z, [])
    got = [summed if k == 0 else swapped(summed, 2 * k) for k in range(nz)]
    got_x = [swapped(piece, 1) for piece in got]
    state = state.reshape(1, rels)
    ks = [0, *down[:-1]]
    mine = [got[k] for k in ks]
    new = relnew(nz, True, ks, relations, state, mine, across(stacked(mine, [done[2]])), None, [])
    mine = [got_x[k] for k in ks]
    theirs = across(stacked(mine, []))
    rel_new, state_new = relnew(nz, False, ks, relations, state, mine, theirs, new, [])
    return rel_new, state_new.reshape(rels), done


def on_device(
    entities,
    entity_state,
    relations,
    relation_state,
    src_rows,
    rel_ids,
    dst_rows,
    counts,
    neg_blocks,
):
    rounds = src_rows.shape[0]
    rels = relations.shape[1]
    shape = src_rows.shape
    cnt, neg = counts.T, neg_blocks.T
    g_mine, g_other, drel, rel16, ent, state = first_round(
        cnt, neg, src_rows, dst_rows, rel_ids, entities, entity_state.reshape(1, -1), relations
    )
    acc = relsum(0, rel_ids, drel, None, rels)
    ent, state, low = update(ent, state, [g_mine, across(g_other)], [])
    rel = relvec(1, rel_ids, rel16)
    for t in range(1, rounds):
        far = shifted(low, -t)
        own = (low, across(low))
        query, query_t, source, s_hot, d_hot, d_hot_t, *negatives = source_side(
            t, shape, cnt, neg, src_rows, dst_rows, own, rel
        )
        far = held(far, [query, acc])
        far = (far, across(far))
        if t == rounds - 1:
            break
        near = near_products(query_t, far[0])
        gd_mine, gd_other, weight = target_grad(near, far[1], query, query_t, *negatives)
        gd = sum_pair(gd_mine, across(gd_other))
        gs_mine, gs_other, drel = source_grad(
            t, shape, cnt, neg, gd, far, d_hot, query, weight, source, rel, s_hot
        )
        acc = relsum(t, rel_ids, drel, acc, rels)
        rel = relvec(t + 1, rel_ids, rel16)
        grads = [sum_pair(gs_mine, shifted(gd, t), F32), across(gs_other)]
        ent, state, low = update(ent, state, grads, [rel])
    drel, dsource, dterm = last_terms(t, shape, cnt, neg, far, query, query_t, d_hot, source, rel)

    def send(after):
        gs_mine, gs_other, gd_mine, gd_other = both_grads(after, dsource, s_hot, dterm, d_hot_t)
        gd = sum_pair(gd_mine, across(gd_other))
        return [gs_mine, across(gs_other), shifted(gd, t)]

    def finish(grads, after):
        (mine,) = update(ent, state, grads, after, last=True)
        return whole_partition(mine, across(mine))

    rel_new, rel_state, done = relation_update(
        t, rel_ids, drel, acc, relations, relation_state, send, finish
    )
    return (done[0], done[1].reshape(-1), rel_new, rel_state)


def solution(mesh):
    return jax.shard_map(
        on_device,
        mesh=mesh,
        in_specs=(
            P(None, ("groups", "dom")),
            P(("groups", "dom")),
            P(None, "groups"),
            P("groups"),
            P(None, ("groups", "dom", "edge"), None),
            P(None, ("groups", "dom", "edge"), None),
            P(None, ("groups", "dom", "edge"), None),
            P(None, ("groups", "dom", "edge")),
            P(None, ("groups", "dom", "edge")),
        ),
        out_specs=(
            P(None, ("groups", "dom")),
            P(("groups", "dom")),
            P(None, "groups"),
            P("groups"),
        ),
        check_vma=False,
    )
```

profile of v0, /device:TPU:0, one launch (start us, length us, event | category | flops | bytes accessed | tf_op | source)
XLA Modules:
  0.0 138.3 jit_solution(7858925896837291967)
XLA Ops:
  0.6 5.4 %first_round.1 = (f32[400,128]{1,0:T(8,128)S(1)}, bf16[400,128]{1,0:T(8,128)(2,1)S(1)}, bf16[400,512]{1,0:T(8,128)(2,1)S(1)}, bf16[400,2048]{1,0:T(8,128)(2,1)S(...) custom-call(s32[4,6]{1,0:T(4,128)} %bitcast.6, s32[4,6]{1,0:T(4,128)} %bitcast.17, s32[6,4,128]{2,1,0:T(4,128)} %src_ref.11, ...), custom_call_target="tpu_custom_call" | custom-call | flops 1258291200 | bytes 6553600 | tf_op jit(solution)/shard_map/first_round/pallas_call | solution.py:309
  6.6 0.9 collective-permute-done.refs_3_
  8.1 5.7 %collective-permute-start.2 = (bf16[400,128]{1,0:T(8,128)(2,1)S(1)}, bf16[400,128]{1,0:T(8,128)(2,1)S(1)}, u32[]{:S(2)}, u32[]{:S(2)}) collective-permute-start(bf16[400,128]{1,0:T(8,128)(2,1)S(1)} %get-tuple-element.125.own0), channel_id=1, source_target_pairs={{0,14},{2,0},{4,2},{6,4},{8,6},{10,8},{12,10},{14,12},{1,15},{3,1}... | collective-permute-start | bytes 307208 | tf_op jit(solution)/shard_map/ppermute | solution.py:49
  13.8 1.0 relvec.5.rel_ref
  14.8 1.9 %relsum.5.refs_1_.refs_0_ = f32[400,2048]{1,0:T(8,128)S(1)} custom-call(s32[6,4,128]{2,1,0:T(4,128)S(1)} %copy-done.1, bf16[400,512]{1,0:T(8,128)(2,1)S(1)} %get-tuple-element.129.drel_ref), custom_call_target="tpu_custom_call" | custom-call | flops 204800 | bytes 204800 | tf_op jit(solution)/shard_map/relsum/pallas_call | solution.py:113
  16.8 1.8 %source_side.5 = (bf16[400,512]{1,0:T(8,128)(2,1)S(1)}, bf16[512,400]{1,0:T(8,128)(2,1)S(1)}, bf16[400,512]{1,0:T(8,128)(2,1)S(1)}, bf16[256,512]{1,0:T(8,128)(2...) custom-call(s32[4,6]{1,0:T(4,128)S(1)} %bitcast.7, ...), custom_call_target="tpu_custom_call" | custom-call | flops 204800 | bytes 204800 | tf_op jit(solution)/shard_map/source_side/pallas_call | solution.py:381
  19.0 1.0 collective-permute-done.3.far1
  20.0 1.4 target_grad.4
  21.6 1.2 collective-permute-done.4.b_ref
  22.8 1.5 %source_grad.4 = (f32[400,128]{1,0:T(8,128)S(1)}, bf16[400,128]{1,0:T(8,128)(2,1)S(1)}, bf16[400,512]{1,0:T(8,128)(2,1)S(1)}) custom-call(s32[4,6]{1,0:T(4,128)S(1)} %bitcast.8, s32[4,6]{1,0:T(4,128)S(1)} %bitcast.19, bf16[400,128]{1,0:T(8,128)(2,1)S(1)} %sum_pair.9._, bf16[400,128]{1,0:T(8,128)(2,1)S(1)} %held.5.far0, ...), custom_call_target="tpu_custom_call" | custom-call | flops 204800 | bytes 204800 | tf_op jit(solution)/shard_map/source_grad/pallas_call | solution.py:474
  24.5 1.0 relvec.6.refs_4_.rel_ref
  25.6 5.0 %collective-permute-done.5.b_ref = bf16[400,128]{1,0:T(8,128)(2,1)S(1)} collective-permute-done((bf16[400,128]{1,0:T(8,128)(2,1)S(1)}, bf16[400,128]{1,0:T(8,128)(2,1)S(1)}, u32[]{:S(2)}, u32[]{:S(2)}) %collective-permute-start.5) | collective-permute-done | bytes 102432 | tf_op jit(solution)/shard_map/ppermute | solution.py:49
  30.8 2.2 %relsum.6.refs_1_.refs_0_ = f32[400,2048]{1,0:T(8,128)S(1)} custom-call(s32[6,4,128]{2,1,0:T(4,128)S(1)} %copy-done.1, bf16[400,512]{1,0:T(8,128)(2,1)S(1)} %get-tuple-element.147.drel_ref, f32[400,2048]{1,0:T(8,128)S(1)} %relsum.5.refs_1_.refs_0_), custom_call_target="tpu_custom_call", output_to_operand_aliasing={{}: (2, {})} | custom-call | flops 204800 | bytes 204800 | tf_op jit(solution)/shard_map/relsum/pallas_call | solution.py:113
  33.1 1.8 %source_side.6 = (bf16[400,512]{1,0:T(8,128)(2,1)S(1)}, bf16[512,400]{1,0:T(8,128)(2,1)S(1)}, bf16[400,512]{1,0:T(8,128)(2,1)S(1)}, bf16[256,512]{1,0:T(8,128)(2...) custom-call(s32[4,6]{1,0:T(4,128)S(1)} %bitcast.9, ...), custom_call_target="tpu_custom_call" | custom-call | flops 204800 | bytes 204800 | tf_op jit(solution)/shard_map/source_side/pallas_call | solution.py:381
  34.9 1.2 collective-permute-done.8.x_ref
  36.3 1.0 collective-permute-done.9.far1
  37.4 1.4 target_grad.5
  39.0 1.2 collective-permute-done.10.b_ref
  40.1 1.1 collective-permute-start.11
  41.3 1.5 %source_grad.5 = (f32[400,128]{1,0:T(8,128)S(1)}, bf16[400,128]{1,0:T(8,128)(2,1)S(1)}, bf16[400,512]{1,0:T(8,128)(2,1)S(1)}) custom-call(s32[4,6]{1,0:T(4,128)S(1)} %bitcast.10, s32[4,6]{1,0:T(4,128)S(1)} %bitcast.21, bf16[400,128]{1,0:T(8,128)(2,1)S(1)} %sum_pair.11._, bf16[400,128]{1,0:T(8,128)(2,1)S(1)} %held.6.far0, ...), custom_call_target="tpu_custom_call" | custom-call | flops 204800 | bytes 204800 | tf_op jit(solution)/shard_map/source_grad/pallas_call | solution.py:474
  42.8 1.0 relvec.7.refs_4_.rel_ref
  43.9 3.2 %collective-permute-done.11.b_ref = bf16[400,128]{1,0:T(8,128)(2,1)S(1)} collective-permute-done((bf16[400,128]{1,0:T(8,128)(2,1)S(1)}, bf16[400,128]{1,0:T(8,128)(2,1)S(1)}, u32[]{:S(2)}, u32[]{:S(2)}) %collective-permute-start.11) | collective-permute-done | bytes 102432 | tf_op jit(solution)/shard_map/ppermute | solution.py:49
  47.4 2.2 %relsum.7.refs_1_.refs_0_ = f32[400,2048]{1,0:T(8,128)S(1)} custom-call(s32[6,4,128]{2,1,0:T(4,128)S(1)} %copy-done.1, bf16[400,512]{1,0:T(8,128)(2,1)S(1)} %get-tuple-element.165.drel_ref, f32[400,2048]{1,0:T(8,128)S(1)} %relsum.6.refs_1_.refs_0_), custom_call_target="tpu_custom_call", output_to_operand_aliasing={{}: (2, {})} | custom-call | flops 204800 | bytes 204800 | tf_op jit(solution)/shard_map/relsum/pallas_call | solution.py:113
  49.6 1.8 %source_side.7 = (bf16[400,512]{1,0:T(8,128)(2,1)S(1)}, bf16[512,400]{1,0:T(8,128)(2,1)S(1)}, bf16[400,512]{1,0:T(8,128)(2,1)S(1)}, bf16[256,512]{1,0:T(8,128)(2...) custom-call(s32[4,6]{1,0:T(4,128)S(1)} %bitcast.11, ...), custom_call_target="tpu_custom_call" | custom-call | flops 204800 | bytes 204800 | tf_op jit(solution)/shard_map/source_side/pallas_call | solution.py:381
  51.5 2.1 %collective-permute-done.14.x_ref = bf16[400,128]{1,0:T(8,128)(2,1)S(1)} collective-permute-done((bf16[400,128]{1,0:T(8,128)(2,1)S(1)}, bf16[400,128]{1,0:T(8,128)(2,1)S(1)}, u32[]{:S(2)}, u32[]{:S(2)}) %collective-permute-start.14) | collective-permute-done | bytes 102432 | tf_op jit(solution)/shard_map/ppermute | solution.py:49
  53.8 1.0 collective-permute-done.15.far1
  54.8 1.4 target_grad.6
  56.4 1.2 collective-permute-done.16.b_ref
  57.6 1.0 collective-permute-start.17
  58.6 1.5 %source_grad.6 = (f32[400,128]{1,0:T(8,128)S(1)}, bf16[400,128]{1,0:T(8,128)(2,1)S(1)}, bf16[400,512]{1,0:T(8,128)(2,1)S(1)}) custom-call(s32[4,6]{1,0:T(4,128)S(1)} %bitcast.12, s32[4,6]{1,0:T(4,128)S(1)} %bitcast.23, bf16[400,128]{1,0:T(8,128)(2,1)S(1)} %sum_pair.13._, bf16[400,128]{1,0:T(8,128)(2,1)S(1)} %held.7.far0, ...), custom_call_target="tpu_custom_call" | custom-call | flops 204800 | bytes 204800 | tf_op jit(solution)/shard_map/source_grad/pallas_call | solution.py:474
  60.1 1.0 relvec.8.refs_4_.rel_ref
  61.2 5.1 %collective-permute-done.17.b_ref = bf16[400,128]{1,0:T(8,128)(2,1)S(1)} collective-permute-done((bf16[400,128]{1,0:T(8,128)(2,1)S(1)}, bf16[400,128]{1,0:T(8,128)(2,1)S(1)}, u32[]{:S(2)}, u32[]{:S(2)}) %collective-permute-start.17) | collective-permute-done | bytes 102432 | tf_op jit(solution)/shard_map/ppermute | solution.py:49
  66.6 2.2 %relsum.8.refs_1_.refs_0_ = f32[400,2048]{1,0:T(8,128)S(1)} custom-call(s32[6,4,128]{2,1,0:T(4,128)S(1)} %copy-done.1, bf16[400,512]{1,0:T(8,128)(2,1)S(1)} %get-tuple-element.183.drel_ref, f32[400,2048]{1,0:T(8,128)S(1)} %relsum.7.refs_1_.refs_0_), custom_call_target="tpu_custom_call", output_to_operand_aliasing={{}: (2, {})} | custom-call | flops 204800 | bytes 204800 | tf_op jit(solution)/shard_map/relsum/pallas_call | solution.py:113
  68.8 1.8 %source_side.8 = (bf16[400,512]{1,0:T(8,128)(2,1)S(1)}, bf16[512,400]{1,0:T(8,128)(2,1)S(1)}, bf16[400,512]{1,0:T(8,128)(2,1)S(1)}, bf16[256,512]{1,0:T(8,128)(2...) custom-call(s32[4,6]{1,0:T(4,128)S(1)} %bitcast.13, ...), custom_call_target="tpu_custom_call" | custom-call | flops 204800 | bytes 204800 | tf_op jit(solution)/shard_map/source_side/pallas_call | solution.py:381
  70.7 2.9 %collective-permute-done.20.x_ref = bf16[400,128]{1,0:T(8,128)(2,1)S(1)} collective-permute-done((bf16[400,128]{1,0:T(8,128)(2,1)S(1)}, bf16[400,128]{1,0:T(8,128)(2,1)S(1)}, u32[]{:S(2)}, u32[]{:S(2)}) %collective-permute-start.20) | collective-permute-done | bytes 102432 | tf_op jit(solution)/shard_map/ppermute | solution.py:49
  74.0 1.0 collective-permute-done.21.far1
  74.9 1.4 target_grad.7
  76.5 1.2 collective-permute-done.22.b_ref
  77.8 1.5 %source_grad.7 = (f32[400,128]{1,0:T(8,128)S(1)}, bf16[400,128]{1,0:T(8,128)(2,1)S(1)}, bf16[400,512]{1,0:T(8,128)(2,1)S(1)}) custom-call(s32[4,6]{1,0:T(4,128)S(1)} %bitcast.14, s32[4,6]{1,0:T(4,128)S(1)} %bitcast.25, bf16[400,128]{1,0:T(8,128)(2,1)S(1)} %sum_pair.15._, bf16[400,128]{1,0:T(8,128)(2,1)S(1)} %held.8.far0, ...), custom_call_target="tpu_custom_call" | custom-call | flops 204800 | bytes 204800 | tf_op jit(solution)/shard_map/source_grad/pallas_call | solution.py:474
  79.5 1.0 relvec.9.refs_4_.rel_ref
  80.5 5.1 %collective-permute-done.23.b_ref = bf16[400,128]{1,0:T(8,128)(2,1)S(1)} collective-permute-done((bf16[400,128]{1,0:T(8,128)(2,1)S(1)}, bf16[400,128]{1,0:T(8,128)(2,1)S(1)}, u32[]{:S(2)}, u32[]{:S(2)}) %collective-permute-start.23) | collective-permute-done | bytes 102432 | tf_op jit(solution)/shard_map/ppermute | solution.py:49
  86.2 2.2 %relsum.9.refs_1_.acc_ref = f32[400,2048]{1,0:T(8,128)S(1)} custom-call(s32[6,4,128]{2,1,0:T(4,128)S(1)} %copy-done.1, bf16[400,512]{1,0:T(8,128)(2,1)S(1)} %get-tuple-element.200.drel_ref, f32[400,2048]{1,0:T(8,128)S(1)} %relsum.8.refs_1_.refs_0_), custom_call_target="tpu_custom_call", output_to_operand_aliasing={{}: (2, {})} | custom-call | flops 204800 | bytes 204800 | tf_op jit(solution)/shard_map/relsum/pallas_call | solution.py:113
  88.4 2.0 %source_side.9 = (bf16[400,512]{1,0:T(8,128)(2,1)S(1)}, bf16[512,400]{1,0:T(8,128)(2,1)S(1)}, bf16[400,512]{1,0:T(8,128)(2,1)S(1)}, bf16[256,512]{1,0:T(8,128)(2...) custom-call(s32[4,6]{1,0:T(4,128)S(1)} %bitcast.15, ...), custom_call_target="tpu_custom_call" | custom-call | flops 204800 | bytes 204800 | tf_op jit(solution)/shard_map/source_side/pallas_call | solution.py:381
  90.4 2.7 %collective-permute-done.25.x_ref = bf16[400,128]{1,0:T(8,128)(2,1)S(1)} collective-permute-done((bf16[400,128]{1,0:T(8,128)(2,1)S(1)}, bf16[400,128]{1,0:T(8,128)(2,1)S(1)}, u32[]{:S(2)}, u32[]{:S(2)}) %collective-permute-start.25) | collective-permute-done | bytes 102432 | tf_op jit(solution)/shard_map/ppermute | solution.py:49
  93.1 1.3 collective-permute-done.27.far1
  94.4 1.8 %last_terms.1 = (bf16[400,512]{1,0:T(8,128)(2,1)S(1)}, bf16[400,512]{1,0:T(8,128)(2,1)S(1)}, bf16[400,512]{1,0:T(8,128)(2,1)S(1)}) custom-call(s32[4,6]{1,0:T(4,128)S(1)} %bitcast.16, s32[4,6]{1,0:T(4,128)S(1)} %bitcast.27, bf16[400,128]{1,0:T(8,128)(2,1)S(1)} %held.9.far0, bf16[400,128]{1,0:T(8,128)(2,1)S(1)} %collective-permute-done.27.far1, ...), custom_call_target="tpu_custom_call" | custom-call | flops 157286400 | bytes 2457600 | tf_op jit(solution)/shard_map/last_terms/pallas_call | solution.py:504
  100.0 1.4 %collective-permute-start.37 = (bf16[400,128]{1,0:T(8,128)(2,1)S(1)}, bf16[400,128]{1,0:T(8,128)(2,1)S(1)}, u32[]{:S(2)}, u32[]{:S(2)}) collective-permute-start(bf16[400,128]{1,0:T(8,128)(2,1)S(1)} %get-tuple-element.226), channel_id=1, source_target_pairs={{0,2},{2,0},{4,6},{6,4},{8,10},{10,8},{12,14},{14,12},{1,3},{3,1},... | collective-permute-start | bytes 307208 | tf_op jit(solution)/shard_map/ppermute | solution.py:54
  102.0 0.7 collective-permute-start.30
  102.8 2.8 %collective-permute-start.35 = (bf16[400,128]{1,0:T(8,128)(2,1)S(1)}, bf16[400,128]{1,0:T(8,128)(2,1)S(1)}, u32[]{:S(2)}, u32[]{:S(2)}) collective-permute-start(bf16[400,128]{1,0:T(8,128)(2,1)S(1)} %get-tuple-element.224), channel_id=1, source_target_pairs={{0,2},{2,0},{4,6},{6,4},{8,10},{10,8},{12,14},{14,12},{1,3},{3,1},... | collective-permute-start | bytes 307208 | tf_op jit(solution)/shard_map/ppermute | solution.py:54
  106.2 1.5 %collective-permute-start.36 = (bf16[400,128]{1,0:T(8,128)(2,1)S(1)}, bf16[400,128]{1,0:T(8,128)(2,1)S(1)}, u32[]{:S(2)}, u32[]{:S(2)}) collective-permute-start(bf16[400,128]{1,0:T(8,128)(2,1)S(1)} %sum_piece.4.refs_5_), channel_id=1, source_target_pairs={{0,12},{2,14},{4,8},{6,10},{8,4},{10,6},{12,0},{14,2},{1,13},{3,15... | collective-permute-start | bytes 307208 | tf_op jit(solution)/shard_map/ppermute | solution.py:54
  107.7 1.8 %collective-permute-done.37.refs_0_ = bf16[400,128]{1,0:T(8,128)(2,1)S(1)} collective-permute-done((bf16[400,128]{1,0:T(8,128)(2,1)S(1)}, bf16[400,128]{1,0:T(8,128)(2,1)S(1)}, u32[]{:S(2)}, u32[]{:S(2)}) %collective-permute-start.37) | collective-permute-done | bytes 102432 | tf_op jit(solution)/shard_map/ppermute | solution.py:54
  109.6 2.1 %collective-permute-done.39.refs_0_ = bf16[400,128]{1,0:T(8,128)(2,1)S(1)} collective-permute-done((bf16[400,128]{1,0:T(8,128)(2,1)S(1)}, bf16[400,128]{1,0:T(8,128)(2,1)S(1)}, u32[]{:S(2)}, u32[]{:S(2)}) %collective-permute-start.39) | collective-permute-done | bytes 102432 | tf_op jit(solution)/shard_map/ppermute | solution.py:54
  113.1 4.7 %collective-permute-done.38.refs_2_ = bf16[400,128]{1,0:T(8,128)(2,1)S(1)} collective-permute-done((bf16[400,128]{1,0:T(8,128)(2,1)S(1)}, bf16[400,128]{1,0:T(8,128)(2,1)S(1)}, u32[]{:S(2)}, u32[]{:S(2)}) %collective-permute-start.38) | collective-permute-done | bytes 102432 | tf_op jit(solution)/shard_map/ppermute | solution.py:54
  118.5 3.0 %collective-permute-start.44 = (bf16[400,128]{1,0:T(8,128)(2,1)S(1)}, bf16[400,128]{1,0:T(8,128)(2,1)S(1)}, u32[]{:S(2)}, u32[]{:S(2)}) collective-permute-start(bf16[400,128]{1,0:T(8,128)(2,1)S(1)} %sum_piece.7.refs_0_), channel_id=1, source_target_pairs={{0,8},{2,10},{4,12},{6,14},{8,0},{10,2},{12,4},{14,6},{1,9},{3,11}... | collective-permute-start | bytes 307208 | tf_op jit(solution)/shard_map/ppermute | solution.py:54
  121.6 1.3 collective-permute-start.42
  123.2 1.7 %collective-permute-start.47 = (bf16[400,128]{1,0:T(8,128)(2,1)S(1)}, bf16[400,128]{1,0:T(8,128)(2,1)S(1)}, u32[]{:S(2)}, u32[]{:S(2)}) collective-permute-start(bf16[400,128]{1,0:T(8,128)(2,1)S(1)} %collective-permute-done.46.refs_3_), channel_id=1, source_target_pairs={{0,2},{2,0},{4,6},{6,4},{8,10},{10,8},{12,14},{14,12},{1,3},{3,1},... | collective-permute-start | bytes 307208 | tf_op jit(solution)/shard_map/ppermute | solution.py:54
  124.9 3.6 %collective-permute-done.44.refs_2_ = bf16[400,128]{1,0:T(8,128)(2,1)S(1)} collective-permute-done((bf16[400,128]{1,0:T(8,128)(2,1)S(1)}, bf16[400,128]{1,0:T(8,128)(2,1)S(1)}, u32[]{:S(2)}, u32[]{:S(2)}) %collective-permute-start.44) | collective-permute-done | bytes 102432 | tf_op jit(solution)/shard_map/ppermute | solution.py:54
  128.6 0.7 collective-permute-start.45
  129.3 1.3 collective-permute-start.43
  130.6 0.8 whole_partition.1
  131.6 1.7 %collective-permute-done.45.refs_2_ = bf16[400,128]{1,0:T(8,128)(2,1)S(1)} collective-permute-done((bf16[400,128]{1,0:T(8,128)(2,1)S(1)}, bf16[400,128]{1,0:T(8,128)(2,1)S(1)}, u32[]{:S(2)}, u32[]{:S(2)}) %collective-permute-start.45) | collective-permute-done | bytes 102432 | tf_op jit(solution)/shard_map/ppermute | solution.py:54
  133.2 1.1 collective-permute-done.43.refs_1_
  134.5 1.3 relnew.2
  136.2 1.9 %relnew.3 = (f32[400,2048]{1,0:T(8,128)}, f32[1,2048]{1,0:T(1,128)}) custom-call(f32[400,2048]{1,0:T(8,128)S(1)} %copy-done, f32[1,2048]{1,0:T(1,128)S(1)} %bitcast.30, bf16[400,128]{1,0:T(8,128)(2,1)S(1)} %collective-permute-done.41.refs_0_, bf16[400,128]{1,0:T(8,128)(2,1)S(1)} %collective-permute-done.43.refs_1_, ...), custom_call_target="tpu_custom_call", output_to_operand_aliasing={{0}: (7, {})} | custom-call | flops 1638400 | bytes 1638400 | tf_op jit(solution)/shard_map/relnew/pallas_call | solution.py:750
  (112 shorter events, 13.5 us)
Async XLA Ops:
  0.6 13.1 %copy-start.1 = (s32[6,4,128]{2,1,0:T(4,128)S(1)}, s32[6,4,128]{2,1,0:T(4,128)}, u32[]{:S(2)}) copy-start(s32[6,4,128]{2,1,0:T(4,128)} %ids_ref.25) | copy-start | bytes 36868
  6.0 10.7 %copy-start.2 = (s32[6,4,128]{2,1,0:T(4,128)S(1)}, s32[6,4,128]{2,1,0:T(4,128)}, u32[]{:S(2)}) copy-start(s32[6,4,128]{2,1,0:T(4,128)} %src_ref.11) | copy-start | bytes 36868
  6.0 10.7 %copy-start.3 = (s32[6,4,128]{2,1,0:T(4,128)S(1)}, s32[6,4,128]{2,1,0:T(4,128)}, u32[]{:S(2)}) copy-start(s32[6,4,128]{2,1,0:T(4,128)} %dst_ref.11) | copy-start | bytes 36868
  6.0 10.7 %copy-start.4 = (s32[6,4]{0,1:T(4,128)S(1)}, s32[6,4]{0,1:T(4,128)}, u32[]{:S(2)}) copy-start(s32[6,4]{0,1:T(4,128)} %param.16) | copy-start | bytes 292
  6.1 10.7 %copy-start.5 = (s32[6,4]{0,1:T(4,128)S(1)}, s32[6,4]{0,1:T(4,128)}, u32[]{:S(2)}) copy-start(s32[6,4]{0,1:T(4,128)} %param.17) | copy-start | bytes 292
  6.1 1.5 %collective-permute-start = (bf16[400,128]{1,0:T(8,128)(2,1)S(1)}, bf16[400,128]{1,0:T(8,128)(2,1)S(1)}, u32[]{:S(2)}, u32[]{:S(2)}) collective-permute-start(bf16[400,128]{1,0:T(8,128)(2,1)S(1)} %get-tuple-element.122), channel_id=1, source_target_pairs={{0,1},{1,0},{2,3},{3,2},{4,5},{5,4},{6,7},{7,6},{8,9},{9,8},{10,11... | collective-permute-start | bytes 307208 | tf_op jit(solution)/shard_map/ppermute | solution.py:58
  7.7 9.1 %collective-permute-start.1 = (bf16[400,128]{1,0:T(8,128)(2,1)S(1)}, bf16[400,128]{1,0:T(8,128)(2,1)S(1)}, u32[]{:S(2)}, u32[]{:S(2)}) collective-permute-start(bf16[400,128]{1,0:T(8,128)(2,1)S(1)} %get-tuple-element.125.own0), channel_id=1, source_target_pairs={{0,1},{1,0},{2,3},{3,2},{4,5},{5,4},{6,7},{7,6},{8,9},{9,8},{10,11... | collective-permute-start | bytes 307208 | tf_op jit(solution)/shard_map/ppermute | solution.py:58
  8.1 10.5 %collective-permute-start.2 = (bf16[400,128]{1,0:T(8,128)(2,1)S(1)}, bf16[400,128]{1,0:T(8,128)(2,1)S(1)}, u32[]{:S(2)}, u32[]{:S(2)}) collective-permute-start(bf16[400,128]{1,0:T(8,128)(2,1)S(1)} %get-tuple-element.125.own0), channel_id=1, source_target_pairs={{0,14},{2,0},{4,2},{6,4},{8,6},{10,8},{12,10},{14,12},{1,15},{3,1}... | collective-permute-start | bytes 307208 | tf_op jit(solution)/shard_map/ppermute | solution.py:49
  18.6 1.4 collective-permute-start.3
  21.4 1.4 collective-permute-start.4
  22.8 7.8 %collective-permute-start.5 = (bf16[400,128]{1,0:T(8,128)(2,1)S(1)}, bf16[400,128]{1,0:T(8,128)(2,1)S(1)}, u32[]{:S(2)}, u32[]{:S(2)}) collective-permute-start(bf16[400,128]{1,0:T(8,128)(2,1)S(1)} %sum_pair.9._), channel_id=1, source_target_pairs={{0,2},{2,4},{4,6},{6,8},{8,10},{10,12},{12,14},{14,0},{1,3},{3,5},... | collective-permute-start | bytes 307208 | tf_op jit(solution)/shard_map/ppermute | solution.py:49
  24.3 6.3 %collective-permute-start.6 = (bf16[400,128]{1,0:T(8,128)(2,1)S(1)}, bf16[400,128]{1,0:T(8,128)(2,1)S(1)}, u32[]{:S(2)}, u32[]{:S(2)}) collective-permute-start(bf16[400,128]{1,0:T(8,128)(2,1)S(1)} %get-tuple-element.141), channel_id=1, source_target_pairs={{0,1},{1,0},{2,3},{3,2},{4,5},{5,4},{6,7},{7,6},{8,9},{9,8},{10,11... | collective-permute-start | bytes 307208 | tf_op jit(solution)/shard_map/ppermute | solution.py:58
  30.7 2.4 %collective-permute-start.7 = (bf16[400,128]{1,0:T(8,128)(2,1)S(1)}, bf16[400,128]{1,0:T(8,128)(2,1)S(1)}, u32[]{:S(2)}, u32[]{:S(2)}) collective-permute-start(bf16[400,128]{1,0:T(8,128)(2,1)S(1)} %get-tuple-element.144.own0), channel_id=1, source_target_pairs={{0,1},{1,0},{2,3},{3,2},{4,5},{5,4},{6,7},{7,6},{8,9},{9,8},{10,11... | collective-permute-start | bytes 307208 | tf_op jit(solution)/shard_map/ppermute | solution.py:58
  30.8 5.3 %collective-permute-start.8 = (bf16[400,128]{1,0:T(8,128)(2,1)S(1)}, bf16[400,128]{1,0:T(8,128)(2,1)S(1)}, u32[]{:S(2)}, u32[]{:S(2)}) collective-permute-start(bf16[400,128]{1,0:T(8,128)(2,1)S(1)} %get-tuple-element.144.own0), channel_id=1, source_target_pairs={{0,12},{2,14},{4,0},{6,2},{8,4},{10,6},{12,8},{14,10},{1,13},{3,15... | collective-permute-start | bytes 307208 | tf_op jit(solution)/shard_map/ppermute | solution.py:49
  36.1 1.3 collective-permute-start.9
  38.8 1.4 collective-permute-start.10
  40.1 7.0 %collective-permute-start.11 = (bf16[400,128]{1,0:T(8,128)(2,1)S(1)}, bf16[400,128]{1,0:T(8,128)(2,1)S(1)}, u32[]{:S(2)}, u32[]{:S(2)}) collective-permute-start(bf16[400,128]{1,0:T(8,128)(2,1)S(1)} %sum_pair.11._), channel_id=1, source_target_pairs={{0,4},{2,6},{4,8},{6,10},{8,12},{10,14},{12,0},{14,2},{1,5},{3,7},... | collective-permute-start | bytes 307208 | tf_op jit(solution)/shard_map/ppermute | solution.py:49
  42.8 4.4 %collective-permute-start.12 = (bf16[400,128]{1,0:T(8,128)(2,1)S(1)}, bf16[400,128]{1,0:T(8,128)(2,1)S(1)}, u32[]{:S(2)}, u32[]{:S(2)}) collective-permute-start(bf16[400,128]{1,0:T(8,128)(2,1)S(1)} %get-tuple-element.159), channel_id=1, source_target_pairs={{0,1},{1,0},{2,3},{3,2},{4,5},{5,4},{6,7},{7,6},{8,9},{9,8},{10,11... | collective-permute-start | bytes 307208 | tf_op jit(solution)/shard_map/ppermute | solution.py:58
  47.3 2.3 %collective-permute-start.13 = (bf16[400,128]{1,0:T(8,128)(2,1)S(1)}, bf16[400,128]{1,0:T(8,128)(2,1)S(1)}, u32[]{:S(2)}, u32[]{:S(2)}) collective-permute-start(bf16[400,128]{1,0:T(8,128)(2,1)S(1)} %get-tuple-element.162.own0), channel_id=1, source_target_pairs={{0,1},{1,0},{2,3},{3,2},{4,5},{5,4},{6,7},{7,6},{8,9},{9,8},{10,11... | collective-permute-start | bytes 307208 | tf_op jit(solution)/shard_map/ppermute | solution.py:58
  47.4 6.2 %collective-permute-start.14 = (bf16[400,128]{1,0:T(8,128)(2,1)S(1)}, bf16[400,128]{1,0:T(8,128)(2,1)S(1)}, u32[]{:S(2)}, u32[]{:S(2)}) collective-permute-start(bf16[400,128]{1,0:T(8,128)(2,1)S(1)} %get-tuple-element.162.own0), channel_id=1, source_target_pairs={{0,10},{2,12},{4,14},{6,0},{8,2},{10,4},{12,6},{14,8},{1,11},{3,13... | collective-permute-start | bytes 307208 | tf_op jit(solution)/shard_map/ppermute | solution.py:49
  53.5 1.3 collective-permute-start.15
  56.2 1.4 collective-permute-start.16
  57.6 8.7 %collective-permute-start.17 = (bf16[400,128]{1,0:T(8,128)(2,1)S(1)}, bf16[400,128]{1,0:T(8,128)(2,1)S(1)}, u32[]{:S(2)}, u32[]{:S(2)}) collective-permute-start(bf16[400,128]{1,0:T(8,128)(2,1)S(1)} %sum_pair.13._), channel_id=1, source_target_pairs={{0,6},{2,8},{4,10},{6,12},{8,14},{10,0},{12,2},{14,4},{1,7},{3,9},... | collective-permute-start | bytes 307208 | tf_op jit(solution)/shard_map/ppermute | solution.py:49
  60.1 6.3 %collective-permute-start.18 = (bf16[400,128]{1,0:T(8,128)(2,1)S(1)}, bf16[400,128]{1,0:T(8,128)(2,1)S(1)}, u32[]{:S(2)}, u32[]{:S(2)}) collective-permute-start(bf16[400,128]{1,0:T(8,128)(2,1)S(1)} %get-tuple-element.177), channel_id=1, source_target_pairs={{0,1},{1,0},{2,3},{3,2},{4,5},{5,4},{6,7},{7,6},{8,9},{9,8},{10,11... | collective-permute-start | bytes 307208 | tf_op jit(solution)/shard_map/ppermute | solution.py:58
  66.5 2.4 %collective-permute-start.19 = (bf16[400,128]{1,0:T(8,128)(2,1)S(1)}, bf16[400,128]{1,0:T(8,128)(2,1)S(1)}, u32[]{:S(2)}, u32[]{:S(2)}) collective-permute-start(bf16[400,128]{1,0:T(8,128)(2,1)S(1)} %get-tuple-element.180.own0), channel_id=1, source_target_pairs={{0,1},{1,0},{2,3},{3,2},{4,5},{5,4},{6,7},{7,6},{8,9},{9,8},{10,11... | collective-permute-start | bytes 307208 | tf_op jit(solution)/shard_map/ppermute | solution.py:58
  66.6 7.0 %collective-permute-start.20 = (bf16[400,128]{1,0:T(8,128)(2,1)S(1)}, bf16[400,128]{1,0:T(8,128)(2,1)S(1)}, u32[]{:S(2)}, u32[]{:S(2)}) collective-permute-start(bf16[400,128]{1,0:T(8,128)(2,1)S(1)} %get-tuple-element.180.own0), channel_id=1, source_target_pairs={{0,8},{2,10},{4,12},{6,14},{8,0},{10,2},{12,4},{14,6},{1,9},{3,11}... | collective-permute-start | bytes 307208 | tf_op jit(solution)/shard_map/ppermute | solution.py:49
  73.6 1.3 collective-permute-start.21
  76.3 1.4 collective-permute-start.22
  77.7 7.9 %collective-permute-start.23 = (bf16[400,128]{1,0:T(8,128)(2,1)S(1)}, bf16[400,128]{1,0:T(8,128)(2,1)S(1)}, u32[]{:S(2)}, u32[]{:S(2)}) collective-permute-start(bf16[400,128]{1,0:T(8,128)(2,1)S(1)} %sum_pair.15._), channel_id=1, source_target_pairs={{0,8},{2,10},{4,12},{6,14},{8,0},{10,2},{12,4},{14,6},{1,9},{3,11}... | collective-permute-start | bytes 307208 | tf_op jit(solution)/shard_map/ppermute | solution.py:49
  79.3 6.4 %collective-permute-start.24 = (bf16[400,128]{1,0:T(8,128)(2,1)S(1)}, bf16[400,128]{1,0:T(8,128)(2,1)S(1)}, u32[]{:S(2)}, u32[]{:S(2)}) collective-permute-start(bf16[400,128]{1,0:T(8,128)(2,1)S(1)} %get-tuple-element.195), channel_id=1, source_target_pairs={{0,1},{1,0},{2,3},{3,2},{4,5},{5,4},{6,7},{7,6},{8,9},{9,8},{10,11... | collective-permute-start | bytes 307208 | tf_op jit(solution)/shard_map/ppermute | solution.py:58
  85.8 2.6 %collective-permute-start.26 = (bf16[400,128]{1,0:T(8,128)(2,1)S(1)}, bf16[400,128]{1,0:T(8,128)(2,1)S(1)}, u32[]{:S(2)}, u32[]{:S(2)}) collective-permute-start(bf16[400,128]{1,0:T(8,128)(2,1)S(1)} %get-tuple-element.198.own0), channel_id=1, source_target_pairs={{0,1},{1,0},{2,3},{3,2},{4,5},{5,4},{6,7},{7,6},{8,9},{9,8},{10,11... | collective-permute-start | bytes 307208 | tf_op jit(solution)/shard_map/ppermute | solution.py:58
  85.9 7.2 %collective-permute-start.25 = (bf16[400,128]{1,0:T(8,128)(2,1)S(1)}, bf16[400,128]{1,0:T(8,128)(2,1)S(1)}, u32[]{:S(2)}, u32[]{:S(2)}) collective-permute-start(bf16[400,128]{1,0:T(8,128)(2,1)S(1)} %get-tuple-element.198.own0), channel_id=1, source_target_pairs={{0,6},{2,8},{4,10},{6,12},{8,14},{10,0},{12,2},{14,4},{1,7},{3,9},... | collective-permute-start | bytes 307208 | tf_op jit(solution)/shard_map/ppermute | solution.py:49
  93.1 1.3 collective-permute-start.27
  96.9 2.3 %collective-permute-start.32 = (bf16[4,400,128]{2,1,0:T(8,128)(2,1)S(1)}, bf16[4,400,128]{2,1,0:T(8,128)(2,1)S(1)}, u32[]{:S(2)}, u32[]{:S(2)}) collective-permute-start(bf16[4,400,128]{2,1,0:T(8,128)(2,1)S(1)} %get-tuple-element.205._.refs_0_), channel_id=1, source_target_pairs={{0,1},{1,0},{2,3},{3,2},{4,5},{5,4},{6,7},{7,6},{8,9},{9,8},{10,11... | collective-permute-start | bytes 1228808 | tf_op jit(solution)/shard_map/ppermute | solution.py:58
  97.8 5.0 %collective-permute-start.31 = (bf16[4,400,128]{2,1,0:T(8,128)(2,1)S(1)}, bf16[4,400,128]{2,1,0:T(8,128)(2,1)S(1)}, u32[]{:S(2)}, u32[]{:S(2)}) collective-permute-start(bf16[4,400,128]{2,1,0:T(8,128)(2,1)S(1)} %get-tuple-element.215), channel_id=1, source_target_pairs={{0,1},{1,0},{2,3},{3,2},{4,5},{5,4},{6,7},{7,6},{8,9},{9,8},{10,11... | collective-permute-start | bytes 1228808 | tf_op jit(solution)/shard_map/ppermute | solution.py:58
  98.6 2.8 %collective-permute-start.29 = (bf16[400,128]{1,0:T(8,128)(2,1)S(1)}, bf16[400,128]{1,0:T(8,128)(2,1)S(1)}, u32[]{:S(2)}, u32[]{:S(2)}) collective-permute-start(bf16[400,128]{1,0:T(8,128)(2,1)S(1)} %get-tuple-element.213), channel_id=1, source_target_pairs={{0,1},{1,0},{2,3},{3,2},{4,5},{5,4},{6,7},{7,6},{8,9},{9,8},{10,11... | collective-permute-start | bytes 307208 | tf_op jit(solution)/shard_map/ppermute | solution.py:58
  98.8 3.2 %collective-permute-start.28 = (bf16[400,128]{1,0:T(8,128)(2,1)S(1)}, bf16[400,128]{1,0:T(8,128)(2,1)S(1)}, u32[]{:S(2)}, u32[]{:S(2)}) collective-permute-start(bf16[400,128]{1,0:T(8,128)(2,1)S(1)} %get-tuple-element.211), channel_id=1, source_target_pairs={{0,1},{1,0},{2,3},{3,2},{4,5},{5,4},{6,7},{7,6},{8,9},{9,8},{10,11... | collective-permute-start | bytes 307208 | tf_op jit(solution)/shard_map/ppermute | solution.py:58
  99.3 6.9 %collective-permute-start.33 = (bf16[400,128]{1,0:T(8,128)(2,1)S(1)}, bf16[400,128]{1,0:T(8,128)(2,1)S(1)}, u32[]{:S(2)}, u32[]{:S(2)}) collective-permute-start(bf16[400,128]{1,0:T(8,128)(2,1)S(1)} %get-tuple-element.220), channel_id=1, source_target_pairs={{0,2},{2,0},{4,6},{6,4},{8,10},{10,8},{12,14},{14,12},{1,3},{3,1},... | collective-permute-start | bytes 307208 | tf_op jit(solution)/shard_map/ppermute | solution.py:54
  100.0 9.5 %collective-permute-start.37 = (bf16[400,128]{1,0:T(8,128)(2,1)S(1)}, bf16[400,128]{1,0:T(8,128)(2,1)S(1)}, u32[]{:S(2)}, u32[]{:S(2)}) collective-permute-start(bf16[400,128]{1,0:T(8,128)(2,1)S(1)} %get-tuple-element.226), channel_id=1, source_target_pairs={{0,2},{2,0},{4,6},{6,4},{8,10},{10,8},{12,14},{14,12},{1,3},{3,1},... | collective-permute-start | bytes 307208 | tf_op jit(solution)/shard_map/ppermute | solution.py:54
  101.4 10.3 %collective-permute-start.39 = (bf16[400,128]{1,0:T(8,128)(2,1)S(1)}, bf16[400,128]{1,0:T(8,128)(2,1)S(1)}, u32[]{:S(2)}, u32[]{:S(2)}) collective-permute-start(bf16[400,128]{1,0:T(8,128)(2,1)S(1)} %get-tuple-element.228), channel_id=1, source_target_pairs={{0,2},{2,0},{4,6},{6,4},{8,10},{10,8},{12,14},{14,12},{1,3},{3,1},... | collective-permute-start | bytes 307208 | tf_op jit(solution)/shard_map/ppermute | solution.py:54
  102.0 10.4 %collective-permute-start.30 = (bf16[400,128]{1,0:T(8,128)(2,1)S(1)}, bf16[400,128]{1,0:T(8,128)(2,1)S(1)}, u32[]{:S(2)}, u32[]{:S(2)}) collective-permute-start(bf16[400,128]{1,0:T(8,128)(2,1)S(1)} %sum_pair.17), channel_id=1, source_target_pairs={{0,10},{2,12},{4,14},{6,0},{8,2},{10,4},{12,6},{14,8},{1,11},{3,13... | collective-permute-start | bytes 307208 | tf_op jit(solution)/shard_map/ppermute | solution.py:49
  102.8 10.3 %collective-permute-start.35 = (bf16[400,128]{1,0:T(8,128)(2,1)S(1)}, bf16[400,128]{1,0:T(8,128)(2,1)S(1)}, u32[]{:S(2)}, u32[]{:S(2)}) collective-permute-start(bf16[400,128]{1,0:T(8,128)(2,1)S(1)} %get-tuple-element.224), channel_id=1, source_target_pairs={{0,2},{2,0},{4,6},{6,4},{8,10},{10,8},{12,14},{14,12},{1,3},{3,1},... | collective-permute-start | bytes 307208 | tf_op jit(solution)/shard_map/ppermute | solution.py:54
  106.2 28.3 %copy-start = (f32[400,2048]{1,0:T(8,128)S(1)}, f32[400,2048]{1,0:T(8,128)}, u32[]{:S(2)}) copy-start(f32[400,2048]{1,0:T(8,128)} %rel_ref.5) | copy-start | bytes 9830404
  106.2 28.3 %copy-start.6 = (f32[2048]{0:T(1024)S(1)}, f32[2048]{0:T(1024)}, u32[]{:S(2)}) copy-start(f32[2048]{0:T(1024)} %param.12) | copy-start | bytes 24580
  106.2 6.9 %collective-permute-start.36 = (bf16[400,128]{1,0:T(8,128)(2,1)S(1)}, bf16[400,128]{1,0:T(8,128)(2,1)S(1)}, u32[]{:S(2)}, u32[]{:S(2)}) collective-permute-start(bf16[400,128]{1,0:T(8,128)(2,1)S(1)} %sum_piece.4.refs_5_), channel_id=1, source_target_pairs={{0,12},{2,14},{4,8},{6,10},{8,4},{10,6},{12,0},{14,2},{1,13},{3,15... | collective-permute-start | bytes 307208 | tf_op jit(solution)/shard_map/ppermute | solution.py:54
  109.5 8.3 %collective-permute-start.38 = (bf16[400,128]{1,0:T(8,128)(2,1)S(1)}, bf16[400,128]{1,0:T(8,128)(2,1)S(1)}, u32[]{:S(2)}, u32[]{:S(2)}) collective-permute-start(bf16[400,128]{1,0:T(8,128)(2,1)S(1)} %sum_piece.5), channel_id=1, source_target_pairs={{0,8},{2,10},{4,12},{6,14},{8,0},{10,2},{12,4},{14,6},{1,9},{3,11}... | collective-permute-start | bytes 307208 | tf_op jit(solution)/shard_map/ppermute | solution.py:54
  111.7 6.6 %collective-permute-start.40 = (bf16[400,128]{1,0:T(8,128)(2,1)S(1)}, bf16[400,128]{1,0:T(8,128)(2,1)S(1)}, u32[]{:S(2)}, u32[]{:S(2)}) collective-permute-start(bf16[400,128]{1,0:T(8,128)(2,1)S(1)} %sum_piece.6), channel_id=1, source_target_pairs={{0,4},{2,6},{4,0},{6,2},{8,12},{10,14},{12,8},{14,10},{1,5},{3,7},... | collective-permute-start | bytes 307208 | tf_op jit(solution)/shard_map/ppermute | solution.py:54
  112.5 18.1 %collective-permute-start.34 = (f32[408,128]{1,0:T(8,128)S(1)}, f32[408,128]{1,0:T(8,128)S(1)}, u32[]{:S(2)}, u32[]{:S(2)}) collective-permute-start(f32[408,128]{1,0:T(8,128)S(1)} %update.11.mine), channel_id=1, source_target_pairs={{0,1},{1,0},{2,3},{3,2},{4,5},{5,4},{6,7},{7,6},{8,9},{9,8},{10,11... | collective-permute-start | bytes 626696 | tf_op jit(solution)/shard_map/ppermute | solution.py:58
  118.5 4.7 %collective-permute-start.46 = (bf16[400,128]{1,0:T(8,128)(2,1)S(1)}, bf16[400,128]{1,0:T(8,128)(2,1)S(1)}, u32[]{:S(2)}, u32[]{:S(2)}) collective-permute-start(bf16[400,128]{1,0:T(8,128)(2,1)S(1)} %sum_piece.7.refs_0_), channel_id=1, source_target_pairs={{0,4},{2,6},{4,0},{6,2},{8,12},{10,14},{12,8},{14,10},{1,5},{3,7},... | collective-permute-start | bytes 307208 | tf_op jit(solution)/shard_map/ppermute | solution.py:54
  118.5 10.0 %collective-permute-start.44 = (bf16[400,128]{1,0:T(8,128)(2,1)S(1)}, bf16[400,128]{1,0:T(8,128)(2,1)S(1)}, u32[]{:S(2)}, u32[]{:S(2)}) collective-permute-start(bf16[400,128]{1,0:T(8,128)(2,1)S(1)} %sum_piece.7.refs_0_), channel_id=1, source_target_pairs={{0,8},{2,10},{4,12},{6,14},{8,0},{10,2},{12,4},{14,6},{1,9},{3,11}... | collective-permute-start | bytes 307208 | tf_op jit(solution)/shard_map/ppermute | solution.py:54
  121.6 7.7 %collective-permute-start.42 = (bf16[400,128]{1,0:T(8,128)(2,1)S(1)}, bf16[400,128]{1,0:T(8,128)(2,1)S(1)}, u32[]{:S(2)}, u32[]{:S(2)}) collective-permute-start(bf16[400,128]{1,0:T(8,128)(2,1)S(1)} %sum_piece.7.refs_0_), channel_id=1, source_target_pairs={{0,12},{2,14},{4,8},{6,10},{8,4},{10,6},{12,0},{14,2},{1,13},{3,15... | collective-permute-start | bytes 307208 | tf_op jit(solution)/shard_map/ppermute | solution.py:54
  122.9 8.6 %collective-permute-start.41 = (bf16[400,128]{1,0:T(8,128)(2,1)S(1)}, bf16[400,128]{1,0:T(8,128)(2,1)S(1)}, u32[]{:S(2)}, u32[]{:S(2)}) collective-permute-start(bf16[400,128]{1,0:T(8,128)(2,1)S(1)} %sum_piece.7.refs_0_), channel_id=1, source_target_pairs={{0,2},{2,0},{4,6},{6,4},{8,10},{10,8},{12,14},{14,12},{1,3},{3,1},... | collective-permute-start | bytes 307208 | tf_op jit(solution)/shard_map/ppermute | solution.py:54
  123.2 8.3 %collective-permute-start.47 = (bf16[400,128]{1,0:T(8,128)(2,1)S(1)}, bf16[400,128]{1,0:T(8,128)(2,1)S(1)}, u32[]{:S(2)}, u32[]{:S(2)}) collective-permute-start(bf16[400,128]{1,0:T(8,128)(2,1)S(1)} %collective-permute-done.46.refs_3_), channel_id=1, source_target_pairs={{0,2},{2,0},{4,6},{6,4},{8,10},{10,8},{12,14},{14,12},{1,3},{3,1},... | collective-permute-start | bytes 307208 | tf_op jit(solution)/shard_map/ppermute | solution.py:54
  128.6 4.7 %collective-permute-start.45 = (bf16[400,128]{1,0:T(8,128)(2,1)S(1)}, bf16[400,128]{1,0:T(8,128)(2,1)S(1)}, u32[]{:S(2)}, u32[]{:S(2)}) collective-permute-start(bf16[400,128]{1,0:T(8,128)(2,1)S(1)} %collective-permute-done.44.refs_2_), channel_id=1, source_target_pairs={{0,2},{2,0},{4,6},{6,4},{8,10},{10,8},{12,14},{14,12},{1,3},{3,1},... | collective-permute-start | bytes 307208 | tf_op jit(solution)/shard_map/ppermute | solution.py:54
  129.3 5.0 %collective-permute-start.43 = (bf16[400,128]{1,0:T(8,128)(2,1)S(1)}, bf16[400,128]{1,0:T(8,128)(2,1)S(1)}, u32[]{:S(2)}, u32[]{:S(2)}) collective-permute-start(bf16[400,128]{1,0:T(8,128)(2,1)S(1)} %collective-permute-done.42.refs_1_), channel_id=1, source_target_pairs={{0,2},{2,0},{4,6},{6,4},{8,10},{10,8},{12,14},{14,12},{1,3},{3,1},... | collective-permute-start | bytes 307208 | tf_op jit(solution)/shard_map/ppermute | solution.py:54
  131.5 3.0 %collective-permute-start.49 = (bf16[4,400,128]{2,1,0:T(8,128)(2,1)S(1)}, bf16[4,400,128]{2,1,0:T(8,128)(2,1)S(1)}, u32[]{:S(2)}, u32[]{:S(2)}) collective-permute-start(bf16[4,400,128]{2,1,0:T(8,128)(2,1)S(1)} %stacked.3), channel_id=1, source_target_pairs={{0,1},{1,0},{2,3},{3,2},{4,5},{5,4},{6,7},{7,6},{8,9},{9,8},{10,11... | collective-permute-start | bytes 1228808 | tf_op jit(solution)/shard_map/ppermute | solution.py:58
  134.4 1.8 %collective-permute-start.48 = (bf16[4,400,128]{2,1,0:T(8,128)(2,1)S(1)}, bf16[4,400,128]{2,1,0:T(8,128)(2,1)S(1)}, u32[]{:S(2)}, u32[]{:S(2)}) collective-permute-start(bf16[4,400,128]{2,1,0:T(8,128)(2,1)S(1)} %stacked.2), channel_id=1, source_target_pairs={{0,1},{1,0},{2,3},{3,2},{4,5},{5,4},{6,7},{7,6},{8,9},{9,8},{10,11... | collective-permute-start | bytes 1228808 | tf_op jit(solution)/shard_map/ppermute | solution.py:58
where the time goes:
time: 138 us
  waiting for transfers between devices  55.5 us (40%)
  Pallas kernels  51.9 us (38%)
  starting transfers between devices  29.4 us (21%)
  between operations  1.49 us (1%)
    ppermute x10, waiting for transfers between devices, shifted(): return lax.ppermute(x, 'dom', [(i, (i + by) % n) for i in range(n)])  27.3 us
    ppermute x14, waiting for transfers between devices, swapped(): return lax.ppermute(x, 'dom', [(i, i ^ bits) for i in range(n)])  16.9 us
    ppermute x14, starting transfers between devices, swapped(): return lax.ppermute(x, 'dom', [(i, i ^ bits) for i in range(n)])  15.9 us
    ppermute x26, waiting for transfers between devices, across(): return lax.ppermute(x, 'edge', [(0, 1), (1, 0)])  11.2 us
    pallas_call x5, Pallas kernels, relsum(): pl.pallas_call(functools.partial(relsum_kernel, t, acc is None), grid=(re...  10.7 us
    pallas_call x5, Pallas kernels, source_side(): pl.pallas_call(functools.partial(source_kernel, t, shape), in_specs=[anyw...  9.35 us
    ppermute x10, starting transfers between devices, shifted(): return lax.ppermute(x, 'dom', [(i, (i + by) % n) for i in range(n)])  9.12 us
    pallas_call x4, Pallas kernels, source_grad(): pl.pallas_call(functools.partial(source_grad_kernel, t, shape), in_specs=...  5.84 us
  transfers between devices with their start and end apart: 50, of which 29 were waited for; matrix products, arithmetic and copies ran while one was open for 0% of the time, Pallas kernels for 26%

commit v1 on v0

--- a/solution.py
+++ b/solution.py
@@ -338,12 +338,13 @@
     )(*(in_hbm(x) for x in (cnt, neg, src, dst, rel_ids, entities, state, relations)))
 
 
-def source_kernel(
-    t, shape, cnt_ref, neg_ref, src_ref, dst_ref, own0, own1, rel_ref,
-    query_ref, query_t_ref, source_ref, s_hot_ref, d_hot_ref, d_hot_t_ref,
-    v_hot_t_ref, n_hot_ref, n_hot_t_ref, mask_ref, cnt, neg, sems,
-):
-    limits = Limits(t, cnt_ref, neg_ref, cnt, neg, sems)
+def source_kernel(t, shape, last, cnt_ref, neg_ref, src_ref, dst_ref, own0, own1, rel_ref, *refs):
+    query_ref, query_t_ref, source_ref, s_hot_ref, d_hot_ref = refs[:5]
+    if last:
+        (d_hot_t_ref,) = refs[5:]
+    else:
+        v_hot_t_ref, n_hot_ref, n_hot_t_ref, mask_ref, cnt, neg, sems, d_hot_t_ref = refs[5:]
+        limits = Limits(t, cnt_ref, neg_ref, cnt, neg, sems)
     _, blocks, width = shape
     half = own0.shape[1]
     local = localize(place()[2], half)
@@ -357,6 +358,8 @@
     query = make_query(source, rel_ref[...].astype(F32))
     query_ref[...] = query
     query_t_ref[...] = query.T
+    if last:
+        return
     limits.wait()
     row_i = lax.broadcasted_iota(jnp.int32, (width, width), 0)
     col_j = lax.broadcasted_iota(jnp.int32, (width, width), 1)
@@ -377,18 +380,20 @@
     dim, slots = rel.shape
     width = shape[2]
     rows = 2 * own[0].shape[1]
+    last = t == shape[0] - 1
     sds = lambda *shape: jax.ShapeDtypeStruct(shape, BF)
-    return pl.pallas_call(
-        functools.partial(source_kernel, t, shape),
+    outs = [sds(dim, slots), sds(slots, dim), sds(dim, slots), sds(rows, slots), sds(rows, slots)]
+    if last:
+        outs += [sds(slots, rows)]
+    else:
+        outs += [sds(slots, rows), sds(rows, slots), sds(slots, rows)]
+        outs += [jax.ShapeDtypeStruct((width, slots), F32)]
+    return pl.pallas_call(
+        functools.partial(source_kernel, t, shape, last),
         in_specs=[anywhere()] * 2 + [vmem()] * 5,
-        out_specs=[vmem()] * 10,
-        out_shape=[
-            sds(dim, slots), sds(slots, dim), sds(dim, slots),
-            sds(rows, slots), sds(rows, slots), sds(slots, rows),
-            sds(slots, rows), sds(rows, slots), sds(slots, rows),
-            jax.ShapeDtypeStruct((width, slots), F32),
-        ],
-        scratch_shapes=Limits.scratch(shape),
+        out_specs=[vmem()] * len(outs),
+        out_shape=outs,
+        scratch_shapes=[] if last else Limits.scratch(shape) + [pltpu.VMEM((slots, rows), BF)],
         compiler_params=params(),
         cost_estimate=cost(dim * slots, dim * slots),
         name="source_side",
@@ -721,17 +726,17 @@
     )(*parts, *after)
 
 
-def relnew_kernel(nz, same, ks, rel_ref, state_ref, *refs):
-    mine, theirs = refs[: len(ks)], refs[len(ks)]
+def relnew_kernel(nz, kinds, count, first, rel_ref, state_ref, *refs):
+    arrays = refs[:count]
     rel_out, state_out, buf, sems = refs[-4:]
-    w = mine[0].shape[1]
-    state_out[...] = refs[len(ks) + (1 if same else 2)][...]
+    w = buf.shape[2]
+    state_out[...] = refs[count + (0 if first else 1)][...]
     z, x, edge = place()
     copies = []
-    for i in range(2 * len(ks)):
-        owner = 2 * lax.bitwise_xor(z, ks[i // 2]) + (x if same else 1 - x)
-        at = pl.ds(first_column(owner, edge if i % 2 == 0 else 1 - edge, w), w)
-        grad = (mine[i // 2][...] if i % 2 == 0 else theirs[i // 2]).astype(F32)
+    for i, (k, same, own, source, index) in enumerate(kinds):
+        owner = 2 * lax.bitwise_xor(z, k) + (x if same else 1 - x)
+        at = pl.ds(first_column(owner, edge if own else 1 - edge, w), w)
+        grad = (arrays[source][...] if index is None else arrays[source][index]).astype(F32)
         state = state_ref[:, at] + jnp.sum(grad * grad, axis=0, keepdims=True) / grad.shape[0]
         state_out[:, at] = state
         buf[i] = rel_ref[:, at] - grad * (learn_rate / jnp.sqrt(state))
@@ -742,25 +747,31 @@
         copy.wait()
 
 
-def relnew(nz, same, ks, relations, state, mine, theirs, before, after):
+def relnew(nz, relations, state, groups, before, after):
     dim, rels = relations.shape
-    w = mine[0].shape[1]
-    count = 2 * len(ks)
+    w = rels // (4 * nz)
+    kinds, arrays = [], []
+    for ks, same, own, parts in groups:
+        one = not isinstance(parts, list)
+        for i, k in enumerate(ks):
+            kinds.append((k, same, own, len(arrays) + (0 if one else i), i if one else None))
+        arrays += [parts] if one else parts
+    count = len(kinds)
     start = [state] if before is None else list(before)
     return pl.pallas_call(
-        functools.partial(relnew_kernel, nz, same, ks),
-        in_specs=[vmem()] * (3 + len(ks))
+        functools.partial(relnew_kernel, nz, tuple(kinds), len(arrays), before is None),
+        in_specs=[vmem()] * (2 + len(arrays))
         + ([anywhere()] if before else [])
         + [vmem()]
         + [anywhere()] * len(after),
         out_specs=[anywhere(), vmem()],
         out_shape=[jax.ShapeDtypeStruct((dim, rels), F32), jax.ShapeDtypeStruct((1, rels), F32)],
-        input_output_aliases={3 + len(ks): 0} if before else {},
+        input_output_aliases={2 + len(arrays): 0} if before else {},
         scratch_shapes=[pltpu.VMEM((count, dim, w), F32), pltpu.SemaphoreType.DMA((count,))],
         compiler_params=params(),
-        cost_estimate=cost(4 * dim * w * count, 4 * dim * w * count),
+        cost_estimate=cost(dim, dim),
         name="relnew",
-    )(relations, state, *mine, theirs, *start, *after)
+    )(relations, state, *arrays, *start, *after)
 
 
 def relation_update(t, rel_ids, drel, acc, relations, state, send, finish):
@@ -790,10 +801,13 @@
     state = state.reshape(1, rels)
     ks = [0, *down[:-1]]
     mine = [got[k] for k in ks]
-    new = relnew(nz, True, ks, relations, state, mine, across(stacked(mine, [done[2]])), None, [])
-    mine = [got_x[k] for k in ks]
-    theirs = across(stacked(mine, []))
-    rel_new, state_new = relnew(nz, False, ks, relations, state, mine, theirs, new, [])
+    mine_x = [got_x[k] for k in ks]
+    there = across(stacked(mine, [done[2]]))
+    new = relnew(nz, relations, state, [(ks, True, True, mine)], None, [])
+    there_x = across(stacked(mine_x, [new[1]]))
+    groups = [(ks, True, False, there), (ks, False, True, mine_x)]
+    new = relnew(nz, relations, state, groups, new, [])
+    rel_new, state_new = relnew(nz, relations, state, [(ks, False, False, there_x)], new, [])
     return rel_new, state_new.reshape(rels), done
 
 
@@ -821,7 +835,7 @@
     for t in range(1, rounds):
         far = shifted(low, -t)
         own = (low, across(low))
-        query, query_t, source, s_hot, d_hot, d_hot_t, *negatives = source_side(
+        query, query_t, source, s_hot, d_hot, *hots = source_side(
             t, shape, cnt, neg, src_rows, dst_rows, own, rel
         )
         far = held(far, [query, acc])
@@ -829,7 +843,7 @@
         if t == rounds - 1:
             break
         near = near_products(query_t, far[0])
-        gd_mine, gd_other, weight = target_grad(near, far[1], query, query_t, *negatives)
+        gd_mine, gd_other, weight = target_grad(near, far[1], query, query_t, *hots)
         gd = sum_pair(gd_mine, across(gd_other))
         gs_mine, gs_other, drel = source_grad(
             t, shape, cnt, neg, gd, far, d_hot, query, weight, source, rel, s_hot
@@ -841,7 +855,7 @@
     drel, dsource, dterm = last_terms(t, shape, cnt, neg, far, query, query_t, d_hot, source, rel)
 
     def send(after):
-        gs_mine, gs_other, gd_mine, gd_other = both_grads(after, dsource, s_hot, dterm, d_hot_t)
+        gs_mine, gs_other, gd_mine, gd_other = both_grads(after, dsource, s_hot, dterm, hots[0])
         gd = sum_pair(gd_mine, across(gd_other))
         return [gs_mine, across(gs_other), shifted(gd, t)]
 

time: 138 us -> 137 us (level)
  Pallas kernels: 51.9 us -> 47.5 us
  waiting for transfers between devices: 55.5 us -> 59.4 us
    ppermute x10, waiting for transfers between devices: 27.3 us -> 33.3 us  [shifted(): return lax.ppermute(x, 'dom', [(i, (i + by) % n) for i in range(n)])]
    pallas_call x7 -> x8, Pallas kernels: 12.6 us -> 8.13 us  [the longest x5 4.14 us: source_side(): pl.pallas_call(functools.partial(source_kernel, t, shape, last), in_specs...]
    ppermute x10, starting transfers between devices: 9.12 us -> 6.7 us  [shifted(): return lax.ppermute(x, 'dom', [(i, (i + by) % n) for i in range(n)])]
    ppermute x14, waiting for transfers between devices: 16.9 us -> 15 us  [swapped(): return lax.ppermute(x, 'dom', [(i, i ^ bits) for i in range(n)])]
  transfers between devices with their start and end apart: 50 -> 50, of which waited for: 29 -> 27; matrix products, arithmetic and copies ran while one was open for 0% -> 0% of each run, Pallas kernels for 26% -> 23%
where the time goes in v1:
time: 137 us
  waiting for transfers between devices  59.4 us (43%)
  Pallas kernels  47.5 us (35%)
  starting transfers between devices  28.6 us (21%)
  between operations  1.51 us (1%)
    ppermute x10, waiting for transfers between devices, shifted(): return lax.ppermute(x, 'dom', [(i, (i + by) % n) for i in range(n)])  33.3 us
    ppermute x14, starting transfers between devices, swapped(): return lax.ppermute(x, 'dom', [(i, i ^ bits) for i in range(n)])  17.2 us
    ppermute x14, waiting for transfers between devices, swapped(): return lax.ppermute(x, 'dom', [(i, i ^ bits) for i in range(n)])  15 us
    ppermute x26, waiting for transfers between devices, across(): return lax.ppermute(x, 'edge', [(0, 1), (1, 0)])  11.2 us
    pallas_call x5, Pallas kernels, relsum(): pl.pallas_call(functools.partial(relsum_kernel, t, acc is None), grid=(re...  10.7 us
    ppermute x10, starting transfers between devices, shifted(): return lax.ppermute(x, 'dom', [(i, (i + by) % n) for i in range(n)])  6.7 us
    pallas_call x4, Pallas kernels, source_grad(): pl.pallas_call(functools.partial(source_grad_kernel, t, shape), in_specs=...  5.9 us
    pallas_call x4, Pallas kernels, target_grad(): pl.pallas_call(target_kernel, in_specs=[vmem()] * 8, out_specs=[vmem()] *...  5.51 us
  transfers between devices with their start and end apart: 50, of which 27 were waited for; matrix products, arithmetic and copies ran while one was open for 0% of the time, Pallas kernels for 23%

profile of v1, /device:TPU:0, one launch (start us, length us, event | category | flops | bytes accessed | tf_op | source)
XLA Modules:
  0.0 137.1 jit_solution(12670794703120892843)
XLA Ops:
  0.6 5.4 %first_round.1 = (f32[400,128]{1,0:T(8,128)S(1)}, bf16[400,128]{1,0:T(8,128)(2,1)S(1)}, bf16[400,512]{1,0:T(8,128)(2,1)S(1)}, bf16[400,2048]{1,0:T(8,128)(2,1)S(...) custom-call(s32[4,6]{1,0:T(4,128)} %bitcast.6, s32[4,6]{1,0:T(4,128)} %bitcast.17, s32[6,4,128]{2,1,0:T(4,128)} %src_ref.11, ...), custom_call_target="tpu_custom_call" | custom-call | flops 1258291200 | bytes 6553600 | tf_op jit(solution)/shard_map/first_round/pallas_call | solution.py:309
  6.6 0.9 collective-permute-done.refs_3_
  8.1 5.7 %collective-permute-start.2 = (bf16[400,128]{1,0:T(8,128)(2,1)S(1)}, bf16[400,128]{1,0:T(8,128)(2,1)S(1)}, u32[]{:S(2)}, u32[]{:S(2)}) collective-permute-start(bf16[400,128]{1,0:T(8,128)(2,1)S(1)} %get-tuple-element.127.own0), channel_id=1, source_target_pairs={{0,14},{2,0},{4,2},{6,4},{8,6},{10,8},{12,10},{14,12},{1,15},{3,1}... | collective-permute-start | bytes 307208 | tf_op jit(solution)/shard_map/ppermute | solution.py:49
  13.8 1.0 relvec.5.rel_ref
  14.8 1.9 %relsum.5.refs_1_.refs_0_ = f32[400,2048]{1,0:T(8,128)S(1)} custom-call(s32[6,4,128]{2,1,0:T(4,128)S(1)} %copy-done.1, bf16[400,512]{1,0:T(8,128)(2,1)S(1)} %get-tuple-element.131.drel_ref), custom_call_target="tpu_custom_call" | custom-call | flops 204800 | bytes 204800 | tf_op jit(solution)/shard_map/relsum/pallas_call | solution.py:113
  16.8 0.9 source_side.5
  18.1 1.0 collective-permute-done.3.far1
  19.1 1.4 %target_grad.4 = (f32[400,128]{1,0:T(8,128)S(1)}, bf16[400,128]{1,0:T(8,128)(2,1)S(1)}, bf16[128,512]{1,0:T(8,128)(2,1)S(1)}) custom-call(f32[512,128]{1,0:T(8,128)S(1)} %near_products.4.near, bf16[400,128]{1,0:T(8,128)(2,1)S(1)} %collective-permute-done.3.far1, bf16[400,512]{1,0:T(8,128)(2,1)S(1)} %get-tuple-element.130.refs_0_.query_ref, ...), custom_call_target="tpu_custom_call" | custom-call | flops 104857600 | bytes 2457600 | tf_op jit(solution)/shard_map/target_grad/pallas_call | solution.py:447
  20.7 1.2 collective-permute-done.4.b_ref
  21.9 1.5 %source_grad.4 = (f32[400,128]{1,0:T(8,128)S(1)}, bf16[400,128]{1,0:T(8,128)(2,1)S(1)}, bf16[400,512]{1,0:T(8,128)(2,1)S(1)}) custom-call(s32[4,6]{1,0:T(4,128)S(1)} %bitcast.8, s32[4,6]{1,0:T(4,128)S(1)} %bitcast.19, bf16[400,128]{1,0:T(8,128)(2,1)S(1)} %sum_pair.9._, bf16[400,128]{1,0:T(8,128)(2,1)S(1)} %held.5.far0, ...), custom_call_target="tpu_custom_call" | custom-call | flops 204800 | bytes 204800 | tf_op jit(solution)/shard_map/source_grad/pallas_call | solution.py:479
  23.7 1.0 relvec.6.refs_4_.rel_ref
  24.7 4.9 %collective-permute-done.5.b_ref = bf16[400,128]{1,0:T(8,128)(2,1)S(1)} collective-permute-done((bf16[400,128]{1,0:T(8,128)(2,1)S(1)}, bf16[400,128]{1,0:T(8,128)(2,1)S(1)}, u32[]{:S(2)}, u32[]{:S(2)}) %collective-permute-start.5) | collective-permute-done | bytes 102432 | tf_op jit(solution)/shard_map/ppermute | solution.py:49
  29.9 2.2 %relsum.6.refs_1_.refs_0_ = f32[400,2048]{1,0:T(8,128)S(1)} custom-call(s32[6,4,128]{2,1,0:T(4,128)S(1)} %copy-done.1, bf16[400,512]{1,0:T(8,128)(2,1)S(1)} %get-tuple-element.149.drel_ref, f32[400,2048]{1,0:T(8,128)S(1)} %relsum.5.refs_1_.refs_0_), custom_call_target="tpu_custom_call", output_to_operand_aliasing={{}: (2, {})} | custom-call | flops 204800 | bytes 204800 | tf_op jit(solution)/shard_map/relsum/pallas_call | solution.py:113
  32.1 0.9 source_side.6
  33.0 2.1 %collective-permute-done.8.x_ref = bf16[400,128]{1,0:T(8,128)(2,1)S(1)} collective-permute-done((bf16[400,128]{1,0:T(8,128)(2,1)S(1)}, bf16[400,128]{1,0:T(8,128)(2,1)S(1)}, u32[]{:S(2)}, u32[]{:S(2)}) %collective-permute-start.8) | collective-permute-done | bytes 102432 | tf_op jit(solution)/shard_map/ppermute | solution.py:49
  35.4 1.0 collective-permute-done.9.far1
  36.4 1.4 %target_grad.5 = (f32[400,128]{1,0:T(8,128)S(1)}, bf16[400,128]{1,0:T(8,128)(2,1)S(1)}, bf16[128,512]{1,0:T(8,128)(2,1)S(1)}) custom-call(f32[512,128]{1,0:T(8,128)S(1)} %near_products.5.near, bf16[400,128]{1,0:T(8,128)(2,1)S(1)} %collective-permute-done.9.far1, bf16[400,512]{1,0:T(8,128)(2,1)S(1)} %get-tuple-element.148.refs_0_.query_ref, ...), custom_call_target="tpu_custom_call" | custom-call | flops 104857600 | bytes 2457600 | tf_op jit(solution)/shard_map/target_grad/pallas_call | solution.py:447
  38.0 1.2 collective-permute-done.10.b_ref
  39.4 1.5 %source_grad.5 = (f32[400,128]{1,0:T(8,128)S(1)}, bf16[400,128]{1,0:T(8,128)(2,1)S(1)}, bf16[400,512]{1,0:T(8,128)(2,1)S(1)}) custom-call(s32[4,6]{1,0:T(4,128)S(1)} %bitcast.10, s32[4,6]{1,0:T(4,128)S(1)} %bitcast.21, bf16[400,128]{1,0:T(8,128)(2,1)S(1)} %sum_pair.11._, bf16[400,128]{1,0:T(8,128)(2,1)S(1)} %held.6.far0, ...), custom_call_target="tpu_custom_call" | custom-call | flops 204800 | bytes 204800 | tf_op jit(solution)/shard_map/source_grad/pallas_call | solution.py:479
  41.1 1.0 relvec.7.refs_4_.rel_ref
  42.2 4.0 %collective-permute-done.11.b_ref = bf16[400,128]{1,0:T(8,128)(2,1)S(1)} collective-permute-done((bf16[400,128]{1,0:T(8,128)(2,1)S(1)}, bf16[400,128]{1,0:T(8,128)(2,1)S(1)}, u32[]{:S(2)}, u32[]{:S(2)}) %collective-permute-start.11) | collective-permute-done | bytes 102432 | tf_op jit(solution)/shard_map/ppermute | solution.py:49
  46.5 2.2 %relsum.7.refs_1_.refs_0_ = f32[400,2048]{1,0:T(8,128)S(1)} custom-call(s32[6,4,128]{2,1,0:T(4,128)S(1)} %copy-done.1, bf16[400,512]{1,0:T(8,128)(2,1)S(1)} %get-tuple-element.167.drel_ref, f32[400,2048]{1,0:T(8,128)S(1)} %relsum.6.refs_1_.refs_0_), custom_call_target="tpu_custom_call", output_to_operand_aliasing={{}: (2, {})} | custom-call | flops 204800 | bytes 204800 | tf_op jit(solution)/shard_map/relsum/pallas_call | solution.py:113
  48.7 0.9 source_side.7
  49.6 3.0 %collective-permute-done.14.x_ref = bf16[400,128]{1,0:T(8,128)(2,1)S(1)} collective-permute-done((bf16[400,128]{1,0:T(8,128)(2,1)S(1)}, bf16[400,128]{1,0:T(8,128)(2,1)S(1)}, u32[]{:S(2)}, u32[]{:S(2)}) %collective-permute-start.14) | collective-permute-done | bytes 102432 | tf_op jit(solution)/shard_map/ppermute | solution.py:49
  52.9 1.0 collective-permute-done.15.far1
  53.9 1.4 %target_grad.6 = (f32[400,128]{1,0:T(8,128)S(1)}, bf16[400,128]{1,0:T(8,128)(2,1)S(1)}, bf16[128,512]{1,0:T(8,128)(2,1)S(1)}) custom-call(f32[512,128]{1,0:T(8,128)S(1)} %near_products.6.near, bf16[400,128]{1,0:T(8,128)(2,1)S(1)} %collective-permute-done.15.far1, bf16[400,512]{1,0:T(8,128)(2,1)S(1)} %get-tuple-element.166.refs_0_.query_ref, ...), custom_call_target="tpu_custom_call" | custom-call | flops 104857600 | bytes 2457600 | tf_op jit(solution)/shard_map/target_grad/pallas_call | solution.py:447
  55.5 1.2 collective-permute-done.16.b_ref
  56.7 1.5 %source_grad.6 = (f32[400,128]{1,0:T(8,128)S(1)}, bf16[400,128]{1,0:T(8,128)(2,1)S(1)}, bf16[400,512]{1,0:T(8,128)(2,1)S(1)}) custom-call(s32[4,6]{1,0:T(4,128)S(1)} %bitcast.12, s32[4,6]{1,0:T(4,128)S(1)} %bitcast.23, bf16[400,128]{1,0:T(8,128)(2,1)S(1)} %sum_pair.13._, bf16[400,128]{1,0:T(8,128)(2,1)S(1)} %held.7.far0, ...), custom_call_target="tpu_custom_call" | custom-call | flops 204800 | bytes 204800 | tf_op jit(solution)/shard_map/source_grad/pallas_call | solution.py:479
  58.4 1.0 relvec.8.refs_4_.rel_ref
  59.5 6.2 %collective-permute-done.17.b_ref = bf16[400,128]{1,0:T(8,128)(2,1)S(1)} collective-permute-done((bf16[400,128]{1,0:T(8,128)(2,1)S(1)}, bf16[400,128]{1,0:T(8,128)(2,1)S(1)}, u32[]{:S(2)}, u32[]{:S(2)}) %collective-permute-start.17) | collective-permute-done | bytes 102432 | tf_op jit(solution)/shard_map/ppermute | solution.py:49
  66.0 2.2 %relsum.8.refs_1_.refs_0_ = f32[400,2048]{1,0:T(8,128)S(1)} custom-call(s32[6,4,128]{2,1,0:T(4,128)S(1)} %copy-done.1, bf16[400,512]{1,0:T(8,128)(2,1)S(1)} %get-tuple-element.185.drel_ref, f32[400,2048]{1,0:T(8,128)S(1)} %relsum.7.refs_1_.refs_0_), custom_call_target="tpu_custom_call", output_to_operand_aliasing={{}: (2, {})} | custom-call | flops 204800 | bytes 204800 | tf_op jit(solution)/shard_map/relsum/pallas_call | solution.py:113
  68.2 0.9 source_side.8
  69.1 3.8 %collective-permute-done.20.x_ref = bf16[400,128]{1,0:T(8,128)(2,1)S(1)} collective-permute-done((bf16[400,128]{1,0:T(8,128)(2,1)S(1)}, bf16[400,128]{1,0:T(8,128)(2,1)S(1)}, u32[]{:S(2)}, u32[]{:S(2)}) %collective-permute-start.20) | collective-permute-done | bytes 102432 | tf_op jit(solution)/shard_map/ppermute | solution.py:49
  73.3 0.9 collective-permute-done.21.far1
  74.2 1.4 %target_grad.7 = (f32[400,128]{1,0:T(8,128)S(1)}, bf16[400,128]{1,0:T(8,128)(2,1)S(1)}, bf16[128,512]{1,0:T(8,128)(2,1)S(1)}) custom-call(f32[512,128]{1,0:T(8,128)S(1)} %near_products.7.near, bf16[400,128]{1,0:T(8,128)(2,1)S(1)} %collective-permute-done.21.far1, bf16[400,512]{1,0:T(8,128)(2,1)S(1)} %get-tuple-element.184.refs_0_.query_ref, ...), custom_call_target="tpu_custom_call" | custom-call | flops 104857600 | bytes 2457600 | tf_op jit(solution)/shard_map/target_grad/pallas_call | solution.py:447
  75.8 1.2 collective-permute-done.22.b_ref
  77.1 1.5 %source_grad.7 = (f32[400,128]{1,0:T(8,128)S(1)}, bf16[400,128]{1,0:T(8,128)(2,1)S(1)}, bf16[400,512]{1,0:T(8,128)(2,1)S(1)}) custom-call(s32[4,6]{1,0:T(4,128)S(1)} %bitcast.14, s32[4,6]{1,0:T(4,128)S(1)} %bitcast.25, bf16[400,128]{1,0:T(8,128)(2,1)S(1)} %sum_pair.15._, bf16[400,128]{1,0:T(8,128)(2,1)S(1)} %held.8.far0, ...), custom_call_target="tpu_custom_call" | custom-call | flops 204800 | bytes 204800 | tf_op jit(solution)/shard_map/source_grad/pallas_call | solution.py:479
  78.8 1.0 relvec.9.refs_4_.rel_ref
  79.8 5.1 %collective-permute-done.23.b_ref = bf16[400,128]{1,0:T(8,128)(2,1)S(1)} collective-permute-done((bf16[400,128]{1,0:T(8,128)(2,1)S(1)}, bf16[400,128]{1,0:T(8,128)(2,1)S(1)}, u32[]{:S(2)}, u32[]{:S(2)}) %collective-permute-start.23) | collective-permute-done | bytes 102432 | tf_op jit(solution)/shard_map/ppermute | solution.py:49
  85.4 2.2 %relsum.9.refs_1_.acc_ref = f32[400,2048]{1,0:T(8,128)S(1)} custom-call(s32[6,4,128]{2,1,0:T(4,128)S(1)} %copy-done.1, bf16[400,512]{1,0:T(8,128)(2,1)S(1)} %get-tuple-element.202.drel_ref, f32[400,2048]{1,0:T(8,128)S(1)} %relsum.8.refs_1_.refs_0_), custom_call_target="tpu_custom_call", output_to_operand_aliasing={{}: (2, {})} | custom-call | flops 204800 | bytes 204800 | tf_op jit(solution)/shard_map/relsum/pallas_call | solution.py:113
  88.2 4.2 %collective-permute-done.25.x_ref = bf16[400,128]{1,0:T(8,128)(2,1)S(1)} collective-permute-done((bf16[400,128]{1,0:T(8,128)(2,1)S(1)}, bf16[400,128]{1,0:T(8,128)(2,1)S(1)}, u32[]{:S(2)}, u32[]{:S(2)}) %collective-permute-start.25) | collective-permute-done | bytes 102432 | tf_op jit(solution)/shard_map/ppermute | solution.py:49
  92.4 1.3 collective-permute-done.27.far1
  93.7 1.8 %last_terms.1 = (bf16[400,512]{1,0:T(8,128)(2,1)S(1)}, bf16[400,512]{1,0:T(8,128)(2,1)S(1)}, bf16[400,512]{1,0:T(8,128)(2,1)S(1)}) custom-call(s32[4,6]{1,0:T(4,128)S(1)} %bitcast.16, s32[4,6]{1,0:T(4,128)S(1)} %bitcast.27, bf16[400,128]{1,0:T(8,128)(2,1)S(1)} %held.9.far0, bf16[400,128]{1,0:T(8,128)(2,1)S(1)} %collective-permute-done.27.far1, ...), custom_call_target="tpu_custom_call" | custom-call | flops 157286400 | bytes 2457600 | tf_op jit(solution)/shard_map/last_terms/pallas_call | solution.py:509
  95.6 0.7 pieces.2
  96.4 0.7 pieces.3
  98.6 0.9 collective-permute-start.33
  99.5 1.2 collective-permute-start.37
  100.7 0.8 collective-permute-start.39
  101.7 3.0 %collective-permute-start.35 = (bf16[400,128]{1,0:T(8,128)(2,1)S(1)}, bf16[400,128]{1,0:T(8,128)(2,1)S(1)}, u32[]{:S(2)}, u32[]{:S(2)}) collective-permute-start(bf16[400,128]{1,0:T(8,128)(2,1)S(1)} %get-tuple-element.226), channel_id=1, source_target_pairs={{0,2},{2,0},{4,6},{6,4},{8,10},{10,8},{12,14},{14,12},{1,3},{3,1},... | collective-permute-start | bytes 307208 | tf_op jit(solution)/shard_map/ppermute | solution.py:54
  104.8 2.1 %collective-permute-start.36 = (bf16[400,128]{1,0:T(8,128)(2,1)S(1)}, bf16[400,128]{1,0:T(8,128)(2,1)S(1)}, u32[]{:S(2)}, u32[]{:S(2)}) collective-permute-start(bf16[400,128]{1,0:T(8,128)(2,1)S(1)} %sum_piece.4.refs_5_), channel_id=1, source_target_pairs={{0,12},{2,14},{4,8},{6,10},{8,4},{10,6},{12,0},{14,2},{1,13},{3,15... | collective-permute-start | bytes 307208 | tf_op jit(solution)/shard_map/ppermute | solution.py:54
  106.9 1.9 %collective-permute-done.37.refs_0_ = bf16[400,128]{1,0:T(8,128)(2,1)S(1)} collective-permute-done((bf16[400,128]{1,0:T(8,128)(2,1)S(1)}, bf16[400,128]{1,0:T(8,128)(2,1)S(1)}, u32[]{:S(2)}, u32[]{:S(2)}) %collective-permute-start.37) | collective-permute-done | bytes 102432 | tf_op jit(solution)/shard_map/ppermute | solution.py:54
  108.9 2.1 %collective-permute-done.39.refs_0_ = bf16[400,128]{1,0:T(8,128)(2,1)S(1)} collective-permute-done((bf16[400,128]{1,0:T(8,128)(2,1)S(1)}, bf16[400,128]{1,0:T(8,128)(2,1)S(1)}, u32[]{:S(2)}, u32[]{:S(2)}) %collective-permute-start.39) | collective-permute-done | bytes 102432 | tf_op jit(solution)/shard_map/ppermute | solution.py:54
  112.4 4.7 %collective-permute-done.38.refs_2_ = bf16[400,128]{1,0:T(8,128)(2,1)S(1)} collective-permute-done((bf16[400,128]{1,0:T(8,128)(2,1)S(1)}, bf16[400,128]{1,0:T(8,128)(2,1)S(1)}, u32[]{:S(2)}, u32[]{:S(2)}) %collective-permute-start.38) | collective-permute-done | bytes 102432 | tf_op jit(solution)/shard_map/ppermute | solution.py:54
  117.7 2.7 %collective-permute-start.44 = (bf16[400,128]{1,0:T(8,128)(2,1)S(1)}, bf16[400,128]{1,0:T(8,128)(2,1)S(1)}, u32[]{:S(2)}, u32[]{:S(2)}) collective-permute-start(bf16[400,128]{1,0:T(8,128)(2,1)S(1)} %sum_piece.7.refs_0_), channel_id=1, source_target_pairs={{0,8},{2,10},{4,12},{6,14},{8,0},{10,2},{12,4},{14,6},{1,9},{3,11}... | collective-permute-start | bytes 307208 | tf_op jit(solution)/shard_map/ppermute | solution.py:54
  120.5 1.6 %collective-permute-start.42 = (bf16[400,128]{1,0:T(8,128)(2,1)S(1)}, bf16[400,128]{1,0:T(8,128)(2,1)S(1)}, u32[]{:S(2)}, u32[]{:S(2)}) collective-permute-start(bf16[400,128]{1,0:T(8,128)(2,1)S(1)} %sum_piece.7.refs_0_), channel_id=1, source_target_pairs={{0,12},{2,14},{4,8},{6,10},{8,4},{10,6},{12,0},{14,2},{1,13},{3,15... | collective-permute-start | bytes 307208 | tf_op jit(solution)/shard_map/ppermute | solution.py:54
  122.5 1.7 %collective-permute-start.47 = (bf16[400,128]{1,0:T(8,128)(2,1)S(1)}, bf16[400,128]{1,0:T(8,128)(2,1)S(1)}, u32[]{:S(2)}, u32[]{:S(2)}) collective-permute-start(bf16[400,128]{1,0:T(8,128)(2,1)S(1)} %collective-permute-done.46.refs_3_), channel_id=1, source_target_pairs={{0,2},{2,0},{4,6},{6,4},{8,10},{10,8},{12,14},{14,12},{1,3},{3,1},... | collective-permute-start | bytes 307208 | tf_op jit(solution)/shard_map/ppermute | solution.py:54
  124.2 3.5 %collective-permute-done.44.refs_2_ = bf16[400,128]{1,0:T(8,128)(2,1)S(1)} collective-permute-done((bf16[400,128]{1,0:T(8,128)(2,1)S(1)}, bf16[400,128]{1,0:T(8,128)(2,1)S(1)}, u32[]{:S(2)}, u32[]{:S(2)}) %collective-permute-start.44) | collective-permute-done | bytes 102432 | tf_op jit(solution)/shard_map/ppermute | solution.py:54
  127.7 0.8 collective-permute-start.45
  128.5 1.2 collective-permute-start.43
  129.7 1.0 relnew.3
  130.8 0.8 whole_partition.1
  132.3 1.1 collective-permute-done.43.refs_1_.refs_2_
  133.6 1.3 relnew.4
  135.3 1.6 %relnew.5 = (f32[400,2048]{1,0:T(8,128)}, f32[1,2048]{1,0:T(1,128)}) custom-call(f32[400,2048]{1,0:T(8,128)S(1)} %copy-done, f32[1,2048]{1,0:T(1,128)S(1)} %bitcast.31, bf16[4,400,128]{2,1,0:T(8,128)(2,1)S(1)} %collective-permute-done.48.refs_0_, f32[400,2048]{1,0:T(8,128)} %get-tuple-element.234.refs_1_, ...), custom_call_target="tpu_custom_call", output_to_operand_aliasing={{0}: (3, {})} | custom-call | flops 400 | bytes 400 | tf_op jit(solution)/shard_map/relnew/pallas_call | solution.py:761
  (113 shorter events, 12.3 us)
Async XLA Ops:
  0.6 13.2 %copy-start.1 = (s32[6,4,128]{2,1,0:T(4,128)S(1)}, s32[6,4,128]{2,1,0:T(4,128)}, u32[]{:S(2)}) copy-start(s32[6,4,128]{2,1,0:T(4,128)} %ids_ref.25) | copy-start | bytes 36868
  6.1 10.7 %copy-start.2 = (s32[6,4,128]{2,1,0:T(4,128)S(1)}, s32[6,4,128]{2,1,0:T(4,128)}, u32[]{:S(2)}) copy-start(s32[6,4,128]{2,1,0:T(4,128)} %src_ref.11) | copy-start | bytes 36868
  6.1 10.7 %copy-start.3 = (s32[6,4,128]{2,1,0:T(4,128)S(1)}, s32[6,4,128]{2,1,0:T(4,128)}, u32[]{:S(2)}) copy-start(s32[6,4,128]{2,1,0:T(4,128)} %dst_ref.11) | copy-start | bytes 36868
  6.1 10.7 %copy-start.4 = (s32[6,4]{0,1:T(4,128)S(1)}, s32[6,4]{0,1:T(4,128)}, u32[]{:S(2)}) copy-start(s32[6,4]{0,1:T(4,128)} %param.16) | copy-start | bytes 292
  6.1 10.7 %copy-start.5 = (s32[6,4]{0,1:T(4,128)S(1)}, s32[6,4]{0,1:T(4,128)}, u32[]{:S(2)}) copy-start(s32[6,4]{0,1:T(4,128)} %param.17) | copy-start | bytes 292
  6.1 1.5 %collective-permute-start = (bf16[400,128]{1,0:T(8,128)(2,1)S(1)}, bf16[400,128]{1,0:T(8,128)(2,1)S(1)}, u32[]{:S(2)}, u32[]{:S(2)}) collective-permute-start(bf16[400,128]{1,0:T(8,128)(2,1)S(1)} %get-tuple-element.124), channel_id=1, source_target_pairs={{0,1},{1,0},{2,3},{3,2},{4,5},{5,4},{6,7},{7,6},{8,9},{9,8},{10,11... | collective-permute-start | bytes 307208 | tf_op jit(solution)/shard_map/ppermute | solution.py:58
  7.7 9.1 %collective-permute-start.1 = (bf16[400,128]{1,0:T(8,128)(2,1)S(1)}, bf16[400,128]{1,0:T(8,128)(2,1)S(1)}, u32[]{:S(2)}, u32[]{:S(2)}) collective-permute-start(bf16[400,128]{1,0:T(8,128)(2,1)S(1)} %get-tuple-element.127.own0), channel_id=1, source_target_pairs={{0,1},{1,0},{2,3},{3,2},{4,5},{5,4},{6,7},{7,6},{8,9},{9,8},{10,11... | collective-permute-start | bytes 307208 | tf_op jit(solution)/shard_map/ppermute | solution.py:58
  8.1 9.6 %collective-permute-start.2 = (bf16[400,128]{1,0:T(8,128)(2,1)S(1)}, bf16[400,128]{1,0:T(8,128)(2,1)S(1)}, u32[]{:S(2)}, u32[]{:S(2)}) collective-permute-start(bf16[400,128]{1,0:T(8,128)(2,1)S(1)} %get-tuple-element.127.own0), channel_id=1, source_target_pairs={{0,14},{2,0},{4,2},{6,4},{8,6},{10,8},{12,10},{14,12},{1,15},{3,1}... | collective-permute-start | bytes 307208 | tf_op jit(solution)/shard_map/ppermute | solution.py:49
  17.7 1.4 %collective-permute-start.3 = (bf16[400,128]{1,0:T(8,128)(2,1)S(1)}, bf16[400,128]{1,0:T(8,128)(2,1)S(1)}, u32[]{:S(2)}, u32[]{:S(2)}) collective-permute-start(bf16[400,128]{1,0:T(8,128)(2,1)S(1)} %held.5.far0), channel_id=1, source_target_pairs={{0,1},{1,0},{2,3},{3,2},{4,5},{5,4},{6,7},{7,6},{8,9},{9,8},{10,11... | collective-permute-start | bytes 307208 | tf_op jit(solution)/shard_map/ppermute | solution.py:58
  20.5 1.4 %collective-permute-start.4 = (bf16[400,128]{1,0:T(8,128)(2,1)S(1)}, bf16[400,128]{1,0:T(8,128)(2,1)S(1)}, u32[]{:S(2)}, u32[]{:S(2)}) collective-permute-start(bf16[400,128]{1,0:T(8,128)(2,1)S(1)} %get-tuple-element.137), channel_id=1, source_target_pairs={{0,1},{1,0},{2,3},{3,2},{4,5},{5,4},{6,7},{7,6},{8,9},{9,8},{10,11... | collective-permute-start | bytes 307208 | tf_op jit(solution)/shard_map/ppermute | solution.py:58
  21.9 7.7 %collective-permute-start.5 = (bf16[400,128]{1,0:T(8,128)(2,1)S(1)}, bf16[400,128]{1,0:T(8,128)(2,1)S(1)}, u32[]{:S(2)}, u32[]{:S(2)}) collective-permute-start(bf16[400,128]{1,0:T(8,128)(2,1)S(1)} %sum_pair.9._), channel_id=1, source_target_pairs={{0,2},{2,4},{4,6},{6,8},{8,10},{10,12},{12,14},{14,0},{1,3},{3,5},... | collective-permute-start | bytes 307208 | tf_op jit(solution)/shard_map/ppermute | solution.py:49
  23.4 6.2 %collective-permute-start.6 = (bf16[400,128]{1,0:T(8,128)(2,1)S(1)}, bf16[400,128]{1,0:T(8,128)(2,1)S(1)}, u32[]{:S(2)}, u32[]{:S(2)}) collective-permute-start(bf16[400,128]{1,0:T(8,128)(2,1)S(1)} %get-tuple-element.143), channel_id=1, source_target_pairs={{0,1},{1,0},{2,3},{3,2},{4,5},{5,4},{6,7},{7,6},{8,9},{9,8},{10,11... | collective-permute-start | bytes 307208 | tf_op jit(solution)/shard_map/ppermute | solution.py:58
  29.7 2.4 %collective-permute-start.7 = (bf16[400,128]{1,0:T(8,128)(2,1)S(1)}, bf16[400,128]{1,0:T(8,128)(2,1)S(1)}, u32[]{:S(2)}, u32[]{:S(2)}) collective-permute-start(bf16[400,128]{1,0:T(8,128)(2,1)S(1)} %get-tuple-element.146.own0), channel_id=1, source_target_pairs={{0,1},{1,0},{2,3},{3,2},{4,5},{5,4},{6,7},{7,6},{8,9},{9,8},{10,11... | collective-permute-start | bytes 307208 | tf_op jit(solution)/shard_map/ppermute | solution.py:58
  29.8 5.3 %collective-permute-start.8 = (bf16[400,128]{1,0:T(8,128)(2,1)S(1)}, bf16[400,128]{1,0:T(8,128)(2,1)S(1)}, u32[]{:S(2)}, u32[]{:S(2)}) collective-permute-start(bf16[400,128]{1,0:T(8,128)(2,1)S(1)} %get-tuple-element.146.own0), channel_id=1, source_target_pairs={{0,12},{2,14},{4,0},{6,2},{8,4},{10,6},{12,8},{14,10},{1,13},{3,15... | collective-permute-start | bytes 307208 | tf_op jit(solution)/shard_map/ppermute | solution.py:49
  35.1 1.3 collective-permute-start.9
  37.8 1.4 %collective-permute-start.10 = (bf16[400,128]{1,0:T(8,128)(2,1)S(1)}, bf16[400,128]{1,0:T(8,128)(2,1)S(1)}, u32[]{:S(2)}, u32[]{:S(2)}) collective-permute-start(bf16[400,128]{1,0:T(8,128)(2,1)S(1)} %get-tuple-element.155), channel_id=1, source_target_pairs={{0,1},{1,0},{2,3},{3,2},{4,5},{5,4},{6,7},{7,6},{8,9},{9,8},{10,11... | collective-permute-start | bytes 307208 | tf_op jit(solution)/shard_map/ppermute | solution.py:58
  39.2 7.0 %collective-permute-start.11 = (bf16[400,128]{1,0:T(8,128)(2,1)S(1)}, bf16[400,128]{1,0:T(8,128)(2,1)S(1)}, u32[]{:S(2)}, u32[]{:S(2)}) collective-permute-start(bf16[400,128]{1,0:T(8,128)(2,1)S(1)} %sum_pair.11._), channel_id=1, source_target_pairs={{0,4},{2,6},{4,8},{6,10},{8,12},{10,14},{12,0},{14,2},{1,5},{3,7},... | collective-permute-start | bytes 307208 | tf_op jit(solution)/shard_map/ppermute | solution.py:49
  40.9 5.3 %collective-permute-start.12 = (bf16[400,128]{1,0:T(8,128)(2,1)S(1)}, bf16[400,128]{1,0:T(8,128)(2,1)S(1)}, u32[]{:S(2)}, u32[]{:S(2)}) collective-permute-start(bf16[400,128]{1,0:T(8,128)(2,1)S(1)} %get-tuple-element.161), channel_id=1, source_target_pairs={{0,1},{1,0},{2,3},{3,2},{4,5},{5,4},{6,7},{7,6},{8,9},{9,8},{10,11... | collective-permute-start | bytes 307208 | tf_op jit(solution)/shard_map/ppermute | solution.py:58
  46.3 2.4 %collective-permute-start.13 = (bf16[400,128]{1,0:T(8,128)(2,1)S(1)}, bf16[400,128]{1,0:T(8,128)(2,1)S(1)}, u32[]{:S(2)}, u32[]{:S(2)}) collective-permute-start(bf16[400,128]{1,0:T(8,128)(2,1)S(1)} %get-tuple-element.164.own0), channel_id=1, source_target_pairs={{0,1},{1,0},{2,3},{3,2},{4,5},{5,4},{6,7},{7,6},{8,9},{9,8},{10,11... | collective-permute-start | bytes 307208 | tf_op jit(solution)/shard_map/ppermute | solution.py:58
  46.4 6.2 %collective-permute-start.14 = (bf16[400,128]{1,0:T(8,128)(2,1)S(1)}, bf16[400,128]{1,0:T(8,128)(2,1)S(1)}, u32[]{:S(2)}, u32[]{:S(2)}) collective-permute-start(bf16[400,128]{1,0:T(8,128)(2,1)S(1)} %get-tuple-element.164.own0), channel_id=1, source_target_pairs={{0,10},{2,12},{4,14},{6,0},{8,2},{10,4},{12,6},{14,8},{1,11},{3,13... | collective-permute-start | bytes 307208 | tf_op jit(solution)/shard_map/ppermute | solution.py:49
  52.6 1.3 collective-permute-start.15
  55.3 1.4 %collective-permute-start.16 = (bf16[400,128]{1,0:T(8,128)(2,1)S(1)}, bf16[400,128]{1,0:T(8,128)(2,1)S(1)}, u32[]{:S(2)}, u32[]{:S(2)}) collective-permute-start(bf16[400,128]{1,0:T(8,128)(2,1)S(1)} %get-tuple-element.173), channel_id=1, source_target_pairs={{0,1},{1,0},{2,3},{3,2},{4,5},{5,4},{6,7},{7,6},{8,9},{9,8},{10,11... | collective-permute-start | bytes 307208 | tf_op jit(solution)/shard_map/ppermute | solution.py:58
  56.7 9.0 %collective-permute-start.17 = (bf16[400,128]{1,0:T(8,128)(2,1)S(1)}, bf16[400,128]{1,0:T(8,128)(2,1)S(1)}, u32[]{:S(2)}, u32[]{:S(2)}) collective-permute-start(bf16[400,128]{1,0:T(8,128)(2,1)S(1)} %sum_pair.13._), channel_id=1, source_target_pairs={{0,6},{2,8},{4,10},{6,12},{8,14},{10,0},{12,2},{14,4},{1,7},{3,9},... | collective-permute-start | bytes 307208 | tf_op jit(solution)/shard_map/ppermute | solution.py:49
  58.2 7.5 %collective-permute-start.18 = (bf16[400,128]{1,0:T(8,128)(2,1)S(1)}, bf16[400,128]{1,0:T(8,128)(2,1)S(1)}, u32[]{:S(2)}, u32[]{:S(2)}) collective-permute-start(bf16[400,128]{1,0:T(8,128)(2,1)S(1)} %get-tuple-element.179), channel_id=1, source_target_pairs={{0,1},{1,0},{2,3},{3,2},{4,5},{5,4},{6,7},{7,6},{8,9},{9,8},{10,11... | collective-permute-start | bytes 307208 | tf_op jit(solution)/shard_map/ppermute | solution.py:58
  65.8 2.4 %collective-permute-start.19 = (bf16[400,128]{1,0:T(8,128)(2,1)S(1)}, bf16[400,128]{1,0:T(8,128)(2,1)S(1)}, u32[]{:S(2)}, u32[]{:S(2)}) collective-permute-start(bf16[400,128]{1,0:T(8,128)(2,1)S(1)} %get-tuple-element.182.own0), channel_id=1, source_target_pairs={{0,1},{1,0},{2,3},{3,2},{4,5},{5,4},{6,7},{7,6},{8,9},{9,8},{10,11... | collective-permute-start | bytes 307208 | tf_op jit(solution)/shard_map/ppermute | solution.py:58
  65.9 7.0 %collective-permute-start.20 = (bf16[400,128]{1,0:T(8,128)(2,1)S(1)}, bf16[400,128]{1,0:T(8,128)(2,1)S(1)}, u32[]{:S(2)}, u32[]{:S(2)}) collective-permute-start(bf16[400,128]{1,0:T(8,128)(2,1)S(1)} %get-tuple-element.182.own0), channel_id=1, source_target_pairs={{0,8},{2,10},{4,12},{6,14},{8,0},{10,2},{12,4},{14,6},{1,9},{3,11}... | collective-permute-start | bytes 307208 | tf_op jit(solution)/shard_map/ppermute | solution.py:49
  72.9 1.3 collective-permute-start.21
  75.6 1.4 %collective-permute-start.22 = (bf16[400,128]{1,0:T(8,128)(2,1)S(1)}, bf16[400,128]{1,0:T(8,128)(2,1)S(1)}, u32[]{:S(2)}, u32[]{:S(2)}) collective-permute-start(bf16[400,128]{1,0:T(8,128)(2,1)S(1)} %get-tuple-element.191), channel_id=1, source_target_pairs={{0,1},{1,0},{2,3},{3,2},{4,5},{5,4},{6,7},{7,6},{8,9},{9,8},{10,11... | collective-permute-start | bytes 307208 | tf_op jit(solution)/shard_map/ppermute | solution.py:58
  77.0 7.9 %collective-permute-start.23 = (bf16[400,128]{1,0:T(8,128)(2,1)S(1)}, bf16[400,128]{1,0:T(8,128)(2,1)S(1)}, u32[]{:S(2)}, u32[]{:S(2)}) collective-permute-start(bf16[400,128]{1,0:T(8,128)(2,1)S(1)} %sum_pair.15._), channel_id=1, source_target_pairs={{0,8},{2,10},{4,12},{6,14},{8,0},{10,2},{12,4},{14,6},{1,9},{3,11}... | collective-permute-start | bytes 307208 | tf_op jit(solution)/shard_map/ppermute | solution.py:49
  78.5 6.3 %collective-permute-start.24 = (bf16[400,128]{1,0:T(8,128)(2,1)S(1)}, bf16[400,128]{1,0:T(8,128)(2,1)S(1)}, u32[]{:S(2)}, u32[]{:S(2)}) collective-permute-start(bf16[400,128]{1,0:T(8,128)(2,1)S(1)} %get-tuple-element.197), channel_id=1, source_target_pairs={{0,1},{1,0},{2,3},{3,2},{4,5},{5,4},{6,7},{7,6},{8,9},{9,8},{10,11... | collective-permute-start | bytes 307208 | tf_op jit(solution)/shard_map/ppermute | solution.py:58
  85.0 2.6 %collective-permute-start.26 = (bf16[400,128]{1,0:T(8,128)(2,1)S(1)}, bf16[400,128]{1,0:T(8,128)(2,1)S(1)}, u32[]{:S(2)}, u32[]{:S(2)}) collective-permute-start(bf16[400,128]{1,0:T(8,128)(2,1)S(1)} %get-tuple-element.200.own0), channel_id=1, source_target_pairs={{0,1},{1,0},{2,3},{3,2},{4,5},{5,4},{6,7},{7,6},{8,9},{9,8},{10,11... | collective-permute-start | bytes 307208 | tf_op jit(solution)/shard_map/ppermute | solution.py:58
  85.1 7.3 %collective-permute-start.25 = (bf16[400,128]{1,0:T(8,128)(2,1)S(1)}, bf16[400,128]{1,0:T(8,128)(2,1)S(1)}, u32[]{:S(2)}, u32[]{:S(2)}) collective-permute-start(bf16[400,128]{1,0:T(8,128)(2,1)S(1)} %get-tuple-element.200.own0), channel_id=1, source_target_pairs={{0,6},{2,8},{4,10},{6,12},{8,14},{10,0},{12,2},{14,4},{1,7},{3,9},... | collective-permute-start | bytes 307208 | tf_op jit(solution)/shard_map/ppermute | solution.py:49
  92.4 1.3 collective-permute-start.27
  96.2 2.3 %collective-permute-start.32 = (bf16[4,400,128]{2,1,0:T(8,128)(2,1)S(1)}, bf16[4,400,128]{2,1,0:T(8,128)(2,1)S(1)}, u32[]{:S(2)}, u32[]{:S(2)}) collective-permute-start(bf16[4,400,128]{2,1,0:T(8,128)(2,1)S(1)} %get-tuple-element.207._.refs_0_), channel_id=1, source_target_pairs={{0,1},{1,0},{2,3},{3,2},{4,5},{5,4},{6,7},{7,6},{8,9},{9,8},{10,11... | collective-permute-start | bytes 1228808 | tf_op jit(solution)/shard_map/ppermute | solution.py:58
  97.1 4.6 %collective-permute-start.31 = (bf16[4,400,128]{2,1,0:T(8,128)(2,1)S(1)}, bf16[4,400,128]{2,1,0:T(8,128)(2,1)S(1)}, u32[]{:S(2)}, u32[]{:S(2)}) collective-permute-start(bf16[4,400,128]{2,1,0:T(8,128)(2,1)S(1)} %get-tuple-element.217), channel_id=1, source_target_pairs={{0,1},{1,0},{2,3},{3,2},{4,5},{5,4},{6,7},{7,6},{8,9},{9,8},{10,11... | collective-permute-start | bytes 1228808 | tf_op jit(solution)/shard_map/ppermute | solution.py:58
  97.9 31.8 %copy-start = (f32[400,2048]{1,0:T(8,128)S(1)}, f32[400,2048]{1,0:T(8,128)}, u32[]{:S(2)}) copy-start(f32[400,2048]{1,0:T(8,128)} %rel_ref.7) | copy-start | bytes 9830404
  97.9 31.8 %copy-start.6 = (f32[2048]{0:T(1024)S(1)}, f32[2048]{0:T(1024)}, u32[]{:S(2)}) copy-start(f32[2048]{0:T(1024)} %param.12) | copy-start | bytes 24580
  98.0 2.8 %collective-permute-start.29 = (bf16[400,128]{1,0:T(8,128)(2,1)S(1)}, bf16[400,128]{1,0:T(8,128)(2,1)S(1)}, u32[]{:S(2)}, u32[]{:S(2)}) collective-permute-start(bf16[400,128]{1,0:T(8,128)(2,1)S(1)} %get-tuple-element.215), channel_id=1, source_target_pairs={{0,1},{1,0},{2,3},{3,2},{4,5},{5,4},{6,7},{7,6},{8,9},{9,8},{10,11... | collective-permute-start | bytes 307208 | tf_op jit(solution)/shard_map/ppermute | solution.py:58
  98.2 3.4 %collective-permute-start.28 = (bf16[400,128]{1,0:T(8,128)(2,1)S(1)}, bf16[400,128]{1,0:T(8,128)(2,1)S(1)}, u32[]{:S(2)}, u32[]{:S(2)}) collective-permute-start(bf16[400,128]{1,0:T(8,128)(2,1)S(1)} %get-tuple-element.213), channel_id=1, source_target_pairs={{0,1},{1,0},{2,3},{3,2},{4,5},{5,4},{6,7},{7,6},{8,9},{9,8},{10,11... | collective-permute-start | bytes 307208 | tf_op jit(solution)/shard_map/ppermute | solution.py:58
  98.6 6.1 %collective-permute-start.33 = (bf16[400,128]{1,0:T(8,128)(2,1)S(1)}, bf16[400,128]{1,0:T(8,128)(2,1)S(1)}, u32[]{:S(2)}, u32[]{:S(2)}) collective-permute-start(bf16[400,128]{1,0:T(8,128)(2,1)S(1)} %get-tuple-element.222), channel_id=1, source_target_pairs={{0,2},{2,0},{4,6},{6,4},{8,10},{10,8},{12,14},{14,12},{1,3},{3,1},... | collective-permute-start | bytes 307208 | tf_op jit(solution)/shard_map/ppermute | solution.py:54
  99.5 9.3 %collective-permute-start.37 = (bf16[400,128]{1,0:T(8,128)(2,1)S(1)}, bf16[400,128]{1,0:T(8,128)(2,1)S(1)}, u32[]{:S(2)}, u32[]{:S(2)}) collective-permute-start(bf16[400,128]{1,0:T(8,128)(2,1)S(1)} %get-tuple-element.228), channel_id=1, source_target_pairs={{0,2},{2,0},{4,6},{6,4},{8,10},{10,8},{12,14},{14,12},{1,3},{3,1},... | collective-permute-start | bytes 307208 | tf_op jit(solution)/shard_map/ppermute | solution.py:54
  100.7 10.3 %collective-permute-start.39 = (bf16[400,128]{1,0:T(8,128)(2,1)S(1)}, bf16[400,128]{1,0:T(8,128)(2,1)S(1)}, u32[]{:S(2)}, u32[]{:S(2)}) collective-permute-start(bf16[400,128]{1,0:T(8,128)(2,1)S(1)} %get-tuple-element.230), channel_id=1, source_target_pairs={{0,2},{2,0},{4,6},{6,4},{8,10},{10,8},{12,14},{14,12},{1,3},{3,1},... | collective-permute-start | bytes 307208 | tf_op jit(solution)/shard_map/ppermute | solution.py:54
  101.6 10.1 %collective-permute-start.30 = (bf16[400,128]{1,0:T(8,128)(2,1)S(1)}, bf16[400,128]{1,0:T(8,128)(2,1)S(1)}, u32[]{:S(2)}, u32[]{:S(2)}) collective-permute-start(bf16[400,128]{1,0:T(8,128)(2,1)S(1)} %sum_pair.17), channel_id=1, source_target_pairs={{0,10},{2,12},{4,14},{6,0},{8,2},{10,4},{12,6},{14,8},{1,11},{3,13... | collective-permute-start | bytes 307208 | tf_op jit(solution)/shard_map/ppermute | solution.py:49
  101.7 10.7 %collective-permute-start.35 = (bf16[400,128]{1,0:T(8,128)(2,1)S(1)}, bf16[400,128]{1,0:T(8,128)(2,1)S(1)}, u32[]{:S(2)}, u32[]{:S(2)}) collective-permute-start(bf16[400,128]{1,0:T(8,128)(2,1)S(1)} %get-tuple-element.226), channel_id=1, source_target_pairs={{0,2},{2,0},{4,6},{6,4},{8,10},{10,8},{12,14},{14,12},{1,3},{3,1},... | collective-permute-start | bytes 307208 | tf_op jit(solution)/shard_map/ppermute | solution.py:54
  104.8 7.6 %collective-permute-start.36 = (bf16[400,128]{1,0:T(8,128)(2,1)S(1)}, bf16[400,128]{1,0:T(8,128)(2,1)S(1)}, u32[]{:S(2)}, u32[]{:S(2)}) collective-permute-start(bf16[400,128]{1,0:T(8,128)(2,1)S(1)} %sum_piece.4.refs_5_), channel_id=1, source_target_pairs={{0,12},{2,14},{4,8},{6,10},{8,4},{10,6},{12,0},{14,2},{1,13},{3,15... | collective-permute-start | bytes 307208 | tf_op jit(solution)/shard_map/ppermute | solution.py:54
  108.8 8.2 %collective-permute-start.38 = (bf16[400,128]{1,0:T(8,128)(2,1)S(1)}, bf16[400,128]{1,0:T(8,128)(2,1)S(1)}, u32[]{:S(2)}, u32[]{:S(2)}) collective-permute-start(bf16[400,128]{1,0:T(8,128)(2,1)S(1)} %sum_piece.5), channel_id=1, source_target_pairs={{0,8},{2,10},{4,12},{6,14},{8,0},{10,2},{12,4},{14,6},{1,9},{3,11}... | collective-permute-start | bytes 307208 | tf_op jit(solution)/shard_map/ppermute | solution.py:54
  111.0 6.5 %collective-permute-start.40 = (bf16[400,128]{1,0:T(8,128)(2,1)S(1)}, bf16[400,128]{1,0:T(8,128)(2,1)S(1)}, u32[]{:S(2)}, u32[]{:S(2)}) collective-permute-start(bf16[400,128]{1,0:T(8,128)(2,1)S(1)} %sum_piece.6), channel_id=1, source_target_pairs={{0,4},{2,6},{4,0},{6,2},{8,12},{10,14},{12,8},{14,10},{1,5},{3,7},... | collective-permute-start | bytes 307208 | tf_op jit(solution)/shard_map/ppermute | solution.py:54
  111.8 19.0 %collective-permute-start.34 = (f32[408,128]{1,0:T(8,128)S(1)}, f32[408,128]{1,0:T(8,128)S(1)}, u32[]{:S(2)}, u32[]{:S(2)}) collective-permute-start(f32[408,128]{1,0:T(8,128)S(1)} %update.11.mine), channel_id=1, source_target_pairs={{0,1},{1,0},{2,3},{3,2},{4,5},{5,4},{6,7},{7,6},{8,9},{9,8},{10,11... | collective-permute-start | bytes 626696 | tf_op jit(solution)/shard_map/ppermute | solution.py:58
  117.7 4.8 %collective-permute-start.46 = (bf16[400,128]{1,0:T(8,128)(2,1)S(1)}, bf16[400,128]{1,0:T(8,128)(2,1)S(1)}, u32[]{:S(2)}, u32[]{:S(2)}) collective-permute-start(bf16[400,128]{1,0:T(8,128)(2,1)S(1)} %sum_piece.7.refs_0_), channel_id=1, source_target_pairs={{0,4},{2,6},{4,0},{6,2},{8,12},{10,14},{12,8},{14,10},{1,5},{3,7},... | collective-permute-start | bytes 307208 | tf_op jit(solution)/shard_map/ppermute | solution.py:54
  117.7 9.9 %collective-permute-start.44 = (bf16[400,128]{1,0:T(8,128)(2,1)S(1)}, bf16[400,128]{1,0:T(8,128)(2,1)S(1)}, u32[]{:S(2)}, u32[]{:S(2)}) collective-permute-start(bf16[400,128]{1,0:T(8,128)(2,1)S(1)} %sum_piece.7.refs_0_), channel_id=1, source_target_pairs={{0,8},{2,10},{4,12},{6,14},{8,0},{10,2},{12,4},{14,6},{1,9},{3,11}... | collective-permute-start | bytes 307208 | tf_op jit(solution)/shard_map/ppermute | solution.py:54
  120.5 8.0 %collective-permute-start.42 = (bf16[400,128]{1,0:T(8,128)(2,1)S(1)}, bf16[400,128]{1,0:T(8,128)(2,1)S(1)}, u32[]{:S(2)}, u32[]{:S(2)}) collective-permute-start(bf16[400,128]{1,0:T(8,128)(2,1)S(1)} %sum_piece.7.refs_0_), channel_id=1, source_target_pairs={{0,12},{2,14},{4,8},{6,10},{8,4},{10,6},{12,0},{14,2},{1,13},{3,15... | collective-permute-start | bytes 307208 | tf_op jit(solution)/shard_map/ppermute | solution.py:54
  122.1 9.6 %collective-permute-start.41 = (bf16[400,128]{1,0:T(8,128)(2,1)S(1)}, bf16[400,128]{1,0:T(8,128)(2,1)S(1)}, u32[]{:S(2)}, u32[]{:S(2)}) collective-permute-start(bf16[400,128]{1,0:T(8,128)(2,1)S(1)} %sum_piece.7.refs_0_), channel_id=1, source_target_pairs={{0,2},{2,0},{4,6},{6,4},{8,10},{10,8},{12,14},{14,12},{1,3},{3,1},... | collective-permute-start | bytes 307208 | tf_op jit(solution)/shard_map/ppermute | solution.py:54
  122.5 9.2 %collective-permute-start.47 = (bf16[400,128]{1,0:T(8,128)(2,1)S(1)}, bf16[400,128]{1,0:T(8,128)(2,1)S(1)}, u32[]{:S(2)}, u32[]{:S(2)}) collective-permute-start(bf16[400,128]{1,0:T(8,128)(2,1)S(1)} %collective-permute-done.46.refs_3_), channel_id=1, source_target_pairs={{0,2},{2,0},{4,6},{6,4},{8,10},{10,8},{12,14},{14,12},{1,3},{3,1},... | collective-permute-start | bytes 307208 | tf_op jit(solution)/shard_map/ppermute | solution.py:54
  127.7 4.7 %collective-permute-start.45 = (bf16[400,128]{1,0:T(8,128)(2,1)S(1)}, bf16[400,128]{1,0:T(8,128)(2,1)S(1)}, u32[]{:S(2)}, u32[]{:S(2)}) collective-permute-start(bf16[400,128]{1,0:T(8,128)(2,1)S(1)} %collective-permute-done.44.refs_2_), channel_id=1, source_target_pairs={{0,2},{2,0},{4,6},{6,4},{8,10},{10,8},{12,14},{14,12},{1,3},{3,1},... | collective-permute-start | bytes 307208 | tf_op jit(solution)/shard_map/ppermute | solution.py:54
  128.5 4.9 %collective-permute-start.43 = (bf16[400,128]{1,0:T(8,128)(2,1)S(1)}, bf16[400,128]{1,0:T(8,128)(2,1)S(1)}, u32[]{:S(2)}, u32[]{:S(2)}) collective-permute-start(bf16[400,128]{1,0:T(8,128)(2,1)S(1)} %collective-permute-done.42.refs_1_), channel_id=1, source_target_pairs={{0,2},{2,0},{4,6},{6,4},{8,10},{10,8},{12,14},{14,12},{1,3},{3,1},... | collective-permute-start | bytes 307208 | tf_op jit(solution)/shard_map/ppermute | solution.py:54
  131.6 1.9 %collective-permute-start.49 = (bf16[4,400,128]{2,1,0:T(8,128)(2,1)S(1)}, bf16[4,400,128]{2,1,0:T(8,128)(2,1)S(1)}, u32[]{:S(2)}, u32[]{:S(2)}) collective-permute-start(bf16[4,400,128]{2,1,0:T(8,128)(2,1)S(1)} %stacked.3), channel_id=1, source_target_pairs={{0,1},{1,0},{2,3},{3,2},{4,5},{5,4},{6,7},{7,6},{8,9},{9,8},{10,11... | collective-permute-start | bytes 1228808 | tf_op jit(solution)/shard_map/ppermute | solution.py:58
  133.5 1.8 %collective-permute-start.48 = (bf16[4,400,128]{2,1,0:T(8,128)(2,1)S(1)}, bf16[4,400,128]{2,1,0:T(8,128)(2,1)S(1)}, u32[]{:S(2)}, u32[]{:S(2)}) collective-permute-start(bf16[4,400,128]{2,1,0:T(8,128)(2,1)S(1)} %stacked.2), channel_id=1, source_target_pairs={{0,1},{1,0},{2,3},{3,2},{4,5},{5,4},{6,7},{7,6},{8,9},{9,8},{10,11... | collective-permute-start | bytes 1228808 | tf_op jit(solution)/shard_map/ppermute | solution.py:58

commit v2 on v1

--- a/solution.py
+++ b/solution.py
@@ -726,9 +726,10 @@
     )(*parts, *after)
 
 
-def relnew_kernel(nz, kinds, count, first, rel_ref, state_ref, *refs):
+def relnew_kernel(nz, kinds, count, first, last, rel_ref, state_ref, *refs):
     arrays = refs[:count]
-    rel_out, state_out, buf, sems = refs[-4:]
+    rel_out, state_to, buf, sems = refs[-5:-1] if last else refs[-4:]
+    state_out = refs[-1] if last else state_to
     w = buf.shape[2]
     state_out[...] = refs[count + (0 if first else 1)][...]
     z, x, edge = place()
@@ -743,11 +744,15 @@
         copy = pltpu.make_async_copy(buf.at[i], rel_out.at[:, at], sems.at[i])
         copy.start()
         copies.append(copy)
+    if last:
+        copy = pltpu.make_async_copy(state_out, state_to, sems.at[len(kinds)])
+        copy.start()
+        copies.append(copy)
     for copy in copies:
         copy.wait()
 
 
-def relnew(nz, relations, state, groups, before, after):
+def relnew(nz, relations, state, groups, before, last=False):
     dim, rels = relations.shape
     w = rels // (4 * nz)
     kinds, arrays = [], []
@@ -759,19 +764,19 @@
     count = len(kinds)
     start = [state] if before is None else list(before)
     return pl.pallas_call(
-        functools.partial(relnew_kernel, nz, tuple(kinds), len(arrays), before is None),
+        functools.partial(relnew_kernel, nz, tuple(kinds), len(arrays), before is None, last),
         in_specs=[vmem()] * (2 + len(arrays))
         + ([anywhere()] if before else [])
-        + [vmem()]
-        + [anywhere()] * len(after),
-        out_specs=[anywhere(), vmem()],
+        + [vmem()],
+        out_specs=[anywhere(), anywhere() if last else vmem()],
         out_shape=[jax.ShapeDtypeStruct((dim, rels), F32), jax.ShapeDtypeStruct((1, rels), F32)],
         input_output_aliases={2 + len(arrays): 0} if before else {},
-        scratch_shapes=[pltpu.VMEM((count, dim, w), F32), pltpu.SemaphoreType.DMA((count,))],
+        scratch_shapes=[pltpu.VMEM((count, dim, w), F32), pltpu.SemaphoreType.DMA((count + 1,))]
+        + ([pltpu.VMEM((1, rels), F32)] if last else []),
         compiler_params=params(),
         cost_estimate=cost(dim, dim),
         name="relnew",
-    )(relations, state, *arrays, *start, *after)
+    )(relations, state, *arrays, *start)
 
 
 def relation_update(t, rel_ids, drel, acc, relations, state, send, finish):
@@ -803,11 +808,12 @@
     mine = [got[k] for k in ks]
     mine_x = [got_x[k] for k in ks]
     there = across(stacked(mine, [done[2]]))
-    new = relnew(nz, relations, state, [(ks, True, True, mine)], None, [])
+    new = relnew(nz, relations, state, [(ks, True, True, mine)], None)
     there_x = across(stacked(mine_x, [new[1]]))
     groups = [(ks, True, False, there), (ks, False, True, mine_x)]
-    new = relnew(nz, relations, state, groups, new, [])
-    rel_new, state_new = relnew(nz, relations, state, [(ks, False, False, there_x)], new, [])
+    new = relnew(nz, relations, state, groups, new)
+    groups = [(ks, False, False, there_x)]
+    rel_new, state_new = relnew(nz, relations, state, groups, new, last=True)
     return rel_new, state_new.reshape(rels), done
 
 

time: 137 us -> 137 us (level)
  no operation moved by 1% of the time
where the time goes in v2:
time: 137 us
  waiting for transfers between devices  59.3 us (43%)
  Pallas kernels  47 us (34%)
  starting transfers between devices  28.6 us (21%)
  between operations  1.51 us (1%)
    ppermute x10, waiting for transfers between devices, shifted(): return lax.ppermute(x, 'dom', [(i, (i + by) % n) for i in range(n)])  33.3 us
    ppermute x14, starting transfers between devices, swapped(): return lax.ppermute(x, 'dom', [(i, i ^ bits) for i in range(n)])  17.3 us
    ppermute x14, waiting for transfers between devices, swapped(): return lax.ppermute(x, 'dom', [(i, i ^ bits) for i in range(n)])  14.9 us
    ppermute x26, waiting for transfers between devices, across(): return lax.ppermute(x, 'edge', [(0, 1), (1, 0)])  11.2 us
    pallas_call x5, Pallas kernels, relsum(): pl.pallas_call(functools.partial(relsum_kernel, t, acc is None), grid=(re...  10.7 us
    ppermute x10, starting transfers between devices, shifted(): return lax.ppermute(x, 'dom', [(i, (i + by) % n) for i in range(n)])  6.68 us
    pallas_call x4, Pallas kernels, source_grad(): pl.pallas_call(functools.partial(source_grad_kernel, t, shape), in_specs=...  5.92 us
    pallas_call x4, Pallas kernels, target_grad(): pl.pallas_call(target_kernel, in_specs=[vmem()] * 8, out_specs=[vmem()] *...  5.51 us
  transfers between devices with their start and end apart: 50, of which 27 were waited for; matrix products, arithmetic and copies ran while one was open for 0% of the time, Pallas kernels for 23%

profile of v2, /device:TPU:0, one launch (start us, length us, event | category | flops | bytes accessed | tf_op | source)
XLA Modules:
  0.0 136.5 jit_solution(6989372415079852619)
XLA Ops:
  0.6 5.4 %first_round.1 = (f32[400,128]{1,0:T(8,128)S(1)}, bf16[400,128]{1,0:T(8,128)(2,1)S(1)}, bf16[400,512]{1,0:T(8,128)(2,1)S(1)}, bf16[400,2048]{1,0:T(8,128)(2,1)S(...) custom-call(s32[4,6]{1,0:T(4,128)} %bitcast.6, s32[4,6]{1,0:T(4,128)} %bitcast.17, s32[6,4,128]{2,1,0:T(4,128)} %src_ref.11, ...), custom_call_target="tpu_custom_call" | custom-call | flops 1258291200 | bytes 6553600 | tf_op jit(solution)/shard_map/first_round/pallas_call | solution.py:309
  6.6 0.9 collective-permute-done.refs_3_
  8.1 5.7 %collective-permute-start.2 = (bf16[400,128]{1,0:T(8,128)(2,1)S(1)}, bf16[400,128]{1,0:T(8,128)(2,1)S(1)}, u32[]{:S(2)}, u32[]{:S(2)}) collective-permute-start(bf16[400,128]{1,0:T(8,128)(2,1)S(1)} %get-tuple-element.127.own0), channel_id=1, source_target_pairs={{0,14},{2,0},{4,2},{6,4},{8,6},{10,8},{12,10},{14,12},{1,15},{3,1}... | collective-permute-start | bytes 307208 | tf_op jit(solution)/shard_map/ppermute | solution.py:49
  13.8 1.0 relvec.5.rel_ref
  14.8 1.9 %relsum.5.refs_1_.refs_0_ = f32[400,2048]{1,0:T(8,128)S(1)} custom-call(s32[6,4,128]{2,1,0:T(4,128)S(1)} %copy-done.1, bf16[400,512]{1,0:T(8,128)(2,1)S(1)} %get-tuple-element.131.drel_ref), custom_call_target="tpu_custom_call" | custom-call | flops 204800 | bytes 204800 | tf_op jit(solution)/shard_map/relsum/pallas_call | solution.py:113
  16.8 0.9 source_side.5
  18.1 1.0 collective-permute-done.3.far1
  19.1 1.4 %target_grad.4 = (f32[400,128]{1,0:T(8,128)S(1)}, bf16[400,128]{1,0:T(8,128)(2,1)S(1)}, bf16[128,512]{1,0:T(8,128)(2,1)S(1)}) custom-call(f32[512,128]{1,0:T(8,128)S(1)} %near_products.4.near, bf16[400,128]{1,0:T(8,128)(2,1)S(1)} %collective-permute-done.3.far1, bf16[400,512]{1,0:T(8,128)(2,1)S(1)} %get-tuple-element.130.refs_0_.query_ref, ...), custom_call_target="tpu_custom_call" | custom-call | flops 104857600 | bytes 2457600 | tf_op jit(solution)/shard_map/target_grad/pallas_call | solution.py:447
  20.7 1.2 collective-permute-done.4.b_ref
  21.9 1.5 %source_grad.4 = (f32[400,128]{1,0:T(8,128)S(1)}, bf16[400,128]{1,0:T(8,128)(2,1)S(1)}, bf16[400,512]{1,0:T(8,128)(2,1)S(1)}) custom-call(s32[4,6]{1,0:T(4,128)S(1)} %bitcast.8, s32[4,6]{1,0:T(4,128)S(1)} %bitcast.19, bf16[400,128]{1,0:T(8,128)(2,1)S(1)} %sum_pair.9._, bf16[400,128]{1,0:T(8,128)(2,1)S(1)} %held.5.far0, ...), custom_call_target="tpu_custom_call" | custom-call | flops 204800 | bytes 204800 | tf_op jit(solution)/shard_map/source_grad/pallas_call | solution.py:479
  23.6 1.0 relvec.6.refs_4_.rel_ref
  24.7 4.9 %collective-permute-done.5.b_ref = bf16[400,128]{1,0:T(8,128)(2,1)S(1)} collective-permute-done((bf16[400,128]{1,0:T(8,128)(2,1)S(1)}, bf16[400,128]{1,0:T(8,128)(2,1)S(1)}, u32[]{:S(2)}, u32[]{:S(2)}) %collective-permute-start.5) | collective-permute-done | bytes 102432 | tf_op jit(solution)/shard_map/ppermute | solution.py:49
  29.9 2.2 %relsum.6.refs_1_.refs_0_ = f32[400,2048]{1,0:T(8,128)S(1)} custom-call(s32[6,4,128]{2,1,0:T(4,128)S(1)} %copy-done.1, bf16[400,512]{1,0:T(8,128)(2,1)S(1)} %get-tuple-element.149.drel_ref, f32[400,2048]{1,0:T(8,128)S(1)} %relsum.5.refs_1_.refs_0_), custom_call_target="tpu_custom_call", output_to_operand_aliasing={{}: (2, {})} | custom-call | flops 204800 | bytes 204800 | tf_op jit(solution)/shard_map/relsum/pallas_call | solution.py:113
  32.1 0.9 source_side.6
  33.0 2.1 %collective-permute-done.8.x_ref = bf16[400,128]{1,0:T(8,128)(2,1)S(1)} collective-permute-done((bf16[400,128]{1,0:T(8,128)(2,1)S(1)}, bf16[400,128]{1,0:T(8,128)(2,1)S(1)}, u32[]{:S(2)}, u32[]{:S(2)}) %collective-permute-start.8) | collective-permute-done | bytes 102432 | tf_op jit(solution)/shard_map/ppermute | solution.py:49
  35.4 1.0 collective-permute-done.9.far1
  36.4 1.4 %target_grad.5 = (f32[400,128]{1,0:T(8,128)S(1)}, bf16[400,128]{1,0:T(8,128)(2,1)S(1)}, bf16[128,512]{1,0:T(8,128)(2,1)S(1)}) custom-call(f32[512,128]{1,0:T(8,128)S(1)} %near_products.5.near, bf16[400,128]{1,0:T(8,128)(2,1)S(1)} %collective-permute-done.9.far1, bf16[400,512]{1,0:T(8,128)(2,1)S(1)} %get-tuple-element.148.refs_0_.query_ref, ...), custom_call_target="tpu_custom_call" | custom-call | flops 104857600 | bytes 2457600 | tf_op jit(solution)/shard_map/target_grad/pallas_call | solution.py:447
  38.0 1.2 collective-permute-done.10.b_ref
  39.4 1.5 %source_grad.5 = (f32[400,128]{1,0:T(8,128)S(1)}, bf16[400,128]{1,0:T(8,128)(2,1)S(1)}, bf16[400,512]{1,0:T(8,128)(2,1)S(1)}) custom-call(s32[4,6]{1,0:T(4,128)S(1)} %bitcast.10, s32[4,6]{1,0:T(4,128)S(1)} %bitcast.21, bf16[400,128]{1,0:T(8,128)(2,1)S(1)} %sum_pair.11._, bf16[400,128]{1,0:T(8,128)(2,1)S(1)} %held.6.far0, ...), custom_call_target="tpu_custom_call" | custom-call | flops 204800 | bytes 204800 | tf_op jit(solution)/shard_map/source_grad/pallas_call | solution.py:479
  41.1 1.0 relvec.7.refs_4_.rel_ref
  42.2 4.0 %collective-permute-done.11.b_ref = bf16[400,128]{1,0:T(8,128)(2,1)S(1)} collective-permute-done((bf16[400,128]{1,0:T(8,128)(2,1)S(1)}, bf16[400,128]{1,0:T(8,128)(2,1)S(1)}, u32[]{:S(2)}, u32[]{:S(2)}) %collective-permute-start.11) | collective-permute-done | bytes 102432 | tf_op jit(solution)/shard_map/ppermute | solution.py:49
  46.5 2.2 %relsum.7.refs_1_.refs_0_ = f32[400,2048]{1,0:T(8,128)S(1)} custom-call(s32[6,4,128]{2,1,0:T(4,128)S(1)} %copy-done.1, bf16[400,512]{1,0:T(8,128)(2,1)S(1)} %get-tuple-element.167.drel_ref, f32[400,2048]{1,0:T(8,128)S(1)} %relsum.6.refs_1_.refs_0_), custom_call_target="tpu_custom_call", output_to_operand_aliasing={{}: (2, {})} | custom-call | flops 204800 | bytes 204800 | tf_op jit(solution)/shard_map/relsum/pallas_call | solution.py:113
  48.7 0.9 source_side.7
  49.6 3.0 %collective-permute-done.14.x_ref = bf16[400,128]{1,0:T(8,128)(2,1)S(1)} collective-permute-done((bf16[400,128]{1,0:T(8,128)(2,1)S(1)}, bf16[400,128]{1,0:T(8,128)(2,1)S(1)}, u32[]{:S(2)}, u32[]{:S(2)}) %collective-permute-start.14) | collective-permute-done | bytes 102432 | tf_op jit(solution)/shard_map/ppermute | solution.py:49
  52.9 1.0 collective-permute-done.15.far1
  53.9 1.4 %target_grad.6 = (f32[400,128]{1,0:T(8,128)S(1)}, bf16[400,128]{1,0:T(8,128)(2,1)S(1)}, bf16[128,512]{1,0:T(8,128)(2,1)S(1)}) custom-call(f32[512,128]{1,0:T(8,128)S(1)} %near_products.6.near, bf16[400,128]{1,0:T(8,128)(2,1)S(1)} %collective-permute-done.15.far1, bf16[400,512]{1,0:T(8,128)(2,1)S(1)} %get-tuple-element.166.refs_0_.query_ref, ...), custom_call_target="tpu_custom_call" | custom-call | flops 104857600 | bytes 2457600 | tf_op jit(solution)/shard_map/target_grad/pallas_call | solution.py:447
  55.5 1.2 collective-permute-done.16.b_ref
  56.7 1.5 %source_grad.6 = (f32[400,128]{1,0:T(8,128)S(1)}, bf16[400,128]{1,0:T(8,128)(2,1)S(1)}, bf16[400,512]{1,0:T(8,128)(2,1)S(1)}) custom-call(s32[4,6]{1,0:T(4,128)S(1)} %bitcast.12, s32[4,6]{1,0:T(4,128)S(1)} %bitcast.23, bf16[400,128]{1,0:T(8,128)(2,1)S(1)} %sum_pair.13._, bf16[400,128]{1,0:T(8,128)(2,1)S(1)} %held.7.far0, ...), custom_call_target="tpu_custom_call" | custom-call | flops 204800 | bytes 204800 | tf_op jit(solution)/shard_map/source_grad/pallas_call | solution.py:479
  58.4 1.0 relvec.8.refs_4_.rel_ref
  59.5 6.2 %collective-permute-done.17.b_ref = bf16[400,128]{1,0:T(8,128)(2,1)S(1)} collective-permute-done((bf16[400,128]{1,0:T(8,128)(2,1)S(1)}, bf16[400,128]{1,0:T(8,128)(2,1)S(1)}, u32[]{:S(2)}, u32[]{:S(2)}) %collective-permute-start.17) | collective-permute-done | bytes 102432 | tf_op jit(solution)/shard_map/ppermute | solution.py:49
  66.0 2.2 %relsum.8.refs_1_.refs_0_ = f32[400,2048]{1,0:T(8,128)S(1)} custom-call(s32[6,4,128]{2,1,0:T(4,128)S(1)} %copy-done.1, bf16[400,512]{1,0:T(8,128)(2,1)S(1)} %get-tuple-element.185.drel_ref, f32[400,2048]{1,0:T(8,128)S(1)} %relsum.7.refs_1_.refs_0_), custom_call_target="tpu_custom_call", output_to_operand_aliasing={{}: (2, {})} | custom-call | flops 204800 | bytes 204800 | tf_op jit(solution)/shard_map/relsum/pallas_call | solution.py:113
  68.2 0.9 source_side.8
  69.1 3.8 %collective-permute-done.20.x_ref = bf16[400,128]{1,0:T(8,128)(2,1)S(1)} collective-permute-done((bf16[400,128]{1,0:T(8,128)(2,1)S(1)}, bf16[400,128]{1,0:T(8,128)(2,1)S(1)}, u32[]{:S(2)}, u32[]{:S(2)}) %collective-permute-start.20) | collective-permute-done | bytes 102432 | tf_op jit(solution)/shard_map/ppermute | solution.py:49
  73.3 0.9 collective-permute-done.21.far1
  74.2 1.4 %target_grad.7 = (f32[400,128]{1,0:T(8,128)S(1)}, bf16[400,128]{1,0:T(8,128)(2,1)S(1)}, bf16[128,512]{1,0:T(8,128)(2,1)S(1)}) custom-call(f32[512,128]{1,0:T(8,128)S(1)} %near_products.7.near, bf16[400,128]{1,0:T(8,128)(2,1)S(1)} %collective-permute-done.21.far1, bf16[400,512]{1,0:T(8,128)(2,1)S(1)} %get-tuple-element.184.refs_0_.query_ref, ...), custom_call_target="tpu_custom_call" | custom-call | flops 104857600 | bytes 2457600 | tf_op jit(solution)/shard_map/target_grad/pallas_call | solution.py:447
  75.8 1.2 collective-permute-done.22.b_ref
  77.1 1.5 %source_grad.7 = (f32[400,128]{1,0:T(8,128)S(1)}, bf16[400,128]{1,0:T(8,128)(2,1)S(1)}, bf16[400,512]{1,0:T(8,128)(2,1)S(1)}) custom-call(s32[4,6]{1,0:T(4,128)S(1)} %bitcast.14, s32[4,6]{1,0:T(4,128)S(1)} %bitcast.25, bf16[400,128]{1,0:T(8,128)(2,1)S(1)} %sum_pair.15._, bf16[400,128]{1,0:T(8,128)(2,1)S(1)} %held.8.far0, ...), custom_call_target="tpu_custom_call" | custom-call | flops 204800 | bytes 204800 | tf_op jit(solution)/shard_map/source_grad/pallas_call | solution.py:479
  78.8 1.0 relvec.9.refs_4_.rel_ref
  79.8 5.1 %collective-permute-done.23.b_ref = bf16[400,128]{1,0:T(8,128)(2,1)S(1)} collective-permute-done((bf16[400,128]{1,0:T(8,128)(2,1)S(1)}, bf16[400,128]{1,0:T(8,128)(2,1)S(1)}, u32[]{:S(2)}, u32[]{:S(2)}) %collective-permute-start.23) | collective-permute-done | bytes 102432 | tf_op jit(solution)/shard_map/ppermute | solution.py:49
  85.4 2.2 %relsum.9.refs_1_.acc_ref = f32[400,2048]{1,0:T(8,128)S(1)} custom-call(s32[6,4,128]{2,1,0:T(4,128)S(1)} %copy-done.1, bf16[400,512]{1,0:T(8,128)(2,1)S(1)} %get-tuple-element.202.drel_ref, f32[400,2048]{1,0:T(8,128)S(1)} %relsum.8.refs_1_.refs_0_), custom_call_target="tpu_custom_call", output_to_operand_aliasing={{}: (2, {})} | custom-call | flops 204800 | bytes 204800 | tf_op jit(solution)/shard_map/relsum/pallas_call | solution.py:113
  88.2 4.2 %collective-permute-done.25.x_ref = bf16[400,128]{1,0:T(8,128)(2,1)S(1)} collective-permute-done((bf16[400,128]{1,0:T(8,128)(2,1)S(1)}, bf16[400,128]{1,0:T(8,128)(2,1)S(1)}, u32[]{:S(2)}, u32[]{:S(2)}) %collective-permute-start.25) | collective-permute-done | bytes 102432 | tf_op jit(solution)/shard_map/ppermute | solution.py:49
  92.4 1.3 collective-permute-done.27.far1
  93.7 1.8 %last_terms.1 = (bf16[400,512]{1,0:T(8,128)(2,1)S(1)}, bf16[400,512]{1,0:T(8,128)(2,1)S(1)}, bf16[400,512]{1,0:T(8,128)(2,1)S(1)}) custom-call(s32[4,6]{1,0:T(4,128)S(1)} %bitcast.16, s32[4,6]{1,0:T(4,128)S(1)} %bitcast.27, bf16[400,128]{1,0:T(8,128)(2,1)S(1)} %held.9.far0, bf16[400,128]{1,0:T(8,128)(2,1)S(1)} %collective-permute-done.27.far1, ...), custom_call_target="tpu_custom_call" | custom-call | flops 157286400 | bytes 2457600 | tf_op jit(solution)/shard_map/last_terms/pallas_call | solution.py:509
  95.6 0.7 pieces.2
  98.6 0.9 collective-permute-start.33
  99.5 1.2 collective-permute-start.37
  100.7 0.8 collective-permute-start.39
  101.7 3.1 %collective-permute-start.35 = (bf16[400,128]{1,0:T(8,128)(2,1)S(1)}, bf16[400,128]{1,0:T(8,128)(2,1)S(1)}, u32[]{:S(2)}, u32[]{:S(2)}) collective-permute-start(bf16[400,128]{1,0:T(8,128)(2,1)S(1)} %get-tuple-element.226), channel_id=1, source_target_pairs={{0,2},{2,0},{4,6},{6,4},{8,10},{10,8},{12,14},{14,12},{1,3},{3,1},... | collective-permute-start | bytes 307208 | tf_op jit(solution)/shard_map/ppermute | solution.py:54
  104.8 2.1 %collective-permute-start.36 = (bf16[400,128]{1,0:T(8,128)(2,1)S(1)}, bf16[400,128]{1,0:T(8,128)(2,1)S(1)}, u32[]{:S(2)}, u32[]{:S(2)}) collective-permute-start(bf16[400,128]{1,0:T(8,128)(2,1)S(1)} %sum_piece.4.refs_5_), channel_id=1, source_target_pairs={{0,12},{2,14},{4,8},{6,10},{8,4},{10,6},{12,0},{14,2},{1,13},{3,15... | collective-permute-start | bytes 307208 | tf_op jit(solution)/shard_map/ppermute | solution.py:54
  106.9 1.9 %collective-permute-done.37.refs_0_ = bf16[400,128]{1,0:T(8,128)(2,1)S(1)} collective-permute-done((bf16[400,128]{1,0:T(8,128)(2,1)S(1)}, bf16[400,128]{1,0:T(8,128)(2,1)S(1)}, u32[]{:S(2)}, u32[]{:S(2)}) %collective-permute-start.37) | collective-permute-done | bytes 102432 | tf_op jit(solution)/shard_map/ppermute | solution.py:54
  108.9 2.1 %collective-permute-done.39.refs_0_ = bf16[400,128]{1,0:T(8,128)(2,1)S(1)} collective-permute-done((bf16[400,128]{1,0:T(8,128)(2,1)S(1)}, bf16[400,128]{1,0:T(8,128)(2,1)S(1)}, u32[]{:S(2)}, u32[]{:S(2)}) %collective-permute-start.39) | collective-permute-done | bytes 102432 | tf_op jit(solution)/shard_map/ppermute | solution.py:54
  111.0 0.7 collective-permute-start.40
  112.4 4.6 %collective-permute-done.38.refs_2_ = bf16[400,128]{1,0:T(8,128)(2,1)S(1)} collective-permute-done((bf16[400,128]{1,0:T(8,128)(2,1)S(1)}, bf16[400,128]{1,0:T(8,128)(2,1)S(1)}, u32[]{:S(2)}, u32[]{:S(2)}) %collective-permute-start.38) | collective-permute-done | bytes 102432 | tf_op jit(solution)/shard_map/ppermute | solution.py:54
  117.7 2.7 %collective-permute-start.44 = (bf16[400,128]{1,0:T(8,128)(2,1)S(1)}, bf16[400,128]{1,0:T(8,128)(2,1)S(1)}, u32[]{:S(2)}, u32[]{:S(2)}) collective-permute-start(bf16[400,128]{1,0:T(8,128)(2,1)S(1)} %sum_piece.7.refs_0_), channel_id=1, source_target_pairs={{0,8},{2,10},{4,12},{6,14},{8,0},{10,2},{12,4},{14,6},{1,9},{3,11}... | collective-permute-start | bytes 307208 | tf_op jit(solution)/shard_map/ppermute | solution.py:54
  120.5 1.6 %collective-permute-start.42 = (bf16[400,128]{1,0:T(8,128)(2,1)S(1)}, bf16[400,128]{1,0:T(8,128)(2,1)S(1)}, u32[]{:S(2)}, u32[]{:S(2)}) collective-permute-start(bf16[400,128]{1,0:T(8,128)(2,1)S(1)} %sum_piece.7.refs_0_), channel_id=1, source_target_pairs={{0,12},{2,14},{4,8},{6,10},{8,4},{10,6},{12,0},{14,2},{1,13},{3,15... | collective-permute-start | bytes 307208 | tf_op jit(solution)/shard_map/ppermute | solution.py:54
  122.5 1.7 %collective-permute-start.47 = (bf16[400,128]{1,0:T(8,128)(2,1)S(1)}, bf16[400,128]{1,0:T(8,128)(2,1)S(1)}, u32[]{:S(2)}, u32[]{:S(2)}) collective-permute-start(bf16[400,128]{1,0:T(8,128)(2,1)S(1)} %collective-permute-done.46.refs_3_), channel_id=1, source_target_pairs={{0,2},{2,0},{4,6},{6,4},{8,10},{10,8},{12,14},{14,12},{1,3},{3,1},... | collective-permute-start | bytes 307208 | tf_op jit(solution)/shard_map/ppermute | solution.py:54
  124.2 3.5 %collective-permute-done.44.refs_2_ = bf16[400,128]{1,0:T(8,128)(2,1)S(1)} collective-permute-done((bf16[400,128]{1,0:T(8,128)(2,1)S(1)}, bf16[400,128]{1,0:T(8,128)(2,1)S(1)}, u32[]{:S(2)}, u32[]{:S(2)}) %collective-permute-start.44) | collective-permute-done | bytes 102432 | tf_op jit(solution)/shard_map/ppermute | solution.py:54
  127.7 0.7 collective-permute-start.45
  128.4 1.3 collective-permute-start.43
  129.7 1.0 relnew.3
  130.8 0.8 whole_partition.1
  132.4 1.1 collective-permute-done.43.refs_1_.refs_2_
  133.6 1.4 relnew.4
  135.3 1.0 relnew.5
  (113 shorter events, 12.3 us)
Async XLA Ops:
  0.6 13.2 %copy-start.1 = (s32[6,4,128]{2,1,0:T(4,128)S(1)}, s32[6,4,128]{2,1,0:T(4,128)}, u32[]{:S(2)}) copy-start(s32[6,4,128]{2,1,0:T(4,128)} %ids_ref.25) | copy-start | bytes 36868
  6.1 10.7 %copy-start.2 = (s32[6,4,128]{2,1,0:T(4,128)S(1)}, s32[6,4,128]{2,1,0:T(4,128)}, u32[]{:S(2)}) copy-start(s32[6,4,128]{2,1,0:T(4,128)} %src_ref.11) | copy-start | bytes 36868
  6.1 10.7 %copy-start.3 = (s32[6,4,128]{2,1,0:T(4,128)S(1)}, s32[6,4,128]{2,1,0:T(4,128)}, u32[]{:S(2)}) copy-start(s32[6,4,128]{2,1,0:T(4,128)} %dst_ref.11) | copy-start | bytes 36868
  6.1 10.7 %copy-start.4 = (s32[6,4]{0,1:T(4,128)S(1)}, s32[6,4]{0,1:T(4,128)}, u32[]{:S(2)}) copy-start(s32[6,4]{0,1:T(4,128)} %param.16) | copy-start | bytes 292
  6.1 10.7 %copy-start.5 = (s32[6,4]{0,1:T(4,128)S(1)}, s32[6,4]{0,1:T(4,128)}, u32[]{:S(2)}) copy-start(s32[6,4]{0,1:T(4,128)} %param.17) | copy-start | bytes 292
  6.1 1.5 %collective-permute-start = (bf16[400,128]{1,0:T(8,128)(2,1)S(1)}, bf16[400,128]{1,0:T(8,128)(2,1)S(1)}, u32[]{:S(2)}, u32[]{:S(2)}) collective-permute-start(bf16[400,128]{1,0:T(8,128)(2,1)S(1)} %get-tuple-element.124), channel_id=1, source_target_pairs={{0,1},{1,0},{2,3},{3,2},{4,5},{5,4},{6,7},{7,6},{8,9},{9,8},{10,11... | collective-permute-start | bytes 307208 | tf_op jit(solution)/shard_map/ppermute | solution.py:58
  7.7 9.1 %collective-permute-start.1 = (bf16[400,128]{1,0:T(8,128)(2,1)S(1)}, bf16[400,128]{1,0:T(8,128)(2,1)S(1)}, u32[]{:S(2)}, u32[]{:S(2)}) collective-permute-start(bf16[400,128]{1,0:T(8,128)(2,1)S(1)} %get-tuple-element.127.own0), channel_id=1, source_target_pairs={{0,1},{1,0},{2,3},{3,2},{4,5},{5,4},{6,7},{7,6},{8,9},{9,8},{10,11... | collective-permute-start | bytes 307208 | tf_op jit(solution)/shard_map/ppermute | solution.py:58
  8.1 9.6 %collective-permute-start.2 = (bf16[400,128]{1,0:T(8,128)(2,1)S(1)}, bf16[400,128]{1,0:T(8,128)(2,1)S(1)}, u32[]{:S(2)}, u32[]{:S(2)}) collective-permute-start(bf16[400,128]{1,0:T(8,128)(2,1)S(1)} %get-tuple-element.127.own0), channel_id=1, source_target_pairs={{0,14},{2,0},{4,2},{6,4},{8,6},{10,8},{12,10},{14,12},{1,15},{3,1}... | collective-permute-start | bytes 307208 | tf_op jit(solution)/shard_map/ppermute | solution.py:49
  17.7 1.4 %collective-permute-start.3 = (bf16[400,128]{1,0:T(8,128)(2,1)S(1)}, bf16[400,128]{1,0:T(8,128)(2,1)S(1)}, u32[]{:S(2)}, u32[]{:S(2)}) collective-permute-start(bf16[400,128]{1,0:T(8,128)(2,1)S(1)} %held.5.far0), channel_id=1, source_target_pairs={{0,1},{1,0},{2,3},{3,2},{4,5},{5,4},{6,7},{7,6},{8,9},{9,8},{10,11... | collective-permute-start | bytes 307208 | tf_op jit(solution)/shard_map/ppermute | solution.py:58
  20.5 1.4 %collective-permute-start.4 = (bf16[400,128]{1,0:T(8,128)(2,1)S(1)}, bf16[400,128]{1,0:T(8,128)(2,1)S(1)}, u32[]{:S(2)}, u32[]{:S(2)}) collective-permute-start(bf16[400,128]{1,0:T(8,128)(2,1)S(1)} %get-tuple-element.137), channel_id=1, source_target_pairs={{0,1},{1,0},{2,3},{3,2},{4,5},{5,4},{6,7},{7,6},{8,9},{9,8},{10,11... | collective-permute-start | bytes 307208 | tf_op jit(solution)/shard_map/ppermute | solution.py:58
  21.9 7.7 %collective-permute-start.5 = (bf16[400,128]{1,0:T(8,128)(2,1)S(1)}, bf16[400,128]{1,0:T(8,128)(2,1)S(1)}, u32[]{:S(2)}, u32[]{:S(2)}) collective-permute-start(bf16[400,128]{1,0:T(8,128)(2,1)S(1)} %sum_pair.9._), channel_id=1, source_target_pairs={{0,2},{2,4},{4,6},{6,8},{8,10},{10,12},{12,14},{14,0},{1,3},{3,5},... | collective-permute-start | bytes 307208 | tf_op jit(solution)/shard_map/ppermute | solution.py:49
  23.4 6.2 %collective-permute-start.6 = (bf16[400,128]{1,0:T(8,128)(2,1)S(1)}, bf16[400,128]{1,0:T(8,128)(2,1)S(1)}, u32[]{:S(2)}, u32[]{:S(2)}) collective-permute-start(bf16[400,128]{1,0:T(8,128)(2,1)S(1)} %get-tuple-element.143), channel_id=1, source_target_pairs={{0,1},{1,0},{2,3},{3,2},{4,5},{5,4},{6,7},{7,6},{8,9},{9,8},{10,11... | collective-permute-start | bytes 307208 | tf_op jit(solution)/shard_map/ppermute | solution.py:58
  29.7 2.4 %collective-permute-start.7 = (bf16[400,128]{1,0:T(8,128)(2,1)S(1)}, bf16[400,128]{1,0:T(8,128)(2,1)S(1)}, u32[]{:S(2)}, u32[]{:S(2)}) collective-permute-start(bf16[400,128]{1,0:T(8,128)(2,1)S(1)} %get-tuple-element.146.own0), channel_id=1, source_target_pairs={{0,1},{1,0},{2,3},{3,2},{4,5},{5,4},{6,7},{7,6},{8,9},{9,8},{10,11... | collective-permute-start | bytes 307208 | tf_op jit(solution)/shard_map/ppermute | solution.py:58
  29.8 5.3 %collective-permute-start.8 = (bf16[400,128]{1,0:T(8,128)(2,1)S(1)}, bf16[400,128]{1,0:T(8,128)(2,1)S(1)}, u32[]{:S(2)}, u32[]{:S(2)}) collective-permute-start(bf16[400,128]{1,0:T(8,128)(2,1)S(1)} %get-tuple-element.146.own0), channel_id=1, source_target_pairs={{0,12},{2,14},{4,0},{6,2},{8,4},{10,6},{12,8},{14,10},{1,13},{3,15... | collective-permute-start | bytes 307208 | tf_op jit(solution)/shard_map/ppermute | solution.py:49
  35.1 1.3 collective-permute-start.9
  37.8 1.4 %collective-permute-start.10 = (bf16[400,128]{1,0:T(8,128)(2,1)S(1)}, bf16[400,128]{1,0:T(8,128)(2,1)S(1)}, u32[]{:S(2)}, u32[]{:S(2)}) collective-permute-start(bf16[400,128]{1,0:T(8,128)(2,1)S(1)} %get-tuple-element.155), channel_id=1, source_target_pairs={{0,1},{1,0},{2,3},{3,2},{4,5},{5,4},{6,7},{7,6},{8,9},{9,8},{10,11... | collective-permute-start | bytes 307208 | tf_op jit(solution)/shard_map/ppermute | solution.py:58
  39.2 7.0 %collective-permute-start.11 = (bf16[400,128]{1,0:T(8,128)(2,1)S(1)}, bf16[400,128]{1,0:T(8,128)(2,1)S(1)}, u32[]{:S(2)}, u32[]{:S(2)}) collective-permute-start(bf16[400,128]{1,0:T(8,128)(2,1)S(1)} %sum_pair.11._), channel_id=1, source_target_pairs={{0,4},{2,6},{4,8},{6,10},{8,12},{10,14},{12,0},{14,2},{1,5},{3,7},... | collective-permute-start | bytes 307208 | tf_op jit(solution)/shard_map/ppermute | solution.py:49
  40.9 5.3 %collective-permute-start.12 = (bf16[400,128]{1,0:T(8,128)(2,1)S(1)}, bf16[400,128]{1,0:T(8,128)(2,1)S(1)}, u32[]{:S(2)}, u32[]{:S(2)}) collective-permute-start(bf16[400,128]{1,0:T(8,128)(2,1)S(1)} %get-tuple-element.161), channel_id=1, source_target_pairs={{0,1},{1,0},{2,3},{3,2},{4,5},{5,4},{6,7},{7,6},{8,9},{9,8},{10,11... | collective-permute-start | bytes 307208 | tf_op jit(solution)/shard_map/ppermute | solution.py:58
  46.3 2.4 %collective-permute-start.13 = (bf16[400,128]{1,0:T(8,128)(2,1)S(1)}, bf16[400,128]{1,0:T(8,128)(2,1)S(1)}, u32[]{:S(2)}, u32[]{:S(2)}) collective-permute-start(bf16[400,128]{1,0:T(8,128)(2,1)S(1)} %get-tuple-element.164.own0), channel_id=1, source_target_pairs={{0,1},{1,0},{2,3},{3,2},{4,5},{5,4},{6,7},{7,6},{8,9},{9,8},{10,11... | collective-permute-start | bytes 307208 | tf_op jit(solution)/shard_map/ppermute | solution.py:58
  46.4 6.2 %collective-permute-start.14 = (bf16[400,128]{1,0:T(8,128)(2,1)S(1)}, bf16[400,128]{1,0:T(8,128)(2,1)S(1)}, u32[]{:S(2)}, u32[]{:S(2)}) collective-permute-start(bf16[400,128]{1,0:T(8,128)(2,1)S(1)} %get-tuple-element.164.own0), channel_id=1, source_target_pairs={{0,10},{2,12},{4,14},{6,0},{8,2},{10,4},{12,6},{14,8},{1,11},{3,13... | collective-permute-start | bytes 307208 | tf_op jit(solution)/shard_map/ppermute | solution.py:49
  52.6 1.3 collective-permute-start.15
  55.3 1.4 %collective-permute-start.16 = (bf16[400,128]{1,0:T(8,128)(2,1)S(1)}, bf16[400,128]{1,0:T(8,128)(2,1)S(1)}, u32[]{:S(2)}, u32[]{:S(2)}) collective-permute-start(bf16[400,128]{1,0:T(8,128)(2,1)S(1)} %get-tuple-element.173), channel_id=1, source_target_pairs={{0,1},{1,0},{2,3},{3,2},{4,5},{5,4},{6,7},{7,6},{8,9},{9,8},{10,11... | collective-permute-start | bytes 307208 | tf_op jit(solution)/shard_map/ppermute | solution.py:58
  56.7 9.0 %collective-permute-start.17 = (bf16[400,128]{1,0:T(8,128)(2,1)S(1)}, bf16[400,128]{1,0:T(8,128)(2,1)S(1)}, u32[]{:S(2)}, u32[]{:S(2)}) collective-permute-start(bf16[400,128]{1,0:T(8,128)(2,1)S(1)} %sum_pair.13._), channel_id=1, source_target_pairs={{0,6},{2,8},{4,10},{6,12},{8,14},{10,0},{12,2},{14,4},{1,7},{3,9},... | collective-permute-start | bytes 307208 | tf_op jit(solution)/shard_map/ppermute | solution.py:49
  58.2 7.5 %collective-permute-start.18 = (bf16[400,128]{1,0:T(8,128)(2,1)S(1)}, bf16[400,128]{1,0:T(8,128)(2,1)S(1)}, u32[]{:S(2)}, u32[]{:S(2)}) collective-permute-start(bf16[400,128]{1,0:T(8,128)(2,1)S(1)} %get-tuple-element.179), channel_id=1, source_target_pairs={{0,1},{1,0},{2,3},{3,2},{4,5},{5,4},{6,7},{7,6},{8,9},{9,8},{10,11... | collective-permute-start | bytes 307208 | tf_op jit(solution)/shard_map/ppermute | solution.py:58
  65.8 2.4 %collective-permute-start.19 = (bf16[400,128]{1,0:T(8,128)(2,1)S(1)}, bf16[400,128]{1,0:T(8,128)(2,1)S(1)}, u32[]{:S(2)}, u32[]{:S(2)}) collective-permute-start(bf16[400,128]{1,0:T(8,128)(2,1)S(1)} %get-tuple-element.182.own0), channel_id=1, source_target_pairs={{0,1},{1,0},{2,3},{3,2},{4,5},{5,4},{6,7},{7,6},{8,9},{9,8},{10,11... | collective-permute-start | bytes 307208 | tf_op jit(solution)/shard_map/ppermute | solution.py:58
  65.9 7.0 %collective-permute-start.20 = (bf16[400,128]{1,0:T(8,128)(2,1)S(1)}, bf16[400,128]{1,0:T(8,128)(2,1)S(1)}, u32[]{:S(2)}, u32[]{:S(2)}) collective-permute-start(bf16[400,128]{1,0:T(8,128)(2,1)S(1)} %get-tuple-element.182.own0), channel_id=1, source_target_pairs={{0,8},{2,10},{4,12},{6,14},{8,0},{10,2},{12,4},{14,6},{1,9},{3,11}... | collective-permute-start | bytes 307208 | tf_op jit(solution)/shard_map/ppermute | solution.py:49
  72.9 1.3 collective-permute-start.21
  75.6 1.4 %collective-permute-start.22 = (bf16[400,128]{1,0:T(8,128)(2,1)S(1)}, bf16[400,128]{1,0:T(8,128)(2,1)S(1)}, u32[]{:S(2)}, u32[]{:S(2)}) collective-permute-start(bf16[400,128]{1,0:T(8,128)(2,1)S(1)} %get-tuple-element.191), channel_id=1, source_target_pairs={{0,1},{1,0},{2,3},{3,2},{4,5},{5,4},{6,7},{7,6},{8,9},{9,8},{10,11... | collective-permute-start | bytes 307208 | tf_op jit(solution)/shard_map/ppermute | solution.py:58
  77.0 7.9 %collective-permute-start.23 = (bf16[400,128]{1,0:T(8,128)(2,1)S(1)}, bf16[400,128]{1,0:T(8,128)(2,1)S(1)}, u32[]{:S(2)}, u32[]{:S(2)}) collective-permute-start(bf16[400,128]{1,0:T(8,128)(2,1)S(1)} %sum_pair.15._), channel_id=1, source_target_pairs={{0,8},{2,10},{4,12},{6,14},{8,0},{10,2},{12,4},{14,6},{1,9},{3,11}... | collective-permute-start | bytes 307208 | tf_op jit(solution)/shard_map/ppermute | solution.py:49
  78.5 6.3 %collective-permute-start.24 = (bf16[400,128]{1,0:T(8,128)(2,1)S(1)}, bf16[400,128]{1,0:T(8,128)(2,1)S(1)}, u32[]{:S(2)}, u32[]{:S(2)}) collective-permute-start(bf16[400,128]{1,0:T(8,128)(2,1)S(1)} %get-tuple-element.197), channel_id=1, source_target_pairs={{0,1},{1,0},{2,3},{3,2},{4,5},{5,4},{6,7},{7,6},{8,9},{9,8},{10,11... | collective-permute-start | bytes 307208 | tf_op jit(solution)/shard_map/ppermute | solution.py:58
  85.0 2.6 %collective-permute-start.26 = (bf16[400,128]{1,0:T(8,128)(2,1)S(1)}, bf16[400,128]{1,0:T(8,128)(2,1)S(1)}, u32[]{:S(2)}, u32[]{:S(2)}) collective-permute-start(bf16[400,128]{1,0:T(8,128)(2,1)S(1)} %get-tuple-element.200.own0), channel_id=1, source_target_pairs={{0,1},{1,0},{2,3},{3,2},{4,5},{5,4},{6,7},{7,6},{8,9},{9,8},{10,11... | collective-permute-start | bytes 307208 | tf_op jit(solution)/shard_map/ppermute | solution.py:58
  85.1 7.3 %collective-permute-start.25 = (bf16[400,128]{1,0:T(8,128)(2,1)S(1)}, bf16[400,128]{1,0:T(8,128)(2,1)S(1)}, u32[]{:S(2)}, u32[]{:S(2)}) collective-permute-start(bf16[400,128]{1,0:T(8,128)(2,1)S(1)} %get-tuple-element.200.own0), channel_id=1, source_target_pairs={{0,6},{2,8},{4,10},{6,12},{8,14},{10,0},{12,2},{14,4},{1,7},{3,9},... | collective-permute-start | bytes 307208 | tf_op jit(solution)/shard_map/ppermute | solution.py:49
  92.4 1.3 collective-permute-start.27
  96.2 2.3 %collective-permute-start.32 = (bf16[4,400,128]{2,1,0:T(8,128)(2,1)S(1)}, bf16[4,400,128]{2,1,0:T(8,128)(2,1)S(1)}, u32[]{:S(2)}, u32[]{:S(2)}) collective-permute-start(bf16[4,400,128]{2,1,0:T(8,128)(2,1)S(1)} %get-tuple-element.207._.refs_0_), channel_id=1, source_target_pairs={{0,1},{1,0},{2,3},{3,2},{4,5},{5,4},{6,7},{7,6},{8,9},{9,8},{10,11... | collective-permute-start | bytes 1228808 | tf_op jit(solution)/shard_map/ppermute | solution.py:58
  97.1 4.6 %collective-permute-start.31 = (bf16[4,400,128]{2,1,0:T(8,128)(2,1)S(1)}, bf16[4,400,128]{2,1,0:T(8,128)(2,1)S(1)}, u32[]{:S(2)}, u32[]{:S(2)}) collective-permute-start(bf16[4,400,128]{2,1,0:T(8,128)(2,1)S(1)} %get-tuple-element.217), channel_id=1, source_target_pairs={{0,1},{1,0},{2,3},{3,2},{4,5},{5,4},{6,7},{7,6},{8,9},{9,8},{10,11... | collective-permute-start | bytes 1228808 | tf_op jit(solution)/shard_map/ppermute | solution.py:58
  97.9 31.8 %copy-start = (f32[400,2048]{1,0:T(8,128)S(1)}, f32[400,2048]{1,0:T(8,128)}, u32[]{:S(2)}) copy-start(f32[400,2048]{1,0:T(8,128)} %rel_ref.7) | copy-start | bytes 9830404
  97.9 31.8 %copy-start.6 = (f32[2048]{0:T(1024)S(1)}, f32[2048]{0:T(1024)}, u32[]{:S(2)}) copy-start(f32[2048]{0:T(1024)} %param.12) | copy-start | bytes 24580
  97.9 2.8 %collective-permute-start.29 = (bf16[400,128]{1,0:T(8,128)(2,1)S(1)}, bf16[400,128]{1,0:T(8,128)(2,1)S(1)}, u32[]{:S(2)}, u32[]{:S(2)}) collective-permute-start(bf16[400,128]{1,0:T(8,128)(2,1)S(1)} %get-tuple-element.215), channel_id=1, source_target_pairs={{0,1},{1,0},{2,3},{3,2},{4,5},{5,4},{6,7},{7,6},{8,9},{9,8},{10,11... | collective-permute-start | bytes 307208 | tf_op jit(solution)/shard_map/ppermute | solution.py:58
  98.2 3.4 %collective-permute-start.28 = (bf16[400,128]{1,0:T(8,128)(2,1)S(1)}, bf16[400,128]{1,0:T(8,128)(2,1)S(1)}, u32[]{:S(2)}, u32[]{:S(2)}) collective-permute-start(bf16[400,128]{1,0:T(8,128)(2,1)S(1)} %get-tuple-element.213), channel_id=1, source_target_pairs={{0,1},{1,0},{2,3},{3,2},{4,5},{5,4},{6,7},{7,6},{8,9},{9,8},{10,11... | collective-permute-start | bytes 307208 | tf_op jit(solution)/shard_map/ppermute | solution.py:58
  98.6 6.2 %collective-permute-start.33 = (bf16[400,128]{1,0:T(8,128)(2,1)S(1)}, bf16[400,128]{1,0:T(8,128)(2,1)S(1)}, u32[]{:S(2)}, u32[]{:S(2)}) collective-permute-start(bf16[400,128]{1,0:T(8,128)(2,1)S(1)} %get-tuple-element.222), channel_id=1, source_target_pairs={{0,2},{2,0},{4,6},{6,4},{8,10},{10,8},{12,14},{14,12},{1,3},{3,1},... | collective-permute-start | bytes 307208 | tf_op jit(solution)/shard_map/ppermute | solution.py:54
  99.5 9.3 %collective-permute-start.37 = (bf16[400,128]{1,0:T(8,128)(2,1)S(1)}, bf16[400,128]{1,0:T(8,128)(2,1)S(1)}, u32[]{:S(2)}, u32[]{:S(2)}) collective-permute-start(bf16[400,128]{1,0:T(8,128)(2,1)S(1)} %get-tuple-element.228), channel_id=1, source_target_pairs={{0,2},{2,0},{4,6},{6,4},{8,10},{10,8},{12,14},{14,12},{1,3},{3,1},... | collective-permute-start | bytes 307208 | tf_op jit(solution)/shard_map/ppermute | solution.py:54
  100.7 10.3 %collective-permute-start.39 = (bf16[400,128]{1,0:T(8,128)(2,1)S(1)}, bf16[400,128]{1,0:T(8,128)(2,1)S(1)}, u32[]{:S(2)}, u32[]{:S(2)}) collective-permute-start(bf16[400,128]{1,0:T(8,128)(2,1)S(1)} %get-tuple-element.230), channel_id=1, source_target_pairs={{0,2},{2,0},{4,6},{6,4},{8,10},{10,8},{12,14},{14,12},{1,3},{3,1},... | collective-permute-start | bytes 307208 | tf_op jit(solution)/shard_map/ppermute | solution.py:54
  101.6 10.2 %collective-permute-start.30 = (bf16[400,128]{1,0:T(8,128)(2,1)S(1)}, bf16[400,128]{1,0:T(8,128)(2,1)S(1)}, u32[]{:S(2)}, u32[]{:S(2)}) collective-permute-start(bf16[400,128]{1,0:T(8,128)(2,1)S(1)} %sum_pair.17), channel_id=1, source_target_pairs={{0,10},{2,12},{4,14},{6,0},{8,2},{10,4},{12,6},{14,8},{1,11},{3,13... | collective-permute-start | bytes 307208 | tf_op jit(solution)/shard_map/ppermute | solution.py:49
  101.7 10.7 %collective-permute-start.35 = (bf16[400,128]{1,0:T(8,128)(2,1)S(1)}, bf16[400,128]{1,0:T(8,128)(2,1)S(1)}, u32[]{:S(2)}, u32[]{:S(2)}) collective-permute-start(bf16[400,128]{1,0:T(8,128)(2,1)S(1)} %get-tuple-element.226), channel_id=1, source_target_pairs={{0,2},{2,0},{4,6},{6,4},{8,10},{10,8},{12,14},{14,12},{1,3},{3,1},... | collective-permute-start | bytes 307208 | tf_op jit(solution)/shard_map/ppermute | solution.py:54
  104.8 7.6 %collective-permute-start.36 = (bf16[400,128]{1,0:T(8,128)(2,1)S(1)}, bf16[400,128]{1,0:T(8,128)(2,1)S(1)}, u32[]{:S(2)}, u32[]{:S(2)}) collective-permute-start(bf16[400,128]{1,0:T(8,128)(2,1)S(1)} %sum_piece.4.refs_5_), channel_id=1, source_target_pairs={{0,12},{2,14},{4,8},{6,10},{8,4},{10,6},{12,0},{14,2},{1,13},{3,15... | collective-permute-start | bytes 307208 | tf_op jit(solution)/shard_map/ppermute | solution.py:54
  108.8 8.2 %collective-permute-start.38 = (bf16[400,128]{1,0:T(8,128)(2,1)S(1)}, bf16[400,128]{1,0:T(8,128)(2,1)S(1)}, u32[]{:S(2)}, u32[]{:S(2)}) collective-permute-start(bf16[400,128]{1,0:T(8,128)(2,1)S(1)} %sum_piece.5), channel_id=1, source_target_pairs={{0,8},{2,10},{4,12},{6,14},{8,0},{10,2},{12,4},{14,6},{1,9},{3,11}... | collective-permute-start | bytes 307208 | tf_op jit(solution)/shard_map/ppermute | solution.py:54
  111.0 6.6 %collective-permute-start.40 = (bf16[400,128]{1,0:T(8,128)(2,1)S(1)}, bf16[400,128]{1,0:T(8,128)(2,1)S(1)}, u32[]{:S(2)}, u32[]{:S(2)}) collective-permute-start(bf16[400,128]{1,0:T(8,128)(2,1)S(1)} %sum_piece.6), channel_id=1, source_target_pairs={{0,4},{2,6},{4,0},{6,2},{8,12},{10,14},{12,8},{14,10},{1,5},{3,7},... | collective-permute-start | bytes 307208 | tf_op jit(solution)/shard_map/ppermute | solution.py:54
  111.8 18.9 %collective-permute-start.34 = (f32[408,128]{1,0:T(8,128)S(1)}, f32[408,128]{1,0:T(8,128)S(1)}, u32[]{:S(2)}, u32[]{:S(2)}) collective-permute-start(f32[408,128]{1,0:T(8,128)S(1)} %update.11.mine), channel_id=1, source_target_pairs={{0,1},{1,0},{2,3},{3,2},{4,5},{5,4},{6,7},{7,6},{8,9},{9,8},{10,11... | collective-permute-start | bytes 626696 | tf_op jit(solution)/shard_map/ppermute | solution.py:58
  117.7 4.8 %collective-permute-start.46 = (bf16[400,128]{1,0:T(8,128)(2,1)S(1)}, bf16[400,128]{1,0:T(8,128)(2,1)S(1)}, u32[]{:S(2)}, u32[]{:S(2)}) collective-permute-start(bf16[400,128]{1,0:T(8,128)(2,1)S(1)} %sum_piece.7.refs_0_), channel_id=1, source_target_pairs={{0,4},{2,6},{4,0},{6,2},{8,12},{10,14},{12,8},{14,10},{1,5},{3,7},... | collective-permute-start | bytes 307208 | tf_op jit(solution)/shard_map/ppermute | solution.py:54
  117.7 9.9 %collective-permute-start.44 = (bf16[400,128]{1,0:T(8,128)(2,1)S(1)}, bf16[400,128]{1,0:T(8,128)(2,1)S(1)}, u32[]{:S(2)}, u32[]{:S(2)}) collective-permute-start(bf16[400,128]{1,0:T(8,128)(2,1)S(1)} %sum_piece.7.refs_0_), channel_id=1, source_target_pairs={{0,8},{2,10},{4,12},{6,14},{8,0},{10,2},{12,4},{14,6},{1,9},{3,11}... | collective-permute-start | bytes 307208 | tf_op jit(solution)/shard_map/ppermute | solution.py:54
  120.5 7.9 %collective-permute-start.42 = (bf16[400,128]{1,0:T(8,128)(2,1)S(1)}, bf16[400,128]{1,0:T(8,128)(2,1)S(1)}, u32[]{:S(2)}, u32[]{:S(2)}) collective-permute-start(bf16[400,128]{1,0:T(8,128)(2,1)S(1)} %sum_piece.7.refs_0_), channel_id=1, source_target_pairs={{0,12},{2,14},{4,8},{6,10},{8,4},{10,6},{12,0},{14,2},{1,13},{3,15... | collective-permute-start | bytes 307208 | tf_op jit(solution)/shard_map/ppermute | solution.py:54
  122.1 9.6 %collective-permute-start.41 = (bf16[400,128]{1,0:T(8,128)(2,1)S(1)}, bf16[400,128]{1,0:T(8,128)(2,1)S(1)}, u32[]{:S(2)}, u32[]{:S(2)}) collective-permute-start(bf16[400,128]{1,0:T(8,128)(2,1)S(1)} %sum_piece.7.refs_0_), channel_id=1, source_target_pairs={{0,2},{2,0},{4,6},{6,4},{8,10},{10,8},{12,14},{14,12},{1,3},{3,1},... | collective-permute-start | bytes 307208 | tf_op jit(solution)/shard_map/ppermute | solution.py:54
  122.5 9.2 %collective-permute-start.47 = (bf16[400,128]{1,0:T(8,128)(2,1)S(1)}, bf16[400,128]{1,0:T(8,128)(2,1)S(1)}, u32[]{:S(2)}, u32[]{:S(2)}) collective-permute-start(bf16[400,128]{1,0:T(8,128)(2,1)S(1)} %collective-permute-done.46.refs_3_), channel_id=1, source_target_pairs={{0,2},{2,0},{4,6},{6,4},{8,10},{10,8},{12,14},{14,12},{1,3},{3,1},... | collective-permute-start | bytes 307208 | tf_op jit(solution)/shard_map/ppermute | solution.py:54
  127.7 4.7 %collective-permute-start.45 = (bf16[400,128]{1,0:T(8,128)(2,1)S(1)}, bf16[400,128]{1,0:T(8,128)(2,1)S(1)}, u32[]{:S(2)}, u32[]{:S(2)}) collective-permute-start(bf16[400,128]{1,0:T(8,128)(2,1)S(1)} %collective-permute-done.44.refs_2_), channel_id=1, source_target_pairs={{0,2},{2,0},{4,6},{6,4},{8,10},{10,8},{12,14},{14,12},{1,3},{3,1},... | collective-permute-start | bytes 307208 | tf_op jit(solution)/shard_map/ppermute | solution.py:54
  128.4 5.0 %collective-permute-start.43 = (bf16[400,128]{1,0:T(8,128)(2,1)S(1)}, bf16[400,128]{1,0:T(8,128)(2,1)S(1)}, u32[]{:S(2)}, u32[]{:S(2)}) collective-permute-start(bf16[400,128]{1,0:T(8,128)(2,1)S(1)} %collective-permute-done.42.refs_1_), channel_id=1, source_target_pairs={{0,2},{2,0},{4,6},{6,4},{8,10},{10,8},{12,14},{14,12},{1,3},{3,1},... | collective-permute-start | bytes 307208 | tf_op jit(solution)/shard_map/ppermute | solution.py:54
  131.6 1.9 %collective-permute-start.49 = (bf16[4,400,128]{2,1,0:T(8,128)(2,1)S(1)}, bf16[4,400,128]{2,1,0:T(8,128)(2,1)S(1)}, u32[]{:S(2)}, u32[]{:S(2)}) collective-permute-start(bf16[4,400,128]{2,1,0:T(8,128)(2,1)S(1)} %stacked.3), channel_id=1, source_target_pairs={{0,1},{1,0},{2,3},{3,2},{4,5},{5,4},{6,7},{7,6},{8,9},{9,8},{10,11... | collective-permute-start | bytes 1228808 | tf_op jit(solution)/shard_map/ppermute | solution.py:58
  133.5 1.8 %collective-permute-start.48 = (bf16[4,400,128]{2,1,0:T(8,128)(2,1)S(1)}, bf16[4,400,128]{2,1,0:T(8,128)(2,1)S(1)}, u32[]{:S(2)}, u32[]{:S(2)}) collective-permute-start(bf16[4,400,128]{2,1,0:T(8,128)(2,1)S(1)} %stacked.2), channel_id=1, source_target_pairs={{0,1},{1,0},{2,3},{3,2},{4,5},{5,4},{6,7},{7,6},{8,9},{9,8},{10,11... | collective-permute-start | bytes 1228808 | tf_op jit(solution)/shard_map/ppermute | solution.py:58

commit v3 on v2

--- a/solution.py
+++ b/solution.py
@@ -97,28 +97,23 @@
 
 
 def relsum_kernel(t, first, ids_ref, drel_ref, *refs):
-    step = pl.program_id(0)
     out_ref = refs[-1]
-    tile = out_ref.shape[1]
-    hot = one_hot(ids_ref, t, tile, lambda i: i - step * tile)
-    part = mm(drel_ref[...], hot, NT)
-    out_ref[...] = part if first else refs[0][...] + part
+    rels = out_ref.shape[1]
+    tile = min(rels, 512)
+    drel = drel_ref[...]
+    for lo in range(0, rels, tile):
+        hot = one_hot(ids_ref, t, tile, lambda i, lo=lo: i - lo)
+        part = mm(drel, hot, NT)
+        out_ref[:, lo : lo + tile] = part if first else refs[0][:, lo : lo + tile] + part
 
 
 def relsum(t, rel_ids, drel, acc, rels):
     width, slots = drel.shape
-    tile = min(rels, 512)
-    wide = pl.BlockSpec((width, tile), lambda i: (0, i))
     ins = [rel_ids, drel] + ([] if acc is None else [acc])
     return pl.pallas_call(
         functools.partial(relsum_kernel, t, acc is None),
-        grid=(rels // tile,),
-        in_specs=[
-            pl.BlockSpec(rel_ids.shape, lambda i: (0, 0, 0)),
-            pl.BlockSpec((width, slots), lambda i: (0, 0)),
-        ]
-        + ([] if acc is None else [wide]),
-        out_specs=wide,
+        in_specs=[vmem()] * len(ins),
+        out_specs=vmem(),
         out_shape=jax.ShapeDtypeStruct((width, rels), F32),
         input_output_aliases={} if acc is None else {2: 0},
         compiler_params=params(),

time: 137 us -> 136 us (level)
  Pallas kernels: 47 us -> 42.4 us
  waiting for transfers between devices: 59.3 us -> 62.6 us
    pallas_call x5, Pallas kernels: 10.7 us -> 6.22 us  [relsum(): pl.pallas_call(functools.partial(relsum_kernel, t, acc is None), in_specs...]
    ppermute x10, waiting for transfers between devices: 33.3 us -> 36.4 us  [shifted(): return lax.ppermute(x, 'dom', [(i, (i + by) % n) for i in range(n)])]
  transfers between devices with their start and end apart: 50 -> 50, of which waited for: 27 -> 27; matrix products, arithmetic and copies ran while one was open for 0% -> 0% of each run, Pallas kernels for 23% -> 20%
where the time goes in v3:
time: 136 us
  waiting for transfers between devices  62.6 us (46%)
  Pallas kernels  42.4 us (31%)
  starting transfers between devices  29.7 us (22%)
  between operations  1.52 us (1%)
    ppermute x10, waiting for transfers between devices, shifted(): return lax.ppermute(x, 'dom', [(i, (i + by) % n) for i in range(n)])  36.4 us
    ppermute x14, starting transfers between devices, swapped(): return lax.ppermute(x, 'dom', [(i, i ^ bits) for i in range(n)])  17.5 us
    ppermute x14, waiting for transfers between devices, swapped(): return lax.ppermute(x, 'dom', [(i, i ^ bits) for i in range(n)])  15 us
    ppermute x26, waiting for transfers between devices, across(): return lax.ppermute(x, 'edge', [(0, 1), (1, 0)])  11.2 us
    ppermute x10, starting transfers between devices, shifted(): return lax.ppermute(x, 'dom', [(i, (i + by) % n) for i in range(n)])  7.52 us
    pallas_call x5, Pallas kernels, relsum(): pl.pallas_call(functools.partial(relsum_kernel, t, acc is None), in_specs...  6.22 us
    pallas_call x4, Pallas kernels, source_grad(): pl.pallas_call(functools.partial(source_grad_kernel, t, shape), in_specs=...  5.9 us
    pallas_call x4, Pallas kernels, target_grad(): pl.pallas_call(target_kernel, in_specs=[vmem()] * 8, out_specs=[vmem()] *...  5.5 us
  transfers between devices with their start and end apart: 50, of which 27 were waited for; matrix products, arithmetic and copies ran while one was open for 0% of the time, Pallas kernels for 20%

profile of v3, /device:TPU:0, one launch (start us, length us, event | category | flops | bytes accessed | tf_op | source)
XLA Modules:
  0.0 136.2 jit_solution(11548031032384471892)
XLA Ops:
  0.6 5.4 %first_round.1 = (f32[400,128]{1,0:T(8,128)S(1)}, bf16[400,128]{1,0:T(8,128)(2,1)S(1)}, bf16[400,512]{1,0:T(8,128)(2,1)S(1)}, bf16[400,2048]{1,0:T(8,128)(2,1)S(...) custom-call(s32[4,6]{1,0:T(4,128)} %bitcast.6, s32[4,6]{1,0:T(4,128)} %bitcast.17, s32[6,4,128]{2,1,0:T(4,128)} %src_ref.11, ...), custom_call_target="tpu_custom_call" | custom-call | flops 1258291200 | bytes 6553600 | tf_op jit(solution)/shard_map/first_round/pallas_call | solution.py:304
  6.6 0.9 collective-permute-done.refs_3_
  8.1 5.7 %collective-permute-start.2 = (bf16[400,128]{1,0:T(8,128)(2,1)S(1)}, bf16[400,128]{1,0:T(8,128)(2,1)S(1)}, u32[]{:S(2)}, u32[]{:S(2)}) collective-permute-start(bf16[400,128]{1,0:T(8,128)(2,1)S(1)} %get-tuple-element.127.own0), channel_id=1, source_target_pairs={{0,14},{2,0},{4,2},{6,4},{8,6},{10,8},{12,10},{14,12},{1,15},{3,1}... | collective-permute-start | bytes 307208 | tf_op jit(solution)/shard_map/ppermute | solution.py:49
  13.8 1.0 relvec.5.rel_ref
  14.8 1.0 relsum.5.refs_1_.refs_0_
  15.9 0.9 source_side.5
  17.3 1.0 collective-permute-done.3.far1
  18.2 1.4 %target_grad.4 = (f32[400,128]{1,0:T(8,128)S(1)}, bf16[400,128]{1,0:T(8,128)(2,1)S(1)}, bf16[128,512]{1,0:T(8,128)(2,1)S(1)}) custom-call(f32[512,128]{1,0:T(8,128)S(1)} %near_products.4.near, bf16[400,128]{1,0:T(8,128)(2,1)S(1)} %collective-permute-done.3.far1, bf16[400,512]{1,0:T(8,128)(2,1)S(1)} %get-tuple-element.130.refs_0_.query_ref, ...), custom_call_target="tpu_custom_call" | custom-call | flops 104857600 | bytes 2457600 | tf_op jit(solution)/shard_map/target_grad/pallas_call | solution.py:442
  19.8 1.2 collective-permute-done.4.b_ref
  21.1 1.5 %source_grad.4 = (f32[400,128]{1,0:T(8,128)S(1)}, bf16[400,128]{1,0:T(8,128)(2,1)S(1)}, bf16[400,512]{1,0:T(8,128)(2,1)S(1)}) custom-call(s32[4,6]{1,0:T(4,128)S(1)} %bitcast.8, s32[4,6]{1,0:T(4,128)S(1)} %bitcast.19, bf16[400,128]{1,0:T(8,128)(2,1)S(1)} %sum_pair.9._, bf16[400,128]{1,0:T(8,128)(2,1)S(1)} %held.5.far0, ...), custom_call_target="tpu_custom_call" | custom-call | flops 204800 | bytes 204800 | tf_op jit(solution)/shard_map/source_grad/pallas_call | solution.py:474
  22.8 1.0 relvec.6.refs_4_.rel_ref
  23.8 5.1 %collective-permute-done.5.b_ref = bf16[400,128]{1,0:T(8,128)(2,1)S(1)} collective-permute-done((bf16[400,128]{1,0:T(8,128)(2,1)S(1)}, bf16[400,128]{1,0:T(8,128)(2,1)S(1)}, u32[]{:S(2)}, u32[]{:S(2)}) %collective-permute-start.5) | collective-permute-done | bytes 102432 | tf_op jit(solution)/shard_map/ppermute | solution.py:49
  29.7 1.3 relsum.6.refs_1_.refs_0_
  31.0 0.9 source_side.6
  31.9 2.6 %collective-permute-done.8.x_ref = bf16[400,128]{1,0:T(8,128)(2,1)S(1)} collective-permute-done((bf16[400,128]{1,0:T(8,128)(2,1)S(1)}, bf16[400,128]{1,0:T(8,128)(2,1)S(1)}, u32[]{:S(2)}, u32[]{:S(2)}) %collective-permute-start.8) | collective-permute-done | bytes 102432 | tf_op jit(solution)/shard_map/ppermute | solution.py:49
  34.8 1.0 collective-permute-done.9.far1
  35.8 1.4 %target_grad.5 = (f32[400,128]{1,0:T(8,128)S(1)}, bf16[400,128]{1,0:T(8,128)(2,1)S(1)}, bf16[128,512]{1,0:T(8,128)(2,1)S(1)}) custom-call(f32[512,128]{1,0:T(8,128)S(1)} %near_products.5.near, bf16[400,128]{1,0:T(8,128)(2,1)S(1)} %collective-permute-done.9.far1, bf16[400,512]{1,0:T(8,128)(2,1)S(1)} %get-tuple-element.148.refs_0_.query_ref, ...), custom_call_target="tpu_custom_call" | custom-call | flops 104857600 | bytes 2457600 | tf_op jit(solution)/shard_map/target_grad/pallas_call | solution.py:442
  37.4 1.2 collective-permute-done.10.b_ref
  38.6 1.5 %source_grad.5 = (f32[400,128]{1,0:T(8,128)S(1)}, bf16[400,128]{1,0:T(8,128)(2,1)S(1)}, bf16[400,512]{1,0:T(8,128)(2,1)S(1)}) custom-call(s32[4,6]{1,0:T(4,128)S(1)} %bitcast.10, s32[4,6]{1,0:T(4,128)S(1)} %bitcast.21, bf16[400,128]{1,0:T(8,128)(2,1)S(1)} %sum_pair.11._, bf16[400,128]{1,0:T(8,128)(2,1)S(1)} %held.6.far0, ...), custom_call_target="tpu_custom_call" | custom-call | flops 204800 | bytes 204800 | tf_op jit(solution)/shard_map/source_grad/pallas_call | solution.py:474
  40.3 1.0 relvec.7.refs_4_.rel_ref
  41.4 4.0 %collective-permute-done.11.b_ref = bf16[400,128]{1,0:T(8,128)(2,1)S(1)} collective-permute-done((bf16[400,128]{1,0:T(8,128)(2,1)S(1)}, bf16[400,128]{1,0:T(8,128)(2,1)S(1)}, u32[]{:S(2)}, u32[]{:S(2)}) %collective-permute-start.11) | collective-permute-done | bytes 102432 | tf_op jit(solution)/shard_map/ppermute | solution.py:49
  46.1 1.3 relsum.7.refs_1_.refs_0_
  47.4 0.9 source_side.7
  48.3 3.5 %collective-permute-done.14.x_ref = bf16[400,128]{1,0:T(8,128)(2,1)S(1)} collective-permute-done((bf16[400,128]{1,0:T(8,128)(2,1)S(1)}, bf16[400,128]{1,0:T(8,128)(2,1)S(1)}, u32[]{:S(2)}, u32[]{:S(2)}) %collective-permute-start.14) | collective-permute-done | bytes 102432 | tf_op jit(solution)/shard_map/ppermute | solution.py:49
  52.1 1.0 collective-permute-done.15.far1
  53.1 1.4 %target_grad.6 = (f32[400,128]{1,0:T(8,128)S(1)}, bf16[400,128]{1,0:T(8,128)(2,1)S(1)}, bf16[128,512]{1,0:T(8,128)(2,1)S(1)}) custom-call(f32[512,128]{1,0:T(8,128)S(1)} %near_products.6.near, bf16[400,128]{1,0:T(8,128)(2,1)S(1)} %collective-permute-done.15.far1, bf16[400,512]{1,0:T(8,128)(2,1)S(1)} %get-tuple-element.166.refs_0_.query_ref, ...), custom_call_target="tpu_custom_call" | custom-call | flops 104857600 | bytes 2457600 | tf_op jit(solution)/shard_map/target_grad/pallas_call | solution.py:442
  54.7 1.2 collective-permute-done.16.b_ref
  56.2 1.5 %source_grad.6 = (f32[400,128]{1,0:T(8,128)S(1)}, bf16[400,128]{1,0:T(8,128)(2,1)S(1)}, bf16[400,512]{1,0:T(8,128)(2,1)S(1)}) custom-call(s32[4,6]{1,0:T(4,128)S(1)} %bitcast.12, s32[4,6]{1,0:T(4,128)S(1)} %bitcast.23, bf16[400,128]{1,0:T(8,128)(2,1)S(1)} %sum_pair.13._, bf16[400,128]{1,0:T(8,128)(2,1)S(1)} %held.7.far0, ...), custom_call_target="tpu_custom_call" | custom-call | flops 204800 | bytes 204800 | tf_op jit(solution)/shard_map/source_grad/pallas_call | solution.py:474
  57.9 1.0 relvec.8.refs_4_.rel_ref
  58.9 6.2 %collective-permute-done.17.b_ref = bf16[400,128]{1,0:T(8,128)(2,1)S(1)} collective-permute-done((bf16[400,128]{1,0:T(8,128)(2,1)S(1)}, bf16[400,128]{1,0:T(8,128)(2,1)S(1)}, u32[]{:S(2)}, u32[]{:S(2)}) %collective-permute-start.17) | collective-permute-done | bytes 102432 | tf_op jit(solution)/shard_map/ppermute | solution.py:49
  65.4 1.3 relsum.8.refs_1_.refs_0_
  66.7 0.9 source_side.8
  67.6 4.7 %collective-permute-done.20.x_ref = bf16[400,128]{1,0:T(8,128)(2,1)S(1)} collective-permute-done((bf16[400,128]{1,0:T(8,128)(2,1)S(1)}, bf16[400,128]{1,0:T(8,128)(2,1)S(1)}, u32[]{:S(2)}, u32[]{:S(2)}) %collective-permute-start.20) | collective-permute-done | bytes 102432 | tf_op jit(solution)/shard_map/ppermute | solution.py:49
  72.7 0.9 collective-permute-done.21.far1
  73.7 1.4 %target_grad.7 = (f32[400,128]{1,0:T(8,128)S(1)}, bf16[400,128]{1,0:T(8,128)(2,1)S(1)}, bf16[128,512]{1,0:T(8,128)(2,1)S(1)}) custom-call(f32[512,128]{1,0:T(8,128)S(1)} %near_products.7.near, bf16[400,128]{1,0:T(8,128)(2,1)S(1)} %collective-permute-done.21.far1, bf16[400,512]{1,0:T(8,128)(2,1)S(1)} %get-tuple-element.184.refs_0_.query_ref, ...), custom_call_target="tpu_custom_call" | custom-call | flops 104857600 | bytes 2457600 | tf_op jit(solution)/shard_map/target_grad/pallas_call | solution.py:442
  75.3 1.2 collective-permute-done.22.b_ref
  76.5 1.5 %source_grad.7 = (f32[400,128]{1,0:T(8,128)S(1)}, bf16[400,128]{1,0:T(8,128)(2,1)S(1)}, bf16[400,512]{1,0:T(8,128)(2,1)S(1)}) custom-call(s32[4,6]{1,0:T(4,128)S(1)} %bitcast.14, s32[4,6]{1,0:T(4,128)S(1)} %bitcast.25, bf16[400,128]{1,0:T(8,128)(2,1)S(1)} %sum_pair.15._, bf16[400,128]{1,0:T(8,128)(2,1)S(1)} %held.8.far0, ...), custom_call_target="tpu_custom_call" | custom-call | flops 204800 | bytes 204800 | tf_op jit(solution)/shard_map/source_grad/pallas_call | solution.py:474
  78.2 1.0 relvec.9.refs_4_.rel_ref
  79.3 5.2 %collective-permute-done.23.b_ref = bf16[400,128]{1,0:T(8,128)(2,1)S(1)} collective-permute-done((bf16[400,128]{1,0:T(8,128)(2,1)S(1)}, bf16[400,128]{1,0:T(8,128)(2,1)S(1)}, u32[]{:S(2)}, u32[]{:S(2)}) %collective-permute-start.23) | collective-permute-done | bytes 102432 | tf_op jit(solution)/shard_map/ppermute | solution.py:49
  85.0 1.3 relsum.9.refs_1_.acc_ref
  86.9 5.0 %collective-permute-done.25.x_ref = bf16[400,128]{1,0:T(8,128)(2,1)S(1)} collective-permute-done((bf16[400,128]{1,0:T(8,128)(2,1)S(1)}, bf16[400,128]{1,0:T(8,128)(2,1)S(1)}, u32[]{:S(2)}, u32[]{:S(2)}) %collective-permute-start.25) | collective-permute-done | bytes 102432 | tf_op jit(solution)/shard_map/ppermute | solution.py:49
  91.9 1.3 collective-permute-done.27.far1
  93.2 1.8 %last_terms.1 = (bf16[400,512]{1,0:T(8,128)(2,1)S(1)}, bf16[400,512]{1,0:T(8,128)(2,1)S(1)}, bf16[400,512]{1,0:T(8,128)(2,1)S(1)}) custom-call(s32[4,6]{1,0:T(4,128)S(1)} %bitcast.16, s32[4,6]{1,0:T(4,128)S(1)} %bitcast.27, bf16[400,128]{1,0:T(8,128)(2,1)S(1)} %held.9.far0, bf16[400,128]{1,0:T(8,128)(2,1)S(1)} %collective-permute-done.27.far1, ...), custom_call_target="tpu_custom_call" | custom-call | flops 157286400 | bytes 2457600 | tf_op jit(solution)/shard_map/last_terms/pallas_call | solution.py:504
  95.9 0.7 pieces.3
  98.1 1.0 collective-permute-start.33
  99.1 1.1 collective-permute-start.37
  100.2 0.9 collective-permute-start.39
  101.3 3.1 %collective-permute-start.35 = (bf16[400,128]{1,0:T(8,128)(2,1)S(1)}, bf16[400,128]{1,0:T(8,128)(2,1)S(1)}, u32[]{:S(2)}, u32[]{:S(2)}) collective-permute-start(bf16[400,128]{1,0:T(8,128)(2,1)S(1)} %get-tuple-element.226), channel_id=1, source_target_pairs={{0,2},{2,0},{4,6},{6,4},{8,10},{10,8},{12,14},{14,12},{1,3},{3,1},... | collective-permute-start | bytes 307208 | tf_op jit(solution)/shard_map/ppermute | solution.py:54
  104.4 2.1 %collective-permute-start.36 = (bf16[400,128]{1,0:T(8,128)(2,1)S(1)}, bf16[400,128]{1,0:T(8,128)(2,1)S(1)}, u32[]{:S(2)}, u32[]{:S(2)}) collective-permute-start(bf16[400,128]{1,0:T(8,128)(2,1)S(1)} %sum_piece.4.refs_5_), channel_id=1, source_target_pairs={{0,12},{2,14},{4,8},{6,10},{8,4},{10,6},{12,0},{14,2},{1,13},{3,15... | collective-permute-start | bytes 307208 | tf_op jit(solution)/shard_map/ppermute | solution.py:54
  106.5 1.8 %collective-permute-done.37.refs_0_ = bf16[400,128]{1,0:T(8,128)(2,1)S(1)} collective-permute-done((bf16[400,128]{1,0:T(8,128)(2,1)S(1)}, bf16[400,128]{1,0:T(8,128)(2,1)S(1)}, u32[]{:S(2)}, u32[]{:S(2)}) %collective-permute-start.37) | collective-permute-done | bytes 102432 | tf_op jit(solution)/shard_map/ppermute | solution.py:54
  108.4 2.1 %collective-permute-done.39.refs_0_ = bf16[400,128]{1,0:T(8,128)(2,1)S(1)} collective-permute-done((bf16[400,128]{1,0:T(8,128)(2,1)S(1)}, bf16[400,128]{1,0:T(8,128)(2,1)S(1)}, u32[]{:S(2)}, u32[]{:S(2)}) %collective-permute-start.39) | collective-permute-done | bytes 102432 | tf_op jit(solution)/shard_map/ppermute | solution.py:54
  110.5 0.7 collective-permute-start.40
  111.9 4.8 %collective-permute-done.38.refs_2_ = bf16[400,128]{1,0:T(8,128)(2,1)S(1)} collective-permute-done((bf16[400,128]{1,0:T(8,128)(2,1)S(1)}, bf16[400,128]{1,0:T(8,128)(2,1)S(1)}, u32[]{:S(2)}, u32[]{:S(2)}) %collective-permute-start.38) | collective-permute-done | bytes 102432 | tf_op jit(solution)/shard_map/ppermute | solution.py:54
  117.3 2.7 %collective-permute-start.44 = (bf16[400,128]{1,0:T(8,128)(2,1)S(1)}, bf16[400,128]{1,0:T(8,128)(2,1)S(1)}, u32[]{:S(2)}, u32[]{:S(2)}) collective-permute-start(bf16[400,128]{1,0:T(8,128)(2,1)S(1)} %sum_piece.7.refs_0_), channel_id=1, source_target_pairs={{0,8},{2,10},{4,12},{6,14},{8,0},{10,2},{12,4},{14,6},{1,9},{3,11}... | collective-permute-start | bytes 307208 | tf_op jit(solution)/shard_map/ppermute | solution.py:54
  120.0 1.7 %collective-permute-start.42 = (bf16[400,128]{1,0:T(8,128)(2,1)S(1)}, bf16[400,128]{1,0:T(8,128)(2,1)S(1)}, u32[]{:S(2)}, u32[]{:S(2)}) collective-permute-start(bf16[400,128]{1,0:T(8,128)(2,1)S(1)} %sum_piece.7.refs_0_), channel_id=1, source_target_pairs={{0,12},{2,14},{4,8},{6,10},{8,4},{10,6},{12,0},{14,2},{1,13},{3,15... | collective-permute-start | bytes 307208 | tf_op jit(solution)/shard_map/ppermute | solution.py:54
  122.1 1.6 %collective-permute-start.47 = (bf16[400,128]{1,0:T(8,128)(2,1)S(1)}, bf16[400,128]{1,0:T(8,128)(2,1)S(1)}, u32[]{:S(2)}, u32[]{:S(2)}) collective-permute-start(bf16[400,128]{1,0:T(8,128)(2,1)S(1)} %collective-permute-done.46.refs_3_), channel_id=1, source_target_pairs={{0,2},{2,0},{4,6},{6,4},{8,10},{10,8},{12,14},{14,12},{1,3},{3,1},... | collective-permute-start | bytes 307208 | tf_op jit(solution)/shard_map/ppermute | solution.py:54
  123.7 3.6 %collective-permute-done.44.refs_2_ = bf16[400,128]{1,0:T(8,128)(2,1)S(1)} collective-permute-done((bf16[400,128]{1,0:T(8,128)(2,1)S(1)}, bf16[400,128]{1,0:T(8,128)(2,1)S(1)}, u32[]{:S(2)}, u32[]{:S(2)}) %collective-permute-start.44) | collective-permute-done | bytes 102432 | tf_op jit(solution)/shard_map/ppermute | solution.py:54
  127.4 0.7 collective-permute-start.45
  128.1 1.3 collective-permute-start.43
  129.4 1.0 relnew.3
  130.5 0.8 whole_partition.1
  132.0 1.1 collective-permute-done.43.refs_1_.refs_2_
  133.3 1.4 relnew.4
  135.0 1.0 relnew.5
  (113 shorter events, 13.1 us)
Async XLA Ops:
  0.6 13.2 %copy-start.1 = (s32[6,4,128]{2,1,0:T(4,128)S(1)}, s32[6,4,128]{2,1,0:T(4,128)}, u32[]{:S(2)}) copy-start(s32[6,4,128]{2,1,0:T(4,128)} %ids_ref.25) | copy-start | bytes 36868
  6.1 9.8 %copy-start.2 = (s32[6,4,128]{2,1,0:T(4,128)S(1)}, s32[6,4,128]{2,1,0:T(4,128)}, u32[]{:S(2)}) copy-start(s32[6,4,128]{2,1,0:T(4,128)} %src_ref.11) | copy-start | bytes 36868
  6.1 9.8 %copy-start.3 = (s32[6,4,128]{2,1,0:T(4,128)S(1)}, s32[6,4,128]{2,1,0:T(4,128)}, u32[]{:S(2)}) copy-start(s32[6,4,128]{2,1,0:T(4,128)} %dst_ref.11) | copy-start | bytes 36868
  6.1 9.8 %copy-start.4 = (s32[6,4]{0,1:T(4,128)S(1)}, s32[6,4]{0,1:T(4,128)}, u32[]{:S(2)}) copy-start(s32[6,4]{0,1:T(4,128)} %param.16) | copy-start | bytes 292
  6.1 9.8 %copy-start.5 = (s32[6,4]{0,1:T(4,128)S(1)}, s32[6,4]{0,1:T(4,128)}, u32[]{:S(2)}) copy-start(s32[6,4]{0,1:T(4,128)} %param.17) | copy-start | bytes 292
  6.1 1.5 %collective-permute-start = (bf16[400,128]{1,0:T(8,128)(2,1)S(1)}, bf16[400,128]{1,0:T(8,128)(2,1)S(1)}, u32[]{:S(2)}, u32[]{:S(2)}) collective-permute-start(bf16[400,128]{1,0:T(8,128)(2,1)S(1)} %get-tuple-element.124), channel_id=1, source_target_pairs={{0,1},{1,0},{2,3},{3,2},{4,5},{5,4},{6,7},{7,6},{8,9},{9,8},{10,11... | collective-permute-start | bytes 307208 | tf_op jit(solution)/shard_map/ppermute | solution.py:58
  7.7 8.2 %collective-permute-start.1 = (bf16[400,128]{1,0:T(8,128)(2,1)S(1)}, bf16[400,128]{1,0:T(8,128)(2,1)S(1)}, u32[]{:S(2)}, u32[]{:S(2)}) collective-permute-start(bf16[400,128]{1,0:T(8,128)(2,1)S(1)} %get-tuple-element.127.own0), channel_id=1, source_target_pairs={{0,1},{1,0},{2,3},{3,2},{4,5},{5,4},{6,7},{7,6},{8,9},{9,8},{10,11... | collective-permute-start | bytes 307208 | tf_op jit(solution)/shard_map/ppermute | solution.py:58
  8.1 8.7 %collective-permute-start.2 = (bf16[400,128]{1,0:T(8,128)(2,1)S(1)}, bf16[400,128]{1,0:T(8,128)(2,1)S(1)}, u32[]{:S(2)}, u32[]{:S(2)}) collective-permute-start(bf16[400,128]{1,0:T(8,128)(2,1)S(1)} %get-tuple-element.127.own0), channel_id=1, source_target_pairs={{0,14},{2,0},{4,2},{6,4},{8,6},{10,8},{12,10},{14,12},{1,15},{3,1}... | collective-permute-start | bytes 307208 | tf_op jit(solution)/shard_map/ppermute | solution.py:49
  16.9 1.4 %collective-permute-start.3 = (bf16[400,128]{1,0:T(8,128)(2,1)S(1)}, bf16[400,128]{1,0:T(8,128)(2,1)S(1)}, u32[]{:S(2)}, u32[]{:S(2)}) collective-permute-start(bf16[400,128]{1,0:T(8,128)(2,1)S(1)} %held.5.far0), channel_id=1, source_target_pairs={{0,1},{1,0},{2,3},{3,2},{4,5},{5,4},{6,7},{7,6},{8,9},{9,8},{10,11... | collective-permute-start | bytes 307208 | tf_op jit(solution)/shard_map/ppermute | solution.py:58
  19.6 1.4 %collective-permute-start.4 = (bf16[400,128]{1,0:T(8,128)(2,1)S(1)}, bf16[400,128]{1,0:T(8,128)(2,1)S(1)}, u32[]{:S(2)}, u32[]{:S(2)}) collective-permute-start(bf16[400,128]{1,0:T(8,128)(2,1)S(1)} %get-tuple-element.137), channel_id=1, source_target_pairs={{0,1},{1,0},{2,3},{3,2},{4,5},{5,4},{6,7},{7,6},{8,9},{9,8},{10,11... | collective-permute-start | bytes 307208 | tf_op jit(solution)/shard_map/ppermute | solution.py:58
  21.0 7.9 %collective-permute-start.5 = (bf16[400,128]{1,0:T(8,128)(2,1)S(1)}, bf16[400,128]{1,0:T(8,128)(2,1)S(1)}, u32[]{:S(2)}, u32[]{:S(2)}) collective-permute-start(bf16[400,128]{1,0:T(8,128)(2,1)S(1)} %sum_pair.9._), channel_id=1, source_target_pairs={{0,2},{2,4},{4,6},{6,8},{8,10},{10,12},{12,14},{14,0},{1,3},{3,5},... | collective-permute-start | bytes 307208 | tf_op jit(solution)/shard_map/ppermute | solution.py:49
  22.6 6.4 %collective-permute-start.6 = (bf16[400,128]{1,0:T(8,128)(2,1)S(1)}, bf16[400,128]{1,0:T(8,128)(2,1)S(1)}, u32[]{:S(2)}, u32[]{:S(2)}) collective-permute-start(bf16[400,128]{1,0:T(8,128)(2,1)S(1)} %get-tuple-element.143), channel_id=1, source_target_pairs={{0,1},{1,0},{2,3},{3,2},{4,5},{5,4},{6,7},{7,6},{8,9},{9,8},{10,11... | collective-permute-start | bytes 307208 | tf_op jit(solution)/shard_map/ppermute | solution.py:58
  29.1 1.8 %collective-permute-start.7 = (bf16[400,128]{1,0:T(8,128)(2,1)S(1)}, bf16[400,128]{1,0:T(8,128)(2,1)S(1)}, u32[]{:S(2)}, u32[]{:S(2)}) collective-permute-start(bf16[400,128]{1,0:T(8,128)(2,1)S(1)} %get-tuple-element.146.own0), channel_id=1, source_target_pairs={{0,1},{1,0},{2,3},{3,2},{4,5},{5,4},{6,7},{7,6},{8,9},{9,8},{10,11... | collective-permute-start | bytes 307208 | tf_op jit(solution)/shard_map/ppermute | solution.py:58
  29.2 5.3 %collective-permute-start.8 = (bf16[400,128]{1,0:T(8,128)(2,1)S(1)}, bf16[400,128]{1,0:T(8,128)(2,1)S(1)}, u32[]{:S(2)}, u32[]{:S(2)}) collective-permute-start(bf16[400,128]{1,0:T(8,128)(2,1)S(1)} %get-tuple-element.146.own0), channel_id=1, source_target_pairs={{0,12},{2,14},{4,0},{6,2},{8,4},{10,6},{12,8},{14,10},{1,13},{3,15... | collective-permute-start | bytes 307208 | tf_op jit(solution)/shard_map/ppermute | solution.py:49
  34.5 1.3 collective-permute-start.9
  37.2 1.4 %collective-permute-start.10 = (bf16[400,128]{1,0:T(8,128)(2,1)S(1)}, bf16[400,128]{1,0:T(8,128)(2,1)S(1)}, u32[]{:S(2)}, u32[]{:S(2)}) collective-permute-start(bf16[400,128]{1,0:T(8,128)(2,1)S(1)} %get-tuple-element.155), channel_id=1, source_target_pairs={{0,1},{1,0},{2,3},{3,2},{4,5},{5,4},{6,7},{7,6},{8,9},{9,8},{10,11... | collective-permute-start | bytes 307208 | tf_op jit(solution)/shard_map/ppermute | solution.py:58
  38.6 6.8 %collective-permute-start.11 = (bf16[400,128]{1,0:T(8,128)(2,1)S(1)}, bf16[400,128]{1,0:T(8,128)(2,1)S(1)}, u32[]{:S(2)}, u32[]{:S(2)}) collective-permute-start(bf16[400,128]{1,0:T(8,128)(2,1)S(1)} %sum_pair.11._), channel_id=1, source_target_pairs={{0,4},{2,6},{4,8},{6,10},{8,12},{10,14},{12,0},{14,2},{1,5},{3,7},... | collective-permute-start | bytes 307208 | tf_op jit(solution)/shard_map/ppermute | solution.py:49
  40.1 5.3 %collective-permute-start.12 = (bf16[400,128]{1,0:T(8,128)(2,1)S(1)}, bf16[400,128]{1,0:T(8,128)(2,1)S(1)}, u32[]{:S(2)}, u32[]{:S(2)}) collective-permute-start(bf16[400,128]{1,0:T(8,128)(2,1)S(1)} %get-tuple-element.161), channel_id=1, source_target_pairs={{0,1},{1,0},{2,3},{3,2},{4,5},{5,4},{6,7},{7,6},{8,9},{9,8},{10,11... | collective-permute-start | bytes 307208 | tf_op jit(solution)/shard_map/ppermute | solution.py:58
  45.5 1.8 %collective-permute-start.13 = (bf16[400,128]{1,0:T(8,128)(2,1)S(1)}, bf16[400,128]{1,0:T(8,128)(2,1)S(1)}, u32[]{:S(2)}, u32[]{:S(2)}) collective-permute-start(bf16[400,128]{1,0:T(8,128)(2,1)S(1)} %get-tuple-element.164.own0), channel_id=1, source_target_pairs={{0,1},{1,0},{2,3},{3,2},{4,5},{5,4},{6,7},{7,6},{8,9},{9,8},{10,11... | collective-permute-start | bytes 307208 | tf_op jit(solution)/shard_map/ppermute | solution.py:58
  45.6 6.2 %collective-permute-start.14 = (bf16[400,128]{1,0:T(8,128)(2,1)S(1)}, bf16[400,128]{1,0:T(8,128)(2,1)S(1)}, u32[]{:S(2)}, u32[]{:S(2)}) collective-permute-start(bf16[400,128]{1,0:T(8,128)(2,1)S(1)} %get-tuple-element.164.own0), channel_id=1, source_target_pairs={{0,10},{2,12},{4,14},{6,0},{8,2},{10,4},{12,6},{14,8},{1,11},{3,13... | collective-permute-start | bytes 307208 | tf_op jit(solution)/shard_map/ppermute | solution.py:49
  51.8 1.3 collective-permute-start.15
  54.5 1.4 %collective-permute-start.16 = (bf16[400,128]{1,0:T(8,128)(2,1)S(1)}, bf16[400,128]{1,0:T(8,128)(2,1)S(1)}, u32[]{:S(2)}, u32[]{:S(2)}) collective-permute-start(bf16[400,128]{1,0:T(8,128)(2,1)S(1)} %get-tuple-element.173), channel_id=1, source_target_pairs={{0,1},{1,0},{2,3},{3,2},{4,5},{5,4},{6,7},{7,6},{8,9},{9,8},{10,11... | collective-permute-start | bytes 307208 | tf_op jit(solution)/shard_map/ppermute | solution.py:58
  55.9 9.2 %collective-permute-start.17 = (bf16[400,128]{1,0:T(8,128)(2,1)S(1)}, bf16[400,128]{1,0:T(8,128)(2,1)S(1)}, u32[]{:S(2)}, u32[]{:S(2)}) collective-permute-start(bf16[400,128]{1,0:T(8,128)(2,1)S(1)} %sum_pair.13._), channel_id=1, source_target_pairs={{0,6},{2,8},{4,10},{6,12},{8,14},{10,0},{12,2},{14,4},{1,7},{3,9},... | collective-permute-start | bytes 307208 | tf_op jit(solution)/shard_map/ppermute | solution.py:49
  57.7 7.5 %collective-permute-start.18 = (bf16[400,128]{1,0:T(8,128)(2,1)S(1)}, bf16[400,128]{1,0:T(8,128)(2,1)S(1)}, u32[]{:S(2)}, u32[]{:S(2)}) collective-permute-start(bf16[400,128]{1,0:T(8,128)(2,1)S(1)} %get-tuple-element.179), channel_id=1, source_target_pairs={{0,1},{1,0},{2,3},{3,2},{4,5},{5,4},{6,7},{7,6},{8,9},{9,8},{10,11... | collective-permute-start | bytes 307208 | tf_op jit(solution)/shard_map/ppermute | solution.py:58
  65.3 1.5 %collective-permute-start.19 = (bf16[400,128]{1,0:T(8,128)(2,1)S(1)}, bf16[400,128]{1,0:T(8,128)(2,1)S(1)}, u32[]{:S(2)}, u32[]{:S(2)}) collective-permute-start(bf16[400,128]{1,0:T(8,128)(2,1)S(1)} %get-tuple-element.182.own0), channel_id=1, source_target_pairs={{0,1},{1,0},{2,3},{3,2},{4,5},{5,4},{6,7},{7,6},{8,9},{9,8},{10,11... | collective-permute-start | bytes 307208 | tf_op jit(solution)/shard_map/ppermute | solution.py:58
  65.3 7.0 %collective-permute-start.20 = (bf16[400,128]{1,0:T(8,128)(2,1)S(1)}, bf16[400,128]{1,0:T(8,128)(2,1)S(1)}, u32[]{:S(2)}, u32[]{:S(2)}) collective-permute-start(bf16[400,128]{1,0:T(8,128)(2,1)S(1)} %get-tuple-element.182.own0), channel_id=1, source_target_pairs={{0,8},{2,10},{4,12},{6,14},{8,0},{10,2},{12,4},{14,6},{1,9},{3,11}... | collective-permute-start | bytes 307208 | tf_op jit(solution)/shard_map/ppermute | solution.py:49
  72.4 1.3 collective-permute-start.21
  75.1 1.4 %collective-permute-start.22 = (bf16[400,128]{1,0:T(8,128)(2,1)S(1)}, bf16[400,128]{1,0:T(8,128)(2,1)S(1)}, u32[]{:S(2)}, u32[]{:S(2)}) collective-permute-start(bf16[400,128]{1,0:T(8,128)(2,1)S(1)} %get-tuple-element.191), channel_id=1, source_target_pairs={{0,1},{1,0},{2,3},{3,2},{4,5},{5,4},{6,7},{7,6},{8,9},{9,8},{10,11... | collective-permute-start | bytes 307208 | tf_op jit(solution)/shard_map/ppermute | solution.py:58
  76.5 8.0 %collective-permute-start.23 = (bf16[400,128]{1,0:T(8,128)(2,1)S(1)}, bf16[400,128]{1,0:T(8,128)(2,1)S(1)}, u32[]{:S(2)}, u32[]{:S(2)}) collective-permute-start(bf16[400,128]{1,0:T(8,128)(2,1)S(1)} %sum_pair.15._), channel_id=1, source_target_pairs={{0,8},{2,10},{4,12},{6,14},{8,0},{10,2},{12,4},{14,6},{1,9},{3,11}... | collective-permute-start | bytes 307208 | tf_op jit(solution)/shard_map/ppermute | solution.py:49
  78.0 6.5 %collective-permute-start.24 = (bf16[400,128]{1,0:T(8,128)(2,1)S(1)}, bf16[400,128]{1,0:T(8,128)(2,1)S(1)}, u32[]{:S(2)}, u32[]{:S(2)}) collective-permute-start(bf16[400,128]{1,0:T(8,128)(2,1)S(1)} %get-tuple-element.197), channel_id=1, source_target_pairs={{0,1},{1,0},{2,3},{3,2},{4,5},{5,4},{6,7},{7,6},{8,9},{9,8},{10,11... | collective-permute-start | bytes 307208 | tf_op jit(solution)/shard_map/ppermute | solution.py:58
  84.6 1.7 %collective-permute-start.26 = (bf16[400,128]{1,0:T(8,128)(2,1)S(1)}, bf16[400,128]{1,0:T(8,128)(2,1)S(1)}, u32[]{:S(2)}, u32[]{:S(2)}) collective-permute-start(bf16[400,128]{1,0:T(8,128)(2,1)S(1)} %get-tuple-element.200.own0), channel_id=1, source_target_pairs={{0,1},{1,0},{2,3},{3,2},{4,5},{5,4},{6,7},{7,6},{8,9},{9,8},{10,11... | collective-permute-start | bytes 307208 | tf_op jit(solution)/shard_map/ppermute | solution.py:58
  84.7 7.2 %collective-permute-start.25 = (bf16[400,128]{1,0:T(8,128)(2,1)S(1)}, bf16[400,128]{1,0:T(8,128)(2,1)S(1)}, u32[]{:S(2)}, u32[]{:S(2)}) collective-permute-start(bf16[400,128]{1,0:T(8,128)(2,1)S(1)} %get-tuple-element.200.own0), channel_id=1, source_target_pairs={{0,6},{2,8},{4,10},{6,12},{8,14},{10,0},{12,2},{14,4},{1,7},{3,9},... | collective-permute-start | bytes 307208 | tf_op jit(solution)/shard_map/ppermute | solution.py:49
  91.9 1.3 collective-permute-start.27
  95.7 2.3 %collective-permute-start.32 = (bf16[4,400,128]{2,1,0:T(8,128)(2,1)S(1)}, bf16[4,400,128]{2,1,0:T(8,128)(2,1)S(1)}, u32[]{:S(2)}, u32[]{:S(2)}) collective-permute-start(bf16[4,400,128]{2,1,0:T(8,128)(2,1)S(1)} %get-tuple-element.207._.refs_0_), channel_id=1, source_target_pairs={{0,1},{1,0},{2,3},{3,2},{4,5},{5,4},{6,7},{7,6},{8,9},{9,8},{10,11... | collective-permute-start | bytes 1228808 | tf_op jit(solution)/shard_map/ppermute | solution.py:58
  96.6 4.7 %collective-permute-start.31 = (bf16[4,400,128]{2,1,0:T(8,128)(2,1)S(1)}, bf16[4,400,128]{2,1,0:T(8,128)(2,1)S(1)}, u32[]{:S(2)}, u32[]{:S(2)}) collective-permute-start(bf16[4,400,128]{2,1,0:T(8,128)(2,1)S(1)} %get-tuple-element.217), channel_id=1, source_target_pairs={{0,1},{1,0},{2,3},{3,2},{4,5},{5,4},{6,7},{7,6},{8,9},{9,8},{10,11... | collective-permute-start | bytes 1228808 | tf_op jit(solution)/shard_map/ppermute | solution.py:58
  97.4 32.0 %copy-start = (f32[400,2048]{1,0:T(8,128)S(1)}, f32[400,2048]{1,0:T(8,128)}, u32[]{:S(2)}) copy-start(f32[400,2048]{1,0:T(8,128)} %rel_ref.7) | copy-start | bytes 9830404
  97.4 32.0 %copy-start.6 = (f32[2048]{0:T(1024)S(1)}, f32[2048]{0:T(1024)}, u32[]{:S(2)}) copy-start(f32[2048]{0:T(1024)} %param.12) | copy-start | bytes 24580
  97.4 2.8 %collective-permute-start.29 = (bf16[400,128]{1,0:T(8,128)(2,1)S(1)}, bf16[400,128]{1,0:T(8,128)(2,1)S(1)}, u32[]{:S(2)}, u32[]{:S(2)}) collective-permute-start(bf16[400,128]{1,0:T(8,128)(2,1)S(1)} %get-tuple-element.215), channel_id=1, source_target_pairs={{0,1},{1,0},{2,3},{3,2},{4,5},{5,4},{6,7},{7,6},{8,9},{9,8},{10,11... | collective-permute-start | bytes 307208 | tf_op jit(solution)/shard_map/ppermute | solution.py:58
  97.6 3.5 %collective-permute-start.28 = (bf16[400,128]{1,0:T(8,128)(2,1)S(1)}, bf16[400,128]{1,0:T(8,128)(2,1)S(1)}, u32[]{:S(2)}, u32[]{:S(2)}) collective-permute-start(bf16[400,128]{1,0:T(8,128)(2,1)S(1)} %get-tuple-element.213), channel_id=1, source_target_pairs={{0,1},{1,0},{2,3},{3,2},{4,5},{5,4},{6,7},{7,6},{8,9},{9,8},{10,11... | collective-permute-start | bytes 307208 | tf_op jit(solution)/shard_map/ppermute | solution.py:58
  98.1 6.2 %collective-permute-start.33 = (bf16[400,128]{1,0:T(8,128)(2,1)S(1)}, bf16[400,128]{1,0:T(8,128)(2,1)S(1)}, u32[]{:S(2)}, u32[]{:S(2)}) collective-permute-start(bf16[400,128]{1,0:T(8,128)(2,1)S(1)} %get-tuple-element.222), channel_id=1, source_target_pairs={{0,2},{2,0},{4,6},{6,4},{8,10},{10,8},{12,14},{14,12},{1,3},{3,1},... | collective-permute-start | bytes 307208 | tf_op jit(solution)/shard_map/ppermute | solution.py:54
  99.1 9.2 %collective-permute-start.37 = (bf16[400,128]{1,0:T(8,128)(2,1)S(1)}, bf16[400,128]{1,0:T(8,128)(2,1)S(1)}, u32[]{:S(2)}, u32[]{:S(2)}) collective-permute-start(bf16[400,128]{1,0:T(8,128)(2,1)S(1)} %get-tuple-element.228), channel_id=1, source_target_pairs={{0,2},{2,0},{4,6},{6,4},{8,10},{10,8},{12,14},{14,12},{1,3},{3,1},... | collective-permute-start | bytes 307208 | tf_op jit(solution)/shard_map/ppermute | solution.py:54
  100.2 10.3 %collective-permute-start.39 = (bf16[400,128]{1,0:T(8,128)(2,1)S(1)}, bf16[400,128]{1,0:T(8,128)(2,1)S(1)}, u32[]{:S(2)}, u32[]{:S(2)}) collective-permute-start(bf16[400,128]{1,0:T(8,128)(2,1)S(1)} %get-tuple-element.230), channel_id=1, source_target_pairs={{0,2},{2,0},{4,6},{6,4},{8,10},{10,8},{12,14},{14,12},{1,3},{3,1},... | collective-permute-start | bytes 307208 | tf_op jit(solution)/shard_map/ppermute | solution.py:54
  101.2 10.1 %collective-permute-start.30 = (bf16[400,128]{1,0:T(8,128)(2,1)S(1)}, bf16[400,128]{1,0:T(8,128)(2,1)S(1)}, u32[]{:S(2)}, u32[]{:S(2)}) collective-permute-start(bf16[400,128]{1,0:T(8,128)(2,1)S(1)} %sum_pair.17), channel_id=1, source_target_pairs={{0,10},{2,12},{4,14},{6,0},{8,2},{10,4},{12,6},{14,8},{1,11},{3,13... | collective-permute-start | bytes 307208 | tf_op jit(solution)/shard_map/ppermute | solution.py:49
  101.3 10.6 %collective-permute-start.35 = (bf16[400,128]{1,0:T(8,128)(2,1)S(1)}, bf16[400,128]{1,0:T(8,128)(2,1)S(1)}, u32[]{:S(2)}, u32[]{:S(2)}) collective-permute-start(bf16[400,128]{1,0:T(8,128)(2,1)S(1)} %get-tuple-element.226), channel_id=1, source_target_pairs={{0,2},{2,0},{4,6},{6,4},{8,10},{10,8},{12,14},{14,12},{1,3},{3,1},... | collective-permute-start | bytes 307208 | tf_op jit(solution)/shard_map/ppermute | solution.py:54
  104.4 7.5 %collective-permute-start.36 = (bf16[400,128]{1,0:T(8,128)(2,1)S(1)}, bf16[400,128]{1,0:T(8,128)(2,1)S(1)}, u32[]{:S(2)}, u32[]{:S(2)}) collective-permute-start(bf16[400,128]{1,0:T(8,128)(2,1)S(1)} %sum_piece.4.refs_5_), channel_id=1, source_target_pairs={{0,12},{2,14},{4,8},{6,10},{8,4},{10,6},{12,0},{14,2},{1,13},{3,15... | collective-permute-start | bytes 307208 | tf_op jit(solution)/shard_map/ppermute | solution.py:54
  108.3 8.3 %collective-permute-start.38 = (bf16[400,128]{1,0:T(8,128)(2,1)S(1)}, bf16[400,128]{1,0:T(8,128)(2,1)S(1)}, u32[]{:S(2)}, u32[]{:S(2)}) collective-permute-start(bf16[400,128]{1,0:T(8,128)(2,1)S(1)} %sum_piece.5), channel_id=1, source_target_pairs={{0,8},{2,10},{4,12},{6,14},{8,0},{10,2},{12,4},{14,6},{1,9},{3,11}... | collective-permute-start | bytes 307208 | tf_op jit(solution)/shard_map/ppermute | solution.py:54
  110.5 6.7 %collective-permute-start.40 = (bf16[400,128]{1,0:T(8,128)(2,1)S(1)}, bf16[400,128]{1,0:T(8,128)(2,1)S(1)}, u32[]{:S(2)}, u32[]{:S(2)}) collective-permute-start(bf16[400,128]{1,0:T(8,128)(2,1)S(1)} %sum_piece.6), channel_id=1, source_target_pairs={{0,4},{2,6},{4,0},{6,2},{8,12},{10,14},{12,8},{14,10},{1,5},{3,7},... | collective-permute-start | bytes 307208 | tf_op jit(solution)/shard_map/ppermute | solution.py:54
  111.3 19.1 %collective-permute-start.34 = (f32[408,128]{1,0:T(8,128)S(1)}, f32[408,128]{1,0:T(8,128)S(1)}, u32[]{:S(2)}, u32[]{:S(2)}) collective-permute-start(f32[408,128]{1,0:T(8,128)S(1)} %update.11.mine), channel_id=1, source_target_pairs={{0,1},{1,0},{2,3},{3,2},{4,5},{5,4},{6,7},{7,6},{8,9},{9,8},{10,11... | collective-permute-start | bytes 626696 | tf_op jit(solution)/shard_map/ppermute | solution.py:58
  117.3 4.9 %collective-permute-start.46 = (bf16[400,128]{1,0:T(8,128)(2,1)S(1)}, bf16[400,128]{1,0:T(8,128)(2,1)S(1)}, u32[]{:S(2)}, u32[]{:S(2)}) collective-permute-start(bf16[400,128]{1,0:T(8,128)(2,1)S(1)} %sum_piece.7.refs_0_), channel_id=1, source_target_pairs={{0,4},{2,6},{4,0},{6,2},{8,12},{10,14},{12,8},{14,10},{1,5},{3,7},... | collective-permute-start | bytes 307208 | tf_op jit(solution)/shard_map/ppermute | solution.py:54
  117.3 10.1 %collective-permute-start.44 = (bf16[400,128]{1,0:T(8,128)(2,1)S(1)}, bf16[400,128]{1,0:T(8,128)(2,1)S(1)}, u32[]{:S(2)}, u32[]{:S(2)}) collective-permute-start(bf16[400,128]{1,0:T(8,128)(2,1)S(1)} %sum_piece.7.refs_0_), channel_id=1, source_target_pairs={{0,8},{2,10},{4,12},{6,14},{8,0},{10,2},{12,4},{14,6},{1,9},{3,11}... | collective-permute-start | bytes 307208 | tf_op jit(solution)/shard_map/ppermute | solution.py:54
  120.0 8.0 %collective-permute-start.42 = (bf16[400,128]{1,0:T(8,128)(2,1)S(1)}, bf16[400,128]{1,0:T(8,128)(2,1)S(1)}, u32[]{:S(2)}, u32[]{:S(2)}) collective-permute-start(bf16[400,128]{1,0:T(8,128)(2,1)S(1)} %sum_piece.7.refs_0_), channel_id=1, source_target_pairs={{0,12},{2,14},{4,8},{6,10},{8,4},{10,6},{12,0},{14,2},{1,13},{3,15... | collective-permute-start | bytes 307208 | tf_op jit(solution)/shard_map/ppermute | solution.py:54
  121.7 9.7 %collective-permute-start.41 = (bf16[400,128]{1,0:T(8,128)(2,1)S(1)}, bf16[400,128]{1,0:T(8,128)(2,1)S(1)}, u32[]{:S(2)}, u32[]{:S(2)}) collective-permute-start(bf16[400,128]{1,0:T(8,128)(2,1)S(1)} %sum_piece.7.refs_0_), channel_id=1, source_target_pairs={{0,2},{2,0},{4,6},{6,4},{8,10},{10,8},{12,14},{14,12},{1,3},{3,1},... | collective-permute-start | bytes 307208 | tf_op jit(solution)/shard_map/ppermute | solution.py:54
  122.1 9.3 %collective-permute-start.47 = (bf16[400,128]{1,0:T(8,128)(2,1)S(1)}, bf16[400,128]{1,0:T(8,128)(2,1)S(1)}, u32[]{:S(2)}, u32[]{:S(2)}) collective-permute-start(bf16[400,128]{1,0:T(8,128)(2,1)S(1)} %collective-permute-done.46.refs_3_), channel_id=1, source_target_pairs={{0,2},{2,0},{4,6},{6,4},{8,10},{10,8},{12,14},{14,12},{1,3},{3,1},... | collective-permute-start | bytes 307208 | tf_op jit(solution)/shard_map/ppermute | solution.py:54
  127.4 4.7 %collective-permute-start.45 = (bf16[400,128]{1,0:T(8,128)(2,1)S(1)}, bf16[400,128]{1,0:T(8,128)(2,1)S(1)}, u32[]{:S(2)}, u32[]{:S(2)}) collective-permute-start(bf16[400,128]{1,0:T(8,128)(2,1)S(1)} %collective-permute-done.44.refs_2_), channel_id=1, source_target_pairs={{0,2},{2,0},{4,6},{6,4},{8,10},{10,8},{12,14},{14,12},{1,3},{3,1},... | collective-permute-start | bytes 307208 | tf_op jit(solution)/shard_map/ppermute | solution.py:54
  128.1 5.1 %collective-permute-start.43 = (bf16[400,128]{1,0:T(8,128)(2,1)S(1)}, bf16[400,128]{1,0:T(8,128)(2,1)S(1)}, u32[]{:S(2)}, u32[]{:S(2)}) collective-permute-start(bf16[400,128]{1,0:T(8,128)(2,1)S(1)} %collective-permute-done.42.refs_1_), channel_id=1, source_target_pairs={{0,2},{2,0},{4,6},{6,4},{8,10},{10,8},{12,14},{14,12},{1,3},{3,1},... | collective-permute-start | bytes 307208 | tf_op jit(solution)/shard_map/ppermute | solution.py:54
  131.3 1.9 %collective-permute-start.49 = (bf16[4,400,128]{2,1,0:T(8,128)(2,1)S(1)}, bf16[4,400,128]{2,1,0:T(8,128)(2,1)S(1)}, u32[]{:S(2)}, u32[]{:S(2)}) collective-permute-start(bf16[4,400,128]{2,1,0:T(8,128)(2,1)S(1)} %stacked.3), channel_id=1, source_target_pairs={{0,1},{1,0},{2,3},{3,2},{4,5},{5,4},{6,7},{7,6},{8,9},{9,8},{10,11... | collective-permute-start | bytes 1228808 | tf_op jit(solution)/shard_map/ppermute | solution.py:58
  133.2 1.8 %collective-permute-start.48 = (bf16[4,400,128]{2,1,0:T(8,128)(2,1)S(1)}, bf16[4,400,128]{2,1,0:T(8,128)(2,1)S(1)}, u32[]{:S(2)}, u32[]{:S(2)}) collective-permute-start(bf16[4,400,128]{2,1,0:T(8,128)(2,1)S(1)} %stacked.2), channel_id=1, source_target_pairs={{0,1},{1,0},{2,3},{3,2},{4,5},{5,4},{6,7},{7,6},{8,9},{9,8},{10,11... | collective-permute-start | bytes 1228808 | tf_op jit(solution)/shard_map/ppermute | solution.py:58

commit v4 on v3

--- a/solution.py
+++ b/solution.py
@@ -789,13 +789,17 @@
     theirs = across(other_s)
     down = range(nz - 1, -1, -1)
     from_x = {k: swapped(to_x[k], 1) for k in down}
-    turned = {
-        k: sum_piece(k, mine_s[k], theirs, [from_x[k]], grads[1:2] if k == nz - 1 else [])
-        for k in down[:-1]
-    }
-    from_z = [swapped(turned[k], 2 * k) for k in down[:-1]]
-    done = finish(grads, [turned[nz - 1]])
-    summed = sum_piece(0, mine_s[0], theirs, [from_x[0]] + from_z, [])
+    addends = {k: [from_x[k]] for k in range(nz)}
+    turned = []
+    bit = 1
+    while bit < nz:
+        for k in reversed(range(bit, nz, 2 * bit)):
+            after = [] if turned else grads[1:2]
+            turned.append(sum_piece(k, mine_s[k], theirs, addends[k], after))
+            addends[k ^ bit].append(swapped(turned[-1], 2 * bit))
+        bit *= 2
+    done = finish(grads, [turned[-1]])
+    summed = sum_piece(0, mine_s[0], theirs, addends[0], [])
     got = [summed if k == 0 else swapped(summed, 2 * k) for k in range(nz)]
     got_x = [swapped(piece, 1) for piece in got]
     state = state.reshape(1, rels)

time: 136 us -> 135 us (level)
  starting transfers between devices: 29.7 us -> 27.6 us
    ppermute x14, starting transfers between devices: 17.5 us -> 13.3 us  [swapped(): return lax.ppermute(x, 'dom', [(i, i ^ bits) for i in range(n)])]
    ppermute x10, starting transfers between devices: 7.52 us -> 9.95 us  [shifted(): return lax.ppermute(x, 'dom', [(i, (i + by) % n) for i in range(n)])]
  transfers between devices with their start and end apart: 50 -> 50, of which waited for: 27 -> 28; matrix products, arithmetic and copies ran while one was open for 0% -> 0% of each run, Pallas kernels for 20% -> 20%
where the time goes in v4:
time: 135 us
  waiting for transfers between devices  63.1 us (47%)
  Pallas kernels  42.5 us (31%)
  starting transfers between devices  27.6 us (20%)
  between operations  1.53 us (1%)
    ppermute x10, waiting for transfers between devices, shifted(): return lax.ppermute(x, 'dom', [(i, (i + by) % n) for i in range(n)])  36.4 us
    ppermute x14, waiting for transfers between devices, swapped(): return lax.ppermute(x, 'dom', [(i, i ^ bits) for i in range(n)])  15.5 us
    ppermute x14, starting transfers between devices, swapped(): return lax.ppermute(x, 'dom', [(i, i ^ bits) for i in range(n)])  13.3 us
    ppermute x26, waiting for transfers between devices, across(): return lax.ppermute(x, 'edge', [(0, 1), (1, 0)])  11.2 us
    ppermute x10, starting transfers between devices, shifted(): return lax.ppermute(x, 'dom', [(i, (i + by) % n) for i in range(n)])  9.95 us
    pallas_call x5, Pallas kernels, relsum(): pl.pallas_call(functools.partial(relsum_kernel, t, acc is None), in_specs...  6.22 us
    pallas_call x4, Pallas kernels, source_grad(): pl.pallas_call(functools.partial(source_grad_kernel, t, shape), in_specs=...  5.91 us
    pallas_call x4, Pallas kernels, target_grad(): pl.pallas_call(target_kernel, in_specs=[vmem()] * 8, out_specs=[vmem()] *...  5.5 us
  transfers between devices with their start and end apart: 50, of which 28 were waited for; matrix products, arithmetic and copies ran while one was open for 0% of the time, Pallas kernels for 20%

profile of v4, /device:TPU:0, one launch (start us, length us, event | category | flops | bytes accessed | tf_op | source)
XLA Modules:
  0.0 134.7 jit_solution(3379674794160820471)
XLA Ops:
  0.6 5.4 %first_round.1 = (f32[400,128]{1,0:T(8,128)S(1)}, bf16[400,128]{1,0:T(8,128)(2,1)S(1)}, bf16[400,512]{1,0:T(8,128)(2,1)S(1)}, bf16[400,2048]{1,0:T(8,128)(2,1)S(...) custom-call(s32[4,6]{1,0:T(4,128)} %bitcast.6, s32[4,6]{1,0:T(4,128)} %bitcast.17, s32[6,4,128]{2,1,0:T(4,128)} %src_ref.11, ...), custom_call_target="tpu_custom_call" | custom-call | flops 1258291200 | bytes 6553600 | tf_op jit(solution)/shard_map/first_round/pallas_call | solution.py:304
  6.6 0.9 collective-permute-done.refs_3_
  8.1 5.7 %collective-permute-start.2 = (bf16[400,128]{1,0:T(8,128)(2,1)S(1)}, bf16[400,128]{1,0:T(8,128)(2,1)S(1)}, u32[]{:S(2)}, u32[]{:S(2)}) collective-permute-start(bf16[400,128]{1,0:T(8,128)(2,1)S(1)} %get-tuple-element.127.own0), channel_id=1, source_target_pairs={{0,14},{2,0},{4,2},{6,4},{8,6},{10,8},{12,10},{14,12},{1,15},{3,1}... | collective-permute-start | bytes 307208 | tf_op jit(solution)/shard_map/ppermute | solution.py:49
  13.8 1.0 relvec.5.rel_ref
  14.8 1.0 relsum.5.refs_1_.refs_0_
  15.9 0.9 source_side.5
  17.3 1.0 collective-permute-done.3.far1
  18.2 1.4 %target_grad.4 = (f32[400,128]{1,0:T(8,128)S(1)}, bf16[400,128]{1,0:T(8,128)(2,1)S(1)}, bf16[128,512]{1,0:T(8,128)(2,1)S(1)}) custom-call(f32[512,128]{1,0:T(8,128)S(1)} %near_products.4.near, bf16[400,128]{1,0:T(8,128)(2,1)S(1)} %collective-permute-done.3.far1, bf16[400,512]{1,0:T(8,128)(2,1)S(1)} %get-tuple-element.130.refs_0_.query_ref, ...), custom_call_target="tpu_custom_call" | custom-call | flops 104857600 | bytes 2457600 | tf_op jit(solution)/shard_map/target_grad/pallas_call | solution.py:442
  19.9 1.2 collective-permute-done.4.b_ref
  21.1 1.5 %source_grad.4 = (f32[400,128]{1,0:T(8,128)S(1)}, bf16[400,128]{1,0:T(8,128)(2,1)S(1)}, bf16[400,512]{1,0:T(8,128)(2,1)S(1)}) custom-call(s32[4,6]{1,0:T(4,128)S(1)} %bitcast.8, s32[4,6]{1,0:T(4,128)S(1)} %bitcast.19, bf16[400,128]{1,0:T(8,128)(2,1)S(1)} %sum_pair.9._, bf16[400,128]{1,0:T(8,128)(2,1)S(1)} %held.5.far0, ...), custom_call_target="tpu_custom_call" | custom-call | flops 204800 | bytes 204800 | tf_op jit(solution)/shard_map/source_grad/pallas_call | solution.py:474
  22.8 1.0 relvec.6.refs_4_.rel_ref
  23.8 5.1 %collective-permute-done.5.b_ref = bf16[400,128]{1,0:T(8,128)(2,1)S(1)} collective-permute-done((bf16[400,128]{1,0:T(8,128)(2,1)S(1)}, bf16[400,128]{1,0:T(8,128)(2,1)S(1)}, u32[]{:S(2)}, u32[]{:S(2)}) %collective-permute-start.5) | collective-permute-done | bytes 102432 | tf_op jit(solution)/shard_map/ppermute | solution.py:49
  29.7 1.3 relsum.6.refs_1_.refs_0_
  31.0 0.9 source_side.6
  31.9 2.6 %collective-permute-done.8.x_ref = bf16[400,128]{1,0:T(8,128)(2,1)S(1)} collective-permute-done((bf16[400,128]{1,0:T(8,128)(2,1)S(1)}, bf16[400,128]{1,0:T(8,128)(2,1)S(1)}, u32[]{:S(2)}, u32[]{:S(2)}) %collective-permute-start.8) | collective-permute-done | bytes 102432 | tf_op jit(solution)/shard_map/ppermute | solution.py:49
  34.8 1.0 collective-permute-done.9.far1
  35.8 1.4 %target_grad.5 = (f32[400,128]{1,0:T(8,128)S(1)}, bf16[400,128]{1,0:T(8,128)(2,1)S(1)}, bf16[128,512]{1,0:T(8,128)(2,1)S(1)}) custom-call(f32[512,128]{1,0:T(8,128)S(1)} %near_products.5.near, bf16[400,128]{1,0:T(8,128)(2,1)S(1)} %collective-permute-done.9.far1, bf16[400,512]{1,0:T(8,128)(2,1)S(1)} %get-tuple-element.148.refs_0_.query_ref, ...), custom_call_target="tpu_custom_call" | custom-call | flops 104857600 | bytes 2457600 | tf_op jit(solution)/shard_map/target_grad/pallas_call | solution.py:442
  37.4 1.2 collective-permute-done.10.b_ref
  38.6 1.5 %source_grad.5 = (f32[400,128]{1,0:T(8,128)S(1)}, bf16[400,128]{1,0:T(8,128)(2,1)S(1)}, bf16[400,512]{1,0:T(8,128)(2,1)S(1)}) custom-call(s32[4,6]{1,0:T(4,128)S(1)} %bitcast.10, s32[4,6]{1,0:T(4,128)S(1)} %bitcast.21, bf16[400,128]{1,0:T(8,128)(2,1)S(1)} %sum_pair.11._, bf16[400,128]{1,0:T(8,128)(2,1)S(1)} %held.6.far0, ...), custom_call_target="tpu_custom_call" | custom-call | flops 204800 | bytes 204800 | tf_op jit(solution)/shard_map/source_grad/pallas_call | solution.py:474
  40.3 1.0 relvec.7.refs_4_.rel_ref
  41.4 4.0 %collective-permute-done.11.b_ref = bf16[400,128]{1,0:T(8,128)(2,1)S(1)} collective-permute-done((bf16[400,128]{1,0:T(8,128)(2,1)S(1)}, bf16[400,128]{1,0:T(8,128)(2,1)S(1)}, u32[]{:S(2)}, u32[]{:S(2)}) %collective-permute-start.11) | collective-permute-done | bytes 102432 | tf_op jit(solution)/shard_map/ppermute | solution.py:49
  46.1 1.3 relsum.7.refs_1_.refs_0_
  47.4 0.9 source_side.7
  48.3 3.5 %collective-permute-done.14.x_ref = bf16[400,128]{1,0:T(8,128)(2,1)S(1)} collective-permute-done((bf16[400,128]{1,0:T(8,128)(2,1)S(1)}, bf16[400,128]{1,0:T(8,128)(2,1)S(1)}, u32[]{:S(2)}, u32[]{:S(2)}) %collective-permute-start.14) | collective-permute-done | bytes 102432 | tf_op jit(solution)/shard_map/ppermute | solution.py:49
  52.1 1.0 collective-permute-done.15.far1
  53.1 1.4 %target_grad.6 = (f32[400,128]{1,0:T(8,128)S(1)}, bf16[400,128]{1,0:T(8,128)(2,1)S(1)}, bf16[128,512]{1,0:T(8,128)(2,1)S(1)}) custom-call(f32[512,128]{1,0:T(8,128)S(1)} %near_products.6.near, bf16[400,128]{1,0:T(8,128)(2,1)S(1)} %collective-permute-done.15.far1, bf16[400,512]{1,0:T(8,128)(2,1)S(1)} %get-tuple-element.166.refs_0_.query_ref, ...), custom_call_target="tpu_custom_call" | custom-call | flops 104857600 | bytes 2457600 | tf_op jit(solution)/shard_map/target_grad/pallas_call | solution.py:442
  54.7 1.2 collective-permute-done.16.b_ref
  56.2 1.5 %source_grad.6 = (f32[400,128]{1,0:T(8,128)S(1)}, bf16[400,128]{1,0:T(8,128)(2,1)S(1)}, bf16[400,512]{1,0:T(8,128)(2,1)S(1)}) custom-call(s32[4,6]{1,0:T(4,128)S(1)} %bitcast.12, s32[4,6]{1,0:T(4,128)S(1)} %bitcast.23, bf16[400,128]{1,0:T(8,128)(2,1)S(1)} %sum_pair.13._, bf16[400,128]{1,0:T(8,128)(2,1)S(1)} %held.7.far0, ...), custom_call_target="tpu_custom_call" | custom-call | flops 204800 | bytes 204800 | tf_op jit(solution)/shard_map/source_grad/pallas_call | solution.py:474
  57.9 1.0 relvec.8.refs_4_.rel_ref
  58.9 6.2 %collective-permute-done.17.b_ref = bf16[400,128]{1,0:T(8,128)(2,1)S(1)} collective-permute-done((bf16[400,128]{1,0:T(8,128)(2,1)S(1)}, bf16[400,128]{1,0:T(8,128)(2,1)S(1)}, u32[]{:S(2)}, u32[]{:S(2)}) %collective-permute-start.17) | collective-permute-done | bytes 102432 | tf_op jit(solution)/shard_map/ppermute | solution.py:49
  65.4 1.3 relsum.8.refs_1_.refs_0_
  66.7 0.9 source_side.8
  67.6 4.8 %collective-permute-done.20.x_ref = bf16[400,128]{1,0:T(8,128)(2,1)S(1)} collective-permute-done((bf16[400,128]{1,0:T(8,128)(2,1)S(1)}, bf16[400,128]{1,0:T(8,128)(2,1)S(1)}, u32[]{:S(2)}, u32[]{:S(2)}) %collective-permute-start.20) | collective-permute-done | bytes 102432 | tf_op jit(solution)/shard_map/ppermute | solution.py:49
  72.7 0.9 collective-permute-done.21.far1
  73.7 1.4 %target_grad.7 = (f32[400,128]{1,0:T(8,128)S(1)}, bf16[400,128]{1,0:T(8,128)(2,1)S(1)}, bf16[128,512]{1,0:T(8,128)(2,1)S(1)}) custom-call(f32[512,128]{1,0:T(8,128)S(1)} %near_products.7.near, bf16[400,128]{1,0:T(8,128)(2,1)S(1)} %collective-permute-done.21.far1, bf16[400,512]{1,0:T(8,128)(2,1)S(1)} %get-tuple-element.184.refs_0_.query_ref, ...), custom_call_target="tpu_custom_call" | custom-call | flops 104857600 | bytes 2457600 | tf_op jit(solution)/shard_map/target_grad/pallas_call | solution.py:442
  75.3 1.2 collective-permute-done.22.b_ref
  76.5 1.5 %source_grad.7 = (f32[400,128]{1,0:T(8,128)S(1)}, bf16[400,128]{1,0:T(8,128)(2,1)S(1)}, bf16[400,512]{1,0:T(8,128)(2,1)S(1)}) custom-call(s32[4,6]{1,0:T(4,128)S(1)} %bitcast.14, s32[4,6]{1,0:T(4,128)S(1)} %bitcast.25, bf16[400,128]{1,0:T(8,128)(2,1)S(1)} %sum_pair.15._, bf16[400,128]{1,0:T(8,128)(2,1)S(1)} %held.8.far0, ...), custom_call_target="tpu_custom_call" | custom-call | flops 204800 | bytes 204800 | tf_op jit(solution)/shard_map/source_grad/pallas_call | solution.py:474
  78.2 1.0 relvec.9.refs_4_.rel_ref
  79.3 5.2 %collective-permute-done.23.b_ref = bf16[400,128]{1,0:T(8,128)(2,1)S(1)} collective-permute-done((bf16[400,128]{1,0:T(8,128)(2,1)S(1)}, bf16[400,128]{1,0:T(8,128)(2,1)S(1)}, u32[]{:S(2)}, u32[]{:S(2)}) %collective-permute-start.23) | collective-permute-done | bytes 102432 | tf_op jit(solution)/shard_map/ppermute | solution.py:49
  85.0 1.3 relsum.9.refs_1_.acc_ref
  86.9 5.0 %collective-permute-done.25.x_ref = bf16[400,128]{1,0:T(8,128)(2,1)S(1)} collective-permute-done((bf16[400,128]{1,0:T(8,128)(2,1)S(1)}, bf16[400,128]{1,0:T(8,128)(2,1)S(1)}, u32[]{:S(2)}, u32[]{:S(2)}) %collective-permute-start.25) | collective-permute-done | bytes 102432 | tf_op jit(solution)/shard_map/ppermute | solution.py:49
  91.9 1.3 collective-permute-done.27.far1
  93.2 1.8 %last_terms.1 = (bf16[400,512]{1,0:T(8,128)(2,1)S(1)}, bf16[400,512]{1,0:T(8,128)(2,1)S(1)}, bf16[400,512]{1,0:T(8,128)(2,1)S(1)}) custom-call(s32[4,6]{1,0:T(4,128)S(1)} %bitcast.16, s32[4,6]{1,0:T(4,128)S(1)} %bitcast.27, bf16[400,128]{1,0:T(8,128)(2,1)S(1)} %held.9.far0, bf16[400,128]{1,0:T(8,128)(2,1)S(1)} %collective-permute-done.27.far1, ...), custom_call_target="tpu_custom_call" | custom-call | flops 157286400 | bytes 2457600 | tf_op jit(solution)/shard_map/last_terms/pallas_call | solution.py:504
  97.7 1.0 collective-permute-start.34
  98.8 1.1 collective-permute-start.33
  99.9 0.9 collective-permute-start.38
  100.8 2.6 %collective-permute-done.34.refs_0_ = bf16[400,128]{1,0:T(8,128)(2,1)S(1)} collective-permute-done((bf16[400,128]{1,0:T(8,128)(2,1)S(1)}, bf16[400,128]{1,0:T(8,128)(2,1)S(1)}, u32[]{:S(2)}, u32[]{:S(2)}) %collective-permute-start.34) | collective-permute-done | bytes 102432 | tf_op jit(solution)/shard_map/ppermute | solution.py:54
  103.6 2.5 %collective-permute-start.30 = (bf16[400,128]{1,0:T(8,128)(2,1)S(1)}, bf16[400,128]{1,0:T(8,128)(2,1)S(1)}, u32[]{:S(2)}, u32[]{:S(2)}) collective-permute-start(bf16[400,128]{1,0:T(8,128)(2,1)S(1)} %sum_pair.17), channel_id=1, source_target_pairs={{0,10},{2,12},{4,14},{6,0},{8,2},{10,4},{12,6},{14,8},{1,11},{3,13... | collective-permute-start | bytes 307208 | tf_op jit(solution)/shard_map/ppermute | solution.py:49
  106.2 1.5 %collective-permute-start.37 = (bf16[400,128]{1,0:T(8,128)(2,1)S(1)}, bf16[400,128]{1,0:T(8,128)(2,1)S(1)}, u32[]{:S(2)}, u32[]{:S(2)}) collective-permute-start(bf16[400,128]{1,0:T(8,128)(2,1)S(1)} %get-tuple-element.228), channel_id=1, source_target_pairs={{0,2},{2,0},{4,6},{6,4},{8,10},{10,8},{12,14},{14,12},{1,3},{3,1},... | collective-permute-start | bytes 307208 | tf_op jit(solution)/shard_map/ppermute | solution.py:54
  107.7 1.3 collective-permute-done.38.refs_0_
  109.2 1.8 %collective-permute-start.40 = (bf16[400,128]{1,0:T(8,128)(2,1)S(1)}, bf16[400,128]{1,0:T(8,128)(2,1)S(1)}, u32[]{:S(2)}, u32[]{:S(2)}) collective-permute-start(bf16[400,128]{1,0:T(8,128)(2,1)S(1)} %sum_piece.5.refs_5_), channel_id=1, source_target_pairs={{0,8},{2,10},{4,12},{6,14},{8,0},{10,2},{12,4},{14,6},{1,9},{3,11}... | collective-permute-start | bytes 307208 | tf_op jit(solution)/shard_map/ppermute | solution.py:54
  111.7 2.4 %collective-permute-done.39.refs_1_ = bf16[400,128]{1,0:T(8,128)(2,1)S(1)} collective-permute-done((bf16[400,128]{1,0:T(8,128)(2,1)S(1)}, bf16[400,128]{1,0:T(8,128)(2,1)S(1)}, u32[]{:S(2)}, u32[]{:S(2)}) %collective-permute-start.39) | collective-permute-done | bytes 102432 | tf_op jit(solution)/shard_map/ppermute | solution.py:54
  114.1 2.6 %collective-permute-done.40.refs_2_ = bf16[400,128]{1,0:T(8,128)(2,1)S(1)} collective-permute-done((bf16[400,128]{1,0:T(8,128)(2,1)S(1)}, bf16[400,128]{1,0:T(8,128)(2,1)S(1)}, u32[]{:S(2)}, u32[]{:S(2)}) %collective-permute-start.40) | collective-permute-done | bytes 102432 | tf_op jit(solution)/shard_map/ppermute | solution.py:54
  117.1 2.0 %collective-permute-start.44 = (bf16[400,128]{1,0:T(8,128)(2,1)S(1)}, bf16[400,128]{1,0:T(8,128)(2,1)S(1)}, u32[]{:S(2)}, u32[]{:S(2)}) collective-permute-start(bf16[400,128]{1,0:T(8,128)(2,1)S(1)} %sum_piece.7.refs_0_), channel_id=1, source_target_pairs={{0,8},{2,10},{4,12},{6,14},{8,0},{10,2},{12,4},{14,6},{1,9},{3,11}... | collective-permute-start | bytes 307208 | tf_op jit(solution)/shard_map/ppermute | solution.py:54
  119.0 2.2 %collective-permute-start.42 = (bf16[400,128]{1,0:T(8,128)(2,1)S(1)}, bf16[400,128]{1,0:T(8,128)(2,1)S(1)}, u32[]{:S(2)}, u32[]{:S(2)}) collective-permute-start(bf16[400,128]{1,0:T(8,128)(2,1)S(1)} %sum_piece.7.refs_0_), channel_id=1, source_target_pairs={{0,12},{2,14},{4,8},{6,10},{8,4},{10,6},{12,0},{14,2},{1,13},{3,15... | collective-permute-start | bytes 307208 | tf_op jit(solution)/shard_map/ppermute | solution.py:54
  121.5 1.7 %collective-permute-done.46.refs_3_ = bf16[400,128]{1,0:T(8,128)(2,1)S(1)} collective-permute-done((bf16[400,128]{1,0:T(8,128)(2,1)S(1)}, bf16[400,128]{1,0:T(8,128)(2,1)S(1)}, u32[]{:S(2)}, u32[]{:S(2)}) %collective-permute-start.46) | collective-permute-done | bytes 102432 | tf_op jit(solution)/shard_map/ppermute | solution.py:54
  123.2 2.6 %collective-permute-done.44.refs_2_ = bf16[400,128]{1,0:T(8,128)(2,1)S(1)} collective-permute-done((bf16[400,128]{1,0:T(8,128)(2,1)S(1)}, bf16[400,128]{1,0:T(8,128)(2,1)S(1)}, u32[]{:S(2)}, u32[]{:S(2)}) %collective-permute-start.44) | collective-permute-done | bytes 102432 | tf_op jit(solution)/shard_map/ppermute | solution.py:54
  125.9 0.7 collective-permute-start.45
  126.5 1.4 %collective-permute-start.43 = (bf16[400,128]{1,0:T(8,128)(2,1)S(1)}, bf16[400,128]{1,0:T(8,128)(2,1)S(1)}, u32[]{:S(2)}, u32[]{:S(2)}) collective-permute-start(bf16[400,128]{1,0:T(8,128)(2,1)S(1)} %collective-permute-done.42.refs_1_), channel_id=1, source_target_pairs={{0,2},{2,0},{4,6},{6,4},{8,10},{10,8},{12,14},{14,12},{1,3},{3,1},... | collective-permute-start | bytes 307208 | tf_op jit(solution)/shard_map/ppermute | solution.py:54
  127.9 1.0 relnew.3
  129.0 0.8 whole_partition.1
  130.5 1.1 collective-permute-done.43.refs_1_.refs_2_
  131.7 1.4 %relnew.4 = (f32[400,2048]{1,0:T(8,128)}, f32[1,2048]{1,0:T(1,128)S(1)}) custom-call(f32[400,2048]{1,0:T(8,128)S(1)} %copy-done, f32[1,2048]{1,0:T(1,128)S(1)} %bitcast.30, bf16[4,400,128]{2,1,0:T(8,128)(2,1)S(1)} %collective-permute-done.49.refs_0_, bf16[400,128]{1,0:T(8,128)(2,1)S(1)} %collective-permute-done.41.refs_0_.refs_1_, ...), custom_call_target="tpu_custom_call", output_to_operand_aliasing={{0}: (7, {})} | custom-call | flops 400 | bytes 400 | tf_op jit(solution)/shard_map/relnew/pallas_call | solution.py:761
  133.5 1.0 relnew.5
  (113 shorter events, 13.1 us)
Async XLA Ops:
  0.6 13.2 %copy-start.1 = (s32[6,4,128]{2,1,0:T(4,128)S(1)}, s32[6,4,128]{2,1,0:T(4,128)}, u32[]{:S(2)}) copy-start(s32[6,4,128]{2,1,0:T(4,128)} %ids_ref.25) | copy-start | bytes 36868
  6.1 9.8 %copy-start.2 = (s32[6,4,128]{2,1,0:T(4,128)S(1)}, s32[6,4,128]{2,1,0:T(4,128)}, u32[]{:S(2)}) copy-start(s32[6,4,128]{2,1,0:T(4,128)} %src_ref.11) | copy-start | bytes 36868
  6.1 9.8 %copy-start.3 = (s32[6,4,128]{2,1,0:T(4,128)S(1)}, s32[6,4,128]{2,1,0:T(4,128)}, u32[]{:S(2)}) copy-start(s32[6,4,128]{2,1,0:T(4,128)} %dst_ref.11) | copy-start | bytes 36868
  6.1 9.8 %copy-start.4 = (s32[6,4]{0,1:T(4,128)S(1)}, s32[6,4]{0,1:T(4,128)}, u32[]{:S(2)}) copy-start(s32[6,4]{0,1:T(4,128)} %param.16) | copy-start | bytes 292
  6.1 9.8 %copy-start.5 = (s32[6,4]{0,1:T(4,128)S(1)}, s32[6,4]{0,1:T(4,128)}, u32[]{:S(2)}) copy-start(s32[6,4]{0,1:T(4,128)} %param.17) | copy-start | bytes 292
  6.1 1.5 %collective-permute-start = (bf16[400,128]{1,0:T(8,128)(2,1)S(1)}, bf16[400,128]{1,0:T(8,128)(2,1)S(1)}, u32[]{:S(2)}, u32[]{:S(2)}) collective-permute-start(bf16[400,128]{1,0:T(8,128)(2,1)S(1)} %get-tuple-element.124), channel_id=1, source_target_pairs={{0,1},{1,0},{2,3},{3,2},{4,5},{5,4},{6,7},{7,6},{8,9},{9,8},{10,11... | collective-permute-start | bytes 307208 | tf_op jit(solution)/shard_map/ppermute | solution.py:58
  7.7 8.2 %collective-permute-start.1 = (bf16[400,128]{1,0:T(8,128)(2,1)S(1)}, bf16[400,128]{1,0:T(8,128)(2,1)S(1)}, u32[]{:S(2)}, u32[]{:S(2)}) collective-permute-start(bf16[400,128]{1,0:T(8,128)(2,1)S(1)} %get-tuple-element.127.own0), channel_id=1, source_target_pairs={{0,1},{1,0},{2,3},{3,2},{4,5},{5,4},{6,7},{7,6},{8,9},{9,8},{10,11... | collective-permute-start | bytes 307208 | tf_op jit(solution)/shard_map/ppermute | solution.py:58
  8.1 8.7 %collective-permute-start.2 = (bf16[400,128]{1,0:T(8,128)(2,1)S(1)}, bf16[400,128]{1,0:T(8,128)(2,1)S(1)}, u32[]{:S(2)}, u32[]{:S(2)}) collective-permute-start(bf16[400,128]{1,0:T(8,128)(2,1)S(1)} %get-tuple-element.127.own0), channel_id=1, source_target_pairs={{0,14},{2,0},{4,2},{6,4},{8,6},{10,8},{12,10},{14,12},{1,15},{3,1}... | collective-permute-start | bytes 307208 | tf_op jit(solution)/shard_map/ppermute | solution.py:49
  16.9 1.4 %collective-permute-start.3 = (bf16[400,128]{1,0:T(8,128)(2,1)S(1)}, bf16[400,128]{1,0:T(8,128)(2,1)S(1)}, u32[]{:S(2)}, u32[]{:S(2)}) collective-permute-start(bf16[400,128]{1,0:T(8,128)(2,1)S(1)} %held.5.far0), channel_id=1, source_target_pairs={{0,1},{1,0},{2,3},{3,2},{4,5},{5,4},{6,7},{7,6},{8,9},{9,8},{10,11... | collective-permute-start | bytes 307208 | tf_op jit(solution)/shard_map/ppermute | solution.py:58
  19.6 1.4 %collective-permute-start.4 = (bf16[400,128]{1,0:T(8,128)(2,1)S(1)}, bf16[400,128]{1,0:T(8,128)(2,1)S(1)}, u32[]{:S(2)}, u32[]{:S(2)}) collective-permute-start(bf16[400,128]{1,0:T(8,128)(2,1)S(1)} %get-tuple-element.137), channel_id=1, source_target_pairs={{0,1},{1,0},{2,3},{3,2},{4,5},{5,4},{6,7},{7,6},{8,9},{9,8},{10,11... | collective-permute-start | bytes 307208 | tf_op jit(solution)/shard_map/ppermute | solution.py:58
  21.0 7.9 %collective-permute-start.5 = (bf16[400,128]{1,0:T(8,128)(2,1)S(1)}, bf16[400,128]{1,0:T(8,128)(2,1)S(1)}, u32[]{:S(2)}, u32[]{:S(2)}) collective-permute-start(bf16[400,128]{1,0:T(8,128)(2,1)S(1)} %sum_pair.9._), channel_id=1, source_target_pairs={{0,2},{2,4},{4,6},{6,8},{8,10},{10,12},{12,14},{14,0},{1,3},{3,5},... | collective-permute-start | bytes 307208 | tf_op jit(solution)/shard_map/ppermute | solution.py:49
  22.6 6.4 %collective-permute-start.6 = (bf16[400,128]{1,0:T(8,128)(2,1)S(1)}, bf16[400,128]{1,0:T(8,128)(2,1)S(1)}, u32[]{:S(2)}, u32[]{:S(2)}) collective-permute-start(bf16[400,128]{1,0:T(8,128)(2,1)S(1)} %get-tuple-element.143), channel_id=1, source_target_pairs={{0,1},{1,0},{2,3},{3,2},{4,5},{5,4},{6,7},{7,6},{8,9},{9,8},{10,11... | collective-permute-start | bytes 307208 | tf_op jit(solution)/shard_map/ppermute | solution.py:58
  29.1 1.8 %collective-permute-start.7 = (bf16[400,128]{1,0:T(8,128)(2,1)S(1)}, bf16[400,128]{1,0:T(8,128)(2,1)S(1)}, u32[]{:S(2)}, u32[]{:S(2)}) collective-permute-start(bf16[400,128]{1,0:T(8,128)(2,1)S(1)} %get-tuple-element.146.own0), channel_id=1, source_target_pairs={{0,1},{1,0},{2,3},{3,2},{4,5},{5,4},{6,7},{7,6},{8,9},{9,8},{10,11... | collective-permute-start | bytes 307208 | tf_op jit(solution)/shard_map/ppermute | solution.py:58
  29.2 5.3 %collective-permute-start.8 = (bf16[400,128]{1,0:T(8,128)(2,1)S(1)}, bf16[400,128]{1,0:T(8,128)(2,1)S(1)}, u32[]{:S(2)}, u32[]{:S(2)}) collective-permute-start(bf16[400,128]{1,0:T(8,128)(2,1)S(1)} %get-tuple-element.146.own0), channel_id=1, source_target_pairs={{0,12},{2,14},{4,0},{6,2},{8,4},{10,6},{12,8},{14,10},{1,13},{3,15... | collective-permute-start | bytes 307208 | tf_op jit(solution)/shard_map/ppermute | solution.py:49
  34.5 1.3 collective-permute-start.9
  37.2 1.4 %collective-permute-start.10 = (bf16[400,128]{1,0:T(8,128)(2,1)S(1)}, bf16[400,128]{1,0:T(8,128)(2,1)S(1)}, u32[]{:S(2)}, u32[]{:S(2)}) collective-permute-start(bf16[400,128]{1,0:T(8,128)(2,1)S(1)} %get-tuple-element.155), channel_id=1, source_target_pairs={{0,1},{1,0},{2,3},{3,2},{4,5},{5,4},{6,7},{7,6},{8,9},{9,8},{10,11... | collective-permute-start | bytes 307208 | tf_op jit(solution)/shard_map/ppermute | solution.py:58
  38.6 6.8 %collective-permute-start.11 = (bf16[400,128]{1,0:T(8,128)(2,1)S(1)}, bf16[400,128]{1,0:T(8,128)(2,1)S(1)}, u32[]{:S(2)}, u32[]{:S(2)}) collective-permute-start(bf16[400,128]{1,0:T(8,128)(2,1)S(1)} %sum_pair.11._), channel_id=1, source_target_pairs={{0,4},{2,6},{4,8},{6,10},{8,12},{10,14},{12,0},{14,2},{1,5},{3,7},... | collective-permute-start | bytes 307208 | tf_op jit(solution)/shard_map/ppermute | solution.py:49
  40.1 5.3 %collective-permute-start.12 = (bf16[400,128]{1,0:T(8,128)(2,1)S(1)}, bf16[400,128]{1,0:T(8,128)(2,1)S(1)}, u32[]{:S(2)}, u32[]{:S(2)}) collective-permute-start(bf16[400,128]{1,0:T(8,128)(2,1)S(1)} %get-tuple-element.161), channel_id=1, source_target_pairs={{0,1},{1,0},{2,3},{3,2},{4,5},{5,4},{6,7},{7,6},{8,9},{9,8},{10,11... | collective-permute-start | bytes 307208 | tf_op jit(solution)/shard_map/ppermute | solution.py:58
  45.5 1.8 %collective-permute-start.13 = (bf16[400,128]{1,0:T(8,128)(2,1)S(1)}, bf16[400,128]{1,0:T(8,128)(2,1)S(1)}, u32[]{:S(2)}, u32[]{:S(2)}) collective-permute-start(bf16[400,128]{1,0:T(8,128)(2,1)S(1)} %get-tuple-element.164.own0), channel_id=1, source_target_pairs={{0,1},{1,0},{2,3},{3,2},{4,5},{5,4},{6,7},{7,6},{8,9},{9,8},{10,11... | collective-permute-start | bytes 307208 | tf_op jit(solution)/shard_map/ppermute | solution.py:58
  45.6 6.2 %collective-permute-start.14 = (bf16[400,128]{1,0:T(8,128)(2,1)S(1)}, bf16[400,128]{1,0:T(8,128)(2,1)S(1)}, u32[]{:S(2)}, u32[]{:S(2)}) collective-permute-start(bf16[400,128]{1,0:T(8,128)(2,1)S(1)} %get-tuple-element.164.own0), channel_id=1, source_target_pairs={{0,10},{2,12},{4,14},{6,0},{8,2},{10,4},{12,6},{14,8},{1,11},{3,13... | collective-permute-start | bytes 307208 | tf_op jit(solution)/shard_map/ppermute | solution.py:49
  51.8 1.3 collective-permute-start.15
  54.5 1.4 %collective-permute-start.16 = (bf16[400,128]{1,0:T(8,128)(2,1)S(1)}, bf16[400,128]{1,0:T(8,128)(2,1)S(1)}, u32[]{:S(2)}, u32[]{:S(2)}) collective-permute-start(bf16[400,128]{1,0:T(8,128)(2,1)S(1)} %get-tuple-element.173), channel_id=1, source_target_pairs={{0,1},{1,0},{2,3},{3,2},{4,5},{5,4},{6,7},{7,6},{8,9},{9,8},{10,11... | collective-permute-start | bytes 307208 | tf_op jit(solution)/shard_map/ppermute | solution.py:58
  55.9 9.2 %collective-permute-start.17 = (bf16[400,128]{1,0:T(8,128)(2,1)S(1)}, bf16[400,128]{1,0:T(8,128)(2,1)S(1)}, u32[]{:S(2)}, u32[]{:S(2)}) collective-permute-start(bf16[400,128]{1,0:T(8,128)(2,1)S(1)} %sum_pair.13._), channel_id=1, source_target_pairs={{0,6},{2,8},{4,10},{6,12},{8,14},{10,0},{12,2},{14,4},{1,7},{3,9},... | collective-permute-start | bytes 307208 | tf_op jit(solution)/shard_map/ppermute | solution.py:49
  57.7 7.5 %collective-permute-start.18 = (bf16[400,128]{1,0:T(8,128)(2,1)S(1)}, bf16[400,128]{1,0:T(8,128)(2,1)S(1)}, u32[]{:S(2)}, u32[]{:S(2)}) collective-permute-start(bf16[400,128]{1,0:T(8,128)(2,1)S(1)} %get-tuple-element.179), channel_id=1, source_target_pairs={{0,1},{1,0},{2,3},{3,2},{4,5},{5,4},{6,7},{7,6},{8,9},{9,8},{10,11... | collective-permute-start | bytes 307208 | tf_op jit(solution)/shard_map/ppermute | solution.py:58
  65.3 1.5 %collective-permute-start.19 = (bf16[400,128]{1,0:T(8,128)(2,1)S(1)}, bf16[400,128]{1,0:T(8,128)(2,1)S(1)}, u32[]{:S(2)}, u32[]{:S(2)}) collective-permute-start(bf16[400,128]{1,0:T(8,128)(2,1)S(1)} %get-tuple-element.182.own0), channel_id=1, source_target_pairs={{0,1},{1,0},{2,3},{3,2},{4,5},{5,4},{6,7},{7,6},{8,9},{9,8},{10,11... | collective-permute-start | bytes 307208 | tf_op jit(solution)/shard_map/ppermute | solution.py:58
  65.3 7.0 %collective-permute-start.20 = (bf16[400,128]{1,0:T(8,128)(2,1)S(1)}, bf16[400,128]{1,0:T(8,128)(2,1)S(1)}, u32[]{:S(2)}, u32[]{:S(2)}) collective-permute-start(bf16[400,128]{1,0:T(8,128)(2,1)S(1)} %get-tuple-element.182.own0), channel_id=1, source_target_pairs={{0,8},{2,10},{4,12},{6,14},{8,0},{10,2},{12,4},{14,6},{1,9},{3,11}... | collective-permute-start | bytes 307208 | tf_op jit(solution)/shard_map/ppermute | solution.py:49
  72.4 1.3 collective-permute-start.21
  75.1 1.4 %collective-permute-start.22 = (bf16[400,128]{1,0:T(8,128)(2,1)S(1)}, bf16[400,128]{1,0:T(8,128)(2,1)S(1)}, u32[]{:S(2)}, u32[]{:S(2)}) collective-permute-start(bf16[400,128]{1,0:T(8,128)(2,1)S(1)} %get-tuple-element.191), channel_id=1, source_target_pairs={{0,1},{1,0},{2,3},{3,2},{4,5},{5,4},{6,7},{7,6},{8,9},{9,8},{10,11... | collective-permute-start | bytes 307208 | tf_op jit(solution)/shard_map/ppermute | solution.py:58
  76.5 8.0 %collective-permute-start.23 = (bf16[400,128]{1,0:T(8,128)(2,1)S(1)}, bf16[400,128]{1,0:T(8,128)(2,1)S(1)}, u32[]{:S(2)}, u32[]{:S(2)}) collective-permute-start(bf16[400,128]{1,0:T(8,128)(2,1)S(1)} %sum_pair.15._), channel_id=1, source_target_pairs={{0,8},{2,10},{4,12},{6,14},{8,0},{10,2},{12,4},{14,6},{1,9},{3,11}... | collective-permute-start | bytes 307208 | tf_op jit(solution)/shard_map/ppermute | solution.py:49
  78.0 6.4 %collective-permute-start.24 = (bf16[400,128]{1,0:T(8,128)(2,1)S(1)}, bf16[400,128]{1,0:T(8,128)(2,1)S(1)}, u32[]{:S(2)}, u32[]{:S(2)}) collective-permute-start(bf16[400,128]{1,0:T(8,128)(2,1)S(1)} %get-tuple-element.197), channel_id=1, source_target_pairs={{0,1},{1,0},{2,3},{3,2},{4,5},{5,4},{6,7},{7,6},{8,9},{9,8},{10,11... | collective-permute-start | bytes 307208 | tf_op jit(solution)/shard_map/ppermute | solution.py:58
  84.6 1.7 %collective-permute-start.26 = (bf16[400,128]{1,0:T(8,128)(2,1)S(1)}, bf16[400,128]{1,0:T(8,128)(2,1)S(1)}, u32[]{:S(2)}, u32[]{:S(2)}) collective-permute-start(bf16[400,128]{1,0:T(8,128)(2,1)S(1)} %get-tuple-element.200.own0), channel_id=1, source_target_pairs={{0,1},{1,0},{2,3},{3,2},{4,5},{5,4},{6,7},{7,6},{8,9},{9,8},{10,11... | collective-permute-start | bytes 307208 | tf_op jit(solution)/shard_map/ppermute | solution.py:58
  84.7 7.2 %collective-permute-start.25 = (bf16[400,128]{1,0:T(8,128)(2,1)S(1)}, bf16[400,128]{1,0:T(8,128)(2,1)S(1)}, u32[]{:S(2)}, u32[]{:S(2)}) collective-permute-start(bf16[400,128]{1,0:T(8,128)(2,1)S(1)} %get-tuple-element.200.own0), channel_id=1, source_target_pairs={{0,6},{2,8},{4,10},{6,12},{8,14},{10,0},{12,2},{14,4},{1,7},{3,9},... | collective-permute-start | bytes 307208 | tf_op jit(solution)/shard_map/ppermute | solution.py:49
  91.9 1.3 collective-permute-start.27
  95.7 1.9 %collective-permute-start.32 = (bf16[4,400,128]{2,1,0:T(8,128)(2,1)S(1)}, bf16[4,400,128]{2,1,0:T(8,128)(2,1)S(1)}, u32[]{:S(2)}, u32[]{:S(2)}) collective-permute-start(bf16[4,400,128]{2,1,0:T(8,128)(2,1)S(1)} %get-tuple-element.207._.refs_0_), channel_id=1, source_target_pairs={{0,1},{1,0},{2,3},{3,2},{4,5},{5,4},{6,7},{7,6},{8,9},{9,8},{10,11... | collective-permute-start | bytes 1228808 | tf_op jit(solution)/shard_map/ppermute | solution.py:58
  96.6 4.3 %collective-permute-start.31 = (bf16[4,400,128]{2,1,0:T(8,128)(2,1)S(1)}, bf16[4,400,128]{2,1,0:T(8,128)(2,1)S(1)}, u32[]{:S(2)}, u32[]{:S(2)}) collective-permute-start(bf16[4,400,128]{2,1,0:T(8,128)(2,1)S(1)} %get-tuple-element.217), channel_id=1, source_target_pairs={{0,1},{1,0},{2,3},{3,2},{4,5},{5,4},{6,7},{7,6},{8,9},{9,8},{10,11... | collective-permute-start | bytes 1228808 | tf_op jit(solution)/shard_map/ppermute | solution.py:58
  97.4 30.5 %copy-start = (f32[400,2048]{1,0:T(8,128)S(1)}, f32[400,2048]{1,0:T(8,128)}, u32[]{:S(2)}) copy-start(f32[400,2048]{1,0:T(8,128)} %rel_ref.7) | copy-start | bytes 9830404
  97.4 30.5 %copy-start.6 = (f32[2048]{0:T(1024)S(1)}, f32[2048]{0:T(1024)}, u32[]{:S(2)}) copy-start(f32[2048]{0:T(1024)} %param.12) | copy-start | bytes 24580
  97.4 2.5 %collective-permute-start.28 = (bf16[400,128]{1,0:T(8,128)(2,1)S(1)}, bf16[400,128]{1,0:T(8,128)(2,1)S(1)}, u32[]{:S(2)}, u32[]{:S(2)}) collective-permute-start(bf16[400,128]{1,0:T(8,128)(2,1)S(1)} %get-tuple-element.213), channel_id=1, source_target_pairs={{0,1},{1,0},{2,3},{3,2},{4,5},{5,4},{6,7},{7,6},{8,9},{9,8},{10,11... | collective-permute-start | bytes 307208 | tf_op jit(solution)/shard_map/ppermute | solution.py:58
  97.7 5.8 %collective-permute-start.34 = (bf16[400,128]{1,0:T(8,128)(2,1)S(1)}, bf16[400,128]{1,0:T(8,128)(2,1)S(1)}, u32[]{:S(2)}, u32[]{:S(2)}) collective-permute-start(bf16[400,128]{1,0:T(8,128)(2,1)S(1)} %get-tuple-element.224), channel_id=1, source_target_pairs={{0,2},{2,0},{4,6},{6,4},{8,10},{10,8},{12,14},{14,12},{1,3},{3,1},... | collective-permute-start | bytes 307208 | tf_op jit(solution)/shard_map/ppermute | solution.py:54
  98.7 4.9 %collective-permute-start.29 = (bf16[400,128]{1,0:T(8,128)(2,1)S(1)}, bf16[400,128]{1,0:T(8,128)(2,1)S(1)}, u32[]{:S(2)}, u32[]{:S(2)}) collective-permute-start(bf16[400,128]{1,0:T(8,128)(2,1)S(1)} %get-tuple-element.215), channel_id=1, source_target_pairs={{0,1},{1,0},{2,3},{3,2},{4,5},{5,4},{6,7},{7,6},{8,9},{9,8},{10,11... | collective-permute-start | bytes 307208 | tf_op jit(solution)/shard_map/ppermute | solution.py:58
  98.8 10.3 %collective-permute-start.33 = (bf16[400,128]{1,0:T(8,128)(2,1)S(1)}, bf16[400,128]{1,0:T(8,128)(2,1)S(1)}, u32[]{:S(2)}, u32[]{:S(2)}) collective-permute-start(bf16[400,128]{1,0:T(8,128)(2,1)S(1)} %get-tuple-element.222), channel_id=1, source_target_pairs={{0,2},{2,0},{4,6},{6,4},{8,10},{10,8},{12,14},{14,12},{1,3},{3,1},... | collective-permute-start | bytes 307208 | tf_op jit(solution)/shard_map/ppermute | solution.py:54
  99.9 9.1 %collective-permute-start.38 = (bf16[400,128]{1,0:T(8,128)(2,1)S(1)}, bf16[400,128]{1,0:T(8,128)(2,1)S(1)}, u32[]{:S(2)}, u32[]{:S(2)}) collective-permute-start(bf16[400,128]{1,0:T(8,128)(2,1)S(1)} %get-tuple-element.230), channel_id=1, source_target_pairs={{0,2},{2,0},{4,6},{6,4},{8,10},{10,8},{12,14},{14,12},{1,3},{3,1},... | collective-permute-start | bytes 307208 | tf_op jit(solution)/shard_map/ppermute | solution.py:54
  103.5 5.6 %collective-permute-start.35 = (bf16[400,128]{1,0:T(8,128)(2,1)S(1)}, bf16[400,128]{1,0:T(8,128)(2,1)S(1)}, u32[]{:S(2)}, u32[]{:S(2)}) collective-permute-start(bf16[400,128]{1,0:T(8,128)(2,1)S(1)} %sum_piece.4), channel_id=1, source_target_pairs={{0,4},{2,6},{4,0},{6,2},{8,12},{10,14},{12,8},{14,10},{1,5},{3,7},... | collective-permute-start | bytes 307208 | tf_op jit(solution)/shard_map/ppermute | solution.py:54
  103.6 7.3 %collective-permute-start.30 = (bf16[400,128]{1,0:T(8,128)(2,1)S(1)}, bf16[400,128]{1,0:T(8,128)(2,1)S(1)}, u32[]{:S(2)}, u32[]{:S(2)}) collective-permute-start(bf16[400,128]{1,0:T(8,128)(2,1)S(1)} %sum_pair.17), channel_id=1, source_target_pairs={{0,10},{2,12},{4,14},{6,0},{8,2},{10,4},{12,6},{14,8},{1,11},{3,13... | collective-permute-start | bytes 307208 | tf_op jit(solution)/shard_map/ppermute | solution.py:49
  106.2 5.5 %collective-permute-start.37 = (bf16[400,128]{1,0:T(8,128)(2,1)S(1)}, bf16[400,128]{1,0:T(8,128)(2,1)S(1)}, u32[]{:S(2)}, u32[]{:S(2)}) collective-permute-start(bf16[400,128]{1,0:T(8,128)(2,1)S(1)} %get-tuple-element.228), channel_id=1, source_target_pairs={{0,2},{2,0},{4,6},{6,4},{8,10},{10,8},{12,14},{14,12},{1,3},{3,1},... | collective-permute-start | bytes 307208 | tf_op jit(solution)/shard_map/ppermute | solution.py:54
  109.0 5.1 %collective-permute-start.39 = (bf16[400,128]{1,0:T(8,128)(2,1)S(1)}, bf16[400,128]{1,0:T(8,128)(2,1)S(1)}, u32[]{:S(2)}, u32[]{:S(2)}) collective-permute-start(bf16[400,128]{1,0:T(8,128)(2,1)S(1)} %sum_piece.6), channel_id=1, source_target_pairs={{0,4},{2,6},{4,0},{6,2},{8,12},{10,14},{12,8},{14,10},{1,5},{3,7},... | collective-permute-start | bytes 307208 | tf_op jit(solution)/shard_map/ppermute | solution.py:54
  109.2 7.5 %collective-permute-start.40 = (bf16[400,128]{1,0:T(8,128)(2,1)S(1)}, bf16[400,128]{1,0:T(8,128)(2,1)S(1)}, u32[]{:S(2)}, u32[]{:S(2)}) collective-permute-start(bf16[400,128]{1,0:T(8,128)(2,1)S(1)} %sum_piece.5.refs_5_), channel_id=1, source_target_pairs={{0,8},{2,10},{4,12},{6,14},{8,0},{10,2},{12,4},{14,6},{1,9},{3,11}... | collective-permute-start | bytes 307208 | tf_op jit(solution)/shard_map/ppermute | solution.py:54
  111.1 17.9 %collective-permute-start.36 = (f32[408,128]{1,0:T(8,128)S(1)}, f32[408,128]{1,0:T(8,128)S(1)}, u32[]{:S(2)}, u32[]{:S(2)}) collective-permute-start(f32[408,128]{1,0:T(8,128)S(1)} %update.11.mine), channel_id=1, source_target_pairs={{0,1},{1,0},{2,3},{3,2},{4,5},{5,4},{6,7},{7,6},{8,9},{9,8},{10,11... | collective-permute-start | bytes 626696 | tf_op jit(solution)/shard_map/ppermute | solution.py:58
  116.8 6.4 %collective-permute-start.46 = (bf16[400,128]{1,0:T(8,128)(2,1)S(1)}, bf16[400,128]{1,0:T(8,128)(2,1)S(1)}, u32[]{:S(2)}, u32[]{:S(2)}) collective-permute-start(bf16[400,128]{1,0:T(8,128)(2,1)S(1)} %sum_piece.7.refs_0_), channel_id=1, source_target_pairs={{0,4},{2,6},{4,0},{6,2},{8,12},{10,14},{12,8},{14,10},{1,5},{3,7},... | collective-permute-start | bytes 307208 | tf_op jit(solution)/shard_map/ppermute | solution.py:54
  117.1 8.8 %collective-permute-start.44 = (bf16[400,128]{1,0:T(8,128)(2,1)S(1)}, bf16[400,128]{1,0:T(8,128)(2,1)S(1)}, u32[]{:S(2)}, u32[]{:S(2)}) collective-permute-start(bf16[400,128]{1,0:T(8,128)(2,1)S(1)} %sum_piece.7.refs_0_), channel_id=1, source_target_pairs={{0,8},{2,10},{4,12},{6,14},{8,0},{10,2},{12,4},{14,6},{1,9},{3,11}... | collective-permute-start | bytes 307208 | tf_op jit(solution)/shard_map/ppermute | solution.py:54
  119.0 7.5 %collective-permute-start.42 = (bf16[400,128]{1,0:T(8,128)(2,1)S(1)}, bf16[400,128]{1,0:T(8,128)(2,1)S(1)}, u32[]{:S(2)}, u32[]{:S(2)}) collective-permute-start(bf16[400,128]{1,0:T(8,128)(2,1)S(1)} %sum_piece.7.refs_0_), channel_id=1, source_target_pairs={{0,12},{2,14},{4,8},{6,10},{8,4},{10,6},{12,0},{14,2},{1,13},{3,15... | collective-permute-start | bytes 307208 | tf_op jit(solution)/shard_map/ppermute | solution.py:54
  121.2 8.7 %collective-permute-start.41 = (bf16[400,128]{1,0:T(8,128)(2,1)S(1)}, bf16[400,128]{1,0:T(8,128)(2,1)S(1)}, u32[]{:S(2)}, u32[]{:S(2)}) collective-permute-start(bf16[400,128]{1,0:T(8,128)(2,1)S(1)} %sum_piece.7.refs_0_), channel_id=1, source_target_pairs={{0,2},{2,0},{4,6},{6,4},{8,10},{10,8},{12,14},{14,12},{1,3},{3,1},... | collective-permute-start | bytes 307208 | tf_op jit(solution)/shard_map/ppermute | solution.py:54
  123.2 6.7 %collective-permute-start.47 = (bf16[400,128]{1,0:T(8,128)(2,1)S(1)}, bf16[400,128]{1,0:T(8,128)(2,1)S(1)}, u32[]{:S(2)}, u32[]{:S(2)}) collective-permute-start(bf16[400,128]{1,0:T(8,128)(2,1)S(1)} %collective-permute-done.46.refs_3_), channel_id=1, source_target_pairs={{0,2},{2,0},{4,6},{6,4},{8,10},{10,8},{12,14},{14,12},{1,3},{3,1},... | collective-permute-start | bytes 307208 | tf_op jit(solution)/shard_map/ppermute | solution.py:54
  125.9 4.7 %collective-permute-start.45 = (bf16[400,128]{1,0:T(8,128)(2,1)S(1)}, bf16[400,128]{1,0:T(8,128)(2,1)S(1)}, u32[]{:S(2)}, u32[]{:S(2)}) collective-permute-start(bf16[400,128]{1,0:T(8,128)(2,1)S(1)} %collective-permute-done.44.refs_2_), channel_id=1, source_target_pairs={{0,2},{2,0},{4,6},{6,4},{8,10},{10,8},{12,14},{14,12},{1,3},{3,1},... | collective-permute-start | bytes 307208 | tf_op jit(solution)/shard_map/ppermute | solution.py:54
  126.5 5.1 %collective-permute-start.43 = (bf16[400,128]{1,0:T(8,128)(2,1)S(1)}, bf16[400,128]{1,0:T(8,128)(2,1)S(1)}, u32[]{:S(2)}, u32[]{:S(2)}) collective-permute-start(bf16[400,128]{1,0:T(8,128)(2,1)S(1)} %collective-permute-done.42.refs_1_), channel_id=1, source_target_pairs={{0,2},{2,0},{4,6},{6,4},{8,10},{10,8},{12,14},{14,12},{1,3},{3,1},... | collective-permute-start | bytes 307208 | tf_op jit(solution)/shard_map/ppermute | solution.py:54
  129.8 1.9 %collective-permute-start.49 = (bf16[4,400,128]{2,1,0:T(8,128)(2,1)S(1)}, bf16[4,400,128]{2,1,0:T(8,128)(2,1)S(1)}, u32[]{:S(2)}, u32[]{:S(2)}) collective-permute-start(bf16[4,400,128]{2,1,0:T(8,128)(2,1)S(1)} %stacked.3), channel_id=1, source_target_pairs={{0,1},{1,0},{2,3},{3,2},{4,5},{5,4},{6,7},{7,6},{8,9},{9,8},{10,11... | collective-permute-start | bytes 1228808 | tf_op jit(solution)/shard_map/ppermute | solution.py:58
  131.7 1.8 %collective-permute-start.48 = (bf16[4,400,128]{2,1,0:T(8,128)(2,1)S(1)}, bf16[4,400,128]{2,1,0:T(8,128)(2,1)S(1)}, u32[]{:S(2)}, u32[]{:S(2)}) collective-permute-start(bf16[4,400,128]{2,1,0:T(8,128)(2,1)S(1)} %stacked.2), channel_id=1, source_target_pairs={{0,1},{1,0},{2,3},{3,2},{4,5},{5,4},{6,7},{7,6},{8,9},{9,8},{10,11... | collective-permute-start | bytes 1228808 | tf_op jit(solution)/shard_map/ppermute | solution.py:58

commit v5 on v4

--- a/solution.py
+++ b/solution.py
@@ -783,12 +783,12 @@
         return relations - learn_rate * total / jnp.sqrt(state)[None, :], state, finish(send(drel), [])
     nz = n // 2
     mine_x, other_x = pieces(t, n, False, rel_ids, drel, acc, [])
-    grads = send(other_x)
     mine_s, other_s = pieces(t, n, True, rel_ids, drel, acc, [other_x])
     to_x = add_each(mine_x, across(other_x))
     theirs = across(other_s)
     down = range(nz - 1, -1, -1)
     from_x = {k: swapped(to_x[k], 1) for k in down}
+    grads = send(to_x[0])
     addends = {k: [from_x[k]] for k in range(nz)}
     turned = []
     bit = 1

time: 135 us -> 135 us (level)
  starting transfers between devices: 27.6 us -> 29.6 us
  waiting for transfers between devices: 63.1 us -> 61.1 us
    ppermute x14, waiting for transfers between devices: 15.5 us -> 13 us  [swapped(): return lax.ppermute(x, 'dom', [(i, i ^ bits) for i in range(n)])]
    ppermute x14, starting transfers between devices: 13.3 us -> 15.1 us  [swapped(): return lax.ppermute(x, 'dom', [(i, i ^ bits) for i in range(n)])]
where the time goes in v5:
time: 135 us
  waiting for transfers between devices  61.1 us (45%)
  Pallas kernels  42.5 us (31%)
  starting transfers between devices  29.6 us (22%)
  between operations  1.55 us (1%)
    ppermute x10, waiting for transfers between devices, shifted(): return lax.ppermute(x, 'dom', [(i, (i + by) % n) for i in range(n)])  36.4 us
    ppermute x14, starting transfers between devices, swapped(): return lax.ppermute(x, 'dom', [(i, i ^ bits) for i in range(n)])  15.1 us
    ppermute x14, waiting for transfers between devices, swapped(): return lax.ppermute(x, 'dom', [(i, i ^ bits) for i in range(n)])  13 us
    ppermute x26, waiting for transfers between devices, across(): return lax.ppermute(x, 'edge', [(0, 1), (1, 0)])  11.7 us
    ppermute x10, starting transfers between devices, shifted(): return lax.ppermute(x, 'dom', [(i, (i + by) % n) for i in range(n)])  9.92 us
    pallas_call x5, Pallas kernels, relsum(): pl.pallas_call(functools.partial(relsum_kernel, t, acc is None), in_specs...  6.21 us
    pallas_call x4, Pallas kernels, source_grad(): pl.pallas_call(functools.partial(source_grad_kernel, t, shape), in_specs=...  5.9 us
    pallas_call x4, Pallas kernels, target_grad(): pl.pallas_call(target_kernel, in_specs=[vmem()] * 8, out_specs=[vmem()] *...  5.52 us
  transfers between devices with their start and end apart: 50, of which 28 were waited for; matrix products, arithmetic and copies ran while one was open for 0% of the time, Pallas kernels for 20%

profile of v5, /device:TPU:0, one launch (start us, length us, event | category | flops | bytes accessed | tf_op | source)
XLA Modules:
  0.0 134.7 jit_solution(6678038313440871423)
XLA Ops:
  0.6 5.4 %first_round.1 = (f32[400,128]{1,0:T(8,128)S(1)}, bf16[400,128]{1,0:T(8,128)(2,1)S(1)}, bf16[400,512]{1,0:T(8,128)(2,1)S(1)}, bf16[400,2048]{1,0:T(8,128)(2,1)S(...) custom-call(s32[4,6]{1,0:T(4,128)} %bitcast.6, s32[4,6]{1,0:T(4,128)} %bitcast.17, s32[6,4,128]{2,1,0:T(4,128)} %src_ref.11, ...), custom_call_target="tpu_custom_call" | custom-call | flops 1258291200 | bytes 6553600 | tf_op jit(solution)/shard_map/first_round/pallas_call | solution.py:304
  6.6 0.9 collective-permute-done.refs_3_
  8.1 5.7 %collective-permute-start.2 = (bf16[400,128]{1,0:T(8,128)(2,1)S(1)}, bf16[400,128]{1,0:T(8,128)(2,1)S(1)}, u32[]{:S(2)}, u32[]{:S(2)}) collective-permute-start(bf16[400,128]{1,0:T(8,128)(2,1)S(1)} %get-tuple-element.127.own0), channel_id=1, source_target_pairs={{0,14},{2,0},{4,2},{6,4},{8,6},{10,8},{12,10},{14,12},{1,15},{3,1}... | collective-permute-start | bytes 307208 | tf_op jit(solution)/shard_map/ppermute | solution.py:49
  13.8 1.0 relvec.5.rel_ref
  14.8 1.0 relsum.5.refs_1_.refs_0_
  15.9 0.9 source_side.5
  17.3 1.0 collective-permute-done.3.far1
  18.2 1.4 %target_grad.4 = (f32[400,128]{1,0:T(8,128)S(1)}, bf16[400,128]{1,0:T(8,128)(2,1)S(1)}, bf16[128,512]{1,0:T(8,128)(2,1)S(1)}) custom-call(f32[512,128]{1,0:T(8,128)S(1)} %near_products.4.near, bf16[400,128]{1,0:T(8,128)(2,1)S(1)} %collective-permute-done.3.far1, bf16[400,512]{1,0:T(8,128)(2,1)S(1)} %get-tuple-element.130.refs_0_.query_ref, ...), custom_call_target="tpu_custom_call" | custom-call | flops 104857600 | bytes 2457600 | tf_op jit(solution)/shard_map/target_grad/pallas_call | solution.py:442
  19.8 1.2 collective-permute-done.4.b_ref
  21.1 1.5 %source_grad.4 = (f32[400,128]{1,0:T(8,128)S(1)}, bf16[400,128]{1,0:T(8,128)(2,1)S(1)}, bf16[400,512]{1,0:T(8,128)(2,1)S(1)}) custom-call(s32[4,6]{1,0:T(4,128)S(1)} %bitcast.8, s32[4,6]{1,0:T(4,128)S(1)} %bitcast.19, bf16[400,128]{1,0:T(8,128)(2,1)S(1)} %sum_pair.9._, bf16[400,128]{1,0:T(8,128)(2,1)S(1)} %held.5.far0, ...), custom_call_target="tpu_custom_call" | custom-call | flops 204800 | bytes 204800 | tf_op jit(solution)/shard_map/source_grad/pallas_call | solution.py:474
  22.8 1.0 relvec.6.refs_4_.rel_ref
  23.8 5.2 %collective-permute-done.5.b_ref = bf16[400,128]{1,0:T(8,128)(2,1)S(1)} collective-permute-done((bf16[400,128]{1,0:T(8,128)(2,1)S(1)}, bf16[400,128]{1,0:T(8,128)(2,1)S(1)}, u32[]{:S(2)}, u32[]{:S(2)}) %collective-permute-start.5) | collective-permute-done | bytes 102432 | tf_op jit(solution)/shard_map/ppermute | solution.py:49
  29.7 1.3 relsum.6.refs_1_.refs_0_
  31.0 0.9 source_side.6
  31.9 2.6 %collective-permute-done.8.x_ref = bf16[400,128]{1,0:T(8,128)(2,1)S(1)} collective-permute-done((bf16[400,128]{1,0:T(8,128)(2,1)S(1)}, bf16[400,128]{1,0:T(8,128)(2,1)S(1)}, u32[]{:S(2)}, u32[]{:S(2)}) %collective-permute-start.8) | collective-permute-done | bytes 102432 | tf_op jit(solution)/shard_map/ppermute | solution.py:49
  34.8 1.0 collective-permute-done.9.far1
  35.8 1.4 %target_grad.5 = (f32[400,128]{1,0:T(8,128)S(1)}, bf16[400,128]{1,0:T(8,128)(2,1)S(1)}, bf16[128,512]{1,0:T(8,128)(2,1)S(1)}) custom-call(f32[512,128]{1,0:T(8,128)S(1)} %near_products.5.near, bf16[400,128]{1,0:T(8,128)(2,1)S(1)} %collective-permute-done.9.far1, bf16[400,512]{1,0:T(8,128)(2,1)S(1)} %get-tuple-element.148.refs_0_.query_ref, ...), custom_call_target="tpu_custom_call" | custom-call | flops 104857600 | bytes 2457600 | tf_op jit(solution)/shard_map/target_grad/pallas_call | solution.py:442
  37.4 1.2 collective-permute-done.10.b_ref
  38.7 1.5 %source_grad.5 = (f32[400,128]{1,0:T(8,128)S(1)}, bf16[400,128]{1,0:T(8,128)(2,1)S(1)}, bf16[400,512]{1,0:T(8,128)(2,1)S(1)}) custom-call(s32[4,6]{1,0:T(4,128)S(1)} %bitcast.10, s32[4,6]{1,0:T(4,128)S(1)} %bitcast.21, bf16[400,128]{1,0:T(8,128)(2,1)S(1)} %sum_pair.11._, bf16[400,128]{1,0:T(8,128)(2,1)S(1)} %held.6.far0, ...), custom_call_target="tpu_custom_call" | custom-call | flops 204800 | bytes 204800 | tf_op jit(solution)/shard_map/source_grad/pallas_call | solution.py:474
  40.4 1.0 relvec.7.refs_4_.rel_ref
  41.4 4.0 %collective-permute-done.11.b_ref = bf16[400,128]{1,0:T(8,128)(2,1)S(1)} collective-permute-done((bf16[400,128]{1,0:T(8,128)(2,1)S(1)}, bf16[400,128]{1,0:T(8,128)(2,1)S(1)}, u32[]{:S(2)}, u32[]{:S(2)}) %collective-permute-start.11) | collective-permute-done | bytes 102432 | tf_op jit(solution)/shard_map/ppermute | solution.py:49
  46.1 1.3 relsum.7.refs_1_.refs_0_
  47.4 0.9 source_side.7
  48.3 3.5 %collective-permute-done.14.x_ref = bf16[400,128]{1,0:T(8,128)(2,1)S(1)} collective-permute-done((bf16[400,128]{1,0:T(8,128)(2,1)S(1)}, bf16[400,128]{1,0:T(8,128)(2,1)S(1)}, u32[]{:S(2)}, u32[]{:S(2)}) %collective-permute-start.14) | collective-permute-done | bytes 102432 | tf_op jit(solution)/shard_map/ppermute | solution.py:49
  52.1 1.0 collective-permute-done.15.far1
  53.1 1.4 %target_grad.6 = (f32[400,128]{1,0:T(8,128)S(1)}, bf16[400,128]{1,0:T(8,128)(2,1)S(1)}, bf16[128,512]{1,0:T(8,128)(2,1)S(1)}) custom-call(f32[512,128]{1,0:T(8,128)S(1)} %near_products.6.near, bf16[400,128]{1,0:T(8,128)(2,1)S(1)} %collective-permute-done.15.far1, bf16[400,512]{1,0:T(8,128)(2,1)S(1)} %get-tuple-element.166.refs_0_.query_ref, ...), custom_call_target="tpu_custom_call" | custom-call | flops 104857600 | bytes 2457600 | tf_op jit(solution)/shard_map/target_grad/pallas_call | solution.py:442
  54.7 1.2 collective-permute-done.16.b_ref
  56.2 1.5 %source_grad.6 = (f32[400,128]{1,0:T(8,128)S(1)}, bf16[400,128]{1,0:T(8,128)(2,1)S(1)}, bf16[400,512]{1,0:T(8,128)(2,1)S(1)}) custom-call(s32[4,6]{1,0:T(4,128)S(1)} %bitcast.12, s32[4,6]{1,0:T(4,128)S(1)} %bitcast.23, bf16[400,128]{1,0:T(8,128)(2,1)S(1)} %sum_pair.13._, bf16[400,128]{1,0:T(8,128)(2,1)S(1)} %held.7.far0, ...), custom_call_target="tpu_custom_call" | custom-call | flops 204800 | bytes 204800 | tf_op jit(solution)/shard_map/source_grad/pallas_call | solution.py:474
  57.9 1.0 relvec.8.refs_4_.rel_ref
  58.9 6.2 %collective-permute-done.17.b_ref = bf16[400,128]{1,0:T(8,128)(2,1)S(1)} collective-permute-done((bf16[400,128]{1,0:T(8,128)(2,1)S(1)}, bf16[400,128]{1,0:T(8,128)(2,1)S(1)}, u32[]{:S(2)}, u32[]{:S(2)}) %collective-permute-start.17) | collective-permute-done | bytes 102432 | tf_op jit(solution)/shard_map/ppermute | solution.py:49
  65.4 1.3 relsum.8.refs_1_.refs_0_
  66.7 0.9 source_side.8
  67.6 4.8 %collective-permute-done.20.x_ref = bf16[400,128]{1,0:T(8,128)(2,1)S(1)} collective-permute-done((bf16[400,128]{1,0:T(8,128)(2,1)S(1)}, bf16[400,128]{1,0:T(8,128)(2,1)S(1)}, u32[]{:S(2)}, u32[]{:S(2)}) %collective-permute-start.20) | collective-permute-done | bytes 102432 | tf_op jit(solution)/shard_map/ppermute | solution.py:49
  72.7 1.0 collective-permute-done.21.far1
  73.7 1.4 %target_grad.7 = (f32[400,128]{1,0:T(8,128)S(1)}, bf16[400,128]{1,0:T(8,128)(2,1)S(1)}, bf16[128,512]{1,0:T(8,128)(2,1)S(1)}) custom-call(f32[512,128]{1,0:T(8,128)S(1)} %near_products.7.near, bf16[400,128]{1,0:T(8,128)(2,1)S(1)} %collective-permute-done.21.far1, bf16[400,512]{1,0:T(8,128)(2,1)S(1)} %get-tuple-element.184.refs_0_.query_ref, ...), custom_call_target="tpu_custom_call" | custom-call | flops 104857600 | bytes 2457600 | tf_op jit(solution)/shard_map/target_grad/pallas_call | solution.py:442
  75.3 1.2 collective-permute-done.22.b_ref
  76.5 1.5 %source_grad.7 = (f32[400,128]{1,0:T(8,128)S(1)}, bf16[400,128]{1,0:T(8,128)(2,1)S(1)}, bf16[400,512]{1,0:T(8,128)(2,1)S(1)}) custom-call(s32[4,6]{1,0:T(4,128)S(1)} %bitcast.14, s32[4,6]{1,0:T(4,128)S(1)} %bitcast.25, bf16[400,128]{1,0:T(8,128)(2,1)S(1)} %sum_pair.15._, bf16[400,128]{1,0:T(8,128)(2,1)S(1)} %held.8.far0, ...), custom_call_target="tpu_custom_call" | custom-call | flops 204800 | bytes 204800 | tf_op jit(solution)/shard_map/source_grad/pallas_call | solution.py:474
  78.2 1.0 relvec.9.refs_4_.rel_ref
  79.3 5.2 %collective-permute-done.23.b_ref = bf16[400,128]{1,0:T(8,128)(2,1)S(1)} collective-permute-done((bf16[400,128]{1,0:T(8,128)(2,1)S(1)}, bf16[400,128]{1,0:T(8,128)(2,1)S(1)}, u32[]{:S(2)}, u32[]{:S(2)}) %collective-permute-start.23) | collective-permute-done | bytes 102432 | tf_op jit(solution)/shard_map/ppermute | solution.py:49
  85.0 1.3 relsum.9.refs_1_.acc_ref
  86.9 5.0 %collective-permute-done.25.x_ref = bf16[400,128]{1,0:T(8,128)(2,1)S(1)} collective-permute-done((bf16[400,128]{1,0:T(8,128)(2,1)S(1)}, bf16[400,128]{1,0:T(8,128)(2,1)S(1)}, u32[]{:S(2)}, u32[]{:S(2)}) %collective-permute-start.25) | collective-permute-done | bytes 102432 | tf_op jit(solution)/shard_map/ppermute | solution.py:49
  91.9 1.3 collective-permute-done.27.far1
  93.2 1.8 %last_terms.1 = (bf16[400,512]{1,0:T(8,128)(2,1)S(1)}, bf16[400,512]{1,0:T(8,128)(2,1)S(1)}, bf16[400,512]{1,0:T(8,128)(2,1)S(1)}) custom-call(s32[4,6]{1,0:T(4,128)S(1)} %bitcast.16, s32[4,6]{1,0:T(4,128)S(1)} %bitcast.27, bf16[400,128]{1,0:T(8,128)(2,1)S(1)} %held.9.far0, bf16[400,128]{1,0:T(8,128)(2,1)S(1)} %collective-permute-done.27.far1, ...), custom_call_target="tpu_custom_call" | custom-call | flops 157286400 | bytes 2457600 | tf_op jit(solution)/shard_map/last_terms/pallas_call | solution.py:504
  95.0 0.7 pieces.2
  97.6 1.0 collective-permute-start.34
  99.6 1.1 collective-permute-start.33
  100.7 0.9 collective-permute-start.38
  101.6 1.4 %collective-permute-done.34.refs_0_ = bf16[400,128]{1,0:T(8,128)(2,1)S(1)} collective-permute-done((bf16[400,128]{1,0:T(8,128)(2,1)S(1)}, bf16[400,128]{1,0:T(8,128)(2,1)S(1)}, u32[]{:S(2)}, u32[]{:S(2)}) %collective-permute-start.34) | collective-permute-done | bytes 102432 | tf_op jit(solution)/shard_map/ppermute | solution.py:54
  103.2 2.5 %collective-permute-start.31 = (bf16[400,128]{1,0:T(8,128)(2,1)S(1)}, bf16[400,128]{1,0:T(8,128)(2,1)S(1)}, u32[]{:S(2)}, u32[]{:S(2)}) collective-permute-start(bf16[400,128]{1,0:T(8,128)(2,1)S(1)} %sum_pair.17), channel_id=1, source_target_pairs={{0,10},{2,12},{4,14},{6,0},{8,2},{10,4},{12,6},{14,8},{1,11},{3,13... | collective-permute-start | bytes 307208 | tf_op jit(solution)/shard_map/ppermute | solution.py:49
  105.7 1.9 %collective-permute-start.37 = (bf16[400,128]{1,0:T(8,128)(2,1)S(1)}, bf16[400,128]{1,0:T(8,128)(2,1)S(1)}, u32[]{:S(2)}, u32[]{:S(2)}) collective-permute-start(bf16[400,128]{1,0:T(8,128)(2,1)S(1)} %get-tuple-element.212._), channel_id=1, source_target_pairs={{0,2},{2,0},{4,6},{6,4},{8,10},{10,8},{12,14},{14,12},{1,3},{3,1},... | collective-permute-start | bytes 307208 | tf_op jit(solution)/shard_map/ppermute | solution.py:54
  107.6 2.1 %collective-permute-done.38.refs_0_ = bf16[400,128]{1,0:T(8,128)(2,1)S(1)} collective-permute-done((bf16[400,128]{1,0:T(8,128)(2,1)S(1)}, bf16[400,128]{1,0:T(8,128)(2,1)S(1)}, u32[]{:S(2)}, u32[]{:S(2)}) %collective-permute-start.38) | collective-permute-done | bytes 102432 | tf_op jit(solution)/shard_map/ppermute | solution.py:54
  109.9 2.1 %collective-permute-start.40 = (bf16[400,128]{1,0:T(8,128)(2,1)S(1)}, bf16[400,128]{1,0:T(8,128)(2,1)S(1)}, u32[]{:S(2)}, u32[]{:S(2)}) collective-permute-start(bf16[400,128]{1,0:T(8,128)(2,1)S(1)} %sum_piece.5.refs_5_), channel_id=1, source_target_pairs={{0,8},{2,10},{4,12},{6,14},{8,0},{10,2},{12,4},{14,6},{1,9},{3,11}... | collective-permute-start | bytes 307208 | tf_op jit(solution)/shard_map/ppermute | solution.py:54
  112.2 2.3 %collective-permute-done.39.refs_1_ = bf16[400,128]{1,0:T(8,128)(2,1)S(1)} collective-permute-done((bf16[400,128]{1,0:T(8,128)(2,1)S(1)}, bf16[400,128]{1,0:T(8,128)(2,1)S(1)}, u32[]{:S(2)}, u32[]{:S(2)}) %collective-permute-start.39) | collective-permute-done | bytes 102432 | tf_op jit(solution)/shard_map/ppermute | solution.py:54
  114.5 1.1 collective-permute-done.40.refs_2_
  115.7 2.9 %collective-permute-start.46 = (bf16[400,128]{1,0:T(8,128)(2,1)S(1)}, bf16[400,128]{1,0:T(8,128)(2,1)S(1)}, u32[]{:S(2)}, u32[]{:S(2)}) collective-permute-start(bf16[400,128]{1,0:T(8,128)(2,1)S(1)} %sum_piece.7.refs_0_), channel_id=1, source_target_pairs={{0,4},{2,6},{4,0},{6,2},{8,12},{10,14},{12,8},{14,10},{1,5},{3,7},... | collective-permute-start | bytes 307208 | tf_op jit(solution)/shard_map/ppermute | solution.py:54
  118.6 2.4 %collective-permute-start.42 = (bf16[400,128]{1,0:T(8,128)(2,1)S(1)}, bf16[400,128]{1,0:T(8,128)(2,1)S(1)}, u32[]{:S(2)}, u32[]{:S(2)}) collective-permute-start(bf16[400,128]{1,0:T(8,128)(2,1)S(1)} %sum_piece.7.refs_0_), channel_id=1, source_target_pairs={{0,12},{2,14},{4,8},{6,10},{8,4},{10,6},{12,0},{14,2},{1,13},{3,15... | collective-permute-start | bytes 307208 | tf_op jit(solution)/shard_map/ppermute | solution.py:54
  121.0 1.5 %collective-permute-done.46.refs_3_ = bf16[400,128]{1,0:T(8,128)(2,1)S(1)} collective-permute-done((bf16[400,128]{1,0:T(8,128)(2,1)S(1)}, bf16[400,128]{1,0:T(8,128)(2,1)S(1)}, u32[]{:S(2)}, u32[]{:S(2)}) %collective-permute-start.46) | collective-permute-done | bytes 102432 | tf_op jit(solution)/shard_map/ppermute | solution.py:54
  123.1 2.8 %collective-permute-done.44.refs_2_ = bf16[400,128]{1,0:T(8,128)(2,1)S(1)} collective-permute-done((bf16[400,128]{1,0:T(8,128)(2,1)S(1)}, bf16[400,128]{1,0:T(8,128)(2,1)S(1)}, u32[]{:S(2)}, u32[]{:S(2)}) %collective-permute-start.44) | collective-permute-done | bytes 102432 | tf_op jit(solution)/shard_map/ppermute | solution.py:54
  125.9 2.0 %collective-permute-start.43 = (bf16[400,128]{1,0:T(8,128)(2,1)S(1)}, bf16[400,128]{1,0:T(8,128)(2,1)S(1)}, u32[]{:S(2)}, u32[]{:S(2)}) collective-permute-start(bf16[400,128]{1,0:T(8,128)(2,1)S(1)} %collective-permute-done.42.refs_1_), channel_id=1, source_target_pairs={{0,2},{2,0},{4,6},{6,4},{8,10},{10,8},{12,14},{14,12},{1,3},{3,1},... | collective-permute-start | bytes 307208 | tf_op jit(solution)/shard_map/ppermute | solution.py:54
  127.9 1.0 relnew.3
  129.0 0.8 whole_partition.1
  130.5 1.1 collective-permute-done.43.refs_1_.refs_2_
  131.8 1.4 %relnew.4 = (f32[400,2048]{1,0:T(8,128)}, f32[1,2048]{1,0:T(1,128)S(1)}) custom-call(f32[400,2048]{1,0:T(8,128)S(1)} %copy-done, f32[1,2048]{1,0:T(1,128)S(1)} %bitcast.30, bf16[4,400,128]{2,1,0:T(8,128)(2,1)S(1)} %collective-permute-done.49.refs_0_, bf16[400,128]{1,0:T(8,128)(2,1)S(1)} %collective-permute-done.41.refs_0_.refs_1_, ...), custom_call_target="tpu_custom_call", output_to_operand_aliasing={{0}: (7, {})} | custom-call | flops 400 | bytes 400 | tf_op jit(solution)/shard_map/relnew/pallas_call | solution.py:761
  133.5 1.0 relnew.5
  (113 shorter events, 12.6 us)
Async XLA Ops:
  0.6 13.2 %copy-start.1 = (s32[6,4,128]{2,1,0:T(4,128)S(1)}, s32[6,4,128]{2,1,0:T(4,128)}, u32[]{:S(2)}) copy-start(s32[6,4,128]{2,1,0:T(4,128)} %ids_ref.25) | copy-start | bytes 36868
  6.0 9.9 %copy-start.2 = (s32[6,4,128]{2,1,0:T(4,128)S(1)}, s32[6,4,128]{2,1,0:T(4,128)}, u32[]{:S(2)}) copy-start(s32[6,4,128]{2,1,0:T(4,128)} %src_ref.11) | copy-start | bytes 36868
  6.1 9.9 %copy-start.3 = (s32[6,4,128]{2,1,0:T(4,128)S(1)}, s32[6,4,128]{2,1,0:T(4,128)}, u32[]{:S(2)}) copy-start(s32[6,4,128]{2,1,0:T(4,128)} %dst_ref.11) | copy-start | bytes 36868
  6.1 9.9 %copy-start.4 = (s32[6,4]{0,1:T(4,128)S(1)}, s32[6,4]{0,1:T(4,128)}, u32[]{:S(2)}) copy-start(s32[6,4]{0,1:T(4,128)} %param.16) | copy-start | bytes 292
  6.1 9.8 %copy-start.5 = (s32[6,4]{0,1:T(4,128)S(1)}, s32[6,4]{0,1:T(4,128)}, u32[]{:S(2)}) copy-start(s32[6,4]{0,1:T(4,128)} %param.17) | copy-start | bytes 292
  6.1 1.5 %collective-permute-start = (bf16[400,128]{1,0:T(8,128)(2,1)S(1)}, bf16[400,128]{1,0:T(8,128)(2,1)S(1)}, u32[]{:S(2)}, u32[]{:S(2)}) collective-permute-start(bf16[400,128]{1,0:T(8,128)(2,1)S(1)} %get-tuple-element.124), channel_id=1, source_target_pairs={{0,1},{1,0},{2,3},{3,2},{4,5},{5,4},{6,7},{7,6},{8,9},{9,8},{10,11... | collective-permute-start | bytes 307208 | tf_op jit(solution)/shard_map/ppermute | solution.py:58
  7.7 8.2 %collective-permute-start.1 = (bf16[400,128]{1,0:T(8,128)(2,1)S(1)}, bf16[400,128]{1,0:T(8,128)(2,1)S(1)}, u32[]{:S(2)}, u32[]{:S(2)}) collective-permute-start(bf16[400,128]{1,0:T(8,128)(2,1)S(1)} %get-tuple-element.127.own0), channel_id=1, source_target_pairs={{0,1},{1,0},{2,3},{3,2},{4,5},{5,4},{6,7},{7,6},{8,9},{9,8},{10,11... | collective-permute-start | bytes 307208 | tf_op jit(solution)/shard_map/ppermute | solution.py:58
  8.1 8.7 %collective-permute-start.2 = (bf16[400,128]{1,0:T(8,128)(2,1)S(1)}, bf16[400,128]{1,0:T(8,128)(2,1)S(1)}, u32[]{:S(2)}, u32[]{:S(2)}) collective-permute-start(bf16[400,128]{1,0:T(8,128)(2,1)S(1)} %get-tuple-element.127.own0), channel_id=1, source_target_pairs={{0,14},{2,0},{4,2},{6,4},{8,6},{10,8},{12,10},{14,12},{1,15},{3,1}... | collective-permute-start | bytes 307208 | tf_op jit(solution)/shard_map/ppermute | solution.py:49
  16.9 1.4 %collective-permute-start.3 = (bf16[400,128]{1,0:T(8,128)(2,1)S(1)}, bf16[400,128]{1,0:T(8,128)(2,1)S(1)}, u32[]{:S(2)}, u32[]{:S(2)}) collective-permute-start(bf16[400,128]{1,0:T(8,128)(2,1)S(1)} %held.5.far0), channel_id=1, source_target_pairs={{0,1},{1,0},{2,3},{3,2},{4,5},{5,4},{6,7},{7,6},{8,9},{9,8},{10,11... | collective-permute-start | bytes 307208 | tf_op jit(solution)/shard_map/ppermute | solution.py:58
  19.6 1.4 %collective-permute-start.4 = (bf16[400,128]{1,0:T(8,128)(2,1)S(1)}, bf16[400,128]{1,0:T(8,128)(2,1)S(1)}, u32[]{:S(2)}, u32[]{:S(2)}) collective-permute-start(bf16[400,128]{1,0:T(8,128)(2,1)S(1)} %get-tuple-element.137), channel_id=1, source_target_pairs={{0,1},{1,0},{2,3},{3,2},{4,5},{5,4},{6,7},{7,6},{8,9},{9,8},{10,11... | collective-permute-start | bytes 307208 | tf_op jit(solution)/shard_map/ppermute | solution.py:58
  21.0 8.0 %collective-permute-start.5 = (bf16[400,128]{1,0:T(8,128)(2,1)S(1)}, bf16[400,128]{1,0:T(8,128)(2,1)S(1)}, u32[]{:S(2)}, u32[]{:S(2)}) collective-permute-start(bf16[400,128]{1,0:T(8,128)(2,1)S(1)} %sum_pair.9._), channel_id=1, source_target_pairs={{0,2},{2,4},{4,6},{6,8},{8,10},{10,12},{12,14},{14,0},{1,3},{3,5},... | collective-permute-start | bytes 307208 | tf_op jit(solution)/shard_map/ppermute | solution.py:49
  22.6 6.4 %collective-permute-start.6 = (bf16[400,128]{1,0:T(8,128)(2,1)S(1)}, bf16[400,128]{1,0:T(8,128)(2,1)S(1)}, u32[]{:S(2)}, u32[]{:S(2)}) collective-permute-start(bf16[400,128]{1,0:T(8,128)(2,1)S(1)} %get-tuple-element.143), channel_id=1, source_target_pairs={{0,1},{1,0},{2,3},{3,2},{4,5},{5,4},{6,7},{7,6},{8,9},{9,8},{10,11... | collective-permute-start | bytes 307208 | tf_op jit(solution)/shard_map/ppermute | solution.py:58
  29.1 1.8 %collective-permute-start.7 = (bf16[400,128]{1,0:T(8,128)(2,1)S(1)}, bf16[400,128]{1,0:T(8,128)(2,1)S(1)}, u32[]{:S(2)}, u32[]{:S(2)}) collective-permute-start(bf16[400,128]{1,0:T(8,128)(2,1)S(1)} %get-tuple-element.146.own0), channel_id=1, source_target_pairs={{0,1},{1,0},{2,3},{3,2},{4,5},{5,4},{6,7},{7,6},{8,9},{9,8},{10,11... | collective-permute-start | bytes 307208 | tf_op jit(solution)/shard_map/ppermute | solution.py:58
  29.2 5.3 %collective-permute-start.8 = (bf16[400,128]{1,0:T(8,128)(2,1)S(1)}, bf16[400,128]{1,0:T(8,128)(2,1)S(1)}, u32[]{:S(2)}, u32[]{:S(2)}) collective-permute-start(bf16[400,128]{1,0:T(8,128)(2,1)S(1)} %get-tuple-element.146.own0), channel_id=1, source_target_pairs={{0,12},{2,14},{4,0},{6,2},{8,4},{10,6},{12,8},{14,10},{1,13},{3,15... | collective-permute-start | bytes 307208 | tf_op jit(solution)/shard_map/ppermute | solution.py:49
  34.5 1.3 collective-permute-start.9
  37.2 1.4 %collective-permute-start.10 = (bf16[400,128]{1,0:T(8,128)(2,1)S(1)}, bf16[400,128]{1,0:T(8,128)(2,1)S(1)}, u32[]{:S(2)}, u32[]{:S(2)}) collective-permute-start(bf16[400,128]{1,0:T(8,128)(2,1)S(1)} %get-tuple-element.155), channel_id=1, source_target_pairs={{0,1},{1,0},{2,3},{3,2},{4,5},{5,4},{6,7},{7,6},{8,9},{9,8},{10,11... | collective-permute-start | bytes 307208 | tf_op jit(solution)/shard_map/ppermute | solution.py:58
  38.6 6.8 %collective-permute-start.11 = (bf16[400,128]{1,0:T(8,128)(2,1)S(1)}, bf16[400,128]{1,0:T(8,128)(2,1)S(1)}, u32[]{:S(2)}, u32[]{:S(2)}) collective-permute-start(bf16[400,128]{1,0:T(8,128)(2,1)S(1)} %sum_pair.11._), channel_id=1, source_target_pairs={{0,4},{2,6},{4,8},{6,10},{8,12},{10,14},{12,0},{14,2},{1,5},{3,7},... | collective-permute-start | bytes 307208 | tf_op jit(solution)/shard_map/ppermute | solution.py:49
  40.1 5.3 %collective-permute-start.12 = (bf16[400,128]{1,0:T(8,128)(2,1)S(1)}, bf16[400,128]{1,0:T(8,128)(2,1)S(1)}, u32[]{:S(2)}, u32[]{:S(2)}) collective-permute-start(bf16[400,128]{1,0:T(8,128)(2,1)S(1)} %get-tuple-element.161), channel_id=1, source_target_pairs={{0,1},{1,0},{2,3},{3,2},{4,5},{5,4},{6,7},{7,6},{8,9},{9,8},{10,11... | collective-permute-start | bytes 307208 | tf_op jit(solution)/shard_map/ppermute | solution.py:58
  45.5 1.8 %collective-permute-start.13 = (bf16[400,128]{1,0:T(8,128)(2,1)S(1)}, bf16[400,128]{1,0:T(8,128)(2,1)S(1)}, u32[]{:S(2)}, u32[]{:S(2)}) collective-permute-start(bf16[400,128]{1,0:T(8,128)(2,1)S(1)} %get-tuple-element.164.own0), channel_id=1, source_target_pairs={{0,1},{1,0},{2,3},{3,2},{4,5},{5,4},{6,7},{7,6},{8,9},{9,8},{10,11... | collective-permute-start | bytes 307208 | tf_op jit(solution)/shard_map/ppermute | solution.py:58
  45.6 6.2 %collective-permute-start.14 = (bf16[400,128]{1,0:T(8,128)(2,1)S(1)}, bf16[400,128]{1,0:T(8,128)(2,1)S(1)}, u32[]{:S(2)}, u32[]{:S(2)}) collective-permute-start(bf16[400,128]{1,0:T(8,128)(2,1)S(1)} %get-tuple-element.164.own0), channel_id=1, source_target_pairs={{0,10},{2,12},{4,14},{6,0},{8,2},{10,4},{12,6},{14,8},{1,11},{3,13... | collective-permute-start | bytes 307208 | tf_op jit(solution)/shard_map/ppermute | solution.py:49
  51.8 1.3 collective-permute-start.15
  54.5 1.4 %collective-permute-start.16 = (bf16[400,128]{1,0:T(8,128)(2,1)S(1)}, bf16[400,128]{1,0:T(8,128)(2,1)S(1)}, u32[]{:S(2)}, u32[]{:S(2)}) collective-permute-start(bf16[400,128]{1,0:T(8,128)(2,1)S(1)} %get-tuple-element.173), channel_id=1, source_target_pairs={{0,1},{1,0},{2,3},{3,2},{4,5},{5,4},{6,7},{7,6},{8,9},{9,8},{10,11... | collective-permute-start | bytes 307208 | tf_op jit(solution)/shard_map/ppermute | solution.py:58
  55.9 9.2 %collective-permute-start.17 = (bf16[400,128]{1,0:T(8,128)(2,1)S(1)}, bf16[400,128]{1,0:T(8,128)(2,1)S(1)}, u32[]{:S(2)}, u32[]{:S(2)}) collective-permute-start(bf16[400,128]{1,0:T(8,128)(2,1)S(1)} %sum_pair.13._), channel_id=1, source_target_pairs={{0,6},{2,8},{4,10},{6,12},{8,14},{10,0},{12,2},{14,4},{1,7},{3,9},... | collective-permute-start | bytes 307208 | tf_op jit(solution)/shard_map/ppermute | solution.py:49
  57.7 7.5 %collective-permute-start.18 = (bf16[400,128]{1,0:T(8,128)(2,1)S(1)}, bf16[400,128]{1,0:T(8,128)(2,1)S(1)}, u32[]{:S(2)}, u32[]{:S(2)}) collective-permute-start(bf16[400,128]{1,0:T(8,128)(2,1)S(1)} %get-tuple-element.179), channel_id=1, source_target_pairs={{0,1},{1,0},{2,3},{3,2},{4,5},{5,4},{6,7},{7,6},{8,9},{9,8},{10,11... | collective-permute-start | bytes 307208 | tf_op jit(solution)/shard_map/ppermute | solution.py:58
  65.3 1.5 %collective-permute-start.19 = (bf16[400,128]{1,0:T(8,128)(2,1)S(1)}, bf16[400,128]{1,0:T(8,128)(2,1)S(1)}, u32[]{:S(2)}, u32[]{:S(2)}) collective-permute-start(bf16[400,128]{1,0:T(8,128)(2,1)S(1)} %get-tuple-element.182.own0), channel_id=1, source_target_pairs={{0,1},{1,0},{2,3},{3,2},{4,5},{5,4},{6,7},{7,6},{8,9},{9,8},{10,11... | collective-permute-start | bytes 307208 | tf_op jit(solution)/shard_map/ppermute | solution.py:58
  65.3 7.0 %collective-permute-start.20 = (bf16[400,128]{1,0:T(8,128)(2,1)S(1)}, bf16[400,128]{1,0:T(8,128)(2,1)S(1)}, u32[]{:S(2)}, u32[]{:S(2)}) collective-permute-start(bf16[400,128]{1,0:T(8,128)(2,1)S(1)} %get-tuple-element.182.own0), channel_id=1, source_target_pairs={{0,8},{2,10},{4,12},{6,14},{8,0},{10,2},{12,4},{14,6},{1,9},{3,11}... | collective-permute-start | bytes 307208 | tf_op jit(solution)/shard_map/ppermute | solution.py:49
  72.4 1.3 collective-permute-start.21
  75.1 1.4 %collective-permute-start.22 = (bf16[400,128]{1,0:T(8,128)(2,1)S(1)}, bf16[400,128]{1,0:T(8,128)(2,1)S(1)}, u32[]{:S(2)}, u32[]{:S(2)}) collective-permute-start(bf16[400,128]{1,0:T(8,128)(2,1)S(1)} %get-tuple-element.191), channel_id=1, source_target_pairs={{0,1},{1,0},{2,3},{3,2},{4,5},{5,4},{6,7},{7,6},{8,9},{9,8},{10,11... | collective-permute-start | bytes 307208 | tf_op jit(solution)/shard_map/ppermute | solution.py:58
  76.5 8.0 %collective-permute-start.23 = (bf16[400,128]{1,0:T(8,128)(2,1)S(1)}, bf16[400,128]{1,0:T(8,128)(2,1)S(1)}, u32[]{:S(2)}, u32[]{:S(2)}) collective-permute-start(bf16[400,128]{1,0:T(8,128)(2,1)S(1)} %sum_pair.15._), channel_id=1, source_target_pairs={{0,8},{2,10},{4,12},{6,14},{8,0},{10,2},{12,4},{14,6},{1,9},{3,11}... | collective-permute-start | bytes 307208 | tf_op jit(solution)/shard_map/ppermute | solution.py:49
  78.0 6.4 %collective-permute-start.24 = (bf16[400,128]{1,0:T(8,128)(2,1)S(1)}, bf16[400,128]{1,0:T(8,128)(2,1)S(1)}, u32[]{:S(2)}, u32[]{:S(2)}) collective-permute-start(bf16[400,128]{1,0:T(8,128)(2,1)S(1)} %get-tuple-element.197), channel_id=1, source_target_pairs={{0,1},{1,0},{2,3},{3,2},{4,5},{5,4},{6,7},{7,6},{8,9},{9,8},{10,11... | collective-permute-start | bytes 307208 | tf_op jit(solution)/shard_map/ppermute | solution.py:58
  84.6 1.7 %collective-permute-start.26 = (bf16[400,128]{1,0:T(8,128)(2,1)S(1)}, bf16[400,128]{1,0:T(8,128)(2,1)S(1)}, u32[]{:S(2)}, u32[]{:S(2)}) collective-permute-start(bf16[400,128]{1,0:T(8,128)(2,1)S(1)} %get-tuple-element.200.own0), channel_id=1, source_target_pairs={{0,1},{1,0},{2,3},{3,2},{4,5},{5,4},{6,7},{7,6},{8,9},{9,8},{10,11... | collective-permute-start | bytes 307208 | tf_op jit(solution)/shard_map/ppermute | solution.py:58
  84.7 7.2 %collective-permute-start.25 = (bf16[400,128]{1,0:T(8,128)(2,1)S(1)}, bf16[400,128]{1,0:T(8,128)(2,1)S(1)}, u32[]{:S(2)}, u32[]{:S(2)}) collective-permute-start(bf16[400,128]{1,0:T(8,128)(2,1)S(1)} %get-tuple-element.200.own0), channel_id=1, source_target_pairs={{0,6},{2,8},{4,10},{6,12},{8,14},{10,0},{12,2},{14,4},{1,7},{3,9},... | collective-permute-start | bytes 307208 | tf_op jit(solution)/shard_map/ppermute | solution.py:49
  91.9 1.3 collective-permute-start.27
  95.7 1.8 %collective-permute-start.28 = (bf16[4,400,128]{2,1,0:T(8,128)(2,1)S(1)}, bf16[4,400,128]{2,1,0:T(8,128)(2,1)S(1)}, u32[]{:S(2)}, u32[]{:S(2)}) collective-permute-start(bf16[4,400,128]{2,1,0:T(8,128)(2,1)S(1)} %get-tuple-element.211.refs_0_), channel_id=1, source_target_pairs={{0,1},{1,0},{2,3},{3,2},{4,5},{5,4},{6,7},{7,6},{8,9},{9,8},{10,11... | collective-permute-start | bytes 1228808 | tf_op jit(solution)/shard_map/ppermute | solution.py:58
  96.6 4.1 %collective-permute-start.32 = (bf16[4,400,128]{2,1,0:T(8,128)(2,1)S(1)}, bf16[4,400,128]{2,1,0:T(8,128)(2,1)S(1)}, u32[]{:S(2)}, u32[]{:S(2)}) collective-permute-start(bf16[4,400,128]{2,1,0:T(8,128)(2,1)S(1)} %get-tuple-element.222), channel_id=1, source_target_pairs={{0,1},{1,0},{2,3},{3,2},{4,5},{5,4},{6,7},{7,6},{8,9},{9,8},{10,11... | collective-permute-start | bytes 1228808 | tf_op jit(solution)/shard_map/ppermute | solution.py:58
  97.6 30.3 %copy-start = (f32[400,2048]{1,0:T(8,128)S(1)}, f32[400,2048]{1,0:T(8,128)}, u32[]{:S(2)}) copy-start(f32[400,2048]{1,0:T(8,128)} %rel_ref.7) | copy-start | bytes 9830404
  97.6 30.3 %copy-start.6 = (f32[2048]{0:T(1024)S(1)}, f32[2048]{0:T(1024)}, u32[]{:S(2)}) copy-start(f32[2048]{0:T(1024)} %param.12) | copy-start | bytes 24580
  97.6 5.4 %collective-permute-start.34 = (bf16[400,128]{1,0:T(8,128)(2,1)S(1)}, bf16[400,128]{1,0:T(8,128)(2,1)S(1)}, u32[]{:S(2)}, u32[]{:S(2)}) collective-permute-start(bf16[400,128]{1,0:T(8,128)(2,1)S(1)} %get-tuple-element.225), channel_id=1, source_target_pairs={{0,2},{2,0},{4,6},{6,4},{8,10},{10,8},{12,14},{14,12},{1,3},{3,1},... | collective-permute-start | bytes 307208 | tf_op jit(solution)/shard_map/ppermute | solution.py:54
  99.0 4.0 %collective-permute-start.29 = (bf16[400,128]{1,0:T(8,128)(2,1)S(1)}, bf16[400,128]{1,0:T(8,128)(2,1)S(1)}, u32[]{:S(2)}, u32[]{:S(2)}) collective-permute-start(bf16[400,128]{1,0:T(8,128)(2,1)S(1)} %get-tuple-element.218), channel_id=1, source_target_pairs={{0,1},{1,0},{2,3},{3,2},{4,5},{5,4},{6,7},{7,6},{8,9},{9,8},{10,11... | collective-permute-start | bytes 307208 | tf_op jit(solution)/shard_map/ppermute | solution.py:58
  99.1 4.0 %collective-permute-start.30 = (bf16[400,128]{1,0:T(8,128)(2,1)S(1)}, bf16[400,128]{1,0:T(8,128)(2,1)S(1)}, u32[]{:S(2)}, u32[]{:S(2)}) collective-permute-start(bf16[400,128]{1,0:T(8,128)(2,1)S(1)} %get-tuple-element.220), channel_id=1, source_target_pairs={{0,1},{1,0},{2,3},{3,2},{4,5},{5,4},{6,7},{7,6},{8,9},{9,8},{10,11... | collective-permute-start | bytes 307208 | tf_op jit(solution)/shard_map/ppermute | solution.py:58
  99.6 10.3 %collective-permute-start.33 = (bf16[400,128]{1,0:T(8,128)(2,1)S(1)}, bf16[400,128]{1,0:T(8,128)(2,1)S(1)}, u32[]{:S(2)}, u32[]{:S(2)}) collective-permute-start(bf16[400,128]{1,0:T(8,128)(2,1)S(1)} %get-tuple-element.223), channel_id=1, source_target_pairs={{0,2},{2,0},{4,6},{6,4},{8,10},{10,8},{12,14},{14,12},{1,3},{3,1},... | collective-permute-start | bytes 307208 | tf_op jit(solution)/shard_map/ppermute | solution.py:54
  100.7 9.0 %collective-permute-start.38 = (bf16[400,128]{1,0:T(8,128)(2,1)S(1)}, bf16[400,128]{1,0:T(8,128)(2,1)S(1)}, u32[]{:S(2)}, u32[]{:S(2)}) collective-permute-start(bf16[400,128]{1,0:T(8,128)(2,1)S(1)} %get-tuple-element.230), channel_id=1, source_target_pairs={{0,2},{2,0},{4,6},{6,4},{8,10},{10,8},{12,14},{14,12},{1,3},{3,1},... | collective-permute-start | bytes 307208 | tf_op jit(solution)/shard_map/ppermute | solution.py:54
  103.1 6.8 %collective-permute-start.35 = (bf16[400,128]{1,0:T(8,128)(2,1)S(1)}, bf16[400,128]{1,0:T(8,128)(2,1)S(1)}, u32[]{:S(2)}, u32[]{:S(2)}) collective-permute-start(bf16[400,128]{1,0:T(8,128)(2,1)S(1)} %sum_piece.4), channel_id=1, source_target_pairs={{0,4},{2,6},{4,0},{6,2},{8,12},{10,14},{12,8},{14,10},{1,5},{3,7},... | collective-permute-start | bytes 307208 | tf_op jit(solution)/shard_map/ppermute | solution.py:54
  103.2 8.8 %collective-permute-start.31 = (bf16[400,128]{1,0:T(8,128)(2,1)S(1)}, bf16[400,128]{1,0:T(8,128)(2,1)S(1)}, u32[]{:S(2)}, u32[]{:S(2)}) collective-permute-start(bf16[400,128]{1,0:T(8,128)(2,1)S(1)} %sum_pair.17), channel_id=1, source_target_pairs={{0,10},{2,12},{4,14},{6,0},{8,2},{10,4},{12,6},{14,8},{1,11},{3,13... | collective-permute-start | bytes 307208 | tf_op jit(solution)/shard_map/ppermute | solution.py:49
  105.7 6.5 %collective-permute-start.37 = (bf16[400,128]{1,0:T(8,128)(2,1)S(1)}, bf16[400,128]{1,0:T(8,128)(2,1)S(1)}, u32[]{:S(2)}, u32[]{:S(2)}) collective-permute-start(bf16[400,128]{1,0:T(8,128)(2,1)S(1)} %get-tuple-element.212._), channel_id=1, source_target_pairs={{0,2},{2,0},{4,6},{6,4},{8,10},{10,8},{12,14},{14,12},{1,3},{3,1},... | collective-permute-start | bytes 307208 | tf_op jit(solution)/shard_map/ppermute | solution.py:54
  109.8 4.8 %collective-permute-start.39 = (bf16[400,128]{1,0:T(8,128)(2,1)S(1)}, bf16[400,128]{1,0:T(8,128)(2,1)S(1)}, u32[]{:S(2)}, u32[]{:S(2)}) collective-permute-start(bf16[400,128]{1,0:T(8,128)(2,1)S(1)} %sum_piece.6), channel_id=1, source_target_pairs={{0,4},{2,6},{4,0},{6,2},{8,12},{10,14},{12,8},{14,10},{1,5},{3,7},... | collective-permute-start | bytes 307208 | tf_op jit(solution)/shard_map/ppermute | solution.py:54
  109.9 5.7 %collective-permute-start.40 = (bf16[400,128]{1,0:T(8,128)(2,1)S(1)}, bf16[400,128]{1,0:T(8,128)(2,1)S(1)}, u32[]{:S(2)}, u32[]{:S(2)}) collective-permute-start(bf16[400,128]{1,0:T(8,128)(2,1)S(1)} %sum_piece.5.refs_5_), channel_id=1, source_target_pairs={{0,8},{2,10},{4,12},{6,14},{8,0},{10,2},{12,4},{14,6},{1,9},{3,11}... | collective-permute-start | bytes 307208 | tf_op jit(solution)/shard_map/ppermute | solution.py:54
  112.2 16.8 %collective-permute-start.36 = (f32[408,128]{1,0:T(8,128)S(1)}, f32[408,128]{1,0:T(8,128)S(1)}, u32[]{:S(2)}, u32[]{:S(2)}) collective-permute-start(f32[408,128]{1,0:T(8,128)S(1)} %update.11.mine), channel_id=1, source_target_pairs={{0,1},{1,0},{2,3},{3,2},{4,5},{5,4},{6,7},{7,6},{8,9},{9,8},{10,11... | collective-permute-start | bytes 626696 | tf_op jit(solution)/shard_map/ppermute | solution.py:58
  115.7 6.8 %collective-permute-start.46 = (bf16[400,128]{1,0:T(8,128)(2,1)S(1)}, bf16[400,128]{1,0:T(8,128)(2,1)S(1)}, u32[]{:S(2)}, u32[]{:S(2)}) collective-permute-start(bf16[400,128]{1,0:T(8,128)(2,1)S(1)} %sum_piece.7.refs_0_), channel_id=1, source_target_pairs={{0,4},{2,6},{4,0},{6,2},{8,12},{10,14},{12,8},{14,10},{1,5},{3,7},... | collective-permute-start | bytes 307208 | tf_op jit(solution)/shard_map/ppermute | solution.py:54
  118.6 7.3 %collective-permute-start.44 = (bf16[400,128]{1,0:T(8,128)(2,1)S(1)}, bf16[400,128]{1,0:T(8,128)(2,1)S(1)}, u32[]{:S(2)}, u32[]{:S(2)}) collective-permute-start(bf16[400,128]{1,0:T(8,128)(2,1)S(1)} %sum_piece.7.refs_0_), channel_id=1, source_target_pairs={{0,8},{2,10},{4,12},{6,14},{8,0},{10,2},{12,4},{14,6},{1,9},{3,11}... | collective-permute-start | bytes 307208 | tf_op jit(solution)/shard_map/ppermute | solution.py:54
  118.6 7.3 %collective-permute-start.42 = (bf16[400,128]{1,0:T(8,128)(2,1)S(1)}, bf16[400,128]{1,0:T(8,128)(2,1)S(1)}, u32[]{:S(2)}, u32[]{:S(2)}) collective-permute-start(bf16[400,128]{1,0:T(8,128)(2,1)S(1)} %sum_piece.7.refs_0_), channel_id=1, source_target_pairs={{0,12},{2,14},{4,8},{6,10},{8,4},{10,6},{12,0},{14,2},{1,13},{3,15... | collective-permute-start | bytes 307208 | tf_op jit(solution)/shard_map/ppermute | solution.py:54
  121.0 8.9 %collective-permute-start.41 = (bf16[400,128]{1,0:T(8,128)(2,1)S(1)}, bf16[400,128]{1,0:T(8,128)(2,1)S(1)}, u32[]{:S(2)}, u32[]{:S(2)}) collective-permute-start(bf16[400,128]{1,0:T(8,128)(2,1)S(1)} %sum_piece.7.refs_0_), channel_id=1, source_target_pairs={{0,2},{2,0},{4,6},{6,4},{8,10},{10,8},{12,14},{14,12},{1,3},{3,1},... | collective-permute-start | bytes 307208 | tf_op jit(solution)/shard_map/ppermute | solution.py:54
  122.6 7.3 %collective-permute-start.47 = (bf16[400,128]{1,0:T(8,128)(2,1)S(1)}, bf16[400,128]{1,0:T(8,128)(2,1)S(1)}, u32[]{:S(2)}, u32[]{:S(2)}) collective-permute-start(bf16[400,128]{1,0:T(8,128)(2,1)S(1)} %collective-permute-done.46.refs_3_), channel_id=1, source_target_pairs={{0,2},{2,0},{4,6},{6,4},{8,10},{10,8},{12,14},{14,12},{1,3},{3,1},... | collective-permute-start | bytes 307208 | tf_op jit(solution)/shard_map/ppermute | solution.py:54
  125.9 4.7 %collective-permute-start.45 = (bf16[400,128]{1,0:T(8,128)(2,1)S(1)}, bf16[400,128]{1,0:T(8,128)(2,1)S(1)}, u32[]{:S(2)}, u32[]{:S(2)}) collective-permute-start(bf16[400,128]{1,0:T(8,128)(2,1)S(1)} %collective-permute-done.44.refs_2_), channel_id=1, source_target_pairs={{0,2},{2,0},{4,6},{6,4},{8,10},{10,8},{12,14},{14,12},{1,3},{3,1},... | collective-permute-start | bytes 307208 | tf_op jit(solution)/shard_map/ppermute | solution.py:54
  125.9 5.8 %collective-permute-start.43 = (bf16[400,128]{1,0:T(8,128)(2,1)S(1)}, bf16[400,128]{1,0:T(8,128)(2,1)S(1)}, u32[]{:S(2)}, u32[]{:S(2)}) collective-permute-start(bf16[400,128]{1,0:T(8,128)(2,1)S(1)} %collective-permute-done.42.refs_1_), channel_id=1, source_target_pairs={{0,2},{2,0},{4,6},{6,4},{8,10},{10,8},{12,14},{14,12},{1,3},{3,1},... | collective-permute-start | bytes 307208 | tf_op jit(solution)/shard_map/ppermute | solution.py:54
  129.8 1.9 %collective-permute-start.49 = (bf16[4,400,128]{2,1,0:T(8,128)(2,1)S(1)}, bf16[4,400,128]{2,1,0:T(8,128)(2,1)S(1)}, u32[]{:S(2)}, u32[]{:S(2)}) collective-permute-start(bf16[4,400,128]{2,1,0:T(8,128)(2,1)S(1)} %stacked.3), channel_id=1, source_target_pairs={{0,1},{1,0},{2,3},{3,2},{4,5},{5,4},{6,7},{7,6},{8,9},{9,8},{10,11... | collective-permute-start | bytes 1228808 | tf_op jit(solution)/shard_map/ppermute | solution.py:58
  131.7 1.8 %collective-permute-start.48 = (bf16[4,400,128]{2,1,0:T(8,128)(2,1)S(1)}, bf16[4,400,128]{2,1,0:T(8,128)(2,1)S(1)}, u32[]{:S(2)}, u32[]{:S(2)}) collective-permute-start(bf16[4,400,128]{2,1,0:T(8,128)(2,1)S(1)} %stacked.2), channel_id=1, source_target_pairs={{0,1},{1,0},{2,3},{3,2},{4,5},{5,4},{6,7},{7,6},{8,9},{9,8},{10,11... | collective-permute-start | bytes 1228808 | tf_op jit(solution)/shard_map/ppermute | solution.py:58

commit v6 on v5

--- a/solution.py
+++ b/solution.py
@@ -790,14 +790,15 @@
     from_x = {k: swapped(to_x[k], 1) for k in down}
     grads = send(to_x[0])
     addends = {k: [from_x[k]] for k in range(nz)}
+    bits = [1 << i for i in range(nz.bit_length() - 1)]
+    steps = [(bit, k) for bit in bits for k in reversed(range(bit + 2 * bit, nz, 2 * bit))]
+    steps += [(bit, bit) for bit in reversed(bits)]
     turned = []
-    bit = 1
-    while bit < nz:
-        for k in reversed(range(bit, nz, 2 * bit)):
-            after = [] if turned else grads[1:2]
-            turned.append(sum_piece(k, mine_s[k], theirs, addends[k], after))
-            addends[k ^ bit].append(swapped(turned[-1], 2 * bit))
-        bit *= 2
+    for bit, k in steps:
+        after = turned[-1:] if turned else grads[1:2]
+        turned.append(sum_piece(k, mine_s[k], theirs, addends[k], after))
+        there = swapped(turned[-1], 2 * bit)
+        addends[k ^ bit].append(held(there, []) if k == bit == nz // 2 else there)
     done = finish(grads, [turned[-1]])
     summed = sum_piece(0, mine_s[0], theirs, addends[0], [])
     got = [summed if k == 0 else swapped(summed, 2 * k) for k in range(nz)]

time: 135 us -> 136 us (level)
  starting transfers between devices: 29.6 us -> 31.6 us
    ppermute x10, starting transfers between devices: 9.92 us -> 11.6 us  [shifted(): return lax.ppermute(x, 'dom', [(i, (i + by) % n) for i in range(n)])]
where the time goes in v6:
time: 136 us
  waiting for transfers between devices  60.4 us (44%)
  Pallas kernels  42.5 us (31%)
  starting transfers between devices  31.6 us (23%)
  between operations  1.5 us (1%)
    ppermute x10, waiting for transfers between devices, shifted(): return lax.ppermute(x, 'dom', [(i, (i + by) % n) for i in range(n)])  36.3 us
    ppermute x14, starting transfers between devices, swapped(): return lax.ppermute(x, 'dom', [(i, i ^ bits) for i in range(n)])  15.4 us
    ppermute x14, waiting for transfers between devices, swapped(): return lax.ppermute(x, 'dom', [(i, i ^ bits) for i in range(n)])  12.4 us
    ppermute x26, waiting for transfers between devices, across(): return lax.ppermute(x, 'edge', [(0, 1), (1, 0)])  11.7 us
    ppermute x10, starting transfers between devices, shifted(): return lax.ppermute(x, 'dom', [(i, (i + by) % n) for i in range(n)])  11.6 us
    pallas_call x5, Pallas kernels, relsum(): pl.pallas_call(functools.partial(relsum_kernel, t, acc is None), in_specs...  6.22 us
    pallas_call x4, Pallas kernels, source_grad(): pl.pallas_call(functools.partial(source_grad_kernel, t, shape), in_specs=...  5.9 us
    pallas_call x4, Pallas kernels, target_grad(): pl.pallas_call(target_kernel, in_specs=[vmem()] * 8, out_specs=[vmem()] *...  5.51 us
  transfers between devices with their start and end apart: 50, of which 28 were waited for; matrix products, arithmetic and copies ran while one was open for 0% of the time, Pallas kernels for 20%

profile of v6, /device:TPU:0, one launch (start us, length us, event | category | flops | bytes accessed | tf_op | source)
XLA Modules:
  0.0 136.0 jit_solution(8253787534270355630)
XLA Ops:
  0.6 5.4 %first_round.1 = (f32[400,128]{1,0:T(8,128)S(1)}, bf16[400,128]{1,0:T(8,128)(2,1)S(1)}, bf16[400,512]{1,0:T(8,128)(2,1)S(1)}, bf16[400,2048]{1,0:T(8,128)(2,1)S(...) custom-call(s32[4,6]{1,0:T(4,128)} %bitcast.6, s32[4,6]{1,0:T(4,128)} %bitcast.17, s32[6,4,128]{2,1,0:T(4,128)} %src_ref.11, ...), custom_call_target="tpu_custom_call" | custom-call | flops 1258291200 | bytes 6553600 | tf_op jit(solution)/shard_map/first_round/pallas_call | solution.py:304
  6.6 0.9 collective-permute-done.refs_3_
  8.1 5.7 %collective-permute-start.2 = (bf16[400,128]{1,0:T(8,128)(2,1)S(1)}, bf16[400,128]{1,0:T(8,128)(2,1)S(1)}, u32[]{:S(2)}, u32[]{:S(2)}) collective-permute-start(bf16[400,128]{1,0:T(8,128)(2,1)S(1)} %get-tuple-element.127.own0), channel_id=1, source_target_pairs={{0,14},{2,0},{4,2},{6,4},{8,6},{10,8},{12,10},{14,12},{1,15},{3,1}... | collective-permute-start | bytes 307208 | tf_op jit(solution)/shard_map/ppermute | solution.py:49
  13.8 1.0 relvec.5.rel_ref
  14.8 1.0 relsum.5.refs_1_.refs_0_
  15.9 0.9 source_side.5
  17.2 1.0 collective-permute-done.3.far1
  18.2 1.4 %target_grad.4 = (f32[400,128]{1,0:T(8,128)S(1)}, bf16[400,128]{1,0:T(8,128)(2,1)S(1)}, bf16[128,512]{1,0:T(8,128)(2,1)S(1)}) custom-call(f32[512,128]{1,0:T(8,128)S(1)} %near_products.4.near, bf16[400,128]{1,0:T(8,128)(2,1)S(1)} %collective-permute-done.3.far1, bf16[400,512]{1,0:T(8,128)(2,1)S(1)} %get-tuple-element.130.refs_0_.query_ref, ...), custom_call_target="tpu_custom_call" | custom-call | flops 104857600 | bytes 2457600 | tf_op jit(solution)/shard_map/target_grad/pallas_call | solution.py:442
  19.8 1.2 collective-permute-done.4.b_ref
  21.1 1.5 %source_grad.4 = (f32[400,128]{1,0:T(8,128)S(1)}, bf16[400,128]{1,0:T(8,128)(2,1)S(1)}, bf16[400,512]{1,0:T(8,128)(2,1)S(1)}) custom-call(s32[4,6]{1,0:T(4,128)S(1)} %bitcast.8, s32[4,6]{1,0:T(4,128)S(1)} %bitcast.19, bf16[400,128]{1,0:T(8,128)(2,1)S(1)} %sum_pair.9._, bf16[400,128]{1,0:T(8,128)(2,1)S(1)} %held.6.far0, ...), custom_call_target="tpu_custom_call" | custom-call | flops 204800 | bytes 204800 | tf_op jit(solution)/shard_map/source_grad/pallas_call | solution.py:474
  22.8 1.0 relvec.6.refs_4_.rel_ref
  23.8 5.2 %collective-permute-done.5.b_ref = bf16[400,128]{1,0:T(8,128)(2,1)S(1)} collective-permute-done((bf16[400,128]{1,0:T(8,128)(2,1)S(1)}, bf16[400,128]{1,0:T(8,128)(2,1)S(1)}, u32[]{:S(2)}, u32[]{:S(2)}) %collective-permute-start.5) | collective-permute-done | bytes 102432 | tf_op jit(solution)/shard_map/ppermute | solution.py:49
  29.7 1.3 relsum.6.refs_1_.refs_0_
  31.0 0.9 source_side.6
  31.9 2.6 %collective-permute-done.8.x_ref = bf16[400,128]{1,0:T(8,128)(2,1)S(1)} collective-permute-done((bf16[400,128]{1,0:T(8,128)(2,1)S(1)}, bf16[400,128]{1,0:T(8,128)(2,1)S(1)}, u32[]{:S(2)}, u32[]{:S(2)}) %collective-permute-start.8) | collective-permute-done | bytes 102432 | tf_op jit(solution)/shard_map/ppermute | solution.py:49
  34.8 1.0 collective-permute-done.9.far1
  35.8 1.4 %target_grad.5 = (f32[400,128]{1,0:T(8,128)S(1)}, bf16[400,128]{1,0:T(8,128)(2,1)S(1)}, bf16[128,512]{1,0:T(8,128)(2,1)S(1)}) custom-call(f32[512,128]{1,0:T(8,128)S(1)} %near_products.5.near, bf16[400,128]{1,0:T(8,128)(2,1)S(1)} %collective-permute-done.9.far1, bf16[400,512]{1,0:T(8,128)(2,1)S(1)} %get-tuple-element.148.refs_0_.query_ref, ...), custom_call_target="tpu_custom_call" | custom-call | flops 104857600 | bytes 2457600 | tf_op jit(solution)/shard_map/target_grad/pallas_call | solution.py:442
  37.4 1.2 collective-permute-done.10.b_ref
  38.6 1.5 %source_grad.5 = (f32[400,128]{1,0:T(8,128)S(1)}, bf16[400,128]{1,0:T(8,128)(2,1)S(1)}, bf16[400,512]{1,0:T(8,128)(2,1)S(1)}) custom-call(s32[4,6]{1,0:T(4,128)S(1)} %bitcast.10, s32[4,6]{1,0:T(4,128)S(1)} %bitcast.21, bf16[400,128]{1,0:T(8,128)(2,1)S(1)} %sum_pair.11._, bf16[400,128]{1,0:T(8,128)(2,1)S(1)} %held.7.far0, ...), custom_call_target="tpu_custom_call" | custom-call | flops 204800 | bytes 204800 | tf_op jit(solution)/shard_map/source_grad/pallas_call | solution.py:474
  40.3 1.0 relvec.7.refs_4_.rel_ref
  41.4 4.0 %collective-permute-done.11.b_ref = bf16[400,128]{1,0:T(8,128)(2,1)S(1)} collective-permute-done((bf16[400,128]{1,0:T(8,128)(2,1)S(1)}, bf16[400,128]{1,0:T(8,128)(2,1)S(1)}, u32[]{:S(2)}, u32[]{:S(2)}) %collective-permute-start.11) | collective-permute-done | bytes 102432 | tf_op jit(solution)/shard_map/ppermute | solution.py:49
  46.1 1.3 relsum.7.refs_1_.refs_0_
  47.4 0.9 source_side.7
  48.3 3.5 %collective-permute-done.14.x_ref = bf16[400,128]{1,0:T(8,128)(2,1)S(1)} collective-permute-done((bf16[400,128]{1,0:T(8,128)(2,1)S(1)}, bf16[400,128]{1,0:T(8,128)(2,1)S(1)}, u32[]{:S(2)}, u32[]{:S(2)}) %collective-permute-start.14) | collective-permute-done | bytes 102432 | tf_op jit(solution)/shard_map/ppermute | solution.py:49
  52.1 1.0 collective-permute-done.15.far1
  53.1 1.4 %target_grad.6 = (f32[400,128]{1,0:T(8,128)S(1)}, bf16[400,128]{1,0:T(8,128)(2,1)S(1)}, bf16[128,512]{1,0:T(8,128)(2,1)S(1)}) custom-call(f32[512,128]{1,0:T(8,128)S(1)} %near_products.6.near, bf16[400,128]{1,0:T(8,128)(2,1)S(1)} %collective-permute-done.15.far1, bf16[400,512]{1,0:T(8,128)(2,1)S(1)} %get-tuple-element.166.refs_0_.query_ref, ...), custom_call_target="tpu_custom_call" | custom-call | flops 104857600 | bytes 2457600 | tf_op jit(solution)/shard_map/target_grad/pallas_call | solution.py:442
  54.7 1.2 collective-permute-done.16.b_ref
  56.2 1.5 %source_grad.6 = (f32[400,128]{1,0:T(8,128)S(1)}, bf16[400,128]{1,0:T(8,128)(2,1)S(1)}, bf16[400,512]{1,0:T(8,128)(2,1)S(1)}) custom-call(s32[4,6]{1,0:T(4,128)S(1)} %bitcast.12, s32[4,6]{1,0:T(4,128)S(1)} %bitcast.23, bf16[400,128]{1,0:T(8,128)(2,1)S(1)} %sum_pair.13._, bf16[400,128]{1,0:T(8,128)(2,1)S(1)} %held.8.far0, ...), custom_call_target="tpu_custom_call" | custom-call | flops 204800 | bytes 204800 | tf_op jit(solution)/shard_map/source_grad/pallas_call | solution.py:474
  57.9 1.0 relvec.8.refs_4_.rel_ref
  58.9 6.2 %collective-permute-done.17.b_ref = bf16[400,128]{1,0:T(8,128)(2,1)S(1)} collective-permute-done((bf16[400,128]{1,0:T(8,128)(2,1)S(1)}, bf16[400,128]{1,0:T(8,128)(2,1)S(1)}, u32[]{:S(2)}, u32[]{:S(2)}) %collective-permute-start.17) | collective-permute-done | bytes 102432 | tf_op jit(solution)/shard_map/ppermute | solution.py:49
  65.4 1.3 relsum.8.refs_1_.refs_0_
  66.7 0.9 source_side.8
  67.6 4.8 %collective-permute-done.20.x_ref = bf16[400,128]{1,0:T(8,128)(2,1)S(1)} collective-permute-done((bf16[400,128]{1,0:T(8,128)(2,1)S(1)}, bf16[400,128]{1,0:T(8,128)(2,1)S(1)}, u32[]{:S(2)}, u32[]{:S(2)}) %collective-permute-start.20) | collective-permute-done | bytes 102432 | tf_op jit(solution)/shard_map/ppermute | solution.py:49
  72.7 1.0 collective-permute-done.21.far1
  73.7 1.4 %target_grad.7 = (f32[400,128]{1,0:T(8,128)S(1)}, bf16[400,128]{1,0:T(8,128)(2,1)S(1)}, bf16[128,512]{1,0:T(8,128)(2,1)S(1)}) custom-call(f32[512,128]{1,0:T(8,128)S(1)} %near_products.7.near, bf16[400,128]{1,0:T(8,128)(2,1)S(1)} %collective-permute-done.21.far1, bf16[400,512]{1,0:T(8,128)(2,1)S(1)} %get-tuple-element.184.refs_0_.query_ref, ...), custom_call_target="tpu_custom_call" | custom-call | flops 104857600 | bytes 2457600 | tf_op jit(solution)/shard_map/target_grad/pallas_call | solution.py:442
  75.3 1.2 collective-permute-done.22.b_ref
  76.5 1.5 %source_grad.7 = (f32[400,128]{1,0:T(8,128)S(1)}, bf16[400,128]{1,0:T(8,128)(2,1)S(1)}, bf16[400,512]{1,0:T(8,128)(2,1)S(1)}) custom-call(s32[4,6]{1,0:T(4,128)S(1)} %bitcast.14, s32[4,6]{1,0:T(4,128)S(1)} %bitcast.25, bf16[400,128]{1,0:T(8,128)(2,1)S(1)} %sum_pair.15._, bf16[400,128]{1,0:T(8,128)(2,1)S(1)} %held.9.far0, ...), custom_call_target="tpu_custom_call" | custom-call | flops 204800 | bytes 204800 | tf_op jit(solution)/shard_map/source_grad/pallas_call | solution.py:474
  78.2 1.0 relvec.9.refs_4_.rel_ref
  79.3 5.2 %collective-permute-done.23.b_ref = bf16[400,128]{1,0:T(8,128)(2,1)S(1)} collective-permute-done((bf16[400,128]{1,0:T(8,128)(2,1)S(1)}, bf16[400,128]{1,0:T(8,128)(2,1)S(1)}, u32[]{:S(2)}, u32[]{:S(2)}) %collective-permute-start.23) | collective-permute-done | bytes 102432 | tf_op jit(solution)/shard_map/ppermute | solution.py:49
  85.0 1.3 relsum.9.refs_1_.acc_ref
  86.9 5.0 %collective-permute-done.25.x_ref = bf16[400,128]{1,0:T(8,128)(2,1)S(1)} collective-permute-done((bf16[400,128]{1,0:T(8,128)(2,1)S(1)}, bf16[400,128]{1,0:T(8,128)(2,1)S(1)}, u32[]{:S(2)}, u32[]{:S(2)}) %collective-permute-start.25) | collective-permute-done | bytes 102432 | tf_op jit(solution)/shard_map/ppermute | solution.py:49
  91.9 1.3 collective-permute-done.27.far1
  93.2 1.8 %last_terms.1 = (bf16[400,512]{1,0:T(8,128)(2,1)S(1)}, bf16[400,512]{1,0:T(8,128)(2,1)S(1)}, bf16[400,512]{1,0:T(8,128)(2,1)S(1)}) custom-call(s32[4,6]{1,0:T(4,128)S(1)} %bitcast.16, s32[4,6]{1,0:T(4,128)S(1)} %bitcast.27, bf16[400,128]{1,0:T(8,128)(2,1)S(1)} %held.10.far0, bf16[400,128]{1,0:T(8,128)(2,1)S(1)} %collective-permute-done.27.far1, ...), custom_call_target="tpu_custom_call" | custom-call | flops 157286400 | bytes 2457600 | tf_op jit(solution)/shard_map/last_terms/pallas_call | solution.py:504
  97.6 1.0 collective-permute-start.35
  99.6 1.1 collective-permute-start.34
  100.7 2.3 %collective-permute-done.35.refs_0_ = bf16[400,128]{1,0:T(8,128)(2,1)S(1)} collective-permute-done((bf16[400,128]{1,0:T(8,128)(2,1)S(1)}, bf16[400,128]{1,0:T(8,128)(2,1)S(1)}, u32[]{:S(2)}, u32[]{:S(2)}) %collective-permute-start.35) | collective-permute-done | bytes 102432 | tf_op jit(solution)/shard_map/ppermute | solution.py:54
  103.1 0.8 collective-permute-start.33
  104.0 4.2 %collective-permute-start.31 = (bf16[400,128]{1,0:T(8,128)(2,1)S(1)}, bf16[400,128]{1,0:T(8,128)(2,1)S(1)}, u32[]{:S(2)}, u32[]{:S(2)}) collective-permute-start(bf16[400,128]{1,0:T(8,128)(2,1)S(1)} %sum_pair.17), channel_id=1, source_target_pairs={{0,10},{2,12},{4,14},{6,0},{8,2},{10,4},{12,6},{14,8},{1,11},{3,13... | collective-permute-start | bytes 307208 | tf_op jit(solution)/shard_map/ppermute | solution.py:49
  108.1 0.7 collective-permute-done.36.refs_1_
  108.9 1.2 collective-permute-start.39
  110.2 2.6 %collective-permute-start.40 = (bf16[400,128]{1,0:T(8,128)(2,1)S(1)}, bf16[400,128]{1,0:T(8,128)(2,1)S(1)}, u32[]{:S(2)}, u32[]{:S(2)}) collective-permute-start(bf16[400,128]{1,0:T(8,128)(2,1)S(1)} %sum_piece.6.refs_5_), channel_id=1, source_target_pairs={{0,4},{2,6},{4,0},{6,2},{8,12},{10,14},{12,8},{14,10},{1,5},{3,7},... | collective-permute-start | bytes 307208 | tf_op jit(solution)/shard_map/ppermute | solution.py:54
  113.0 3.4 %collective-permute-done.39.x_ref = bf16[400,128]{1,0:T(8,128)(2,1)S(1)} collective-permute-done((bf16[400,128]{1,0:T(8,128)(2,1)S(1)}, bf16[400,128]{1,0:T(8,128)(2,1)S(1)}, u32[]{:S(2)}, u32[]{:S(2)}) %collective-permute-start.39) | collective-permute-done | bytes 102432 | tf_op jit(solution)/shard_map/ppermute | solution.py:54
  116.9 0.7 collective-permute-start.46
  117.6 2.4 %collective-permute-start.44 = (bf16[400,128]{1,0:T(8,128)(2,1)S(1)}, bf16[400,128]{1,0:T(8,128)(2,1)S(1)}, u32[]{:S(2)}, u32[]{:S(2)}) collective-permute-start(bf16[400,128]{1,0:T(8,128)(2,1)S(1)} %sum_piece.7.refs_0_), channel_id=1, source_target_pairs={{0,8},{2,10},{4,12},{6,14},{8,0},{10,2},{12,4},{14,6},{1,9},{3,11}... | collective-permute-start | bytes 307208 | tf_op jit(solution)/shard_map/ppermute | solution.py:54
  120.0 1.3 collective-permute-start.42
  121.6 2.1 %collective-permute-start.47 = (bf16[400,128]{1,0:T(8,128)(2,1)S(1)}, bf16[400,128]{1,0:T(8,128)(2,1)S(1)}, u32[]{:S(2)}, u32[]{:S(2)}) collective-permute-start(bf16[400,128]{1,0:T(8,128)(2,1)S(1)} %collective-permute-done.46.refs_3_), channel_id=1, source_target_pairs={{0,2},{2,0},{4,6},{6,4},{8,10},{10,8},{12,14},{14,12},{1,3},{3,1},... | collective-permute-start | bytes 307208 | tf_op jit(solution)/shard_map/ppermute | solution.py:54
  123.7 3.1 %collective-permute-done.44.refs_2_ = bf16[400,128]{1,0:T(8,128)(2,1)S(1)} collective-permute-done((bf16[400,128]{1,0:T(8,128)(2,1)S(1)}, bf16[400,128]{1,0:T(8,128)(2,1)S(1)}, u32[]{:S(2)}, u32[]{:S(2)}) %collective-permute-start.44) | collective-permute-done | bytes 102432 | tf_op jit(solution)/shard_map/ppermute | solution.py:54
  126.8 1.5 %collective-permute-start.45 = (bf16[400,128]{1,0:T(8,128)(2,1)S(1)}, bf16[400,128]{1,0:T(8,128)(2,1)S(1)}, u32[]{:S(2)}, u32[]{:S(2)}) collective-permute-start(bf16[400,128]{1,0:T(8,128)(2,1)S(1)} %collective-permute-done.44.refs_2_), channel_id=1, source_target_pairs={{0,2},{2,0},{4,6},{6,4},{8,10},{10,8},{12,14},{14,12},{1,3},{3,1},... | collective-permute-start | bytes 307208 | tf_op jit(solution)/shard_map/ppermute | solution.py:54
  128.8 1.0 relnew.3
  129.9 0.8 whole_partition.1
  130.8 0.7 collective-permute-done.45.refs_2_.refs_3_
  131.6 1.4 %collective-permute-done.43.refs_1_.refs_2_ = bf16[400,128]{1,0:T(8,128)(2,1)S(1)} collective-permute-done((bf16[400,128]{1,0:T(8,128)(2,1)S(1)}, bf16[400,128]{1,0:T(8,128)(2,1)S(1)}, u32[]{:S(2)}, u32[]{:S(2)}) %collective-permute-start.43) | collective-permute-done | bytes 102432 | tf_op jit(solution)/shard_map/ppermute | solution.py:54
  133.1 1.4 relnew.4
  134.8 1.0 relnew.5
  (114 shorter events, 13.4 us)
Async XLA Ops:
  0.6 13.2 %copy-start.1 = (s32[6,4,128]{2,1,0:T(4,128)S(1)}, s32[6,4,128]{2,1,0:T(4,128)}, u32[]{:S(2)}) copy-start(s32[6,4,128]{2,1,0:T(4,128)} %ids_ref.25) | copy-start | bytes 36868
  6.1 9.8 %copy-start.2 = (s32[6,4,128]{2,1,0:T(4,128)S(1)}, s32[6,4,128]{2,1,0:T(4,128)}, u32[]{:S(2)}) copy-start(s32[6,4,128]{2,1,0:T(4,128)} %src_ref.11) | copy-start | bytes 36868
  6.1 9.8 %copy-start.3 = (s32[6,4,128]{2,1,0:T(4,128)S(1)}, s32[6,4,128]{2,1,0:T(4,128)}, u32[]{:S(2)}) copy-start(s32[6,4,128]{2,1,0:T(4,128)} %dst_ref.11) | copy-start | bytes 36868
  6.1 9.8 %copy-start.4 = (s32[6,4]{0,1:T(4,128)S(1)}, s32[6,4]{0,1:T(4,128)}, u32[]{:S(2)}) copy-start(s32[6,4]{0,1:T(4,128)} %param.16) | copy-start | bytes 292
  6.1 9.8 %copy-start.5 = (s32[6,4]{0,1:T(4,128)S(1)}, s32[6,4]{0,1:T(4,128)}, u32[]{:S(2)}) copy-start(s32[6,4]{0,1:T(4,128)} %param.17) | copy-start | bytes 292
  6.1 1.5 %collective-permute-start = (bf16[400,128]{1,0:T(8,128)(2,1)S(1)}, bf16[400,128]{1,0:T(8,128)(2,1)S(1)}, u32[]{:S(2)}, u32[]{:S(2)}) collective-permute-start(bf16[400,128]{1,0:T(8,128)(2,1)S(1)} %get-tuple-element.124), channel_id=1, source_target_pairs={{0,1},{1,0},{2,3},{3,2},{4,5},{5,4},{6,7},{7,6},{8,9},{9,8},{10,11... | collective-permute-start | bytes 307208 | tf_op jit(solution)/shard_map/ppermute | solution.py:58
  7.7 8.2 %collective-permute-start.1 = (bf16[400,128]{1,0:T(8,128)(2,1)S(1)}, bf16[400,128]{1,0:T(8,128)(2,1)S(1)}, u32[]{:S(2)}, u32[]{:S(2)}) collective-permute-start(bf16[400,128]{1,0:T(8,128)(2,1)S(1)} %get-tuple-element.127.own0), channel_id=1, source_target_pairs={{0,1},{1,0},{2,3},{3,2},{4,5},{5,4},{6,7},{7,6},{8,9},{9,8},{10,11... | collective-permute-start | bytes 307208 | tf_op jit(solution)/shard_map/ppermute | solution.py:58
  8.1 8.7 %collective-permute-start.2 = (bf16[400,128]{1,0:T(8,128)(2,1)S(1)}, bf16[400,128]{1,0:T(8,128)(2,1)S(1)}, u32[]{:S(2)}, u32[]{:S(2)}) collective-permute-start(bf16[400,128]{1,0:T(8,128)(2,1)S(1)} %get-tuple-element.127.own0), channel_id=1, source_target_pairs={{0,14},{2,0},{4,2},{6,4},{8,6},{10,8},{12,10},{14,12},{1,15},{3,1}... | collective-permute-start | bytes 307208 | tf_op jit(solution)/shard_map/ppermute | solution.py:49
  16.8 1.4 %collective-permute-start.3 = (bf16[400,128]{1,0:T(8,128)(2,1)S(1)}, bf16[400,128]{1,0:T(8,128)(2,1)S(1)}, u32[]{:S(2)}, u32[]{:S(2)}) collective-permute-start(bf16[400,128]{1,0:T(8,128)(2,1)S(1)} %held.6.far0), channel_id=1, source_target_pairs={{0,1},{1,0},{2,3},{3,2},{4,5},{5,4},{6,7},{7,6},{8,9},{9,8},{10,11... | collective-permute-start | bytes 307208 | tf_op jit(solution)/shard_map/ppermute | solution.py:58
  19.6 1.4 %collective-permute-start.4 = (bf16[400,128]{1,0:T(8,128)(2,1)S(1)}, bf16[400,128]{1,0:T(8,128)(2,1)S(1)}, u32[]{:S(2)}, u32[]{:S(2)}) collective-permute-start(bf16[400,128]{1,0:T(8,128)(2,1)S(1)} %get-tuple-element.137), channel_id=1, source_target_pairs={{0,1},{1,0},{2,3},{3,2},{4,5},{5,4},{6,7},{7,6},{8,9},{9,8},{10,11... | collective-permute-start | bytes 307208 | tf_op jit(solution)/shard_map/ppermute | solution.py:58
  21.0 8.0 %collective-permute-start.5 = (bf16[400,128]{1,0:T(8,128)(2,1)S(1)}, bf16[400,128]{1,0:T(8,128)(2,1)S(1)}, u32[]{:S(2)}, u32[]{:S(2)}) collective-permute-start(bf16[400,128]{1,0:T(8,128)(2,1)S(1)} %sum_pair.9._), channel_id=1, source_target_pairs={{0,2},{2,4},{4,6},{6,8},{8,10},{10,12},{12,14},{14,0},{1,3},{3,5},... | collective-permute-start | bytes 307208 | tf_op jit(solution)/shard_map/ppermute | solution.py:49
  22.5 6.4 %collective-permute-start.6 = (bf16[400,128]{1,0:T(8,128)(2,1)S(1)}, bf16[400,128]{1,0:T(8,128)(2,1)S(1)}, u32[]{:S(2)}, u32[]{:S(2)}) collective-permute-start(bf16[400,128]{1,0:T(8,128)(2,1)S(1)} %get-tuple-element.143), channel_id=1, source_target_pairs={{0,1},{1,0},{2,3},{3,2},{4,5},{5,4},{6,7},{7,6},{8,9},{9,8},{10,11... | collective-permute-start | bytes 307208 | tf_op jit(solution)/shard_map/ppermute | solution.py:58
  29.1 1.8 %collective-permute-start.7 = (bf16[400,128]{1,0:T(8,128)(2,1)S(1)}, bf16[400,128]{1,0:T(8,128)(2,1)S(1)}, u32[]{:S(2)}, u32[]{:S(2)}) collective-permute-start(bf16[400,128]{1,0:T(8,128)(2,1)S(1)} %get-tuple-element.146.own0), channel_id=1, source_target_pairs={{0,1},{1,0},{2,3},{3,2},{4,5},{5,4},{6,7},{7,6},{8,9},{9,8},{10,11... | collective-permute-start | bytes 307208 | tf_op jit(solution)/shard_map/ppermute | solution.py:58
  29.2 5.3 %collective-permute-start.8 = (bf16[400,128]{1,0:T(8,128)(2,1)S(1)}, bf16[400,128]{1,0:T(8,128)(2,1)S(1)}, u32[]{:S(2)}, u32[]{:S(2)}) collective-permute-start(bf16[400,128]{1,0:T(8,128)(2,1)S(1)} %get-tuple-element.146.own0), channel_id=1, source_target_pairs={{0,12},{2,14},{4,0},{6,2},{8,4},{10,6},{12,8},{14,10},{1,13},{3,15... | collective-permute-start | bytes 307208 | tf_op jit(solution)/shard_map/ppermute | solution.py:49
  34.5 1.3 collective-permute-start.9
  37.2 1.4 %collective-permute-start.10 = (bf16[400,128]{1,0:T(8,128)(2,1)S(1)}, bf16[400,128]{1,0:T(8,128)(2,1)S(1)}, u32[]{:S(2)}, u32[]{:S(2)}) collective-permute-start(bf16[400,128]{1,0:T(8,128)(2,1)S(1)} %get-tuple-element.155), channel_id=1, source_target_pairs={{0,1},{1,0},{2,3},{3,2},{4,5},{5,4},{6,7},{7,6},{8,9},{9,8},{10,11... | collective-permute-start | bytes 307208 | tf_op jit(solution)/shard_map/ppermute | solution.py:58
  38.6 6.8 %collective-permute-start.11 = (bf16[400,128]{1,0:T(8,128)(2,1)S(1)}, bf16[400,128]{1,0:T(8,128)(2,1)S(1)}, u32[]{:S(2)}, u32[]{:S(2)}) collective-permute-start(bf16[400,128]{1,0:T(8,128)(2,1)S(1)} %sum_pair.11._), channel_id=1, source_target_pairs={{0,4},{2,6},{4,8},{6,10},{8,12},{10,14},{12,0},{14,2},{1,5},{3,7},... | collective-permute-start | bytes 307208 | tf_op jit(solution)/shard_map/ppermute | solution.py:49
  40.1 5.3 %collective-permute-start.12 = (bf16[400,128]{1,0:T(8,128)(2,1)S(1)}, bf16[400,128]{1,0:T(8,128)(2,1)S(1)}, u32[]{:S(2)}, u32[]{:S(2)}) collective-permute-start(bf16[400,128]{1,0:T(8,128)(2,1)S(1)} %get-tuple-element.161), channel_id=1, source_target_pairs={{0,1},{1,0},{2,3},{3,2},{4,5},{5,4},{6,7},{7,6},{8,9},{9,8},{10,11... | collective-permute-start | bytes 307208 | tf_op jit(solution)/shard_map/ppermute | solution.py:58
  45.5 1.8 %collective-permute-start.13 = (bf16[400,128]{1,0:T(8,128)(2,1)S(1)}, bf16[400,128]{1,0:T(8,128)(2,1)S(1)}, u32[]{:S(2)}, u32[]{:S(2)}) collective-permute-start(bf16[400,128]{1,0:T(8,128)(2,1)S(1)} %get-tuple-element.164.own0), channel_id=1, source_target_pairs={{0,1},{1,0},{2,3},{3,2},{4,5},{5,4},{6,7},{7,6},{8,9},{9,8},{10,11... | collective-permute-start | bytes 307208 | tf_op jit(solution)/shard_map/ppermute | solution.py:58
  45.6 6.2 %collective-permute-start.14 = (bf16[400,128]{1,0:T(8,128)(2,1)S(1)}, bf16[400,128]{1,0:T(8,128)(2,1)S(1)}, u32[]{:S(2)}, u32[]{:S(2)}) collective-permute-start(bf16[400,128]{1,0:T(8,128)(2,1)S(1)} %get-tuple-element.164.own0), channel_id=1, source_target_pairs={{0,10},{2,12},{4,14},{6,0},{8,2},{10,4},{12,6},{14,8},{1,11},{3,13... | collective-permute-start | bytes 307208 | tf_op jit(solution)/shard_map/ppermute | solution.py:49
  51.8 1.3 collective-permute-start.15
  54.5 1.4 %collective-permute-start.16 = (bf16[400,128]{1,0:T(8,128)(2,1)S(1)}, bf16[400,128]{1,0:T(8,128)(2,1)S(1)}, u32[]{:S(2)}, u32[]{:S(2)}) collective-permute-start(bf16[400,128]{1,0:T(8,128)(2,1)S(1)} %get-tuple-element.173), channel_id=1, source_target_pairs={{0,1},{1,0},{2,3},{3,2},{4,5},{5,4},{6,7},{7,6},{8,9},{9,8},{10,11... | collective-permute-start | bytes 307208 | tf_op jit(solution)/shard_map/ppermute | solution.py:58
  55.9 9.2 %collective-permute-start.17 = (bf16[400,128]{1,0:T(8,128)(2,1)S(1)}, bf16[400,128]{1,0:T(8,128)(2,1)S(1)}, u32[]{:S(2)}, u32[]{:S(2)}) collective-permute-start(bf16[400,128]{1,0:T(8,128)(2,1)S(1)} %sum_pair.13._), channel_id=1, source_target_pairs={{0,6},{2,8},{4,10},{6,12},{8,14},{10,0},{12,2},{14,4},{1,7},{3,9},... | collective-permute-start | bytes 307208 | tf_op jit(solution)/shard_map/ppermute | solution.py:49
  57.6 7.5 %collective-permute-start.18 = (bf16[400,128]{1,0:T(8,128)(2,1)S(1)}, bf16[400,128]{1,0:T(8,128)(2,1)S(1)}, u32[]{:S(2)}, u32[]{:S(2)}) collective-permute-start(bf16[400,128]{1,0:T(8,128)(2,1)S(1)} %get-tuple-element.179), channel_id=1, source_target_pairs={{0,1},{1,0},{2,3},{3,2},{4,5},{5,4},{6,7},{7,6},{8,9},{9,8},{10,11... | collective-permute-start | bytes 307208 | tf_op jit(solution)/shard_map/ppermute | solution.py:58
  65.2 1.5 %collective-permute-start.19 = (bf16[400,128]{1,0:T(8,128)(2,1)S(1)}, bf16[400,128]{1,0:T(8,128)(2,1)S(1)}, u32[]{:S(2)}, u32[]{:S(2)}) collective-permute-start(bf16[400,128]{1,0:T(8,128)(2,1)S(1)} %get-tuple-element.182.own0), channel_id=1, source_target_pairs={{0,1},{1,0},{2,3},{3,2},{4,5},{5,4},{6,7},{7,6},{8,9},{9,8},{10,11... | collective-permute-start | bytes 307208 | tf_op jit(solution)/shard_map/ppermute | solution.py:58
  65.3 7.0 %collective-permute-start.20 = (bf16[400,128]{1,0:T(8,128)(2,1)S(1)}, bf16[400,128]{1,0:T(8,128)(2,1)S(1)}, u32[]{:S(2)}, u32[]{:S(2)}) collective-permute-start(bf16[400,128]{1,0:T(8,128)(2,1)S(1)} %get-tuple-element.182.own0), channel_id=1, source_target_pairs={{0,8},{2,10},{4,12},{6,14},{8,0},{10,2},{12,4},{14,6},{1,9},{3,11}... | collective-permute-start | bytes 307208 | tf_op jit(solution)/shard_map/ppermute | solution.py:49
  72.4 1.3 collective-permute-start.21
  75.0 1.4 %collective-permute-start.22 = (bf16[400,128]{1,0:T(8,128)(2,1)S(1)}, bf16[400,128]{1,0:T(8,128)(2,1)S(1)}, u32[]{:S(2)}, u32[]{:S(2)}) collective-permute-start(bf16[400,128]{1,0:T(8,128)(2,1)S(1)} %get-tuple-element.191), channel_id=1, source_target_pairs={{0,1},{1,0},{2,3},{3,2},{4,5},{5,4},{6,7},{7,6},{8,9},{9,8},{10,11... | collective-permute-start | bytes 307208 | tf_op jit(solution)/shard_map/ppermute | solution.py:58
  76.5 8.0 %collective-permute-start.23 = (bf16[400,128]{1,0:T(8,128)(2,1)S(1)}, bf16[400,128]{1,0:T(8,128)(2,1)S(1)}, u32[]{:S(2)}, u32[]{:S(2)}) collective-permute-start(bf16[400,128]{1,0:T(8,128)(2,1)S(1)} %sum_pair.15._), channel_id=1, source_target_pairs={{0,8},{2,10},{4,12},{6,14},{8,0},{10,2},{12,4},{14,6},{1,9},{3,11}... | collective-permute-start | bytes 307208 | tf_op jit(solution)/shard_map/ppermute | solution.py:49
  78.0 6.4 %collective-permute-start.24 = (bf16[400,128]{1,0:T(8,128)(2,1)S(1)}, bf16[400,128]{1,0:T(8,128)(2,1)S(1)}, u32[]{:S(2)}, u32[]{:S(2)}) collective-permute-start(bf16[400,128]{1,0:T(8,128)(2,1)S(1)} %get-tuple-element.197), channel_id=1, source_target_pairs={{0,1},{1,0},{2,3},{3,2},{4,5},{5,4},{6,7},{7,6},{8,9},{9,8},{10,11... | collective-permute-start | bytes 307208 | tf_op jit(solution)/shard_map/ppermute | solution.py:58
  84.6 1.7 %collective-permute-start.26 = (bf16[400,128]{1,0:T(8,128)(2,1)S(1)}, bf16[400,128]{1,0:T(8,128)(2,1)S(1)}, u32[]{:S(2)}, u32[]{:S(2)}) collective-permute-start(bf16[400,128]{1,0:T(8,128)(2,1)S(1)} %get-tuple-element.200.own0), channel_id=1, source_target_pairs={{0,1},{1,0},{2,3},{3,2},{4,5},{5,4},{6,7},{7,6},{8,9},{9,8},{10,11... | collective-permute-start | bytes 307208 | tf_op jit(solution)/shard_map/ppermute | solution.py:58
  84.7 7.2 %collective-permute-start.25 = (bf16[400,128]{1,0:T(8,128)(2,1)S(1)}, bf16[400,128]{1,0:T(8,128)(2,1)S(1)}, u32[]{:S(2)}, u32[]{:S(2)}) collective-permute-start(bf16[400,128]{1,0:T(8,128)(2,1)S(1)} %get-tuple-element.200.own0), channel_id=1, source_target_pairs={{0,6},{2,8},{4,10},{6,12},{8,14},{10,0},{12,2},{14,4},{1,7},{3,9},... | collective-permute-start | bytes 307208 | tf_op jit(solution)/shard_map/ppermute | solution.py:49
  91.9 1.3 collective-permute-start.27
  95.7 1.8 %collective-permute-start.28 = (bf16[4,400,128]{2,1,0:T(8,128)(2,1)S(1)}, bf16[4,400,128]{2,1,0:T(8,128)(2,1)S(1)}, u32[]{:S(2)}, u32[]{:S(2)}) collective-permute-start(bf16[4,400,128]{2,1,0:T(8,128)(2,1)S(1)} %get-tuple-element.211.refs_0_), channel_id=1, source_target_pairs={{0,1},{1,0},{2,3},{3,2},{4,5},{5,4},{6,7},{7,6},{8,9},{9,8},{10,11... | collective-permute-start | bytes 1228808 | tf_op jit(solution)/shard_map/ppermute | solution.py:58
  96.6 4.1 %collective-permute-start.32 = (bf16[4,400,128]{2,1,0:T(8,128)(2,1)S(1)}, bf16[4,400,128]{2,1,0:T(8,128)(2,1)S(1)}, u32[]{:S(2)}, u32[]{:S(2)}) collective-permute-start(bf16[4,400,128]{2,1,0:T(8,128)(2,1)S(1)} %get-tuple-element.222), channel_id=1, source_target_pairs={{0,1},{1,0},{2,3},{3,2},{4,5},{5,4},{6,7},{7,6},{8,9},{9,8},{10,11... | collective-permute-start | bytes 1228808 | tf_op jit(solution)/shard_map/ppermute | solution.py:58
  97.6 5.4 %collective-permute-start.35 = (bf16[400,128]{1,0:T(8,128)(2,1)S(1)}, bf16[400,128]{1,0:T(8,128)(2,1)S(1)}, u32[]{:S(2)}, u32[]{:S(2)}) collective-permute-start(bf16[400,128]{1,0:T(8,128)(2,1)S(1)} %get-tuple-element.227), channel_id=1, source_target_pairs={{0,2},{2,0},{4,6},{6,4},{8,10},{10,8},{12,14},{14,12},{1,3},{3,1},... | collective-permute-start | bytes 307208 | tf_op jit(solution)/shard_map/ppermute | solution.py:54
  98.6 30.2 %copy-start = (f32[400,2048]{1,0:T(8,128)S(1)}, f32[400,2048]{1,0:T(8,128)}, u32[]{:S(2)}) copy-start(f32[400,2048]{1,0:T(8,128)} %rel_ref.7) | copy-start | bytes 9830404
  98.6 30.2 %copy-start.6 = (f32[2048]{0:T(1024)S(1)}, f32[2048]{0:T(1024)}, u32[]{:S(2)}) copy-start(f32[2048]{0:T(1024)} %param.12) | copy-start | bytes 24580
  99.0 4.0 %collective-permute-start.29 = (bf16[400,128]{1,0:T(8,128)(2,1)S(1)}, bf16[400,128]{1,0:T(8,128)(2,1)S(1)}, u32[]{:S(2)}, u32[]{:S(2)}) collective-permute-start(bf16[400,128]{1,0:T(8,128)(2,1)S(1)} %get-tuple-element.218), channel_id=1, source_target_pairs={{0,1},{1,0},{2,3},{3,2},{4,5},{5,4},{6,7},{7,6},{8,9},{9,8},{10,11... | collective-permute-start | bytes 307208 | tf_op jit(solution)/shard_map/ppermute | solution.py:58
  99.1 4.9 %collective-permute-start.30 = (bf16[400,128]{1,0:T(8,128)(2,1)S(1)}, bf16[400,128]{1,0:T(8,128)(2,1)S(1)}, u32[]{:S(2)}, u32[]{:S(2)}) collective-permute-start(bf16[400,128]{1,0:T(8,128)(2,1)S(1)} %get-tuple-element.220), channel_id=1, source_target_pairs={{0,1},{1,0},{2,3},{3,2},{4,5},{5,4},{6,7},{7,6},{8,9},{9,8},{10,11... | collective-permute-start | bytes 307208 | tf_op jit(solution)/shard_map/ppermute | solution.py:58
  99.6 8.6 %collective-permute-start.34 = (bf16[400,128]{1,0:T(8,128)(2,1)S(1)}, bf16[400,128]{1,0:T(8,128)(2,1)S(1)}, u32[]{:S(2)}, u32[]{:S(2)}) collective-permute-start(bf16[400,128]{1,0:T(8,128)(2,1)S(1)} %get-tuple-element.225), channel_id=1, source_target_pairs={{0,2},{2,0},{4,6},{6,4},{8,10},{10,8},{12,14},{14,12},{1,3},{3,1},... | collective-permute-start | bytes 307208 | tf_op jit(solution)/shard_map/ppermute | solution.py:54
  103.0 5.8 %collective-permute-start.36 = (bf16[400,128]{1,0:T(8,128)(2,1)S(1)}, bf16[400,128]{1,0:T(8,128)(2,1)S(1)}, u32[]{:S(2)}, u32[]{:S(2)}) collective-permute-start(bf16[400,128]{1,0:T(8,128)(2,1)S(1)} %sum_piece.4.refs_2_), channel_id=1, source_target_pairs={{0,4},{2,6},{4,0},{6,2},{8,12},{10,14},{12,8},{14,10},{1,5},{3,7},... | collective-permute-start | bytes 307208 | tf_op jit(solution)/shard_map/ppermute | solution.py:54
  103.1 7.1 %collective-permute-start.33 = (bf16[400,128]{1,0:T(8,128)(2,1)S(1)}, bf16[400,128]{1,0:T(8,128)(2,1)S(1)}, u32[]{:S(2)}, u32[]{:S(2)}) collective-permute-start(bf16[400,128]{1,0:T(8,128)(2,1)S(1)} %get-tuple-element.223), channel_id=1, source_target_pairs={{0,2},{2,0},{4,6},{6,4},{8,10},{10,8},{12,14},{14,12},{1,3},{3,1},... | collective-permute-start | bytes 307208 | tf_op jit(solution)/shard_map/ppermute | solution.py:54
  104.0 8.8 %collective-permute-start.31 = (bf16[400,128]{1,0:T(8,128)(2,1)S(1)}, bf16[400,128]{1,0:T(8,128)(2,1)S(1)}, u32[]{:S(2)}, u32[]{:S(2)}) collective-permute-start(bf16[400,128]{1,0:T(8,128)(2,1)S(1)} %sum_pair.17), channel_id=1, source_target_pairs={{0,10},{2,12},{4,14},{6,0},{8,2},{10,4},{12,6},{14,8},{1,11},{3,13... | collective-permute-start | bytes 307208 | tf_op jit(solution)/shard_map/ppermute | solution.py:49
  108.1 8.2 %collective-permute-start.38 = (bf16[400,128]{1,0:T(8,128)(2,1)S(1)}, bf16[400,128]{1,0:T(8,128)(2,1)S(1)}, u32[]{:S(2)}, u32[]{:S(2)}) collective-permute-start(bf16[400,128]{1,0:T(8,128)(2,1)S(1)} %get-tuple-element.212._), channel_id=1, source_target_pairs={{0,2},{2,0},{4,6},{6,4},{8,10},{10,8},{12,14},{14,12},{1,3},{3,1},... | collective-permute-start | bytes 307208 | tf_op jit(solution)/shard_map/ppermute | solution.py:54
  108.9 7.4 %collective-permute-start.39 = (bf16[400,128]{1,0:T(8,128)(2,1)S(1)}, bf16[400,128]{1,0:T(8,128)(2,1)S(1)}, u32[]{:S(2)}, u32[]{:S(2)}) collective-permute-start(bf16[400,128]{1,0:T(8,128)(2,1)S(1)} %sum_piece.5.refs_1_), channel_id=1, source_target_pairs={{0,8},{2,10},{4,12},{6,14},{8,0},{10,2},{12,4},{14,6},{1,9},{3,11}... | collective-permute-start | bytes 307208 | tf_op jit(solution)/shard_map/ppermute | solution.py:54
  110.2 6.6 %collective-permute-start.40 = (bf16[400,128]{1,0:T(8,128)(2,1)S(1)}, bf16[400,128]{1,0:T(8,128)(2,1)S(1)}, u32[]{:S(2)}, u32[]{:S(2)}) collective-permute-start(bf16[400,128]{1,0:T(8,128)(2,1)S(1)} %sum_piece.6.refs_5_), channel_id=1, source_target_pairs={{0,4},{2,6},{4,0},{6,2},{8,12},{10,14},{12,8},{14,10},{1,5},{3,7},... | collective-permute-start | bytes 307208 | tf_op jit(solution)/shard_map/ppermute | solution.py:54
  112.9 17.0 %collective-permute-start.37 = (f32[408,128]{1,0:T(8,128)S(1)}, f32[408,128]{1,0:T(8,128)S(1)}, u32[]{:S(2)}, u32[]{:S(2)}) collective-permute-start(f32[408,128]{1,0:T(8,128)S(1)} %update.11.mine), channel_id=1, source_target_pairs={{0,1},{1,0},{2,3},{3,2},{4,5},{5,4},{6,7},{7,6},{8,9},{9,8},{10,11... | collective-permute-start | bytes 626696 | tf_op jit(solution)/shard_map/ppermute | solution.py:58
  116.9 4.7 %collective-permute-start.46 = (bf16[400,128]{1,0:T(8,128)(2,1)S(1)}, bf16[400,128]{1,0:T(8,128)(2,1)S(1)}, u32[]{:S(2)}, u32[]{:S(2)}) collective-permute-start(bf16[400,128]{1,0:T(8,128)(2,1)S(1)} %sum_piece.7.refs_0_), channel_id=1, source_target_pairs={{0,4},{2,6},{4,0},{6,2},{8,12},{10,14},{12,8},{14,10},{1,5},{3,7},... | collective-permute-start | bytes 307208 | tf_op jit(solution)/shard_map/ppermute | solution.py:54
  117.6 9.2 %collective-permute-start.44 = (bf16[400,128]{1,0:T(8,128)(2,1)S(1)}, bf16[400,128]{1,0:T(8,128)(2,1)S(1)}, u32[]{:S(2)}, u32[]{:S(2)}) collective-permute-start(bf16[400,128]{1,0:T(8,128)(2,1)S(1)} %sum_piece.7.refs_0_), channel_id=1, source_target_pairs={{0,8},{2,10},{4,12},{6,14},{8,0},{10,2},{12,4},{14,6},{1,9},{3,11}... | collective-permute-start | bytes 307208 | tf_op jit(solution)/shard_map/ppermute | solution.py:54
  120.0 8.3 %collective-permute-start.42 = (bf16[400,128]{1,0:T(8,128)(2,1)S(1)}, bf16[400,128]{1,0:T(8,128)(2,1)S(1)}, u32[]{:S(2)}, u32[]{:S(2)}) collective-permute-start(bf16[400,128]{1,0:T(8,128)(2,1)S(1)} %sum_piece.7.refs_0_), channel_id=1, source_target_pairs={{0,12},{2,14},{4,8},{6,10},{8,4},{10,6},{12,0},{14,2},{1,13},{3,15... | collective-permute-start | bytes 307208 | tf_op jit(solution)/shard_map/ppermute | solution.py:54
  121.3 9.5 %collective-permute-start.41 = (bf16[400,128]{1,0:T(8,128)(2,1)S(1)}, bf16[400,128]{1,0:T(8,128)(2,1)S(1)}, u32[]{:S(2)}, u32[]{:S(2)}) collective-permute-start(bf16[400,128]{1,0:T(8,128)(2,1)S(1)} %sum_piece.7.refs_0_), channel_id=1, source_target_pairs={{0,2},{2,0},{4,6},{6,4},{8,10},{10,8},{12,14},{14,12},{1,3},{3,1},... | collective-permute-start | bytes 307208 | tf_op jit(solution)/shard_map/ppermute | solution.py:54
  121.6 9.2 %collective-permute-start.47 = (bf16[400,128]{1,0:T(8,128)(2,1)S(1)}, bf16[400,128]{1,0:T(8,128)(2,1)S(1)}, u32[]{:S(2)}, u32[]{:S(2)}) collective-permute-start(bf16[400,128]{1,0:T(8,128)(2,1)S(1)} %collective-permute-done.46.refs_3_), channel_id=1, source_target_pairs={{0,2},{2,0},{4,6},{6,4},{8,10},{10,8},{12,14},{14,12},{1,3},{3,1},... | collective-permute-start | bytes 307208 | tf_op jit(solution)/shard_map/ppermute | solution.py:54
  126.8 4.8 %collective-permute-start.45 = (bf16[400,128]{1,0:T(8,128)(2,1)S(1)}, bf16[400,128]{1,0:T(8,128)(2,1)S(1)}, u32[]{:S(2)}, u32[]{:S(2)}) collective-permute-start(bf16[400,128]{1,0:T(8,128)(2,1)S(1)} %collective-permute-done.44.refs_2_), channel_id=1, source_target_pairs={{0,2},{2,0},{4,6},{6,4},{8,10},{10,8},{12,14},{14,12},{1,3},{3,1},... | collective-permute-start | bytes 307208 | tf_op jit(solution)/shard_map/ppermute | solution.py:54
  128.3 4.7 %collective-permute-start.43 = (bf16[400,128]{1,0:T(8,128)(2,1)S(1)}, bf16[400,128]{1,0:T(8,128)(2,1)S(1)}, u32[]{:S(2)}, u32[]{:S(2)}) collective-permute-start(bf16[400,128]{1,0:T(8,128)(2,1)S(1)} %collective-permute-done.42.refs_1_), channel_id=1, source_target_pairs={{0,2},{2,0},{4,6},{6,4},{8,10},{10,8},{12,14},{14,12},{1,3},{3,1},... | collective-permute-start | bytes 307208 | tf_op jit(solution)/shard_map/ppermute | solution.py:54
  130.7 2.3 %collective-permute-start.49 = (bf16[4,400,128]{2,1,0:T(8,128)(2,1)S(1)}, bf16[4,400,128]{2,1,0:T(8,128)(2,1)S(1)}, u32[]{:S(2)}, u32[]{:S(2)}) collective-permute-start(bf16[4,400,128]{2,1,0:T(8,128)(2,1)S(1)} %stacked.3), channel_id=1, source_target_pairs={{0,1},{1,0},{2,3},{3,2},{4,5},{5,4},{6,7},{7,6},{8,9},{9,8},{10,11... | collective-permute-start | bytes 1228808 | tf_op jit(solution)/shard_map/ppermute | solution.py:58
  133.0 1.8 %collective-permute-start.48 = (bf16[4,400,128]{2,1,0:T(8,128)(2,1)S(1)}, bf16[4,400,128]{2,1,0:T(8,128)(2,1)S(1)}, u32[]{:S(2)}, u32[]{:S(2)}) collective-permute-start(bf16[4,400,128]{2,1,0:T(8,128)(2,1)S(1)} %stacked.2), channel_id=1, source_target_pairs={{0,1},{1,0},{2,3},{3,2},{4,5},{5,4},{6,7},{7,6},{8,9},{9,8},{10,11... | collective-permute-start | bytes 1228808 | tf_op jit(solution)/shard_map/ppermute | solution.py:58

commit v7 on v5

--- a/solution.py
+++ b/solution.py
@@ -425,7 +425,8 @@
     for lo in range(0, slots, width):
         at = slice(lo, lo + width)
         n_hot = n_hot_ref[:, at]
-        scores = mm(high[at], n_hot) + mm(low[at], n_hot)
+        both = jnp.concatenate([high[at], low[at]], axis=1)
+        scores = mm(both, jnp.concatenate([n_hot, n_hot], axis=0))
         weight = (jax.nn.sigmoid(scores) * mask_ref[:, at]).astype(BF)
         w_ref[:, at] = weight
         positive = jax.nn.sigmoid(-products[at]) * v_hot_t_ref[at].astype(F32)

time: 135 us -> 135 us (level)
  transfers between devices with their start and end apart: 50 -> 50, of which waited for: 28 -> 29; matrix products, arithmetic and copies ran while one was open for 0% -> 0% of each run, Pallas kernels for 20% -> 20%
where the time goes in v7:
time: 135 us
  waiting for transfers between devices  61.8 us (46%)
  Pallas kernels  42.5 us (31%)
  starting transfers between devices  28.9 us (21%)
  between operations  1.54 us (1%)
    ppermute x10, waiting for transfers between devices, shifted(): return lax.ppermute(x, 'dom', [(i, (i + by) % n) for i in range(n)])  36.4 us
    ppermute x14, starting transfers between devices, swapped(): return lax.ppermute(x, 'dom', [(i, i ^ bits) for i in range(n)])  14.3 us
    ppermute x14, waiting for transfers between devices, swapped(): return lax.ppermute(x, 'dom', [(i, i ^ bits) for i in range(n)])  13.7 us
    ppermute x26, waiting for transfers between devices, across(): return lax.ppermute(x, 'edge', [(0, 1), (1, 0)])  11.7 us
    ppermute x10, starting transfers between devices, shifted(): return lax.ppermute(x, 'dom', [(i, (i + by) % n) for i in range(n)])  9.92 us
    pallas_call x5, Pallas kernels, relsum(): pl.pallas_call(functools.partial(relsum_kernel, t, acc is None), in_specs...  6.21 us
    pallas_call x4, Pallas kernels, source_grad(): pl.pallas_call(functools.partial(source_grad_kernel, t, shape), in_specs=...  5.9 us
    pallas_call x4, Pallas kernels, target_grad(): pl.pallas_call(target_kernel, in_specs=[vmem()] * 8, out_specs=[vmem()] *...  5.49 us
  transfers between devices with their start and end apart: 50, of which 29 were waited for; matrix products, arithmetic and copies ran while one was open for 0% of the time, Pallas kernels for 20%

profile of v7, /device:TPU:0, one launch (start us, length us, event | category | flops | bytes accessed | tf_op | source)
XLA Modules:
  0.0 134.7 jit_solution(10534130965576701891)
XLA Ops:
  0.6 5.4 %first_round.1 = (f32[400,128]{1,0:T(8,128)S(1)}, bf16[400,128]{1,0:T(8,128)(2,1)S(1)}, bf16[400,512]{1,0:T(8,128)(2,1)S(1)}, bf16[400,2048]{1,0:T(8,128)(2,1)S(...) custom-call(s32[4,6]{1,0:T(4,128)} %bitcast.6, s32[4,6]{1,0:T(4,128)} %bitcast.17, s32[6,4,128]{2,1,0:T(4,128)} %src_ref.11, ...), custom_call_target="tpu_custom_call" | custom-call | flops 1258291200 | bytes 6553600 | tf_op jit(solution)/shard_map/first_round/pallas_call | solution.py:304
  6.6 0.9 collective-permute-done.refs_3_
  8.1 5.7 %collective-permute-start.2 = (bf16[400,128]{1,0:T(8,128)(2,1)S(1)}, bf16[400,128]{1,0:T(8,128)(2,1)S(1)}, u32[]{:S(2)}, u32[]{:S(2)}) collective-permute-start(bf16[400,128]{1,0:T(8,128)(2,1)S(1)} %get-tuple-element.127.own0), channel_id=1, source_target_pairs={{0,14},{2,0},{4,2},{6,4},{8,6},{10,8},{12,10},{14,12},{1,15},{3,1}... | collective-permute-start | bytes 307208 | tf_op jit(solution)/shard_map/ppermute | solution.py:49
  13.8 1.0 relvec.5.rel_ref
  14.9 1.0 relsum.5.refs_1_.refs_0_
  16.0 0.9 source_side.5
  17.3 1.0 collective-permute-done.3.far1
  18.2 1.4 %target_grad.4 = (f32[400,128]{1,0:T(8,128)S(1)}, bf16[400,128]{1,0:T(8,128)(2,1)S(1)}, bf16[128,512]{1,0:T(8,128)(2,1)S(1)}) custom-call(f32[512,128]{1,0:T(8,128)S(1)} %near_products.4.near, bf16[400,128]{1,0:T(8,128)(2,1)S(1)} %collective-permute-done.3.far1, bf16[400,512]{1,0:T(8,128)(2,1)S(1)} %get-tuple-element.130.refs_0_.query_ref, ...), custom_call_target="tpu_custom_call" | custom-call | flops 104857600 | bytes 2457600 | tf_op jit(solution)/shard_map/target_grad/pallas_call | solution.py:443
  19.8 1.2 collective-permute-done.4.b_ref
  21.1 1.5 %source_grad.4 = (f32[400,128]{1,0:T(8,128)S(1)}, bf16[400,128]{1,0:T(8,128)(2,1)S(1)}, bf16[400,512]{1,0:T(8,128)(2,1)S(1)}) custom-call(s32[4,6]{1,0:T(4,128)S(1)} %bitcast.8, s32[4,6]{1,0:T(4,128)S(1)} %bitcast.19, bf16[400,128]{1,0:T(8,128)(2,1)S(1)} %sum_pair.9._, bf16[400,128]{1,0:T(8,128)(2,1)S(1)} %held.5.far0, ...), custom_call_target="tpu_custom_call" | custom-call | flops 204800 | bytes 204800 | tf_op jit(solution)/shard_map/source_grad/pallas_call | solution.py:475
  22.8 1.0 relvec.6.refs_4_.rel_ref
  23.8 5.2 %collective-permute-done.5.b_ref = bf16[400,128]{1,0:T(8,128)(2,1)S(1)} collective-permute-done((bf16[400,128]{1,0:T(8,128)(2,1)S(1)}, bf16[400,128]{1,0:T(8,128)(2,1)S(1)}, u32[]{:S(2)}, u32[]{:S(2)}) %collective-permute-start.5) | collective-permute-done | bytes 102432 | tf_op jit(solution)/shard_map/ppermute | solution.py:49
  29.7 1.3 relsum.6.refs_1_.refs_0_
  31.0 0.9 source_side.6
  31.9 2.6 %collective-permute-done.8.x_ref = bf16[400,128]{1,0:T(8,128)(2,1)S(1)} collective-permute-done((bf16[400,128]{1,0:T(8,128)(2,1)S(1)}, bf16[400,128]{1,0:T(8,128)(2,1)S(1)}, u32[]{:S(2)}, u32[]{:S(2)}) %collective-permute-start.8) | collective-permute-done | bytes 102432 | tf_op jit(solution)/shard_map/ppermute | solution.py:49
  34.8 1.0 collective-permute-done.9.far1
  35.8 1.4 %target_grad.5 = (f32[400,128]{1,0:T(8,128)S(1)}, bf16[400,128]{1,0:T(8,128)(2,1)S(1)}, bf16[128,512]{1,0:T(8,128)(2,1)S(1)}) custom-call(f32[512,128]{1,0:T(8,128)S(1)} %near_products.5.near, bf16[400,128]{1,0:T(8,128)(2,1)S(1)} %collective-permute-done.9.far1, bf16[400,512]{1,0:T(8,128)(2,1)S(1)} %get-tuple-element.148.refs_0_.query_ref, ...), custom_call_target="tpu_custom_call" | custom-call | flops 104857600 | bytes 2457600 | tf_op jit(solution)/shard_map/target_grad/pallas_call | solution.py:443
  37.4 1.2 collective-permute-done.10.b_ref
  38.7 1.5 %source_grad.5 = (f32[400,128]{1,0:T(8,128)S(1)}, bf16[400,128]{1,0:T(8,128)(2,1)S(1)}, bf16[400,512]{1,0:T(8,128)(2,1)S(1)}) custom-call(s32[4,6]{1,0:T(4,128)S(1)} %bitcast.10, s32[4,6]{1,0:T(4,128)S(1)} %bitcast.21, bf16[400,128]{1,0:T(8,128)(2,1)S(1)} %sum_pair.11._, bf16[400,128]{1,0:T(8,128)(2,1)S(1)} %held.6.far0, ...), custom_call_target="tpu_custom_call" | custom-call | flops 204800 | bytes 204800 | tf_op jit(solution)/shard_map/source_grad/pallas_call | solution.py:475
  40.4 1.0 relvec.7.refs_4_.rel_ref
  41.4 4.0 %collective-permute-done.11.b_ref = bf16[400,128]{1,0:T(8,128)(2,1)S(1)} collective-permute-done((bf16[400,128]{1,0:T(8,128)(2,1)S(1)}, bf16[400,128]{1,0:T(8,128)(2,1)S(1)}, u32[]{:S(2)}, u32[]{:S(2)}) %collective-permute-start.11) | collective-permute-done | bytes 102432 | tf_op jit(solution)/shard_map/ppermute | solution.py:49
  46.1 1.3 relsum.7.refs_1_.refs_0_
  47.4 0.9 source_side.7
  48.3 3.5 %collective-permute-done.14.x_ref = bf16[400,128]{1,0:T(8,128)(2,1)S(1)} collective-permute-done((bf16[400,128]{1,0:T(8,128)(2,1)S(1)}, bf16[400,128]{1,0:T(8,128)(2,1)S(1)}, u32[]{:S(2)}, u32[]{:S(2)}) %collective-permute-start.14) | collective-permute-done | bytes 102432 | tf_op jit(solution)/shard_map/ppermute | solution.py:49
  52.1 1.0 collective-permute-done.15.far1
  53.1 1.4 %target_grad.6 = (f32[400,128]{1,0:T(8,128)S(1)}, bf16[400,128]{1,0:T(8,128)(2,1)S(1)}, bf16[128,512]{1,0:T(8,128)(2,1)S(1)}) custom-call(f32[512,128]{1,0:T(8,128)S(1)} %near_products.6.near, bf16[400,128]{1,0:T(8,128)(2,1)S(1)} %collective-permute-done.15.far1, bf16[400,512]{1,0:T(8,128)(2,1)S(1)} %get-tuple-element.166.refs_0_.query_ref, ...), custom_call_target="tpu_custom_call" | custom-call | flops 104857600 | bytes 2457600 | tf_op jit(solution)/shard_map/target_grad/pallas_call | solution.py:443
  54.7 1.2 collective-permute-done.16.b_ref
  56.2 1.5 %source_grad.6 = (f32[400,128]{1,0:T(8,128)S(1)}, bf16[400,128]{1,0:T(8,128)(2,1)S(1)}, bf16[400,512]{1,0:T(8,128)(2,1)S(1)}) custom-call(s32[4,6]{1,0:T(4,128)S(1)} %bitcast.12, s32[4,6]{1,0:T(4,128)S(1)} %bitcast.23, bf16[400,128]{1,0:T(8,128)(2,1)S(1)} %sum_pair.13._, bf16[400,128]{1,0:T(8,128)(2,1)S(1)} %held.7.far0, ...), custom_call_target="tpu_custom_call" | custom-call | flops 204800 | bytes 204800 | tf_op jit(solution)/shard_map/source_grad/pallas_call | solution.py:475
  57.9 1.0 relvec.8.refs_4_.rel_ref
  58.9 6.2 %collective-permute-done.17.b_ref = bf16[400,128]{1,0:T(8,128)(2,1)S(1)} collective-permute-done((bf16[400,128]{1,0:T(8,128)(2,1)S(1)}, bf16[400,128]{1,0:T(8,128)(2,1)S(1)}, u32[]{:S(2)}, u32[]{:S(2)}) %collective-permute-start.17) | collective-permute-done | bytes 102432 | tf_op jit(solution)/shard_map/ppermute | solution.py:49
  65.4 1.3 relsum.8.refs_1_.refs_0_
  66.7 0.9 source_side.8
  67.6 4.8 %collective-permute-done.20.x_ref = bf16[400,128]{1,0:T(8,128)(2,1)S(1)} collective-permute-done((bf16[400,128]{1,0:T(8,128)(2,1)S(1)}, bf16[400,128]{1,0:T(8,128)(2,1)S(1)}, u32[]{:S(2)}, u32[]{:S(2)}) %collective-permute-start.20) | collective-permute-done | bytes 102432 | tf_op jit(solution)/shard_map/ppermute | solution.py:49
  72.7 1.0 collective-permute-done.21.far1
  73.7 1.4 %target_grad.7 = (f32[400,128]{1,0:T(8,128)S(1)}, bf16[400,128]{1,0:T(8,128)(2,1)S(1)}, bf16[128,512]{1,0:T(8,128)(2,1)S(1)}) custom-call(f32[512,128]{1,0:T(8,128)S(1)} %near_products.7.near, bf16[400,128]{1,0:T(8,128)(2,1)S(1)} %collective-permute-done.21.far1, bf16[400,512]{1,0:T(8,128)(2,1)S(1)} %get-tuple-element.184.refs_0_.query_ref, ...), custom_call_target="tpu_custom_call" | custom-call | flops 104857600 | bytes 2457600 | tf_op jit(solution)/shard_map/target_grad/pallas_call | solution.py:443
  75.3 1.2 collective-permute-done.22.b_ref
  76.5 1.5 %source_grad.7 = (f32[400,128]{1,0:T(8,128)S(1)}, bf16[400,128]{1,0:T(8,128)(2,1)S(1)}, bf16[400,512]{1,0:T(8,128)(2,1)S(1)}) custom-call(s32[4,6]{1,0:T(4,128)S(1)} %bitcast.14, s32[4,6]{1,0:T(4,128)S(1)} %bitcast.25, bf16[400,128]{1,0:T(8,128)(2,1)S(1)} %sum_pair.15._, bf16[400,128]{1,0:T(8,128)(2,1)S(1)} %held.8.far0, ...), custom_call_target="tpu_custom_call" | custom-call | flops 204800 | bytes 204800 | tf_op jit(solution)/shard_map/source_grad/pallas_call | solution.py:475
  78.2 1.0 relvec.9.refs_4_.rel_ref
  79.3 5.2 %collective-permute-done.23.b_ref = bf16[400,128]{1,0:T(8,128)(2,1)S(1)} collective-permute-done((bf16[400,128]{1,0:T(8,128)(2,1)S(1)}, bf16[400,128]{1,0:T(8,128)(2,1)S(1)}, u32[]{:S(2)}, u32[]{:S(2)}) %collective-permute-start.23) | collective-permute-done | bytes 102432 | tf_op jit(solution)/shard_map/ppermute | solution.py:49
  85.0 1.3 relsum.9.refs_1_.acc_ref
  86.9 5.0 %collective-permute-done.25.x_ref = bf16[400,128]{1,0:T(8,128)(2,1)S(1)} collective-permute-done((bf16[400,128]{1,0:T(8,128)(2,1)S(1)}, bf16[400,128]{1,0:T(8,128)(2,1)S(1)}, u32[]{:S(2)}, u32[]{:S(2)}) %collective-permute-start.25) | collective-permute-done | bytes 102432 | tf_op jit(solution)/shard_map/ppermute | solution.py:49
  91.9 1.3 collective-permute-done.27.far1
  93.2 1.8 %last_terms.1 = (bf16[400,512]{1,0:T(8,128)(2,1)S(1)}, bf16[400,512]{1,0:T(8,128)(2,1)S(1)}, bf16[400,512]{1,0:T(8,128)(2,1)S(1)}) custom-call(s32[4,6]{1,0:T(4,128)S(1)} %bitcast.16, s32[4,6]{1,0:T(4,128)S(1)} %bitcast.27, bf16[400,128]{1,0:T(8,128)(2,1)S(1)} %held.9.far0, bf16[400,128]{1,0:T(8,128)(2,1)S(1)} %collective-permute-done.27.far1, ...), custom_call_target="tpu_custom_call" | custom-call | flops 157286400 | bytes 2457600 | tf_op jit(solution)/shard_map/last_terms/pallas_call | solution.py:505
  97.7 1.0 collective-permute-start.34
  99.6 1.1 collective-permute-start.33
  100.7 0.9 collective-permute-start.38
  101.6 1.4 %collective-permute-done.34.refs_0_ = bf16[400,128]{1,0:T(8,128)(2,1)S(1)} collective-permute-done((bf16[400,128]{1,0:T(8,128)(2,1)S(1)}, bf16[400,128]{1,0:T(8,128)(2,1)S(1)}, u32[]{:S(2)}, u32[]{:S(2)}) %collective-permute-start.34) | collective-permute-done | bytes 102432 | tf_op jit(solution)/shard_map/ppermute | solution.py:54
  103.2 2.5 %collective-permute-start.31 = (bf16[400,128]{1,0:T(8,128)(2,1)S(1)}, bf16[400,128]{1,0:T(8,128)(2,1)S(1)}, u32[]{:S(2)}, u32[]{:S(2)}) collective-permute-start(bf16[400,128]{1,0:T(8,128)(2,1)S(1)} %sum_pair.17), channel_id=1, source_target_pairs={{0,10},{2,12},{4,14},{6,0},{8,2},{10,4},{12,6},{14,8},{1,11},{3,13... | collective-permute-start | bytes 307208 | tf_op jit(solution)/shard_map/ppermute | solution.py:49
  105.7 1.9 %collective-permute-start.37 = (bf16[400,128]{1,0:T(8,128)(2,1)S(1)}, bf16[400,128]{1,0:T(8,128)(2,1)S(1)}, u32[]{:S(2)}, u32[]{:S(2)}) collective-permute-start(bf16[400,128]{1,0:T(8,128)(2,1)S(1)} %get-tuple-element.212._), channel_id=1, source_target_pairs={{0,2},{2,0},{4,6},{6,4},{8,10},{10,8},{12,14},{14,12},{1,3},{3,1},... | collective-permute-start | bytes 307208 | tf_op jit(solution)/shard_map/ppermute | solution.py:54
  107.6 2.1 %collective-permute-done.38.refs_0_ = bf16[400,128]{1,0:T(8,128)(2,1)S(1)} collective-permute-done((bf16[400,128]{1,0:T(8,128)(2,1)S(1)}, bf16[400,128]{1,0:T(8,128)(2,1)S(1)}, u32[]{:S(2)}, u32[]{:S(2)}) %collective-permute-start.38) | collective-permute-done | bytes 102432 | tf_op jit(solution)/shard_map/ppermute | solution.py:54
  109.9 1.0 collective-permute-start.40
  111.4 3.1 %collective-permute-done.39.refs_1_ = bf16[400,128]{1,0:T(8,128)(2,1)S(1)} collective-permute-done((bf16[400,128]{1,0:T(8,128)(2,1)S(1)}, bf16[400,128]{1,0:T(8,128)(2,1)S(1)}, u32[]{:S(2)}, u32[]{:S(2)}) %collective-permute-start.39) | collective-permute-done | bytes 102432 | tf_op jit(solution)/shard_map/ppermute | solution.py:54
  114.5 1.1 collective-permute-done.40.refs_2_
  115.7 2.9 %collective-permute-start.46 = (bf16[400,128]{1,0:T(8,128)(2,1)S(1)}, bf16[400,128]{1,0:T(8,128)(2,1)S(1)}, u32[]{:S(2)}, u32[]{:S(2)}) collective-permute-start(bf16[400,128]{1,0:T(8,128)(2,1)S(1)} %sum_piece.7.refs_0_), channel_id=1, source_target_pairs={{0,4},{2,6},{4,0},{6,2},{8,12},{10,14},{12,8},{14,10},{1,5},{3,7},... | collective-permute-start | bytes 307208 | tf_op jit(solution)/shard_map/ppermute | solution.py:54
  118.8 2.2 %collective-permute-start.42 = (bf16[400,128]{1,0:T(8,128)(2,1)S(1)}, bf16[400,128]{1,0:T(8,128)(2,1)S(1)}, u32[]{:S(2)}, u32[]{:S(2)}) collective-permute-start(bf16[400,128]{1,0:T(8,128)(2,1)S(1)} %sum_piece.7.refs_0_), channel_id=1, source_target_pairs={{0,12},{2,14},{4,8},{6,10},{8,4},{10,6},{12,0},{14,2},{1,13},{3,15... | collective-permute-start | bytes 307208 | tf_op jit(solution)/shard_map/ppermute | solution.py:54
  121.0 1.1 collective-permute-done.46.refs_3_
  122.2 0.9 collective-permute-start.47
  123.1 2.8 %collective-permute-done.44.refs_2_ = bf16[400,128]{1,0:T(8,128)(2,1)S(1)} collective-permute-done((bf16[400,128]{1,0:T(8,128)(2,1)S(1)}, bf16[400,128]{1,0:T(8,128)(2,1)S(1)}, u32[]{:S(2)}, u32[]{:S(2)}) %collective-permute-start.44) | collective-permute-done | bytes 102432 | tf_op jit(solution)/shard_map/ppermute | solution.py:54
  125.9 2.0 %collective-permute-start.43 = (bf16[400,128]{1,0:T(8,128)(2,1)S(1)}, bf16[400,128]{1,0:T(8,128)(2,1)S(1)}, u32[]{:S(2)}, u32[]{:S(2)}) collective-permute-start(bf16[400,128]{1,0:T(8,128)(2,1)S(1)} %collective-permute-done.42.refs_1_), channel_id=1, source_target_pairs={{0,2},{2,0},{4,6},{6,4},{8,10},{10,8},{12,14},{14,12},{1,3},{3,1},... | collective-permute-start | bytes 307208 | tf_op jit(solution)/shard_map/ppermute | solution.py:54
  127.9 1.0 relnew.3
  128.9 0.8 whole_partition.1
  130.5 1.1 collective-permute-done.43.refs_1_.refs_2_
  131.7 1.4 %relnew.4 = (f32[400,2048]{1,0:T(8,128)}, f32[1,2048]{1,0:T(1,128)S(1)}) custom-call(f32[400,2048]{1,0:T(8,128)S(1)} %copy-done, f32[1,2048]{1,0:T(1,128)S(1)} %bitcast.30, bf16[4,400,128]{2,1,0:T(8,128)(2,1)S(1)} %collective-permute-done.49.refs_0_, bf16[400,128]{1,0:T(8,128)(2,1)S(1)} %collective-permute-done.41.refs_0_.refs_1_, ...), custom_call_target="tpu_custom_call", output_to_operand_aliasing={{0}: (7, {})} | custom-call | flops 400 | bytes 400 | tf_op jit(solution)/shard_map/relnew/pallas_call | solution.py:762
  133.5 1.0 relnew.5
  (113 shorter events, 13.4 us)
Async XLA Ops:
  0.6 13.2 %copy-start.1 = (s32[6,4,128]{2,1,0:T(4,128)S(1)}, s32[6,4,128]{2,1,0:T(4,128)}, u32[]{:S(2)}) copy-start(s32[6,4,128]{2,1,0:T(4,128)} %ids_ref.25) | copy-start | bytes 36868
  6.1 9.9 %copy-start.2 = (s32[6,4,128]{2,1,0:T(4,128)S(1)}, s32[6,4,128]{2,1,0:T(4,128)}, u32[]{:S(2)}) copy-start(s32[6,4,128]{2,1,0:T(4,128)} %src_ref.11) | copy-start | bytes 36868
  6.1 9.9 %copy-start.3 = (s32[6,4,128]{2,1,0:T(4,128)S(1)}, s32[6,4,128]{2,1,0:T(4,128)}, u32[]{:S(2)}) copy-start(s32[6,4,128]{2,1,0:T(4,128)} %dst_ref.11) | copy-start | bytes 36868
  6.1 9.9 %copy-start.4 = (s32[6,4]{0,1:T(4,128)S(1)}, s32[6,4]{0,1:T(4,128)}, u32[]{:S(2)}) copy-start(s32[6,4]{0,1:T(4,128)} %param.16) | copy-start | bytes 292
  6.1 9.9 %copy-start.5 = (s32[6,4]{0,1:T(4,128)S(1)}, s32[6,4]{0,1:T(4,128)}, u32[]{:S(2)}) copy-start(s32[6,4]{0,1:T(4,128)} %param.17) | copy-start | bytes 292
  6.1 1.5 %collective-permute-start = (bf16[400,128]{1,0:T(8,128)(2,1)S(1)}, bf16[400,128]{1,0:T(8,128)(2,1)S(1)}, u32[]{:S(2)}, u32[]{:S(2)}) collective-permute-start(bf16[400,128]{1,0:T(8,128)(2,1)S(1)} %get-tuple-element.124), channel_id=1, source_target_pairs={{0,1},{1,0},{2,3},{3,2},{4,5},{5,4},{6,7},{7,6},{8,9},{9,8},{10,11... | collective-permute-start | bytes 307208 | tf_op jit(solution)/shard_map/ppermute | solution.py:58
  7.7 8.2 %collective-permute-start.1 = (bf16[400,128]{1,0:T(8,128)(2,1)S(1)}, bf16[400,128]{1,0:T(8,128)(2,1)S(1)}, u32[]{:S(2)}, u32[]{:S(2)}) collective-permute-start(bf16[400,128]{1,0:T(8,128)(2,1)S(1)} %get-tuple-element.127.own0), channel_id=1, source_target_pairs={{0,1},{1,0},{2,3},{3,2},{4,5},{5,4},{6,7},{7,6},{8,9},{9,8},{10,11... | collective-permute-start | bytes 307208 | tf_op jit(solution)/shard_map/ppermute | solution.py:58
  8.1 8.7 %collective-permute-start.2 = (bf16[400,128]{1,0:T(8,128)(2,1)S(1)}, bf16[400,128]{1,0:T(8,128)(2,1)S(1)}, u32[]{:S(2)}, u32[]{:S(2)}) collective-permute-start(bf16[400,128]{1,0:T(8,128)(2,1)S(1)} %get-tuple-element.127.own0), channel_id=1, source_target_pairs={{0,14},{2,0},{4,2},{6,4},{8,6},{10,8},{12,10},{14,12},{1,15},{3,1}... | collective-permute-start | bytes 307208 | tf_op jit(solution)/shard_map/ppermute | solution.py:49
  16.9 1.4 %collective-permute-start.3 = (bf16[400,128]{1,0:T(8,128)(2,1)S(1)}, bf16[400,128]{1,0:T(8,128)(2,1)S(1)}, u32[]{:S(2)}, u32[]{:S(2)}) collective-permute-start(bf16[400,128]{1,0:T(8,128)(2,1)S(1)} %held.5.far0), channel_id=1, source_target_pairs={{0,1},{1,0},{2,3},{3,2},{4,5},{5,4},{6,7},{7,6},{8,9},{9,8},{10,11... | collective-permute-start | bytes 307208 | tf_op jit(solution)/shard_map/ppermute | solution.py:58
  19.6 1.4 %collective-permute-start.4 = (bf16[400,128]{1,0:T(8,128)(2,1)S(1)}, bf16[400,128]{1,0:T(8,128)(2,1)S(1)}, u32[]{:S(2)}, u32[]{:S(2)}) collective-permute-start(bf16[400,128]{1,0:T(8,128)(2,1)S(1)} %get-tuple-element.137), channel_id=1, source_target_pairs={{0,1},{1,0},{2,3},{3,2},{4,5},{5,4},{6,7},{7,6},{8,9},{9,8},{10,11... | collective-permute-start | bytes 307208 | tf_op jit(solution)/shard_map/ppermute | solution.py:58
  21.0 8.0 %collective-permute-start.5 = (bf16[400,128]{1,0:T(8,128)(2,1)S(1)}, bf16[400,128]{1,0:T(8,128)(2,1)S(1)}, u32[]{:S(2)}, u32[]{:S(2)}) collective-permute-start(bf16[400,128]{1,0:T(8,128)(2,1)S(1)} %sum_pair.9._), channel_id=1, source_target_pairs={{0,2},{2,4},{4,6},{6,8},{8,10},{10,12},{12,14},{14,0},{1,3},{3,5},... | collective-permute-start | bytes 307208 | tf_op jit(solution)/shard_map/ppermute | solution.py:49
  22.6 6.4 %collective-permute-start.6 = (bf16[400,128]{1,0:T(8,128)(2,1)S(1)}, bf16[400,128]{1,0:T(8,128)(2,1)S(1)}, u32[]{:S(2)}, u32[]{:S(2)}) collective-permute-start(bf16[400,128]{1,0:T(8,128)(2,1)S(1)} %get-tuple-element.143), channel_id=1, source_target_pairs={{0,1},{1,0},{2,3},{3,2},{4,5},{5,4},{6,7},{7,6},{8,9},{9,8},{10,11... | collective-permute-start | bytes 307208 | tf_op jit(solution)/shard_map/ppermute | solution.py:58
  29.1 1.8 %collective-permute-start.7 = (bf16[400,128]{1,0:T(8,128)(2,1)S(1)}, bf16[400,128]{1,0:T(8,128)(2,1)S(1)}, u32[]{:S(2)}, u32[]{:S(2)}) collective-permute-start(bf16[400,128]{1,0:T(8,128)(2,1)S(1)} %get-tuple-element.146.own0), channel_id=1, source_target_pairs={{0,1},{1,0},{2,3},{3,2},{4,5},{5,4},{6,7},{7,6},{8,9},{9,8},{10,11... | collective-permute-start | bytes 307208 | tf_op jit(solution)/shard_map/ppermute | solution.py:58
  29.2 5.3 %collective-permute-start.8 = (bf16[400,128]{1,0:T(8,128)(2,1)S(1)}, bf16[400,128]{1,0:T(8,128)(2,1)S(1)}, u32[]{:S(2)}, u32[]{:S(2)}) collective-permute-start(bf16[400,128]{1,0:T(8,128)(2,1)S(1)} %get-tuple-element.146.own0), channel_id=1, source_target_pairs={{0,12},{2,14},{4,0},{6,2},{8,4},{10,6},{12,8},{14,10},{1,13},{3,15... | collective-permute-start | bytes 307208 | tf_op jit(solution)/shard_map/ppermute | solution.py:49
  34.5 1.3 collective-permute-start.9
  37.2 1.4 %collective-permute-start.10 = (bf16[400,128]{1,0:T(8,128)(2,1)S(1)}, bf16[400,128]{1,0:T(8,128)(2,1)S(1)}, u32[]{:S(2)}, u32[]{:S(2)}) collective-permute-start(bf16[400,128]{1,0:T(8,128)(2,1)S(1)} %get-tuple-element.155), channel_id=1, source_target_pairs={{0,1},{1,0},{2,3},{3,2},{4,5},{5,4},{6,7},{7,6},{8,9},{9,8},{10,11... | collective-permute-start | bytes 307208 | tf_op jit(solution)/shard_map/ppermute | solution.py:58
  38.6 6.8 %collective-permute-start.11 = (bf16[400,128]{1,0:T(8,128)(2,1)S(1)}, bf16[400,128]{1,0:T(8,128)(2,1)S(1)}, u32[]{:S(2)}, u32[]{:S(2)}) collective-permute-start(bf16[400,128]{1,0:T(8,128)(2,1)S(1)} %sum_pair.11._), channel_id=1, source_target_pairs={{0,4},{2,6},{4,8},{6,10},{8,12},{10,14},{12,0},{14,2},{1,5},{3,7},... | collective-permute-start | bytes 307208 | tf_op jit(solution)/shard_map/ppermute | solution.py:49
  40.1 5.3 %collective-permute-start.12 = (bf16[400,128]{1,0:T(8,128)(2,1)S(1)}, bf16[400,128]{1,0:T(8,128)(2,1)S(1)}, u32[]{:S(2)}, u32[]{:S(2)}) collective-permute-start(bf16[400,128]{1,0:T(8,128)(2,1)S(1)} %get-tuple-element.161), channel_id=1, source_target_pairs={{0,1},{1,0},{2,3},{3,2},{4,5},{5,4},{6,7},{7,6},{8,9},{9,8},{10,11... | collective-permute-start | bytes 307208 | tf_op jit(solution)/shard_map/ppermute | solution.py:58
  45.5 1.8 %collective-permute-start.13 = (bf16[400,128]{1,0:T(8,128)(2,1)S(1)}, bf16[400,128]{1,0:T(8,128)(2,1)S(1)}, u32[]{:S(2)}, u32[]{:S(2)}) collective-permute-start(bf16[400,128]{1,0:T(8,128)(2,1)S(1)} %get-tuple-element.164.own0), channel_id=1, source_target_pairs={{0,1},{1,0},{2,3},{3,2},{4,5},{5,4},{6,7},{7,6},{8,9},{9,8},{10,11... | collective-permute-start | bytes 307208 | tf_op jit(solution)/shard_map/ppermute | solution.py:58
  45.6 6.2 %collective-permute-start.14 = (bf16[400,128]{1,0:T(8,128)(2,1)S(1)}, bf16[400,128]{1,0:T(8,128)(2,1)S(1)}, u32[]{:S(2)}, u32[]{:S(2)}) collective-permute-start(bf16[400,128]{1,0:T(8,128)(2,1)S(1)} %get-tuple-element.164.own0), channel_id=1, source_target_pairs={{0,10},{2,12},{4,14},{6,0},{8,2},{10,4},{12,6},{14,8},{1,11},{3,13... | collective-permute-start | bytes 307208 | tf_op jit(solution)/shard_map/ppermute | solution.py:49
  51.8 1.3 collective-permute-start.15
  54.5 1.4 %collective-permute-start.16 = (bf16[400,128]{1,0:T(8,128)(2,1)S(1)}, bf16[400,128]{1,0:T(8,128)(2,1)S(1)}, u32[]{:S(2)}, u32[]{:S(2)}) collective-permute-start(bf16[400,128]{1,0:T(8,128)(2,1)S(1)} %get-tuple-element.173), channel_id=1, source_target_pairs={{0,1},{1,0},{2,3},{3,2},{4,5},{5,4},{6,7},{7,6},{8,9},{9,8},{10,11... | collective-permute-start | bytes 307208 | tf_op jit(solution)/shard_map/ppermute | solution.py:58
  55.9 9.2 %collective-permute-start.17 = (bf16[400,128]{1,0:T(8,128)(2,1)S(1)}, bf16[400,128]{1,0:T(8,128)(2,1)S(1)}, u32[]{:S(2)}, u32[]{:S(2)}) collective-permute-start(bf16[400,128]{1,0:T(8,128)(2,1)S(1)} %sum_pair.13._), channel_id=1, source_target_pairs={{0,6},{2,8},{4,10},{6,12},{8,14},{10,0},{12,2},{14,4},{1,7},{3,9},... | collective-permute-start | bytes 307208 | tf_op jit(solution)/shard_map/ppermute | solution.py:49
  57.7 7.5 %collective-permute-start.18 = (bf16[400,128]{1,0:T(8,128)(2,1)S(1)}, bf16[400,128]{1,0:T(8,128)(2,1)S(1)}, u32[]{:S(2)}, u32[]{:S(2)}) collective-permute-start(bf16[400,128]{1,0:T(8,128)(2,1)S(1)} %get-tuple-element.179), channel_id=1, source_target_pairs={{0,1},{1,0},{2,3},{3,2},{4,5},{5,4},{6,7},{7,6},{8,9},{9,8},{10,11... | collective-permute-start | bytes 307208 | tf_op jit(solution)/shard_map/ppermute | solution.py:58
  65.3 1.5 %collective-permute-start.19 = (bf16[400,128]{1,0:T(8,128)(2,1)S(1)}, bf16[400,128]{1,0:T(8,128)(2,1)S(1)}, u32[]{:S(2)}, u32[]{:S(2)}) collective-permute-start(bf16[400,128]{1,0:T(8,128)(2,1)S(1)} %get-tuple-element.182.own0), channel_id=1, source_target_pairs={{0,1},{1,0},{2,3},{3,2},{4,5},{5,4},{6,7},{7,6},{8,9},{9,8},{10,11... | collective-permute-start | bytes 307208 | tf_op jit(solution)/shard_map/ppermute | solution.py:58
  65.3 7.0 %collective-permute-start.20 = (bf16[400,128]{1,0:T(8,128)(2,1)S(1)}, bf16[400,128]{1,0:T(8,128)(2,1)S(1)}, u32[]{:S(2)}, u32[]{:S(2)}) collective-permute-start(bf16[400,128]{1,0:T(8,128)(2,1)S(1)} %get-tuple-element.182.own0), channel_id=1, source_target_pairs={{0,8},{2,10},{4,12},{6,14},{8,0},{10,2},{12,4},{14,6},{1,9},{3,11}... | collective-permute-start | bytes 307208 | tf_op jit(solution)/shard_map/ppermute | solution.py:49
  72.4 1.3 collective-permute-start.21
  75.1 1.4 %collective-permute-start.22 = (bf16[400,128]{1,0:T(8,128)(2,1)S(1)}, bf16[400,128]{1,0:T(8,128)(2,1)S(1)}, u32[]{:S(2)}, u32[]{:S(2)}) collective-permute-start(bf16[400,128]{1,0:T(8,128)(2,1)S(1)} %get-tuple-element.191), channel_id=1, source_target_pairs={{0,1},{1,0},{2,3},{3,2},{4,5},{5,4},{6,7},{7,6},{8,9},{9,8},{10,11... | collective-permute-start | bytes 307208 | tf_op jit(solution)/shard_map/ppermute | solution.py:58
  76.5 8.0 %collective-permute-start.23 = (bf16[400,128]{1,0:T(8,128)(2,1)S(1)}, bf16[400,128]{1,0:T(8,128)(2,1)S(1)}, u32[]{:S(2)}, u32[]{:S(2)}) collective-permute-start(bf16[400,128]{1,0:T(8,128)(2,1)S(1)} %sum_pair.15._), channel_id=1, source_target_pairs={{0,8},{2,10},{4,12},{6,14},{8,0},{10,2},{12,4},{14,6},{1,9},{3,11}... | collective-permute-start | bytes 307208 | tf_op jit(solution)/shard_map/ppermute | solution.py:49
  78.0 6.4 %collective-permute-start.24 = (bf16[400,128]{1,0:T(8,128)(2,1)S(1)}, bf16[400,128]{1,0:T(8,128)(2,1)S(1)}, u32[]{:S(2)}, u32[]{:S(2)}) collective-permute-start(bf16[400,128]{1,0:T(8,128)(2,1)S(1)} %get-tuple-element.197), channel_id=1, source_target_pairs={{0,1},{1,0},{2,3},{3,2},{4,5},{5,4},{6,7},{7,6},{8,9},{9,8},{10,11... | collective-permute-start | bytes 307208 | tf_op jit(solution)/shard_map/ppermute | solution.py:58
  84.6 1.7 %collective-permute-start.26 = (bf16[400,128]{1,0:T(8,128)(2,1)S(1)}, bf16[400,128]{1,0:T(8,128)(2,1)S(1)}, u32[]{:S(2)}, u32[]{:S(2)}) collective-permute-start(bf16[400,128]{1,0:T(8,128)(2,1)S(1)} %get-tuple-element.200.own0), channel_id=1, source_target_pairs={{0,1},{1,0},{2,3},{3,2},{4,5},{5,4},{6,7},{7,6},{8,9},{9,8},{10,11... | collective-permute-start | bytes 307208 | tf_op jit(solution)/shard_map/ppermute | solution.py:58
  84.7 7.2 %collective-permute-start.25 = (bf16[400,128]{1,0:T(8,128)(2,1)S(1)}, bf16[400,128]{1,0:T(8,128)(2,1)S(1)}, u32[]{:S(2)}, u32[]{:S(2)}) collective-permute-start(bf16[400,128]{1,0:T(8,128)(2,1)S(1)} %get-tuple-element.200.own0), channel_id=1, source_target_pairs={{0,6},{2,8},{4,10},{6,12},{8,14},{10,0},{12,2},{14,4},{1,7},{3,9},... | collective-permute-start | bytes 307208 | tf_op jit(solution)/shard_map/ppermute | solution.py:49
  91.9 1.3 collective-permute-start.27
  95.7 1.8 %collective-permute-start.28 = (bf16[4,400,128]{2,1,0:T(8,128)(2,1)S(1)}, bf16[4,400,128]{2,1,0:T(8,128)(2,1)S(1)}, u32[]{:S(2)}, u32[]{:S(2)}) collective-permute-start(bf16[4,400,128]{2,1,0:T(8,128)(2,1)S(1)} %get-tuple-element.211.refs_0_), channel_id=1, source_target_pairs={{0,1},{1,0},{2,3},{3,2},{4,5},{5,4},{6,7},{7,6},{8,9},{9,8},{10,11... | collective-permute-start | bytes 1228808 | tf_op jit(solution)/shard_map/ppermute | solution.py:58
  96.6 4.1 %collective-permute-start.32 = (bf16[4,400,128]{2,1,0:T(8,128)(2,1)S(1)}, bf16[4,400,128]{2,1,0:T(8,128)(2,1)S(1)}, u32[]{:S(2)}, u32[]{:S(2)}) collective-permute-start(bf16[4,400,128]{2,1,0:T(8,128)(2,1)S(1)} %get-tuple-element.222), channel_id=1, source_target_pairs={{0,1},{1,0},{2,3},{3,2},{4,5},{5,4},{6,7},{7,6},{8,9},{9,8},{10,11... | collective-permute-start | bytes 1228808 | tf_op jit(solution)/shard_map/ppermute | solution.py:58
  97.6 30.3 %copy-start = (f32[400,2048]{1,0:T(8,128)S(1)}, f32[400,2048]{1,0:T(8,128)}, u32[]{:S(2)}) copy-start(f32[400,2048]{1,0:T(8,128)} %rel_ref.7) | copy-start | bytes 9830404
  97.6 30.3 %copy-start.6 = (f32[2048]{0:T(1024)S(1)}, f32[2048]{0:T(1024)}, u32[]{:S(2)}) copy-start(f32[2048]{0:T(1024)} %param.12) | copy-start | bytes 24580
  97.7 5.4 %collective-permute-start.34 = (bf16[400,128]{1,0:T(8,128)(2,1)S(1)}, bf16[400,128]{1,0:T(8,128)(2,1)S(1)}, u32[]{:S(2)}, u32[]{:S(2)}) collective-permute-start(bf16[400,128]{1,0:T(8,128)(2,1)S(1)} %get-tuple-element.225), channel_id=1, source_target_pairs={{0,2},{2,0},{4,6},{6,4},{8,10},{10,8},{12,14},{14,12},{1,3},{3,1},... | collective-permute-start | bytes 307208 | tf_op jit(solution)/shard_map/ppermute | solution.py:54
  99.0 4.0 %collective-permute-start.29 = (bf16[400,128]{1,0:T(8,128)(2,1)S(1)}, bf16[400,128]{1,0:T(8,128)(2,1)S(1)}, u32[]{:S(2)}, u32[]{:S(2)}) collective-permute-start(bf16[400,128]{1,0:T(8,128)(2,1)S(1)} %get-tuple-element.218), channel_id=1, source_target_pairs={{0,1},{1,0},{2,3},{3,2},{4,5},{5,4},{6,7},{7,6},{8,9},{9,8},{10,11... | collective-permute-start | bytes 307208 | tf_op jit(solution)/shard_map/ppermute | solution.py:58
  99.1 4.1 %collective-permute-start.30 = (bf16[400,128]{1,0:T(8,128)(2,1)S(1)}, bf16[400,128]{1,0:T(8,128)(2,1)S(1)}, u32[]{:S(2)}, u32[]{:S(2)}) collective-permute-start(bf16[400,128]{1,0:T(8,128)(2,1)S(1)} %get-tuple-element.220), channel_id=1, source_target_pairs={{0,1},{1,0},{2,3},{3,2},{4,5},{5,4},{6,7},{7,6},{8,9},{9,8},{10,11... | collective-permute-start | bytes 307208 | tf_op jit(solution)/shard_map/ppermute | solution.py:58
  99.6 10.3 %collective-permute-start.33 = (bf16[400,128]{1,0:T(8,128)(2,1)S(1)}, bf16[400,128]{1,0:T(8,128)(2,1)S(1)}, u32[]{:S(2)}, u32[]{:S(2)}) collective-permute-start(bf16[400,128]{1,0:T(8,128)(2,1)S(1)} %get-tuple-element.223), channel_id=1, source_target_pairs={{0,2},{2,0},{4,6},{6,4},{8,10},{10,8},{12,14},{14,12},{1,3},{3,1},... | collective-permute-start | bytes 307208 | tf_op jit(solution)/shard_map/ppermute | solution.py:54
  100.7 9.0 %collective-permute-start.38 = (bf16[400,128]{1,0:T(8,128)(2,1)S(1)}, bf16[400,128]{1,0:T(8,128)(2,1)S(1)}, u32[]{:S(2)}, u32[]{:S(2)}) collective-permute-start(bf16[400,128]{1,0:T(8,128)(2,1)S(1)} %get-tuple-element.230), channel_id=1, source_target_pairs={{0,2},{2,0},{4,6},{6,4},{8,10},{10,8},{12,14},{14,12},{1,3},{3,1},... | collective-permute-start | bytes 307208 | tf_op jit(solution)/shard_map/ppermute | solution.py:54
  103.1 6.8 %collective-permute-start.35 = (bf16[400,128]{1,0:T(8,128)(2,1)S(1)}, bf16[400,128]{1,0:T(8,128)(2,1)S(1)}, u32[]{:S(2)}, u32[]{:S(2)}) collective-permute-start(bf16[400,128]{1,0:T(8,128)(2,1)S(1)} %sum_piece.4), channel_id=1, source_target_pairs={{0,4},{2,6},{4,0},{6,2},{8,12},{10,14},{12,8},{14,10},{1,5},{3,7},... | collective-permute-start | bytes 307208 | tf_op jit(solution)/shard_map/ppermute | solution.py:54
  103.2 7.7 %collective-permute-start.31 = (bf16[400,128]{1,0:T(8,128)(2,1)S(1)}, bf16[400,128]{1,0:T(8,128)(2,1)S(1)}, u32[]{:S(2)}, u32[]{:S(2)}) collective-permute-start(bf16[400,128]{1,0:T(8,128)(2,1)S(1)} %sum_pair.17), channel_id=1, source_target_pairs={{0,10},{2,12},{4,14},{6,0},{8,2},{10,4},{12,6},{14,8},{1,11},{3,13... | collective-permute-start | bytes 307208 | tf_op jit(solution)/shard_map/ppermute | solution.py:49
  105.7 5.7 %collective-permute-start.37 = (bf16[400,128]{1,0:T(8,128)(2,1)S(1)}, bf16[400,128]{1,0:T(8,128)(2,1)S(1)}, u32[]{:S(2)}, u32[]{:S(2)}) collective-permute-start(bf16[400,128]{1,0:T(8,128)(2,1)S(1)} %get-tuple-element.212._), channel_id=1, source_target_pairs={{0,2},{2,0},{4,6},{6,4},{8,10},{10,8},{12,14},{14,12},{1,3},{3,1},... | collective-permute-start | bytes 307208 | tf_op jit(solution)/shard_map/ppermute | solution.py:54
  109.8 4.7 %collective-permute-start.39 = (bf16[400,128]{1,0:T(8,128)(2,1)S(1)}, bf16[400,128]{1,0:T(8,128)(2,1)S(1)}, u32[]{:S(2)}, u32[]{:S(2)}) collective-permute-start(bf16[400,128]{1,0:T(8,128)(2,1)S(1)} %sum_piece.6), channel_id=1, source_target_pairs={{0,4},{2,6},{4,0},{6,2},{8,12},{10,14},{12,8},{14,10},{1,5},{3,7},... | collective-permute-start | bytes 307208 | tf_op jit(solution)/shard_map/ppermute | solution.py:54
  109.9 5.7 %collective-permute-start.40 = (bf16[400,128]{1,0:T(8,128)(2,1)S(1)}, bf16[400,128]{1,0:T(8,128)(2,1)S(1)}, u32[]{:S(2)}, u32[]{:S(2)}) collective-permute-start(bf16[400,128]{1,0:T(8,128)(2,1)S(1)} %sum_piece.5.refs_5_), channel_id=1, source_target_pairs={{0,8},{2,10},{4,12},{6,14},{8,0},{10,2},{12,4},{14,6},{1,9},{3,11}... | collective-permute-start | bytes 307208 | tf_op jit(solution)/shard_map/ppermute | solution.py:54
  111.0 17.9 %collective-permute-start.36 = (f32[408,128]{1,0:T(8,128)S(1)}, f32[408,128]{1,0:T(8,128)S(1)}, u32[]{:S(2)}, u32[]{:S(2)}) collective-permute-start(f32[408,128]{1,0:T(8,128)S(1)} %update.11.mine), channel_id=1, source_target_pairs={{0,1},{1,0},{2,3},{3,2},{4,5},{5,4},{6,7},{7,6},{8,9},{9,8},{10,11... | collective-permute-start | bytes 626696 | tf_op jit(solution)/shard_map/ppermute | solution.py:58
  115.7 6.5 %collective-permute-start.46 = (bf16[400,128]{1,0:T(8,128)(2,1)S(1)}, bf16[400,128]{1,0:T(8,128)(2,1)S(1)}, u32[]{:S(2)}, u32[]{:S(2)}) collective-permute-start(bf16[400,128]{1,0:T(8,128)(2,1)S(1)} %sum_piece.7.refs_0_), channel_id=1, source_target_pairs={{0,4},{2,6},{4,0},{6,2},{8,12},{10,14},{12,8},{14,10},{1,5},{3,7},... | collective-permute-start | bytes 307208 | tf_op jit(solution)/shard_map/ppermute | solution.py:54
  118.6 7.3 %collective-permute-start.44 = (bf16[400,128]{1,0:T(8,128)(2,1)S(1)}, bf16[400,128]{1,0:T(8,128)(2,1)S(1)}, u32[]{:S(2)}, u32[]{:S(2)}) collective-permute-start(bf16[400,128]{1,0:T(8,128)(2,1)S(1)} %sum_piece.7.refs_0_), channel_id=1, source_target_pairs={{0,8},{2,10},{4,12},{6,14},{8,0},{10,2},{12,4},{14,6},{1,9},{3,11}... | collective-permute-start | bytes 307208 | tf_op jit(solution)/shard_map/ppermute | solution.py:54
  118.8 7.0 %collective-permute-start.42 = (bf16[400,128]{1,0:T(8,128)(2,1)S(1)}, bf16[400,128]{1,0:T(8,128)(2,1)S(1)}, u32[]{:S(2)}, u32[]{:S(2)}) collective-permute-start(bf16[400,128]{1,0:T(8,128)(2,1)S(1)} %sum_piece.7.refs_0_), channel_id=1, source_target_pairs={{0,12},{2,14},{4,8},{6,10},{8,4},{10,6},{12,0},{14,2},{1,13},{3,15... | collective-permute-start | bytes 307208 | tf_op jit(solution)/shard_map/ppermute | solution.py:54
  121.0 8.8 %collective-permute-start.41 = (bf16[400,128]{1,0:T(8,128)(2,1)S(1)}, bf16[400,128]{1,0:T(8,128)(2,1)S(1)}, u32[]{:S(2)}, u32[]{:S(2)}) collective-permute-start(bf16[400,128]{1,0:T(8,128)(2,1)S(1)} %sum_piece.7.refs_0_), channel_id=1, source_target_pairs={{0,2},{2,0},{4,6},{6,4},{8,10},{10,8},{12,14},{14,12},{1,3},{3,1},... | collective-permute-start | bytes 307208 | tf_op jit(solution)/shard_map/ppermute | solution.py:54
  122.2 7.7 %collective-permute-start.47 = (bf16[400,128]{1,0:T(8,128)(2,1)S(1)}, bf16[400,128]{1,0:T(8,128)(2,1)S(1)}, u32[]{:S(2)}, u32[]{:S(2)}) collective-permute-start(bf16[400,128]{1,0:T(8,128)(2,1)S(1)} %collective-permute-done.46.refs_3_), channel_id=1, source_target_pairs={{0,2},{2,0},{4,6},{6,4},{8,10},{10,8},{12,14},{14,12},{1,3},{3,1},... | collective-permute-start | bytes 307208 | tf_op jit(solution)/shard_map/ppermute | solution.py:54
  125.9 4.7 %collective-permute-start.45 = (bf16[400,128]{1,0:T(8,128)(2,1)S(1)}, bf16[400,128]{1,0:T(8,128)(2,1)S(1)}, u32[]{:S(2)}, u32[]{:S(2)}) collective-permute-start(bf16[400,128]{1,0:T(8,128)(2,1)S(1)} %collective-permute-done.44.refs_2_), channel_id=1, source_target_pairs={{0,2},{2,0},{4,6},{6,4},{8,10},{10,8},{12,14},{14,12},{1,3},{3,1},... | collective-permute-start | bytes 307208 | tf_op jit(solution)/shard_map/ppermute | solution.py:54
  125.9 5.8 %collective-permute-start.43 = (bf16[400,128]{1,0:T(8,128)(2,1)S(1)}, bf16[400,128]{1,0:T(8,128)(2,1)S(1)}, u32[]{:S(2)}, u32[]{:S(2)}) collective-permute-start(bf16[400,128]{1,0:T(8,128)(2,1)S(1)} %collective-permute-done.42.refs_1_), channel_id=1, source_target_pairs={{0,2},{2,0},{4,6},{6,4},{8,10},{10,8},{12,14},{14,12},{1,3},{3,1},... | collective-permute-start | bytes 307208 | tf_op jit(solution)/shard_map/ppermute | solution.py:54
  129.8 1.9 %collective-permute-start.49 = (bf16[4,400,128]{2,1,0:T(8,128)(2,1)S(1)}, bf16[4,400,128]{2,1,0:T(8,128)(2,1)S(1)}, u32[]{:S(2)}, u32[]{:S(2)}) collective-permute-start(bf16[4,400,128]{2,1,0:T(8,128)(2,1)S(1)} %stacked.3), channel_id=1, source_target_pairs={{0,1},{1,0},{2,3},{3,2},{4,5},{5,4},{6,7},{7,6},{8,9},{9,8},{10,11... | collective-permute-start | bytes 1228808 | tf_op jit(solution)/shard_map/ppermute | solution.py:58
  131.6 1.8 %collective-permute-start.48 = (bf16[4,400,128]{2,1,0:T(8,128)(2,1)S(1)}, bf16[4,400,128]{2,1,0:T(8,128)(2,1)S(1)}, u32[]{:S(2)}, u32[]{:S(2)}) collective-permute-start(bf16[4,400,128]{2,1,0:T(8,128)(2,1)S(1)} %stacked.2), channel_id=1, source_target_pairs={{0,1},{1,0},{2,3},{3,2},{4,5},{5,4},{6,7},{7,6},{8,9},{9,8},{10,11... | collective-permute-start | bytes 1228808 | tf_op jit(solution)/shard_map/ppermute | solution.py:58
